TPU v7x, 32 devices: a whole 2x2x4 slice. The times are simulated.
32 devices in a mesh: dp: 4 (over z), expert: 8 (over y, x, core).
Axes of the slice: x: 2, y: 2, z: 4, core: 2. Of those that a mesh axis runs over, the one named last changes fastest.
Arguments:
- tokens: bfloat16 [4096, 2048], P(('dp', 'expert')), may hold values from -6 to 6
- routes: int32 [4096, 8], P(('dp', 'expert')), may hold values from 0 to 31, all different within a row; in each aligned block of 128 rows (0 to 127, 128 to 255, ...) at most 38 rows name the same one
- prefix_len: int32 [4], P('dp'), may hold values from 102 to 512
- query_weight: bfloat16 [2048, 4096], P('dp', 'expert'), may hold values from -0.125 to 0.125
- key_matrix: bfloat16 [2048, 512], P('dp', 'expert'), may hold values from -0.125 to 0.125
- value_matrix: bfloat16 [2048, 512], P('dp', 'expert'), may hold values from -0.125 to 0.125
- out_weight: bfloat16 [4096, 2048], P('dp', 'expert'), may hold values from -2 to 2
- router_weight: bfloat16 [2048, 32], P('dp', 'expert'), may hold values from -0.0625 to 0.0625
- attention_gain: float32 [2048], replicated, may hold values from 0.25 to 1.75
- mixture_gain: float32 [2048], replicated, may hold values from 0.25 to 1.75
- query_gain: float32 [128], replicated, may hold values from 0.25 to 1.75
- key_norm_gain: float32 [128], replicated, may hold values from 0.25 to 1.75
- expert_gate: bfloat16 [32, 2048, 768], P(('dp', 'expert')), may hold values from -0.125 to 0.125
- expert_up: bfloat16 [32, 2048, 768], P(('dp', 'expert')), may hold values from -0.125 to 0.125
- expert_down: bfloat16 [32, 768, 2048], P(('dp', 'expert')), may hold values from -0.875 to 0.875
- cotangent: bfloat16 [4096, 2048], P(('dp', 'expert')), may hold values from -6 to 6
Outputs:
- layer_out: bfloat16 [4096, 2048], P(('dp', 'expert'))
- input_grad: float32 [4096, 2048], P(('dp', 'expert'))
- query_weight_grad: float32 [2048, 4096], P('dp', 'expert')
- key_weight_grad: float32 [2048, 512], P('dp', 'expert')
- value_weight_grad: float32 [2048, 512], P('dp', 'expert')
- out_weight_grad: float32 [4096, 2048], P('dp', 'expert')
- router_grad: float32 [2048, 32], P('dp', 'expert')
- attention_gain_grad: float32 [2048], replicated
- mixture_gain_grad: float32 [2048], replicated
- query_gain_grad: float32 [128], replicated
- key_gain_grad: float32 [128], replicated
- expert_gate_grad: float32 [32, 2048, 768], P(('dp', 'expert'))
- expert_up_grad: float32 [32, 2048, 768], P(('dp', 'expert'))
- expert_down_grad: float32 [32, 768, 2048], P(('dp', 'expert'))
Inputs may be any that keep to these rules, and one draw needn't show every extreme that they name: `routes`: each row names 8 different experts. In the rows of one device no expert is named more than 38 times, and in every draw the rows of some device name some expert exactly 38 times.
All inputs are finite; a program needn't handle non-finite values.
Results may differ from a plain program's by a relative error of at most 0.025.
Values may be sent and summed in bfloat16 or wider, within the bound.
No kernel may reach another device: no remote copies, remote signals or barrier semaphores. Data moves between devices by JAX's collectives and lax.ppermute only.
A program may use at most 256 MiB of HBM per device.

v0:
```python
import math

import jax
import jax.numpy as jnp
from jax import lax
from jax.sharding import PartitionSpec as P

MODEL_WIDTH = 2048
QUERY_HEADS = 32
KEY_VALUE_HEADS = 4
HEAD_SIZE = 128
TOP = 8
EXP_DEV = 1


EPS = 1e-06
ROTARY_BASE = 1000000.0
VERY_NEGATIVE = -1e30


def head_normalize(source, gain_row):
    scaling = lax.rsqrt(jnp.mean(source * source, axis=-1, keepdims=True) + EPS)
    return (source * scaling * gain_row, scaling)


def normalize_back(upstream, source, scaling, gain_row):
    unit_rows = source * scaling
    weighted = upstream * gain_row
    inner_mean = jnp.mean(weighted * unit_rows, axis=-1, keepdims=True)
    return (scaling * (weighted - unit_rows * inner_mean), upstream * unit_rows)


def rotary(offset, span_length):
    half_dim = HEAD_SIZE // 2
    frequency = jnp.power(ROTARY_BASE, -jnp.arange(half_dim, dtype=jnp.float32) * 2.0 / HEAD_SIZE)
    places = (offset + jnp.arange(span_length, dtype=jnp.int32)).astype(jnp.float32)
    angles = places[:, None] * frequency[None, :]
    cosine_lookup = jnp.concatenate([jnp.cos(angles), jnp.cos(angles)], axis=-1)[:, None, :]
    sine_lookup = jnp.concatenate([jnp.sin(angles), jnp.sin(angles)], axis=-1)[:, None, :]
    return (cosine_lookup, sine_lookup)


def rotary_apply(source, cosine_lookup, sine_lookup):
    half_dim = source.shape[-1] // 2
    front_half = source[..., :half_dim]
    back_half = source[..., half_dim:]
    return source * cosine_lookup + jnp.concatenate([-back_half, front_half], axis=-1) * sine_lookup


def rotate_back(upstream, cosine_lookup, sine_lookup):
    half_dim = upstream.shape[-1] // 2
    turned = upstream * sine_lookup
    return upstream * cosine_lookup + jnp.concatenate(
        [turned[..., half_dim:], -turned[..., :half_dim]], axis=-1
    )


def shards(
    tokens,
    routes,
    prefix_len,
    query_weight,
    key_matrix,
    value_matrix,
    out_weight,
    router_weight,
    attention_gain,
    mixture_gain,
    query_gain,
    key_norm_gain,
    expert_gate,
    expert_up,
    expert_down,
    cotangent,
):
    resident_tokens = tokens.shape[0]
    head_groups = QUERY_HEADS // KEY_VALUE_HEADS
    softmax_scale = HEAD_SIZE ** (-0.5)
    query_rows, key_rows, value_rows, out_rows, router_rows = (
        lax.all_gather(query_weight, "dp", axis=0, tiled=True),
        lax.all_gather(key_matrix, "dp", axis=0, tiled=True),
        lax.all_gather(value_matrix, "dp", axis=0, tiled=True),
        lax.all_gather(out_weight, "dp", axis=0, tiled=True),
        lax.all_gather(router_weight, "dp", axis=0, tiled=True),
    )
    query_full, key_full, value_full, out_full, router_full = (
        lax.all_gather(query_rows, "expert", axis=1, tiled=True),
        lax.all_gather(key_rows, "expert", axis=1, tiled=True),
        lax.all_gather(value_rows, "expert", axis=1, tiled=True),
        lax.all_gather(out_rows, "expert", axis=1, tiled=True),
        lax.all_gather(router_rows, "expert", axis=1, tiled=True),
    )
    experts_all = router_full.shape[1]
    dp_count = lax.axis_size("dp")
    expert_count = lax.axis_size("expert")
    devices = dp_count * expert_count
    capacity = max(2, 6 * resident_tokens * TOP // (5 * experts_all))
    residual_in = tokens.astype(jnp.float32)
    normed, scale_attention = head_normalize(residual_in, attention_gain)
    normed_low = normed.astype(jnp.bfloat16)
    query_raw = jnp.dot(normed_low, query_full, preferred_element_type=jnp.float32).reshape(
        resident_tokens, QUERY_HEADS, HEAD_SIZE
    )
    key_unnormed = jnp.dot(normed_low, key_full, preferred_element_type=jnp.float32).reshape(
        resident_tokens, KEY_VALUE_HEADS, HEAD_SIZE
    )
    value_raw = jnp.dot(normed_low, value_full, preferred_element_type=jnp.float32).reshape(
        resident_tokens, KEY_VALUE_HEADS, HEAD_SIZE
    )
    offset = lax.axis_index("expert") * resident_tokens
    cosine_lookup, sine_lookup = rotary(offset, resident_tokens)
    query_normed, scale_query = head_normalize(query_raw, query_gain)
    query_narrow = (
        rotary_apply(query_normed, cosine_lookup, sine_lookup)
        .astype(jnp.bfloat16)
        .reshape(resident_tokens, KEY_VALUE_HEADS, head_groups, HEAD_SIZE)
    )
    key_normed, scale_key = head_normalize(key_unnormed, key_norm_gain)
    key_low = rotary_apply(key_normed, cosine_lookup, sine_lookup).astype(jnp.bfloat16)
    value_narrow = value_raw.astype(jnp.bfloat16)
    every_key, every_value = (
        lax.all_gather(key_low, "expert", axis=0, tiled=True),
        lax.all_gather(value_narrow, "expert", axis=0, tiled=True),
    )
    span_length = every_key.shape[0]
    segment_rows = math.gcd(span_length, 768)
    segment_list = span_length // segment_rows
    key_segments = every_key.reshape(segment_list, segment_rows, KEY_VALUE_HEADS, HEAD_SIZE)
    value_segments = every_value.reshape(segment_list, segment_rows, KEY_VALUE_HEADS, HEAD_SIZE)
    piece_starts = jnp.arange(segment_list, dtype=jnp.int32) * segment_rows
    query_place = offset + jnp.arange(resident_tokens, dtype=jnp.int32)
    prefix = prefix_len[0]

    def scores_of(key_piece, piece_start):
        raw_scores = (
            jnp.einsum(
                "thgd,shd->hgts", query_narrow, key_piece, preferred_element_type=jnp.float32
            )
            * softmax_scale
        )
        key_place = piece_start + jnp.arange(segment_rows, dtype=jnp.int32)
        allowed = (key_place[None, :] <= query_place[:, None]) | (key_place[None, :] < prefix)
        return (raw_scores, allowed)

    def running_stats(running, inputs):
        highest, totals = running
        key_piece, piece_start = inputs
        raw_scores, allowed = scores_of(key_piece, piece_start)
        new_high = jnp.maximum(
            highest, jnp.max(jnp.where(allowed, raw_scores, VERY_NEGATIVE), axis=-1)
        )
        weights_now = jnp.where(allowed, jnp.exp(raw_scores - new_high[..., None]), 0.0)
        totals = totals * jnp.exp(highest - new_high) + jnp.sum(weights_now, axis=-1)
        return ((new_high, totals), None)

    initial_maximum = jnp.full(
        (KEY_VALUE_HEADS, head_groups, resident_tokens), VERY_NEGATIVE, jnp.float32
    )
    initial_sums = jnp.zeros((KEY_VALUE_HEADS, head_groups, resident_tokens), jnp.float32)
    (highest, totals), _ = lax.scan(
        running_stats, (initial_maximum, initial_sums), (key_segments, piece_starts)
    )
    log_total = highest + jnp.log(totals)

    def probabilities(key_piece, piece_start):
        raw_scores, allowed = scores_of(key_piece, piece_start)
        return jnp.where(allowed, jnp.exp(raw_scores - log_total[..., None]), 0.0)

    def attend_piece(accumulated, inputs):
        key_piece, value_piece, piece_start = inputs
        weights_low = probabilities(key_piece, piece_start).astype(jnp.bfloat16)
        accumulated = accumulated + jnp.einsum(
            "hgts,shd->thgd", weights_low, value_piece, preferred_element_type=jnp.float32
        )
        return (accumulated, None)

    attended, _ = lax.scan(
        attend_piece,
        jnp.zeros((resident_tokens, KEY_VALUE_HEADS, head_groups, HEAD_SIZE), jnp.float32),
        (key_segments, value_segments, piece_starts),
    )
    attended_low = attended.reshape(resident_tokens, QUERY_HEADS * HEAD_SIZE).astype(jnp.bfloat16)
    after_attn = residual_in + jnp.dot(attended_low, out_full, preferred_element_type=jnp.float32)
    mixed_in, scale_mixture = head_normalize(after_attn, mixture_gain)
    mixed_low = mixed_in.astype(jnp.bfloat16)
    logits = jnp.dot(mixed_low, router_full, preferred_element_type=jnp.float32)
    expert_ids = jnp.arange(experts_all, dtype=jnp.int32)
    chosen_mask = (routes[:, :, None] == expert_ids[None, None, :]).astype(jnp.float32)
    chosen = jnp.sum(chosen_mask * logits[:, None, :], axis=-1)
    route_weight = jax.nn.softmax(chosen, axis=-1)
    flat_routes = routes.reshape(-1)
    flat_hot = (flat_routes[:, None] == expert_ids[None, :]).astype(jnp.int32)
    slot_rank = jnp.sum(jnp.cumsum(flat_hot, axis=0) * flat_hot, axis=1) - 1
    slot_index = flat_routes * capacity + slot_rank
    outgoing = (
        jnp.zeros((experts_all * capacity, MODEL_WIDTH), jnp.bfloat16)
        .at[slot_index]
        .set(jnp.repeat(mixed_low, TOP, axis=0))
    )
    arrived = lax.all_to_all(
        outgoing.reshape(devices, EXP_DEV * capacity, MODEL_WIDTH),
        ("dp", "expert"),
        split_axis=0,
        concat_axis=0,
        tiled=True,
    )
    arrived = arrived.reshape(devices, EXP_DEV, capacity, MODEL_WIDTH)
    gate_raw = jnp.einsum(
        "necd,edf->necf", arrived, expert_gate, preferred_element_type=jnp.float32
    )
    up_raw = jnp.einsum("necd,edf->necf", arrived, expert_up, preferred_element_type=jnp.float32)
    gate_sig = jax.nn.sigmoid(gate_raw)
    activated = (gate_raw * gate_sig * up_raw).astype(jnp.bfloat16)
    produced = jnp.einsum(
        "necf,efd->necd", activated, expert_down, preferred_element_type=jnp.float32
    ).astype(jnp.bfloat16)
    returned = lax.all_to_all(
        produced.reshape(devices, EXP_DEV * capacity, MODEL_WIDTH),
        ("dp", "expert"),
        split_axis=0,
        concat_axis=0,
        tiled=True,
    )
    picked = (
        returned.reshape(experts_all * capacity, MODEL_WIDTH)[slot_index]
        .reshape(resident_tokens, TOP, MODEL_WIDTH)
        .astype(jnp.float32)
    )
    mixture = jnp.sum(picked * route_weight[:, :, None], axis=1)
    layer_out = (after_attn + mixture).astype(jnp.bfloat16)
    upstream = cotangent.astype(jnp.float32)
    route_grad = jnp.sum(picked * upstream[:, None, :], axis=-1)
    chosen_grad = route_weight * (
        route_grad - jnp.sum(route_weight * route_grad, axis=-1, keepdims=True)
    )
    logit_grad = jnp.sum(chosen_mask * chosen_grad[:, :, None], axis=1).astype(jnp.bfloat16)
    mixed_grad = jnp.dot(logit_grad, router_full.T, preferred_element_type=jnp.float32)
    produced_grad = (
        (route_weight[:, :, None] * upstream[:, None, :])
        .astype(jnp.bfloat16)
        .reshape(resident_tokens * TOP, MODEL_WIDTH)
    )
    outgoing_grad = (
        jnp.zeros((experts_all * capacity, MODEL_WIDTH), jnp.bfloat16)
        .at[slot_index]
        .set(produced_grad)
    )
    arrived_grad = lax.all_to_all(
        outgoing_grad.reshape(devices, EXP_DEV * capacity, MODEL_WIDTH),
        ("dp", "expert"),
        split_axis=0,
        concat_axis=0,
        tiled=True,
    )
    arrived_grad = arrived_grad.reshape(devices, EXP_DEV, capacity, MODEL_WIDTH)
    down_gradient = jnp.einsum(
        "necf,necd->efd", activated, arrived_grad, preferred_element_type=jnp.float32
    )
    activated_grad = jnp.einsum(
        "necd,efd->necf", arrived_grad, expert_down, preferred_element_type=jnp.float32
    )
    gate_grad = (activated_grad * up_raw * gate_sig * (1.0 + gate_raw * (1.0 - gate_sig))).astype(
        jnp.bfloat16
    )
    up_grad = (activated_grad * gate_raw * gate_sig).astype(jnp.bfloat16)
    gate_gradient = jnp.einsum(
        "necd,necf->edf", arrived, gate_grad, preferred_element_type=jnp.float32
    )
    up_gradient = jnp.einsum("necd,necf->edf", arrived, up_grad, preferred_element_type=jnp.float32)
    row_grad = (
        jnp.einsum("necf,edf->necd", gate_grad, expert_gate, preferred_element_type=jnp.float32)
        + jnp.einsum("necf,edf->necd", up_grad, expert_up, preferred_element_type=jnp.float32)
    ).astype(jnp.bfloat16)
    back_rows = lax.all_to_all(
        row_grad.reshape(devices, EXP_DEV * capacity, MODEL_WIDTH),
        ("dp", "expert"),
        split_axis=0,
        concat_axis=0,
        tiled=True,
    )
    back_picked = back_rows.reshape(experts_all * capacity, MODEL_WIDTH)[slot_index].reshape(
        resident_tokens, TOP, MODEL_WIDTH
    )
    mixed_grad = mixed_grad + jnp.sum(back_picked.astype(jnp.float32), axis=1)
    mixture_back, mixture_terms = normalize_back(
        mixed_grad, after_attn, scale_mixture, mixture_gain
    )
    after_grad = upstream + mixture_back
    after_low = after_grad.astype(jnp.bfloat16)
    attended_gradient = jnp.dot(after_low, out_full.T, preferred_element_type=jnp.float32).astype(
        jnp.bfloat16
    )
    attended_gradient = attended_gradient.reshape(
        resident_tokens, KEY_VALUE_HEADS, head_groups, HEAD_SIZE
    )

    def delta_piece(row_delta, inputs):
        key_piece, value_piece, piece_start = inputs
        weights_full = probabilities(key_piece, piece_start)
        prob_grad = jnp.einsum(
            "thgd,shd->hgts", attended_gradient, value_piece, preferred_element_type=jnp.float32
        )
        return (row_delta + jnp.sum(weights_full * prob_grad, axis=-1), None)

    row_delta, _ = lax.scan(
        delta_piece,
        jnp.zeros((KEY_VALUE_HEADS, head_groups, resident_tokens), jnp.float32),
        (key_segments, value_segments, piece_starts),
    )

    def backward_piece(query_sum, inputs):
        key_piece, value_piece, piece_start = inputs
        weights_full = probabilities(key_piece, piece_start)
        weights_low = weights_full.astype(jnp.bfloat16)
        prob_grad = jnp.einsum(
            "thgd,shd->hgts", attended_gradient, value_piece, preferred_element_type=jnp.float32
        )
        score_grad = (weights_full * (prob_grad - row_delta[..., None])).astype(jnp.bfloat16)
        query_sum = query_sum + jnp.einsum(
            "hgts,shd->thgd", score_grad, key_piece, preferred_element_type=jnp.float32
        )
        key_part = (
            jnp.einsum(
                "hgts,thgd->shd", score_grad, query_narrow, preferred_element_type=jnp.float32
            )
            * softmax_scale
        )
        value_part = jnp.einsum(
            "hgts,thgd->shd", weights_low, attended_gradient, preferred_element_type=jnp.float32
        )
        return (query_sum, (key_part, value_part))

    query_sum, (key_portions, value_portions) = lax.scan(
        backward_piece,
        jnp.zeros((resident_tokens, KEY_VALUE_HEADS, head_groups, HEAD_SIZE), jnp.float32),
        (key_segments, value_segments, piece_starts),
    )
    key_grad, value_gradient_full = (
        lax.psum_scatter(
            key_portions.reshape(span_length, KEY_VALUE_HEADS, HEAD_SIZE).astype(jnp.bfloat16),
            "expert",
            scatter_dimension=0,
            tiled=True,
        ).astype(jnp.float32),
        lax.psum_scatter(
            value_portions.reshape(span_length, KEY_VALUE_HEADS, HEAD_SIZE).astype(jnp.bfloat16),
            "expert",
            scatter_dimension=0,
            tiled=True,
        ).astype(jnp.float32),
    )
    query_turn = rotate_back(
        (query_sum * softmax_scale).reshape(resident_tokens, QUERY_HEADS, HEAD_SIZE),
        cosine_lookup,
        sine_lookup,
    )
    query_back, query_terms = normalize_back(query_turn, query_raw, scale_query, query_gain)
    key_turn = rotate_back(key_grad, cosine_lookup, sine_lookup)
    key_reverse, key_terms = normalize_back(key_turn, key_unnormed, scale_key, key_norm_gain)
    query_grad_low = query_back.reshape(resident_tokens, QUERY_HEADS * HEAD_SIZE).astype(
        jnp.bfloat16
    )
    key_gradient_narrow = key_reverse.reshape(resident_tokens, KEY_VALUE_HEADS * HEAD_SIZE).astype(
        jnp.bfloat16
    )
    value_gradient_narrow = value_gradient_full.reshape(
        resident_tokens, KEY_VALUE_HEADS * HEAD_SIZE
    ).astype(jnp.bfloat16)
    normed_grad = (
        jnp.dot(query_grad_low, query_full.T, preferred_element_type=jnp.float32)
        + jnp.dot(key_gradient_narrow, key_full.T, preferred_element_type=jnp.float32)
        + jnp.dot(value_gradient_narrow, value_full.T, preferred_element_type=jnp.float32)
    )
    input_back, attention_terms = normalize_back(
        normed_grad, residual_in, scale_attention, attention_gain
    )
    input_grad = after_grad + input_back
    attention_total, mixture_total, query_total, key_total = lax.psum(
        (
            jnp.sum(attention_terms, axis=0),
            jnp.sum(mixture_terms, axis=0),
            jnp.sum(query_terms, axis=(0, 1)),
            jnp.sum(key_terms, axis=(0, 1)),
        ),
        ("dp", "expert"),
    )
    query_gradient = jnp.dot(normed_low.T, query_grad_low, preferred_element_type=jnp.float32)
    key_gradient = jnp.dot(normed_low.T, key_gradient_narrow, preferred_element_type=jnp.float32)
    value_gradient = jnp.dot(
        normed_low.T, value_gradient_narrow, preferred_element_type=jnp.float32
    )
    out_gradient = jnp.dot(attended_low.T, after_low, preferred_element_type=jnp.float32)
    router_gradient = jnp.dot(mixed_low.T, logit_grad, preferred_element_type=jnp.float32)
    query_share, key_share, value_share, out_share, router_share = (
        lax.psum_scatter(
            query_gradient.astype(jnp.bfloat16), "expert", scatter_dimension=1, tiled=True
        ).astype(jnp.float32),
        lax.psum_scatter(
            key_gradient.astype(jnp.bfloat16), "expert", scatter_dimension=1, tiled=True
        ).astype(jnp.float32),
        lax.psum_scatter(
            value_gradient.astype(jnp.bfloat16), "expert", scatter_dimension=1, tiled=True
        ).astype(jnp.float32),
        lax.psum_scatter(
            out_gradient.astype(jnp.bfloat16), "expert", scatter_dimension=1, tiled=True
        ).astype(jnp.float32),
        lax.psum_scatter(
            router_gradient.astype(jnp.bfloat16), "expert", scatter_dimension=1, tiled=True
        ).astype(jnp.float32),
    )
    query_share, key_share, value_share, out_share, router_share = (
        lax.psum_scatter(
            query_share.astype(jnp.bfloat16), "dp", scatter_dimension=0, tiled=True
        ).astype(jnp.float32),
        lax.psum_scatter(
            key_share.astype(jnp.bfloat16), "dp", scatter_dimension=0, tiled=True
        ).astype(jnp.float32),
        lax.psum_scatter(
            value_share.astype(jnp.bfloat16), "dp", scatter_dimension=0, tiled=True
        ).astype(jnp.float32),
        lax.psum_scatter(
            out_share.astype(jnp.bfloat16), "dp", scatter_dimension=0, tiled=True
        ).astype(jnp.float32),
        lax.psum_scatter(
            router_share.astype(jnp.bfloat16), "dp", scatter_dimension=0, tiled=True
        ).astype(jnp.float32),
    )
    return (
        layer_out,
        input_grad,
        query_share,
        key_share,
        value_share,
        out_share,
        router_share,
        attention_total,
        mixture_total,
        query_total,
        key_total,
        gate_gradient,
        up_gradient,
        down_gradient,
    )


def solution(mesh):
    in_specs = (
        P(("dp", "expert"), None),
        P(("dp", "expert"), None),
        P("dp"),
        P("dp", "expert"),
        P("dp", "expert"),
        P("dp", "expert"),
        P("dp", "expert"),
        P("dp", "expert"),
        P(),
        P(),
        P(),
        P(),
        P(("dp", "expert"), None, None),
        P(("dp", "expert"), None, None),
        P(("dp", "expert"), None, None),
        P(("dp", "expert"), None),
    )
    out_specs = (
        P(("dp", "expert"), None),
        P(("dp", "expert"), None),
        P("dp", "expert"),
        P("dp", "expert"),
        P("dp", "expert"),
        P("dp", "expert"),
        P("dp", "expert"),
        P(),
        P(),
        P(),
        P(),
        P(("dp", "expert"), None, None),
        P(("dp", "expert"), None, None),
        P(("dp", "expert"), None, None),
    )
    return jax.shard_map(shards, mesh=mesh, in_specs=in_specs, out_specs=out_specs, check_vma=False)
```

profile of v0, /device:TPU:0, one launch (start us, length us, event | category | flops | bytes accessed | tf_op | source)
XLA Modules:
  0.0 1742.7 jit_solution(12718168279034576137)
XLA Ops:
  7.2 17.7 %all_gather.39 = bf16[2048,64]{0,1:T(8,128)(2,1)} all-gather(bf16[512,64]{0,1:T(8,128)(2,1)} %param.28), channel_id=1, replica_groups=mesh['dp'=4,'expert'=8] {'dp'}, dimensions={0}, use_global_device_ids=true | all-gather | bytes 327680 | tf_op jit(solution)/shard_map/all_gather | solution.py:81
  25.8 14.9 all_gather.36
  43.8 9.2 all-gather.14.cloned.1.call-done
  61.7 38.8 %all-gather.18.cloned.1.call-done = bf16[2048,512]{1,0:T(8,128)(2,1)} async-done(((bf16[512,512]{1,0:T(8,128)(2,1)}), bf16[2048,512]{1,0:T(8,128)(2,1)}) %all-gather.18.cloned.1.call-update) | async-done | bytes 2097168 | tf_op jit(solution)/shard_map/all_gather | solution.py:80
  100.6 28.5 %all-gather.10.cloned.1.call-done = bf16[2048,512]{0,1:T(8,128)(2,1)} async-done(((bf16[2048,64]{0,1:T(8,128)(2,1)}), bf16[2048,512]{0,1:T(8,128)(2,1)}) %all-gather.10.cloned.1.call-update) | async-done | bytes 2097168 | tf_op jit(solution)/shard_map/all_gather | solution.py:89
  132.6 43.8 %all-gather.22.cloned.1.call-done = bf16[4096,256]{1,0:T(8,128)(2,1)} async-done(((bf16[1024,256]{1,0:T(8,128)(2,1)}), bf16[4096,256]{1,0:T(8,128)(2,1)}) %all-gather.22.cloned.1.call-update) | async-done | bytes 2097168 | tf_op jit(solution)/shard_map/all_gather | solution.py:83
  177.7 9.0 reduce-window.6
  187.9 13.1 all-gather.16.cloned.1.call-done
  203.3 92.6 %all-gather.20.cloned.1.call-done = bf16[2048,4096]{1,0:T(8,128)(2,1)} async-done(((bf16[2048,512]{1,0:T(8,128)(2,1)}), bf16[2048,4096]{1,0:T(8,128)(2,1)}) %all-gather.20.cloned.1.call-update) | async-done | bytes 16777232 | tf_op jit(solution)/shard_map/all_gather | solution.py:87
  295.9 9.7 fusion.147
  316.6 40.0 %while.50 = (s32[]{:T(128)}, f32[4,8,128]{2,1,0:T(8,128)S(1)}, f32[4,8,128]{2,1,0:T(8,128)S(1)}, s32[4]{0:T(128)S(1)}, s32[]{:T(128)}, /*index=5*/bf16[4,256,4,1...) while((s32[]{:T(128)}, f32[4,8,128]{2,1,0:T(8,128)S(1)}, ...), condition=%wide.region_6.7_spmd.clone, body=%wide.region_3.6_spmd.clone.sunk | while | flops 275862400 | bytes 10014860 | solution.py:160
  319.3 4.1 fusion.227
  329.2 4.3 fusion.227
  339.5 4.1 fusion.227
  349.4 4.1 fusion.227
  356.6 28.8 %while.51 = (s32[]{:T(128)}, f32[128,4,8,128]{0,3,2,1:T(8,128)}, bf16[4,256,4,128]{3,1,0,2:T(8,128)(2,1)}, s32[4]{0:T(128)S(1)}, s32[]{:T(128)}, /*index=5*/bf16...) while((s32[]{:T(128)}, f32[128,4,8,128]{0,3,2,1:T(8,128)}, ...), condition=%wide.region_8.9_spmd.clone, body=%wide.region_7.8_spmd.clone.sunk | while | flops 542180224 | bytes 5853843 | solution.py:177
  366.0 4.7 bitcast_add_fusion.5
  373.5 4.7 bitcast_add_fusion.5
  380.9 4.6 bitcast_add_fusion.5
  388.2 28.7 %all-gather.24.cloned.1.call-done = bf16[4096,2048]{1,0:T(8,128)(2,1)} async-done(((bf16[4096,256]{1,0:T(8,128)(2,1)}), bf16[4096,2048]{1,0:T(8,128)(2,1)}) %all-gather.24.cloned.1.call-update) | async-done | bytes 16777232 | tf_op jit(solution)/shard_map/all_gather | solution.py:90
  416.9 8.6 multiply_reduce_fusion.5
  427.4 10.4 scatter_custom_fusion
  437.8 7.4 reshape.444
  445.3 4.7 all-to-all-start
  450.0 121.8 %all_gather.46 = bf16[2048,4]{0,1:T(4,128)(2,1)S(1)} all-gather(bf16[512,4]{0,1:T(4,128)(2,1)S(1)} %copy-done.48), channel_id=1, replica_groups=mesh['dp'=4,'expert'=8] {'dp'}, dimensions={0}, use_global_device_ids=true | all-gather | bytes 20480 | tf_op jit(solution)/shard_map/all_gather | solution.py:84
  571.7 8.9 all-gather
  584.4 10.5 scatter_custom_fusion.1
  594.9 7.5 reshape.450
  606.4 9.8 fusion.100
  616.2 8.7 fusion.96
  625.0 98.2 %all-to-all-done.2 = bf16[32,38,2048]{2,1,0:T(8,128)(2,1)} async-done(((bf16[32,38,2048]{2,1,0:T(8,128)(2,1)}), bf16[32,38,2048]{2,1,0:T(8,128)(2,1)}, u32[]{:S(2)}, u32[]{:S(2)}) %all-to-all-start.2) | async-done | bytes 4980768 | tf_op jit(solution)/shard_map/all_to_all | solution.py:248
  723.2 10.8 fusion.86
  735.3 6.0 convolution_convert_fusion.3
  745.2 6.0 fusion.98
  751.3 7.9 add_convert_fusion
  759.2 102.8 %all-to-all-done.1 = bf16[32,38,2048]{2,1,0:T(8,128)(2,1)} async-done(((bf16[32,38,2048]{2,1,0:T(8,128)(2,1)}), bf16[32,38,2048]{2,1,0:T(8,128)(2,1)}, u32[]{:S(2)}, u32[]{:S(2)}) %all-to-all-start.1) | async-done | bytes 4980768 | tf_op jit(solution)/shard_map/all_to_all | solution.py:217
  866.7 7.5 reshape.449
  874.2 12.0 gather_fusion
  886.2 4.9 fusion.74
  891.2 91.1 %all-to-all-done.3 = bf16[32,38,2048]{2,1,0:T(8,128)(2,1)} async-done(((bf16[32,38,2048]{2,1,0:T(8,128)(2,1)}), bf16[32,38,2048]{2,1,0:T(8,128)(2,1)}, u32[]{:S(2)}, u32[]{:S(2)}) %all-to-all-start.3) | async-done | bytes 4980768 | tf_op jit(solution)/shard_map/all_to_all | solution.py:274
  982.3 7.5 reshape.453
  989.8 12.2 gather_fusion.1
  1002.0 5.1 convert_reduce_fusion
  1010.5 11.4 fusion.121
  1023.1 26.5 %while.52 = (s32[]{:T(128)}, f32[4,8,128]{2,1,0:T(8,128)S(1)}, s32[4]{0:T(128)S(1)}, s32[]{:T(128)}, bf16[4,256,4,128]{3,1,2,0:T(8,128)(2,1)}, /*index=5*/bf16[1...) while((s32[]{:T(128)}, f32[4,8,128]{2,1,0:T(8,128)S(1)}, ...), condition=%wide.region_26.27_spmd.clone, body=%wide.region_24.26_spmd.clone.sunk | while | flops 542184320 | bytes 11162267 | solution.py:305
  1049.6 70.1 %while.53 = (s32[]{:T(128)}, f32[128,4,8,128]{0,3,2,1:T(8,128)}, bf16[4,256,4,128]{3,1,0,2:T(8,128)(2,1)}, bf16[4,256,4,128]{3,1,0,2:T(8,128)(2,1)}, bf16[4,256,...) while((s32[]{:T(128)}, f32[128,4,8,128]{0,3,2,1:T(8,128)}, ...), condition=%wide.region_28.29_spmd.clone, body=%wide.region_27.28_spmd.clone.sunk | while | flops 1353909120 | bytes 79583064 | solution.py:333
  1122.4 32.5 %reduce-scatter.14.cloned.1.call-done = bf16[128,4,128]{2,0,1:T(8,128)(2,1)} async-done(((bf16[1024,4,128]{2,0,1:T(8,128)(2,1)}), bf16[128,4,128]{2,0,1:T(8,128)(2,1)}) %reduce-scatter.14.cloned.1.call-update) | async-done | bytes 131088 | tf_op jit(solution)/shard_map/reduce_scatter | solution.py:339
  1174.4 19.6 %reduce-scatter.16.cloned.1.call-done = bf16[128,4,128]{2,0,1:T(8,128)(2,1)} async-done(((bf16[1024,4,128]{2,0,1:T(8,128)(2,1)}), bf16[128,4,128]{2,0,1:T(8,128)(2,1)}) %reduce-scatter.16.cloned.1.call-update) | async-done | bytes 131088 | tf_op jit(solution)/shard_map/reduce_scatter | solution.py:345
  1197.2 4.9 fusion.153
  1209.4 4.3 multiply_reduce_fusion
  1221.0 5.0 fusion.106
  1226.1 9.4 convolution_convert_fusion.1
  1237.0 8.2 convolution_convert_fusion
  1252.4 42.2 %reduce-scatter.22.cloned.1.call-done = bf16[2048,64]{0,1:T(8,128)(2,1)} async-done(((bf16[2048,512]{0,1:T(8,128)(2,1)}), bf16[2048,64]{0,1:T(8,128)(2,1)}) %reduce-scatter.22.cloned.1.call-update) | async-done | bytes 262160 | tf_op jit(solution)/shard_map/reduce_scatter | solution.py:398
  1294.7 44.5 %reduce-scatter.26.cloned.1.call-done = bf16[2048,64]{0,1:T(8,128)(2,1)} async-done(((bf16[2048,512]{0,1:T(8,128)(2,1)}), bf16[2048,64]{0,1:T(8,128)(2,1)}) %reduce-scatter.26.cloned.1.call-update) | async-done | bytes 262160 | tf_op jit(solution)/shard_map/reduce_scatter | solution.py:401
  1339.2 119.8 %reduce-scatter.18.cloned.1.call-done = bf16[2048,512]{1,0:T(8,128)(2,1)} async-done(((bf16[2048,4096]{1,0:T(8,128)(2,1)}), bf16[2048,512]{1,0:T(8,128)(2,1)}) %reduce-scatter.18.cloned.1.call-update) | async-done | bytes 2097168 | tf_op jit(solution)/shard_map/reduce_scatter | solution.py:395
  1459.1 9.1 convolution_bitcast_fusion.1
  1468.1 8.9 convolution_bitcast_fusion.2
  1477.1 101.7 %reduce-scatter.30.cloned.1.call-done = bf16[4096,256]{1,0:T(8,128)(2,1)} async-done(((bf16[4096,2048]{1,0:T(8,128)(2,1)}), bf16[4096,256]{1,0:T(8,128)(2,1)}) %reduce-scatter.30.cloned.1.call-update) | async-done | bytes 2097168 | tf_op jit(solution)/shard_map/reduce_scatter | solution.py:404
  1578.8 8.6 convolution_bitcast_fusion.3
  1587.5 12.5 fusion.156
  1609.4 39.1 %all-reduce.1 = (f32[2048]{0:T(1024)}, f32[2048]{0:T(1024)}, f32[128]{0:T(128)}, f32[128]{0:T(128)}) all-reduce(f32[2048]{0:T(1024)S(1)} %get-tuple-element.702, f32[2048]{0:T(1024)S(1)} %copy-done.44, f32[128]{0:T(128)S(1)} %copy-done.50, f32[128]{0:T(128)S(1)} %copy-done.49), channel_id=1, replica_groups=mesh['dp'=4,'expert'=8] {'dp','expert'}, use_global_device_ids=true, to_apply=%region_45.46 | all-reduce | flops 4352 | bytes 34816 | tf_op jit(solution)/shard_map/psum | solution.py:378
  1654.8 33.2 %reduce-scatter.20.cloned.1.call-done = bf16[512,512]{1,0:T(8,128)(2,1)} async-done(((bf16[2048,512]{1,0:T(8,128)(2,1)}), bf16[512,512]{1,0:T(8,128)(2,1)}) %reduce-scatter.20.cloned.1.call-update) | async-done | bytes 524304 | tf_op jit(solution)/shard_map/reduce_scatter | solution.py:412
  1690.1 43.2 %reduce-scatter.32.cloned.1.call-done = bf16[1024,256]{1,0:T(8,128)(2,1)} async-done(((bf16[4096,256]{1,0:T(8,128)(2,1)}), bf16[1024,256]{1,0:T(8,128)(2,1)}) %reduce-scatter.32.cloned.1.call-update) | async-done | bytes 524304 | tf_op jit(solution)/shard_map/reduce_scatter | solution.py:421
  (447 shorter events, 260.2 us)
Async XLA Ops:
  7.2 716.0 %copy-start = (bf16[1,768,2048]{2,1,0:T(8,128)(2,1)S(1)}, bf16[1,768,2048]{2,1,0:T(8,128)(2,1)}, u32[]{:S(2)}) copy-start(bf16[1,768,2048]{2,1,0:T(8,128)(2,1)} %param.38) | copy-start | bytes 9437188
  7.2 45.8 %all-gather.14.cloned.1.call-start = ((), (), s32[]{:S(2)}) async-start(), calls=%async_computation.17 | async-start | bytes 2359296 | tf_op jit(solution)/shard_map/all_gather | solution.py:88
  25.0 75.5 %all-gather.18.cloned.1.call-start = ((), (), s32[]{:S(2)}) async-start(), calls=%async_computation.19 | async-start | bytes 2621440 | tf_op jit(solution)/shard_map/all_gather | solution.py:80
  25.7 103.3 %all-gather.10.cloned.1.call-start = ((), (), s32[]{:S(2)}) async-start(), calls=%async_computation.15 | async-start | bytes 2359296 | tf_op jit(solution)/shard_map/all_gather | solution.py:89
  40.7 135.7 %all-gather.22.cloned.1.call-start = ((), (), s32[]{:S(2)}) async-start(), calls=%async_computation.21 | async-start | bytes 2621440 | tf_op jit(solution)/shard_map/all_gather | solution.py:83
  41.3 159.7 %all-gather.16.cloned.1.call-start = ((), (), s32[]{:S(2)}) async-start(), calls=%async_computation.18 | async-start | bytes 1179648 | tf_op jit(solution)/shard_map/all_gather | solution.py:122
  41.8 135.4 %copy-start.23 = (f32[128,128]{1,0:T(8,128)}, f32[128,128]{1,0:T(8,128)S(1)}, u32[]{:S(2)}) copy-start(f32[128,128]{1,0:T(8,128)S(1)} %pad_maximum_fusion.2) | copy-start | bytes 196612
  42.5 133.9 %copy-start.25 = (f32[128,128]{1,0:T(8,128)}, f32[128,128]{1,0:T(8,128)S(1)}, u32[]{:S(2)}) copy-start(f32[128,128]{1,0:T(8,128)S(1)} %get-tuple-element.807) | copy-start | bytes 196612
  43.8 252.1 %copy-start.42 = (f32[128]{0:T(128)}, f32[128]{0:T(128)S(1)}, u32[]{:S(2)}) copy-start(f32[128]{0:T(128)S(1)} %add_rsqrt_fusion.3) | copy-start | bytes 1540
  43.8 85.2 %copy-start.32 = (f32[2048]{0:T(1024)S(1)}, f32[2048]{0:T(1024)}, u32[]{:S(2)}) copy-start(f32[2048]{0:T(1024)} %param.32) | copy-start | bytes 24580
  55.6 76.1 %copy-start.15 = (f32[128,512]{1,0:T(8,128)}, f32[128,512]{1,0:T(8,128)S(1)}, u32[]{:S(2)}) copy-start(f32[128,512]{1,0:T(8,128)S(1)} %fusion.149) | copy-start | bytes 786436
  61.6 115.7 %copy-start.39 = (s32[128,8]{0,1:T(8,128)S(1)}, s32[128,8]{0,1:T(8,128)}, u32[]{:S(2)}) copy-start(s32[128,8]{0,1:T(8,128)} %param.25) | copy-start | bytes 12292
  61.6 234.3 %all-gather.20.cloned.1.call-start = ((), (), s32[]{:S(2)}) async-start(), calls=%async_computation.20 | async-start | bytes 18874368 | tf_op jit(solution)/shard_map/all_gather | solution.py:87
  100.5 256.1 %all-gather.12.cloned.1.call-start = ((), (), s32[]{:S(2)}) async-start(), calls=%async_computation.16 | async-start | bytes 1179648 | tf_op jit(solution)/shard_map/all_gather | solution.py:123
  132.4 284.6 %all-gather.24.cloned.1.call-start = ((), (), s32[]{:S(2)}) async-start(), calls=%async_computation.22 | async-start | bytes 18874368 | tf_op jit(solution)/shard_map/all_gather | solution.py:90
  305.7 4.8 copy-start.45
  416.9 9.5 copy-start.38
  445.3 4.7 copy-start.48
  445.3 157.1 %all-to-all-start = ((bf16[32,38,2048]{2,1,0:T(8,128)(2,1)}), bf16[32,38,2048]{2,1,0:T(8,128)(2,1)}, u32[]{:S(2)}, u32[]{:S(2)}) async-start(bf16[32,38,2048]{2,1,0:T(8,128)(2,1)} %reshape.444), calls=%async_computation | async-start | bytes 10485760 | tf_op jit(solution)/shard_map/all_to_all | solution.py:200
  602.4 120.8 %all-to-all-start.2 = ((bf16[32,38,2048]{2,1,0:T(8,128)(2,1)}), bf16[32,38,2048]{2,1,0:T(8,128)(2,1)}, u32[]{:S(2)}, u32[]{:S(2)}) async-start(bf16[32,38,2048]{2,1,0:T(8,128)(2,1)} %reshape.450), calls=%async_computation.2 | async-start | bytes 10485760 | tf_op jit(solution)/shard_map/all_to_all | solution.py:248
  606.4 9.8 copy-start.52
  741.3 120.7 %all-to-all-start.1 = ((bf16[32,38,2048]{2,1,0:T(8,128)(2,1)}), bf16[32,38,2048]{2,1,0:T(8,128)(2,1)}, u32[]{:S(2)}, u32[]{:S(2)}) async-start(bf16[32,38,2048]{2,1,0:T(8,128)(2,1)} %convolution_convert_fusion.3), calls=%async_computation.1 | async-start | bytes 10485760 | tf_op jit(solution)/shard_map/all_to_all | solution.py:217
  745.2 6.1 copy-start.53
  759.2 106.5 %copy-start.27 = (bf16[4,256,4,128]{3,1,0,2:T(8,128)(2,1)S(1)}, bf16[4,256,4,128]{3,1,0,2:T(8,128)(2,1)}, u32[]{:S(2)}) copy-start(bf16[4,256,4,128]{3,1,0,2:T(8,128)(2,1)} %get-tuple-element.1273) | copy-start | bytes 3145732
  862.0 120.3 %all-to-all-start.3 = ((bf16[32,38,2048]{2,1,0:T(8,128)(2,1)}), bf16[32,38,2048]{2,1,0:T(8,128)(2,1)}, u32[]{:S(2)}, u32[]{:S(2)}) async-start(bf16[32,38,2048]{2,1,0:T(8,128)(2,1)} %add_convert_fusion), calls=%async_computation.3 | async-start | bytes 10485760 | tf_op jit(solution)/shard_map/all_to_all | solution.py:274
  865.6 289.3 %reduce-scatter.14.cloned.1.call-start = ((), (), s32[]{:S(2)}) async-start(), calls=%async_computation.23 | async-start | bytes 1179648 | tf_op jit(solution)/shard_map/reduce_scatter | solution.py:339
  874.2 12.0 copy-start.14
  1002.0 5.2 copy-start.12
  1002.0 6.2 copy-start.21
  1049.6 105.3 %copy-start.24 = (f32[128,128]{1,0:T(8,128)S(1)}, f32[128,128]{1,0:T(8,128)}, u32[]{:S(2)}) copy-start(f32[128,128]{1,0:T(8,128)} %copy-done.23) | copy-start | bytes 196612
  1059.0 4.8 copy-start.4
  1075.9 5.5 copy-start.4
  1093.5 5.5 copy-start.4
  1111.2 5.5 copy-start.4
  1119.7 36.3 %copy-start.16 = (f32[128,512]{1,0:T(8,128)S(1)}, f32[128,512]{1,0:T(8,128)}, u32[]{:S(2)}) copy-start(f32[128,512]{1,0:T(8,128)} %copy-done.15) | copy-start | bytes 786436
  1119.7 36.3 %copy-start.26 = (f32[128,128]{1,0:T(8,128)S(1)}, f32[128,128]{1,0:T(8,128)}, u32[]{:S(2)}) copy-start(f32[128,128]{1,0:T(8,128)} %copy-done.25) | copy-start | bytes 196612
  1119.7 36.3 %copy-start.41 = (f32[128,4]{0,1:T(4,128)S(1)}, f32[128,4]{0,1:T(4,128)}, u32[]{:S(2)}) copy-start(f32[128,4]{0,1:T(4,128)} %copy-done.40) | copy-start | bytes 6148
  1119.7 36.3 %copy-start.47 = (f32[128]{0:T(128)S(1)}, f32[128]{0:T(128)}, u32[]{:S(2)}) copy-start(f32[128]{0:T(128)} %param.35) | copy-start | bytes 1540
  1119.7 38.4 %copy-start.7 = (bf16[128,2048]{1,0:T(8,128)(2,1)S(1)}, bf16[128,2048]{1,0:T(8,128)(2,1)}, u32[]{:S(2)}) copy-start(bf16[128,2048]{1,0:T(8,128)(2,1)} %param.24) | copy-start | bytes 1572868
  1119.7 38.4 %copy-start.33 = (f32[2048]{0:T(1024)S(1)}, f32[2048]{0:T(1024)}, u32[]{:S(2)}) copy-start(f32[2048]{0:T(1024)} %param.32) | copy-start | bytes 24580
  1119.7 38.4 %copy-start.43 = (f32[128]{0:T(128)S(1)}, f32[128]{0:T(128)}, u32[]{:S(2)}) copy-start(f32[128]{0:T(128)} %copy-done.42) | copy-start | bytes 1540
  1119.8 74.2 %reduce-scatter.16.cloned.1.call-start = ((), (), s32[]{:S(2)}) async-start(), calls=%async_computation.24 | async-start | bytes 1179648 | tf_op jit(solution)/shard_map/reduce_scatter | solution.py:345
  1120.3 130.1 %all-reduce.4.cloned.1.call-start = ((), (), s32[]{:S(2)}) async-start(), calls=%async_computation.34 | async-start | bytes 262144
  1122.3 172.3 %reduce-scatter.22.cloned.1.call-start = ((), (), s32[]{:S(2)}) async-start(), calls=%async_computation.27 | async-start | bytes 2359296 | tf_op jit(solution)/shard_map/reduce_scatter | solution.py:398
  1155.8 5.5 copy-start.46
  1160.2 6.2 copy-start.5
  1160.2 178.9 %reduce-scatter.26.cloned.1.call-start = ((), (), s32[]{:S(2)}) async-start(), calls=%async_computation.29 | async-start | bytes 2359296 | tf_op jit(solution)/shard_map/reduce_scatter | solution.py:401
  1197.1 261.8 %reduce-scatter.18.cloned.1.call-start = ((), (), s32[]{:S(2)}) async-start(), calls=%async_computation.25 | async-start | bytes 18874368 | tf_op jit(solution)/shard_map/reduce_scatter | solution.py:395
  1202.1 7.3 copy-start.36
  1235.5 343.3 %reduce-scatter.30.cloned.1.call-start = ((), (), s32[]{:S(2)}) async-start(), calls=%async_computation.31 | async-start | bytes 18874368 | tf_op jit(solution)/shard_map/reduce_scatter | solution.py:404
  1245.2 213.9 %copy-start.57 = (bf16[32,1,38,768]{3,2,0,1:T(8,128)(2,1)S(1)}, bf16[32,1,38,768]{3,2,0,1:T(8,128)(2,1)}, u32[]{:S(2)}) copy-start(bf16[32,1,38,768]{3,2,0,1:T(8,128)(2,1)} %copy-done.56) | copy-start | bytes 5603332
  1245.2 358.1 %reduce-scatter.34.cloned.1.call-start = ((), (), s32[]{:S(2)}) async-start(), calls=%async_computation.33 | async-start | bytes 655360
  1252.3 399.4 %reduce-scatter.24.cloned.1.call-start = ((), (), s32[]{:S(2)}) async-start(), calls=%async_computation.28 | async-start | bytes 327680 | tf_op jit(solution)/shard_map/reduce_scatter | solution.py:415
  1294.6 358.6 %reduce-scatter.28.cloned.1.call-start = ((), (), s32[]{:S(2)}) async-start(), calls=%async_computation.30 | async-start | bytes 327680 | tf_op jit(solution)/shard_map/reduce_scatter | solution.py:418
  1339.2 348.8 %reduce-scatter.20.cloned.1.call-start = ((), (), s32[]{:S(2)}) async-start(), calls=%async_computation.26 | async-start | bytes 2621440 | tf_op jit(solution)/shard_map/reduce_scatter | solution.py:412
  1459.0 274.3 %reduce-scatter.32.cloned.1.call-start = ((), (), s32[]{:S(2)}) async-start(), calls=%async_computation.32 | async-start | bytes 2621440 | tf_op jit(solution)/shard_map/reduce_scatter | solution.py:421
  1459.0 9.1 copy-start.58
  1468.1 110.7 %copy-start.59 = (bf16[32,1,38,768]{3,2,0,1:T(8,128)(2,1)S(1)}, bf16[32,1,38,768]{3,2,0,1:T(8,128)(2,1)}, u32[]{:S(2)}) copy-start(bf16[32,1,38,768]{3,2,0,1:T(8,128)(2,1)} %get-tuple-element.794) | copy-start | bytes 5603332
  1578.8 8.7 copy-start.17
  1587.5 17.4 copy-start.18
  1604.9 4.6 copy-start.44
  1604.9 4.6 copy-start.49
  1604.9 4.6 copy-start.50
  1606.7 128.7 %copy-start.1 = (bf16[1,768,2048]{2,1,0:T(8,128)(2,1)S(1)}, bf16[1,768,2048]{2,1,0:T(8,128)(2,1)}, u32[]{:S(2)}) copy-start(bf16[1,768,2048]{2,1,0:T(8,128)(2,1)} %param.38) | copy-start | bytes 9437188
  (38 other events, 96.2 us)
Sparse Core Ops, SparseCore 0:
  25.1 27.8 all-gather.13
  54.5 45.9 all-gather.17
  102.4 26.5 all-gather.9
  130.5 45.9 all-gather.21
  178.8 22.2 all-gather.15
  202.8 93.0 all-gather.19
  298.4 23.4 all-gather.11
  323.8 93.0 all-gather.23
  1119.9 34.9 reduce-scatter.13
  1157.9 35.9 reduce-scatter.15
  1197.6 52.8 all-reduce.3
  1254.0 40.5 reduce-scatter.21
  1297.9 41.1 reduce-scatter.25
  1343.0 115.9 reduce-scatter.17
  1462.8 115.9 reduce-scatter.29
  1581.6 21.6 reduce-scatter.33
  1605.5 17.8 reduce-scatter.23
  1625.5 17.9 reduce-scatter.27
  1645.9 42.0 reduce-scatter.19
  1690.1 43.1 reduce-scatter.31
where the time goes:
time: 1750 us; the launch traced here: 1740 us
  waiting for transfers between devices  992 us (57%)
  matrix products  250 us (14%)
  blocking collectives  202 us (12%)
  other arithmetic  132 us (8%)
  local copies, waits for them, and re-layouts  131 us (7%)
    all_gather x1, blocking collectives, shards(): lax.all_gather(router_weight, 'dp', axis=0, tiled=True)  122 us
    reduce_scatter x1, waiting for transfers between devices, shards(): lax.psum_scatter(query_gradient.astype(jnp.bfloat16), 'expert', scatter_d...  120 us
    all_to_all x1, waiting for transfers between devices, shards(): lax.all_to_all(produced.reshape(devices, EXP_DEV * capacity, MODEL_WIDTH)...  103 us
    reduce_scatter x1, waiting for transfers between devices, shards(): lax.psum_scatter(out_gradient.astype(jnp.bfloat16), 'expert', scatter_dim...  102 us
    all_to_all x1, waiting for transfers between devices, shards(): lax.all_to_all(outgoing_grad.reshape(devices, EXP_DEV * capacity, MODEL_W...  98.2 us
    all_gather x1, waiting for transfers between devices, shards(): lax.all_gather(query_rows, 'expert', axis=1, tiled=True)  92.6 us
    all_to_all x1, waiting for transfers between devices, shards(): lax.all_to_all(row_grad.reshape(devices, EXP_DEV * capacity, MODEL_WIDTH)...  91.1 us
    reduce_scatter x1, waiting for transfers between devices, shards(): lax.psum_scatter(value_gradient.astype(jnp.bfloat16), 'expert', scatter_d...  44.5 us
  transfers between devices with their start and end apart: 24, of which 20 were waited for; matrix products, arithmetic and copies ran while one was open for 19% of the time, Pallas kernels for 0%

commit v1 on v0

v1 whole, which is shorter than its diff:
```python
import functools
import math

import jax
import jax.numpy as jnp
from jax import lax
from jax.experimental import pallas as pl
from jax.experimental.pallas import tpu as pltpu
from jax.sharding import PartitionSpec as P

QUERY_HEADS = 32
KEY_VALUE_HEADS = 4
HEAD_SIZE = 128
TOP = 8
EPS = 1e-06
ROTARY_BASE = 1000000.0
VERY_NEGATIVE = -1e30
SOFTMAX_SCALE = HEAD_SIZE ** (-0.5)
LOG2_SCALE = SOFTMAX_SCALE * math.log2(math.e)
VMEM_BYTES = 56 * 1024 * 1024
F32 = jnp.float32
BF16 = jnp.bfloat16


def mm(a, b):
    return lax.dot_general(a, b, (((1,), (0,)), ((), ())), preferred_element_type=F32)


def mm_t(a, b):
    return lax.dot_general(a, b, (((1,), (1,)), ((), ())), preferred_element_type=F32)


def t_mm(a, b):
    return lax.dot_general(a, b, (((0,), (0,)), ((), ())), preferred_element_type=F32)


def row_scale(source):
    return lax.rsqrt(jnp.mean(source * source, axis=-1, keepdims=True) + EPS)


def normalize_back(upstream, source, scaling, gain_row):
    unit_rows = source * scaling
    weighted = upstream * gain_row
    inner_mean = jnp.mean(weighted * unit_rows, axis=-1, keepdims=True)
    return (scaling * (weighted - unit_rows * inner_mean), upstream * unit_rows)


def rotary_tables(span):
    half = HEAD_SIZE // 2
    frequency = jnp.power(ROTARY_BASE, -jnp.arange(half, dtype=F32) * 2.0 / HEAD_SIZE)
    angles = jnp.arange(span, dtype=jnp.int32).astype(F32)[:, None] * frequency[None, :]
    cosine, sine = jnp.cos(angles), jnp.sin(angles)
    return (
        jnp.concatenate([cosine, cosine], axis=-1),
        jnp.concatenate([-sine, sine], axis=-1),
    )


def project_kernel(x_ref, wq_ref, wkv_ref, cos_ref, sin_ref, qg_ref, kg_ref,
                   qraw_ref, kraw_ref, q_ref, k_ref, v_ref):
    x = x_ref[...]
    cosine, sine = cos_ref[...], sin_ref[...]
    q = mm(x, wq_ref[...])
    kv = mm(x, wkv_ref[...])
    qraw_ref[...] = q
    kraw_ref[...] = kv[:, :HEAD_SIZE]
    v_ref[...] = kv[:, HEAD_SIZE:].astype(BF16)

    def turned(u, gain):
        n = u * row_scale(u) * gain
        return (n * cosine + pltpu.roll(n, HEAD_SIZE // 2, 1) * sine).astype(BF16)

    for h in range(q.shape[1] // HEAD_SIZE):
        cols = slice(h * HEAD_SIZE, (h + 1) * HEAD_SIZE)
        q_ref[:, cols] = turned(q[:, cols], qg_ref[...])
    k_ref[...] = turned(kv[:, :HEAD_SIZE], kg_ref[...])


def project(x, wq, wkv, width, cosine, sine, q_gain, k_gain):
    span, model = x.shape
    tile = 256
    row = lambda w: pl.BlockSpec((tile, w), lambda i: (i, 0))
    whole = lambda a, b: pl.BlockSpec((a, b), lambda i: (0, 0))
    return pl.pallas_call(
        project_kernel,
        grid=(span // tile,),
        in_specs=[row(model), whole(model, width), whole(model, 2 * HEAD_SIZE), row(HEAD_SIZE), row(HEAD_SIZE),
                  whole(1, HEAD_SIZE), whole(1, HEAD_SIZE)],
        out_specs=[row(width), row(HEAD_SIZE), row(width), row(HEAD_SIZE), row(HEAD_SIZE)],
        out_shape=[
            jax.ShapeDtypeStruct((span, width), F32),
            jax.ShapeDtypeStruct((span, HEAD_SIZE), F32),
            jax.ShapeDtypeStruct((span, width), BF16),
            jax.ShapeDtypeStruct((span, HEAD_SIZE), BF16),
            jax.ShapeDtypeStruct((span, HEAD_SIZE), BF16),
        ],
        compiler_params=pltpu.CompilerParams(vmem_limit_bytes=VMEM_BYTES),
        cost_estimate=pl.CostEstimate(
            flops=2 * span * model * (width + 256), bytes_accessed=2 * model * (span + width + 256) + span * width * 6,
            transcendentals=0),
        name="project",
    )(x, wq, wkv, cosine, sine, q_gain[None], k_gain[None])


def block_limits(span, tile):
    return [(r0, max(r0 + tile, span // 2)) for r0 in range(0, span, tile)]


def masked(values, r0, limit, prefix):
    tile = values.shape[0]
    rows = r0 + lax.broadcasted_iota(jnp.int32, (tile, limit - r0), 0)
    cols = r0 + lax.broadcasted_iota(jnp.int32, (tile, limit - r0), 1)
    right = jnp.where((cols <= rows) | (cols < prefix), values[:, r0:], 0.0)
    return right if r0 == 0 else jnp.concatenate([values[:, :r0], right], axis=1)


def attend_kernel(tile, prefix_ref, q_ref, k_ref, v_ref, o_ref, l_ref, wide_ref):
    span = q_ref.shape[0]

    @pl.when(pl.program_id(0) == 0)
    def _():
        wide_ref[:, :HEAD_SIZE] = v_ref[...]
        wide_ref[:, HEAD_SIZE:] = jnp.ones((span, HEAD_SIZE), BF16)

    prefix = prefix_ref[0]
    for r0, limit in block_limits(span, tile):
        rows = slice(r0, r0 + tile)
        scores = mm_t(q_ref[rows, :], k_ref[:limit, :])
        weights = masked(jnp.exp2(scores * LOG2_SCALE), r0, limit, prefix)
        sums = mm(weights.astype(BF16), wide_ref[:limit, :])
        inverse = 1.0 / sums[:, HEAD_SIZE:]
        o_ref[rows, :] = (sums[:, :HEAD_SIZE] * inverse).astype(BF16)
        l_ref[rows, :] = inverse


def attend(prefix, q, k, v):
    span, width = q.shape
    heads = width // HEAD_SIZE
    head = pl.BlockSpec((span, HEAD_SIZE), lambda h: (0, h))
    shared = pl.BlockSpec((span, HEAD_SIZE), lambda h: (0, 0))
    return pl.pallas_call(
        functools.partial(attend_kernel, 256),
        grid=(heads,),
        in_specs=[pl.BlockSpec(memory_space=pltpu.SMEM), head, shared, shared],
        out_specs=[head, head],
        out_shape=[jax.ShapeDtypeStruct((span, width), BF16), jax.ShapeDtypeStruct((span, width), F32)],
        scratch_shapes=[pltpu.VMEM((span, 2 * HEAD_SIZE), BF16)],
        compiler_params=pltpu.CompilerParams(vmem_limit_bytes=VMEM_BYTES),
        cost_estimate=pl.CostEstimate(
            flops=8 * heads * span * span * HEAD_SIZE, bytes_accessed=8 * span * width,
            transcendentals=heads * span * span),
        name="attend",
    )(prefix, q, k, v)


def attend_back_kernel(tile, prefix_ref, q_ref, k_ref, v_ref, o_ref, l_ref, do_ref, qraw_ref, kraw_ref, cos_ref, sin_ref,
                       qg_ref, kg_ref, dq_ref, dk_ref, dv_ref, qgg_ref, kgg_ref, dk_sum, dv_sum):
    span = q_ref.shape[0]
    step = pl.program_id(0)

    @pl.when(step == 0)
    def _():
        dk_sum[...] = jnp.zeros_like(dk_sum)
        dv_sum[...] = jnp.zeros_like(dv_sum)
        qgg_ref[...] = jnp.zeros_like(qgg_ref)

    def unturned(grad, rows):
        return grad * cos_ref[rows, :] - pltpu.roll(grad, HEAD_SIZE // 2, 1) * sin_ref[rows, :]

    prefix = prefix_ref[0]
    for r0, limit in block_limits(span, tile):
        rows = slice(r0, r0 + tile)
        q, do = q_ref[rows, :], do_ref[rows, :]
        keys, values = k_ref[:limit, :], v_ref[:limit, :]
        weights = masked(jnp.exp2(mm_t(q, keys) * LOG2_SCALE), r0, limit, prefix)
        probs = weights * jnp.concatenate([l_ref[rows, :]] * (limit // HEAD_SIZE), axis=1)
        delta = jnp.sum(do.astype(F32) * o_ref[rows, :].astype(F32), axis=1, keepdims=True)
        score_grad = (probs * (mm_t(do, values) - delta)).astype(BF16)
        dv_sum[:limit, :] += t_mm(probs.astype(BF16), do)
        dk_sum[:limit, :] += t_mm(score_grad, q)
        turn = unturned(mm(score_grad, keys) * SOFTMAX_SCALE, rows)
        raw = qraw_ref[rows, :]
        back, terms = normalize_back(turn, raw, row_scale(raw), qg_ref[...])
        dq_ref[rows, :] = back.astype(BF16)
        qgg_ref[...] += jnp.sum(terms, axis=0, keepdims=True)

    @pl.when(step == pl.num_programs(0) - 1)
    def _():
        raw = kraw_ref[...]
        turn = unturned(dk_sum[...] * SOFTMAX_SCALE, slice(None))
        back, terms = normalize_back(turn, raw, row_scale(raw), kg_ref[...])
        dk_ref[...] = back.astype(BF16)
        dv_ref[...] = dv_sum[...].astype(BF16)
        kgg_ref[...] = jnp.sum(terms, axis=0, keepdims=True)


def attend_back(prefix, q, k, v, o, inverse, do, qraw, kraw, cosine, sine, q_gain, k_gain):
    span, width = q.shape
    heads = width // HEAD_SIZE
    head = pl.BlockSpec((span, HEAD_SIZE), lambda h: (0, h))
    shared = pl.BlockSpec((span, HEAD_SIZE), lambda h: (0, 0))
    gain = pl.BlockSpec((1, HEAD_SIZE), lambda h: (0, 0))
    return pl.pallas_call(
        functools.partial(attend_back_kernel, 256),
        grid=(heads,),
        in_specs=[pl.BlockSpec(memory_space=pltpu.SMEM), head, shared, shared, head, head, head, head, shared, shared,
                  shared, gain, gain],
        out_specs=[head, shared, shared, gain, gain],
        out_shape=[
            jax.ShapeDtypeStruct((span, width), BF16),
            jax.ShapeDtypeStruct((span, HEAD_SIZE), BF16),
            jax.ShapeDtypeStruct((span, HEAD_SIZE), BF16),
            jax.ShapeDtypeStruct((1, HEAD_SIZE), F32),
            jax.ShapeDtypeStruct((1, HEAD_SIZE), F32),
        ],
        scratch_shapes=[pltpu.VMEM((span, HEAD_SIZE), F32), pltpu.VMEM((span, HEAD_SIZE), F32)],
        compiler_params=pltpu.CompilerParams(vmem_limit_bytes=VMEM_BYTES),
        cost_estimate=pl.CostEstimate(
            flops=16 * heads * span * span * HEAD_SIZE, bytes_accessed=16 * span * width,
            transcendentals=heads * span * span),
        name="attend_back",
    )(prefix, q, k, v, o, inverse, do, qraw, kraw, cosine, sine, q_gain[None], k_gain[None])


def unproject_kernel(dq_ref, dk_ref, dv_ref, wq_ref, wkv_ref, x_ref, out_ref, sum_ref):
    total = mm_t(dq_ref[...], wq_ref[...])
    total += mm_t(dk_ref[...], wkv_ref[:, :HEAD_SIZE]) + mm_t(dv_ref[...], wkv_ref[:, HEAD_SIZE:])
    out_ref[...] = total.astype(BF16)
    part = jnp.sum(total * x_ref[...].astype(F32), axis=0, keepdims=True)

    @pl.when(pl.program_id(0) == 0)
    def _():
        sum_ref[...] = part

    @pl.when(pl.program_id(0) > 0)
    def _():
        sum_ref[...] += part


def unproject(dq, dk, dv, wq, wkv, x):
    span, model = x.shape
    width = dq.shape[1]
    tile = 256
    row = lambda w: pl.BlockSpec((tile, w), lambda i: (i, 0))
    whole = lambda a, b: pl.BlockSpec((a, b), lambda i: (0, 0))
    return pl.pallas_call(
        unproject_kernel,
        grid=(span // tile,),
        in_specs=[row(width), row(HEAD_SIZE), row(HEAD_SIZE), whole(model, width), whole(model, 2 * HEAD_SIZE), row(model)],
        out_specs=[row(model), whole(1, model)],
        out_shape=[jax.ShapeDtypeStruct((span, model), BF16), jax.ShapeDtypeStruct((1, model), F32)],
        compiler_params=pltpu.CompilerParams(vmem_limit_bytes=VMEM_BYTES),
        cost_estimate=pl.CostEstimate(
            flops=2 * span * model * (width + 256), bytes_accessed=2 * model * (2 * span + width + 256),
            transcendentals=0),
        name="unproject",
    )(dq, dk, dv, wq, wkv, x)


def shards(
    tokens,
    routes,
    prefix_len,
    query_weight,
    key_matrix,
    value_matrix,
    out_weight,
    router_weight,
    attention_gain,
    mixture_gain,
    query_gain,
    key_norm_gain,
    expert_gate,
    expert_up,
    expert_down,
    cotangent,
):
    planes, members = lax.axis_size("dp"), lax.axis_size("expert")
    devices = planes * members
    plane, member = lax.axis_index("dp"), lax.axis_index("expert")
    own_rows, model = tokens.shape
    span = own_rows * members
    column = own_rows * planes
    experts = devices
    width = query_weight.shape[1]
    piece = key_matrix.shape[1]
    group = HEAD_SIZE // piece
    block_slots = max(2, 6 * own_rows * TOP // (5 * experts))
    slots = planes * block_slots
    pad_experts = -(-experts // HEAD_SIZE) * HEAD_SIZE
    gate, up, down = expert_gate[0], expert_up[0], expert_down[0]

    def gather(array, axis, dimension=0):
        return lax.all_gather(array, axis, axis=dimension, tiled=True)

    def exchange(array, axis):
        return lax.all_to_all(array, axis, split_axis=0, concat_axis=0, tiled=True)

    qkv_part = jnp.concatenate([query_weight, key_matrix, value_matrix], axis=1)
    residual_in = tokens.astype(F32)
    scale_attention = row_scale(residual_in)
    normed_own = (residual_in * scale_attention * attention_gain).astype(BF16)
    normed = gather(normed_own, "expert")
    qkv_rows = gather(qkv_part, "dp")
    kv_own = qkv_rows[:, width:]
    place = member % group
    kv_parts = [kv_own]
    for shift in range(1, group):
        pairs = [(e - e % group + (e % group + shift) % group, e) for e in range(members)]
        kv_parts.append(lax.ppermute(kv_own, "expert", pairs))

    def kv_piece(j):
        value = kv_parts[0]
        for shift in range(1, group):
            value = jnp.where((place + shift) % group == j, kv_parts[shift], value)
        return value

    ordered = [kv_piece(j) for j in range(group)]
    kv_weight = jnp.concatenate([p[:, :piece] for p in ordered] + [p[:, piece:] for p in ordered], axis=1)

    cosine, sine = rotary_tables(span)
    qraw, kraw, query_low, key_low, value_low = project(
        normed, qkv_rows, kv_weight, width, cosine, sine, query_gain, key_norm_gain)
    attended_low, inverse = attend(prefix_len, query_low, key_low, value_low)

    out_columns = gather(out_weight, "dp")
    attended_all = gather(attended_low, "expert").reshape(members, span, width)
    out_by_member = out_columns.reshape(members, width, out_columns.shape[1])
    projected = sum(mm(attended_all[m], out_by_member[m]) for m in range(members))
    out_piece = out_columns.shape[1]
    projected = exchange(projected.astype(BF16), "expert").reshape(members, own_rows, out_piece)
    projected = jnp.transpose(projected, (1, 0, 2)).reshape(own_rows, model)
    out_heads = exchange(out_columns, "expert").reshape(members, width, out_piece)
    out_heads = jnp.transpose(out_heads, (1, 0, 2)).reshape(width, model)

    expert_ids = jnp.arange(experts, dtype=jnp.int32)
    mask_own = jnp.sum((routes[:, :, None] == expert_ids[None, None, :]).astype(F32), axis=1)
    mask_wide = jnp.pad(mask_own, ((0, 0), (0, pad_experts - experts))).astype(BF16)
    upstream_own = jnp.concatenate([cotangent, mask_wide], axis=1)
    upstream_column = gather(upstream_own, "dp")
    mask_plane = lax.dynamic_slice(upstream_column, (0, model + plane * members), (column, members))
    triangle = (jnp.arange(column)[:, None] >= jnp.arange(column)[None, :]).astype(BF16)
    rank = jnp.where(mask_plane > 0, mm(triangle, mask_plane) - 1.0, -1.0).astype(jnp.int32)
    pick = (rank.T[:, None, :] == jnp.arange(slots, dtype=jnp.int32)[None, :, None])
    pick = pick.reshape(members * slots, column).astype(BF16)

    upstream_rows = exchange(mm(pick, upstream_column).astype(BF16), "expert")
    upstream_arrived, mask_arrived = upstream_rows[:, :model], upstream_rows[:, model:model + experts].astype(F32)
    upstream_down = mm_t(upstream_arrived, down)

    router = gather(gather(router_weight.T, "expert"), "dp", 1)

    after_attn = residual_in + projected.astype(F32)
    scale_mixture = row_scale(after_attn)
    mixed_low = (after_attn * scale_mixture * mixture_gain).astype(BF16)
    mixed_column = gather(mixed_low, "dp")
    arrived = exchange(mm(pick, mixed_column).astype(BF16), "expert")

    def route_weights(rows, mask):
        logits = jnp.where(mask > 0, mm_t(rows, router), VERY_NEGATIVE)
        raised = jnp.where(mask > 0, jnp.exp(logits - jnp.max(logits, axis=-1, keepdims=True)), 0.0)
        return raised / jnp.maximum(jnp.sum(raised, axis=-1, keepdims=True), 1e-30)

    own_expert = plane * members + member
    weight_arrived = jnp.sum(
        jnp.where(expert_ids[None, :] == own_expert, route_weights(arrived, mask_arrived), 0.0), axis=-1, keepdims=True)
    weight_own = route_weights(mixed_low, mask_own)

    gate_raw = mm(arrived, gate)
    up_raw = mm(arrived, up)
    gate_sig = jax.nn.sigmoid(gate_raw)
    silu = gate_raw * gate_sig
    activated_full = silu * up_raw
    activated = activated_full.astype(BF16)
    activated_grad = weight_arrived * upstream_down
    gate_grad = (activated_grad * up_raw * gate_sig * (1.0 + gate_raw * (1.0 - gate_sig))).astype(BF16)
    up_grad = (activated_grad * silu).astype(BF16)
    route_grad = jnp.sum(activated.astype(F32) * upstream_down, axis=-1, keepdims=True)
    row_grad = (mm_t(gate_grad, gate) + mm_t(up_grad, up)).astype(BF16)
    here = (expert_ids[None, :] == own_expert).astype(F32)
    route_high = route_grad.astype(BF16)
    route_rest = (route_grad - route_high.astype(F32)).astype(BF16)
    pad_both = -(-2 * experts // HEAD_SIZE) * HEAD_SIZE
    route_columns = jnp.concatenate(
        [here * route_high.astype(F32), here * route_rest.astype(F32),
         jnp.zeros((row_grad.shape[0], pad_both - 2 * experts), F32)], axis=1).astype(BF16)
    back_rows = exchange(jnp.concatenate([row_grad, route_columns], axis=1), "expert")
    back_column = t_mm(pick, back_rows).astype(BF16)
    back_own = lax.psum_scatter(back_column, "dp", scatter_dimension=0, tiled=True).astype(F32)

    produced = (weight_arrived * mm(activated, down)).astype(BF16)
    mixture_rows = exchange(produced, "expert")
    mixture_column = t_mm(pick, mixture_rows).astype(BF16)
    mixture = lax.psum_scatter(mixture_column, "dp", scatter_dimension=0, tiled=True).astype(F32)
    layer_out = (after_attn + mixture).astype(BF16)

    produced_grad = (weight_arrived * upstream_arrived.astype(F32)).astype(BF16)
    down_gradient = t_mm(activated, produced_grad)
    gate_gradient = t_mm(arrived, gate_grad)
    up_gradient = t_mm(arrived, up_grad)

    upstream = cotangent.astype(F32)
    route_back = back_own[:, model:model + experts] + back_own[:, model + experts:model + 2 * experts]
    chosen_grad = weight_own * (route_back - jnp.sum(weight_own * route_back, axis=-1, keepdims=True))
    logit_grad = chosen_grad.astype(BF16)
    mixed_grad = mm(logit_grad, router) + back_own[:, :model]
    mixture_back, mixture_terms = normalize_back(mixed_grad, after_attn, scale_mixture, mixture_gain)
    after_grad = upstream + mixture_back
    after_low = after_grad.astype(BF16)
    router_part = t_mm(logit_grad, mixed_low).astype(BF16)

    after_all = gather(after_low, "expert")
    attended_grad = mm_t(after_all, out_heads).astype(BF16)
    after_columns = lax.dynamic_slice(after_all, (0, member * out_piece), (span, out_piece))
    out_partial = jnp.concatenate([t_mm(attended_all[m], after_columns) for m in range(members)], axis=0)
    out_share = lax.psum_scatter(out_partial.astype(BF16), "dp", scatter_dimension=0, tiled=True).astype(F32)
    dq, dk, dv, query_terms, key_terms = attend_back(
        prefix_len, query_low, key_low, value_low, attended_low, inverse, attended_grad, qraw, kraw, cosine, sine,
        query_gain, key_norm_gain)
    normed_partial, attention_terms = unproject(dq, dk, dv, qkv_rows, kv_weight, normed)
    normed_grad = lax.psum_scatter(normed_partial, "expert", scatter_dimension=0, tiled=True).astype(F32)
    input_back, _ = normalize_back(normed_grad, residual_in, scale_attention, attention_gain)
    input_grad = after_grad + input_back

    query_partial = t_mm(normed, dq).astype(BF16)
    kv_partial = jnp.concatenate([t_mm(normed, dk), t_mm(normed, dv)], axis=1)

    def kv_cols(j):
        start = j * piece
        return jnp.concatenate(
            [lax.dynamic_slice(kv_partial, (0, start), (model, piece)),
             lax.dynamic_slice(kv_partial, (0, HEAD_SIZE + start), (model, piece))], axis=1)

    kv_total = kv_cols(place)
    for shift in range(1, group):
        pairs = [(e, e - e % group + (e % group + shift) % group) for e in range(members)]
        kv_total += lax.ppermute(kv_cols((place + shift) % group).astype(BF16), "expert", pairs).astype(F32)
    qkv_partial = jnp.concatenate([query_partial, kv_total.astype(BF16)], axis=1)
    qkv_share = lax.psum_scatter(qkv_partial, "dp", scatter_dimension=0, tiled=True).astype(F32)
    query_share = qkv_share[:, :width]
    key_share = qkv_share[:, width:width + piece]
    value_share = qkv_share[:, width + piece:]

    router_share = lax.psum_scatter(router_part, "expert", scatter_dimension=0, tiled=True)
    router_share = lax.psum_scatter(router_share, "dp", scatter_dimension=1, tiled=True).astype(F32).T

    attention_total, mixture_total, query_total, key_total = lax.psum(
        (attention_terms[0] / attention_gain, jnp.sum(mixture_terms, axis=0), query_terms[0], key_terms[0]),
        ("dp", "expert"))
    return (
        layer_out,
        input_grad,
        query_share,
        key_share,
        value_share,
        out_share,
        router_share,
        attention_total,
        mixture_total,
        query_total,
        key_total,
        gate_gradient[None],
        up_gradient[None],
        down_gradient[None],
    )


def solution(mesh):
    rows = P(("dp", "expert"), None)
    grid = P("dp", "expert")
    experts = P(("dp", "expert"), None, None)
    in_specs = (rows, rows, P("dp"), grid, grid, grid, grid, grid, P(), P(), P(), P(), experts, experts, experts, rows)
    out_specs = (rows, rows, grid, grid, grid, grid, grid, P(), P(), P(), P(), experts, experts, experts)
    return jax.shard_map(shards, mesh=mesh, in_specs=in_specs, out_specs=out_specs, check_vma=False)
```

time: 1750 us -> 946 us (0.54)
  waiting for transfers between devices: 992 us -> 402 us
  matrix products: 250 us -> 148 us
  other arithmetic: 132 us -> 32.2 us
  local copies, waits for them, and re-layouts: 131 us -> 36.4 us
  Pallas kernels: 0 us -> 40.3 us
  blocking collectives: 202 us -> 240 us
    reduce_scatter x10 -> x5, waiting for transfers between devices: 437 us -> 56 us  [the longest x1 43.6 us: shards(): lax.psum_scatter(back_column, 'dp', scatter_dimension=0, tiled=True)]
    all_to_all x4, waiting for transfers between devices: 292 us -> 31.2 us  [exchange(): return lax.all_to_all(array, axis, split_axis=0, concat_axis=0, tiled=True)]
    all_to_all x0 -> x2, blocking collectives: none -> 125 us  [exchange(): return lax.all_to_all(array, axis, split_axis=0, concat_axis=0, tiled=True)]
    dot_general x60 -> x38, matrix products: 250 us -> 148 us  [the longest x17 62.7 us: t_mm(): lax.dot_general(a, b, (((0,), (0,)), ((), ())), preferred_element_type=F32)]
    all_gather x4 -> x2, blocking collectives: 163 us -> 74.1 us  [gather(): return lax.all_gather(array, axis, axis=dimension, tiled=True)]
    all_gather x8 -> x7, waiting for transfers between devices: 255 us -> 296 us  [gather(): return lax.all_gather(array, axis, axis=dimension, tiled=True)]
    pallas_call x0 -> x4, Pallas kernels: none -> 40.3 us  [the longest x1 15.8 us: attend_back(): pl.pallas_call(functools.partial(attend_back_kernel, 256), grid=(heads,),...]
    reshape x8 -> x0, local copies, waits for them, and re-layouts: 39.7 us -> none  [the longest x1 7.47 us: shards(): back_rows.reshape(experts_all * capacity, MODEL_WIDTH)[slot_index]]
  transfers between devices with their start and end apart: 24 -> 20, of which waited for: 20 -> 13; matrix products, arithmetic and copies ran while one was open for 19% -> 14% of each run, Pallas kernels for 0% -> 4%
where the time goes in v1:
time: 946 us; the launch traced here: 935 us
  waiting for transfers between devices  402 us (42%)
  blocking collectives  240 us (25%)
  matrix products  148 us (16%)
  Pallas kernels  40.3 us (4%)
  local copies, waits for them, and re-layouts  36.4 us (4%)
  other arithmetic  32.2 us (3%)
  starting transfers between devices  19.1 us (2%)
  between operations  16.3 us (2%)
    all_gather x7, waiting for transfers between devices, gather(): return lax.all_gather(array, axis, axis=dimension, tiled=True)  296 us
    all_to_all x2, blocking collectives, exchange(): return lax.all_to_all(array, axis, split_axis=0, concat_axis=0, tiled=True)  125 us
    all_gather x2, blocking collectives, gather(): return lax.all_gather(array, axis, axis=dimension, tiled=True)  74.1 us
    dot_general x17, matrix products, t_mm(): lax.dot_general(a, b, (((0,), (0,)), ((), ())), preferred_element_type=F32)  62.7 us
    dot_general x15, matrix products, mm(): lax.dot_general(a, b, (((1,), (0,)), ((), ())), preferred_element_type=F32)  46.6 us
    reduce_scatter x1, waiting for transfers between devices, shards(): lax.psum_scatter(back_column, 'dp', scatter_dimension=0, tiled=True)  43.6 us
    psum x1, blocking collectives, shards(): lax.psum((attention_terms[0] / attention_gain, jnp.sum(mixture_terms, axi...  41.2 us
    dot_general x6, matrix products, mm_t(): lax.dot_general(a, b, (((1,), (1,)), ((), ())), preferred_element_type=F32)  39.1 us
  transfers between devices with their start and end apart: 20, of which 13 were waited for; matrix products, arithmetic and copies ran while one was open for 14% of the time, Pallas kernels for 4%

profile of v1, /device:TPU:0, one launch (start us, length us, event | category | flops | bytes accessed | tf_op | source)
XLA Modules:
  0.0 935.3 jit_solution(2744020581462370427)
XLA Ops:
  9.3 2.0 pad_maximum_fusion.2
  13.2 2.0 fusion.35
  15.3 2.0 copy.82
  17.4 1.9 fusion.59
  19.9 49.1 %all-gather.11.cloned.1.call-done.wq_ref = bf16[2048,640]{1,0:T(8,128)(2,1)} async-done(((bf16[512,640]{1,0:T(8,128)(2,1)}), bf16[2048,640]{1,0:T(8,128)(2,1)}) %all-gather.11.cloned.1.call-update) | async-done | bytes 2621456 | tf_op jit(solution)/shard_map/all_gather | solution.py:294
  71.6 1.9 fusion.74
  78.2 28.8 %all-gather.9.cloned.1.call-done.x_ref = bf16[1024,2048]{1,0:T(8,128)(2,1)} async-done(((bf16[128,2048]{1,0:T(8,128)(2,1)}), bf16[1024,2048]{1,0:T(8,128)(2,1)}) %all-gather.9.cloned.1.call-update) | async-done | bytes 4194320 | tf_op jit(solution)/shard_map/all_gather | solution.py:294
  107.0 8.5 project.1
  115.5 6.9 attend.1
  122.6 35.0 %all-gather.17.cloned.1.call-done = bf16[512,2176]{0,1:T(8,128)(2,1)} async-done(((bf16[128,2176]{0,1:T(8,128)(2,1)}), bf16[512,2176]{0,1:T(8,128)(2,1)}) %all-gather.17.cloned.1.call-update) | async-done | bytes 2228240 | tf_op jit(solution)/shard_map/all_gather | solution.py:294
  159.8 43.3 %all-gather.15.cloned.1.call-done = bf16[4096,256]{1,0:T(8,128)(2,1)} async-done(((bf16[1024,256]{1,0:T(8,128)(2,1)}), bf16[4096,256]{1,0:T(8,128)(2,1)}) %all-gather.15.cloned.1.call-update) | async-done | bytes 2097168 | tf_op jit(solution)/shard_map/all_gather | solution.py:294
  203.2 55.4 %all-gather.13.cloned.1.call-done = bf16[8192,512]{1,0:T(8,128)(2,1)} async-done(((bf16[1024,512]{1,0:T(8,128)(2,1)}), bf16[8192,512]{1,0:T(8,128)(2,1)}) %all-gather.13.cloned.1.call-update) | async-done | bytes 8388624 | tf_op jit(solution)/shard_map/all_gather | solution.py:294
  260.5 2.1 convolution_add_fusion.7
  268.4 4.4 all-to-all-start
  272.8 7.3 convolution_convert_fusion
  280.1 2.4 all-to-all-done
  282.5 4.7 all-to-all-start.1
  290.8 47.4 %all-gather.19.cloned.1.call-done = bf16[512,2048]{1,0:T(8,128)(2,1)} async-done(((bf16[128,2048]{1,0:T(8,128)(2,1)}), bf16[512,2048]{1,0:T(8,128)(2,1)}) %all-gather.19.cloned.1.call-update) | async-done | bytes 2097168 | tf_op jit(solution)/shard_map/all_gather | solution.py:294
  338.2 6.8 convolution_convert_fusion.1
  345.0 3.1 all-to-all-done.1
  348.1 4.8 all-to-all-start.2
  352.9 60.6 %all-gather = bf16[8,4,512]{2,1,0:T(4,128)(2,1)S(1)} all-gather(bf16[1,4,512]{2,1,0:T(4,128)(2,1)S(1)} %bitcast.103), channel_id=1, replica_groups=mesh['dp'=4,'expert'=8] {'expert'}, dimensions={0}, use_global_device_ids=true | all-gather | bytes 36864 | tf_op jit(solution)/shard_map/all_gather | solution.py:294
  413.6 13.5 %all_gather.34 = bf16[32,2048]{1,0:T(8,128)(2,1)S(1)} all-gather(bf16[32,512]{1,0:T(8,128)(2,1)S(1)} %reshape.162), channel_id=1, replica_groups=mesh['dp'=4,'expert'=8] {'dp'}, dimensions={1}, use_global_device_ids=true | all-gather | bytes 163840 | tf_op jit(solution)/shard_map/all_gather | solution.py:294
  429.9 7.5 fusion.11
  437.4 6.0 fusion.15
  443.4 4.0 fusion.102
  447.5 9.4 %multiply_reduce_fusion = (f32[1216]{0:T(1024)S(1)}, bf16[1216,768]{1,0:T(8,128)(2,1)}, bf16[1216,768]{1,0:T(8,128)(2,1)S(1)}, bf16[1216,768]{1,0:T(8,128)(2,1)}) fusion(f32[1216,768]{1,0:T(8,128)S(1)} %fusion.11, f32[1216,768]{1,0:T(8,128)S(1)} %fusion.15, f32[1216]{0:T(1024)S(1)} %select_reduce_fusion, bf16[1,768,2048]{2,1,0:T(8,128)(2,1)S(1)} %copy-done, ...), kind=kOutput, calls=%fused_computation.16 | convolution fusion | flops 3842947840 | bytes 21210624 | tf_op jit(solution)/shard_map/dot_general | solution.py:30
  456.9 6.5 fusion.13
  465.4 11.7 %add_convert_fusion = bf16[1216,2048]{1,0:T(8,128)(2,1)} fusion(f32[1216,2048]{1,0:T(8,128)} %fusion.13, bf16[1216,768]{1,0:T(8,128)(2,1)} %get-tuple-element.137, bf16[1,2048,768]{2,1,0:T(8,128)(2,1)} %param.29), kind=kOutput, calls=%fused_computation.2 | convolution fusion | flops 3830185984 | bytes 19955712 | tf_op jit(solution)/shard_map/dot_general | solution.py:30
  477.8 8.9 concatenate.43
  486.7 64.5 %all_to_all.60 = bf16[8,152,2176]{2,1,0:T(8,128)(2,1)S(1)} all-to-all(bf16[8,152,2176]{2,1,0:T(8,128)(2,1)} %bitcast.92), channel_id=1, replica_groups=mesh['dp'=4,'expert'=8] {'expert'}, dimensions={0} | all-to-all | bytes 10584064 | tf_op jit(solution)/shard_map/all_to_all | solution.py:297
  551.2 4.6 fusion.2
  557.6 43.6 %reduce-scatter.11.cloned.1.call-done = bf16[128,2176]{1,0:T(8,128)(2,1)} async-done(((bf16[512,2176]{1,0:T(8,128)(2,1)}), bf16[128,2176]{1,0:T(8,128)(2,1)}) %reduce-scatter.11.cloned.1.call-update) | async-done | bytes 557072 | tf_op jit(solution)/shard_map/reduce_scatter | solution.py:389
  602.7 2.6 multiply_reduce_fusion.1
  606.3 2.8 fusion.98
  609.1 4.4 all-to-all-start.5
  614.8 25.7 %all-to-all-done.5 = bf16[8,512,256]{2,1,0:T(8,128)(2,1)} async-done(((bf16[8,512,256]{2,1,0:T(8,128)(2,1)}), bf16[8,512,256]{2,1,0:T(8,128)(2,1)}, u32[]{:S(2)}, u32[]{:S(2)}) %all-to-all-start.5) | async-done | bytes 2097184 | tf_op jit(solution)/shard_map/all_to_all | solution.py:297
  640.5 3.9 copy.88
  644.4 18.5 %all-reduce.5.cloned.1.call-done = bf16[32,2048]{1,0:T(8,128)(2,1)} async-done(((bf16[32,2048]{1,0:T(8,128)(2,1)}), bf16[32,2048]{1,0:T(8,128)(2,1)}) %all-reduce.5.cloned.1.call-update) | async-done | bytes 131088
  664.8 36.9 %all-gather.21.cloned.1.call-done = bf16[1024,2048]{1,0:T(8,128)(2,1)} async-done(((bf16[128,2048]{1,0:T(8,128)(2,1)}), bf16[1024,2048]{1,0:T(8,128)(2,1)}) %all-gather.21.cloned.1.call-update) | async-done | bytes 4194320 | tf_op jit(solution)/shard_map/all_gather | solution.py:294
  701.6 2.7 fusion.30
  704.3 2.6 fusion.29
  706.9 2.4 fusion.28
  709.3 2.4 fusion.27
  711.7 2.4 fusion.26
  714.2 2.4 fusion.25
  716.6 2.4 fusion.24
  719.0 2.4 fusion.23
  721.5 6.2 convolution_convert_fusion.4.do_ref
  727.7 15.8 %attend_back.1 = (bf16[1024,512]{1,0:T(8,128)(2,1)}, bf16[1024,128]{1,0:T(8,128)(2,1)}, bf16[1024,128]{1,0:T(8,128)(2,1)}, f32[1,128]{1,0:T(1,128)}, f32[1,128]{1,0:T(1,128)}) custom-call(s32[1]{0:T(128)S(6)} %copy.106.prefix_ref, bf16[1024,512]{1,0:T(8,128)(2,1)} %get-tuple-element.28.q_ref, bf16[1024,128]{1,0:T(8,128)(2,1)} %get-tuple-element.29.k_ref, ...), custom_call_target="tpu_custom_call" | custom-call | flops 8589934592 | bytes 8388608 | tf_op jit(solution)/shard_map/attend_back/pallas_call | solution.py:203
  747.2 2.4 convolution_convert_fusion.2
  751.6 9.1 unproject.1
  760.7 5.8 multiply_convert_fusion.1
  766.5 60.3 %all_to_all.61 = bf16[8,152,2048]{2,1,0:T(8,128)(2,1)S(1)} all-to-all(bf16[8,152,2048]{2,1,0:T(8,128)(2,1)S(1)} %bitcast.96), channel_id=1, replica_groups=mesh['dp'=4,'expert'=8] {'expert'}, dimensions={0} | all-to-all | bytes 9961472 | tf_op jit(solution)/shard_map/all_to_all | solution.py:297
  826.9 4.2 bitcast_convert_fusion
  831.1 10.7 %convolution_bitcast_fusion.2 = f32[1,2048,768]{2,1,0:T(8,128)} fusion(bf16[1216,2048]{1,0:T(8,128)(2,1)} %bitcast.9, bf16[1216,768]{1,0:T(8,128)(2,1)} %copy-done.22), kind=kOutput, calls=%fused_computation.15 | convolution fusion | flops 3825205248 | bytes 13139968 | tf_op jit(solution)/shard_map/dot_general | solution.py:34
  841.8 8.7 convolution_bitcast_fusion.1
  850.5 8.8 fusion.6
  861.0 41.2 %all-reduce.2 = (f32[2048]{0:T(1024)}, f32[2048]{0:T(1024)}, f32[128]{0:T(128)}, f32[128]{0:T(128)}) all-reduce(f32[2048]{0:T(1024)S(1)} %div.57, f32[2048]{0:T(1024)S(1)} %get-tuple-element.126, f32[128]{0:T(128)S(1)} %bitcast.104, f32[128]{0:T(128)S(1)} %bitcast.105), channel_id=1, replica_groups=mesh['dp'=4,'expert'=8] {'dp','expert'}, use_global_device_ids=true, to_apply=%region_19.20 | all-reduce | flops 4352 | bytes 34816 | tf_op jit(solution)/shard_map/psum | solution.py:447
  902.2 2.1 convert_element_type.215
  904.3 2.2 slice.166
  906.5 2.5 copy.89
  912.2 12.4 %reduce-scatter.9.cloned.1.call-done = bf16[128,2048]{1,0:T(8,128)(2,1)} async-done(((bf16[512,2048]{1,0:T(8,128)(2,1)}), bf16[128,2048]{1,0:T(8,128)(2,1)}) %reduce-scatter.9.cloned.1.call-update) | async-done | bytes 524304 | tf_op jit(solution)/shard_map/reduce_scatter | solution.py:394
  924.6 3.8 fusion.39
  (152 shorter events, 47.7 us)
Async XLA Ops:
  7.2 440.3 %copy-start = (bf16[1,768,2048]{2,1,0:T(8,128)(2,1)S(1)}, bf16[1,768,2048]{2,1,0:T(8,128)(2,1)}, u32[]{:S(2)}) copy-start(bf16[1,768,2048]{2,1,0:T(8,128)(2,1)} %param.30) | copy-start | bytes 9437188
  7.2 8.1 copy-start.13
  7.2 61.8 %all-gather.11.cloned.1.call-start = ((), (), s32[]{:S(2)}) async-start(), calls=%async_computation.13 | async-start | bytes 3276800 | tf_op jit(solution)/shard_map/all_gather | solution.py:294
  11.3 95.6 %all-gather.9.cloned.1.call-start = ((), (), s32[]{:S(2)}) async-start(), calls=%async_computation.12 | async-start | bytes 4718592 | tf_op jit(solution)/shard_map/all_gather | solution.py:294
  12.6 0.5 copy-start.11
  15.2 142.3 %all-gather.17.cloned.1.call-start = ((), (), s32[]{:S(2)}) async-start(), calls=%async_computation.16 | async-start | bytes 2785280 | tf_op jit(solution)/shard_map/all_gather | solution.py:294
  19.3 183.9 %all-gather.15.cloned.1.call-start = ((), (), s32[]{:S(2)}) async-start(), calls=%async_computation.15 | async-start | bytes 2621440 | tf_op jit(solution)/shard_map/all_gather | solution.py:294
  19.8 238.8 %all-gather.13.cloned.1.call-start = ((), (), s32[]{:S(2)}) async-start(), calls=%async_computation.14 | async-start | bytes 9437184 | tf_op jit(solution)/shard_map/all_gather | solution.py:294
  70.9 4.0 collective-permute-start
  258.6 5.8 copy-start.4
  262.6 3.3 copy-start.6
  268.4 14.1 %all-to-all-start = ((bf16[8,128,256]{2,1,0:T(8,128)(2,1)}), bf16[8,128,256]{2,1,0:T(8,128)(2,1)}, u32[]{:S(2)}, u32[]{:S(2)}) async-start(bf16[8,128,256]{2,1,0:T(8,128)(2,1)} %bitcast.100), calls=%async_computation | async-start | bytes 1048576 | tf_op jit(solution)/shard_map/all_to_all | solution.py:297
  282.5 65.6 %all-to-all-start.1 = ((bf16[8,152,2176]{2,1,0:T(8,128)(2,1)}), bf16[8,152,2176]{2,1,0:T(8,128)(2,1)}, u32[]{:S(2)}, u32[]{:S(2)}) async-start(bf16[8,152,2176]{2,1,0:T(8,128)(2,1)} %bitcast.94), calls=%async_computation.1 | async-start | bytes 10584064 | tf_op jit(solution)/shard_map/all_to_all | solution.py:297
  287.2 2.6 copy-start.8
  287.2 51.0 %all-gather.19.cloned.1.call-start = ((), (), s32[]{:S(2)}) async-start(), calls=%async_computation.17 | async-start | bytes 2621440 | tf_op jit(solution)/shard_map/all_gather | solution.py:294
  287.2 1.3 copy-start.3
  288.8 1.0 copy-start.1
  348.1 4.8 copy-start.14
  348.1 81.8 %all-to-all-start.2 = ((bf16[8,152,2048]{2,1,0:T(8,128)(2,1)}), bf16[8,152,2048]{2,1,0:T(8,128)(2,1)}, u32[]{:S(2)}, u32[]{:S(2)}) async-start(bf16[8,152,2048]{2,1,0:T(8,128)(2,1)} %bitcast.95), calls=%async_computation.2 | async-start | bytes 9961472 | tf_op jit(solution)/shard_map/all_to_all | solution.py:297
  352.8 248.3 %reduce-scatter.11.cloned.1.call-start = ((), (), s32[]{:S(2)}) async-start(), calls=%async_computation.19 | async-start | bytes 2785280 | tf_op jit(solution)/shard_map/reduce_scatter | solution.py:389
  429.9 7.5 copy-start.18
  456.9 6.5 copy-start.22
  555.8 107.1 %all-reduce.5.cloned.1.call-start = ((), (), s32[]{:S(2)}) async-start(), calls=%async_computation.25 | async-start | bytes 262144
  601.2 4.1 copy-start.5
  606.2 95.4 %all-gather.21.cloned.1.call-start = ((), (), s32[]{:S(2)}) async-start(), calls=%async_computation.20 | async-start | bytes 4718592 | tf_op jit(solution)/shard_map/all_gather | solution.py:294
  606.3 7.3 copy-start.19
  609.1 31.4 %all-to-all-start.5 = ((bf16[8,512,256]{2,1,0:T(8,128)(2,1)}), bf16[8,512,256]{2,1,0:T(8,128)(2,1)}, u32[]{:S(2)}, u32[]{:S(2)}) async-start(bf16[8,512,256]{2,1,0:T(8,128)(2,1)} %bitcast.93), calls=%async_computation.7 | async-start | bytes 4194304 | tf_op jit(solution)/shard_map/all_to_all | solution.py:297
  613.5 245.9 %reduce-scatter.19.cloned.1.call-start = ((), (), s32[]{:S(2)}) async-start(), calls=%async_computation.24 | async-start | bytes 655360
  664.7 237.5 %reduce-scatter.17.cloned.1.call-start = ((), (), s32[]{:S(2)}) async-start(), calls=%async_computation.23 | async-start | bytes 2621440 | tf_op jit(solution)/shard_map/reduce_scatter | solution.py:416
  701.6 5.3 copy-start.17
  721.4 182.9 %reduce-scatter.15.cloned.1.call-start = ((), (), s32[]{:S(2)}) async-start(), calls=%async_computation.22 | async-start | bytes 3276800 | tf_op jit(solution)/shard_map/reduce_scatter | solution.py:439
  727.7 15.8 %copy-start.2 = (bf16[1024,2048]{1,0:T(8,128)(2,1)S(1)}, bf16[1024,2048]{1,0:T(8,128)(2,1)}, u32[]{:S(2)}) copy-start(bf16[1024,2048]{1,0:T(8,128)(2,1)} %all-gather.9.cloned.1.call-done.x_ref) | copy-start | bytes 12582916
  743.4 1.8 copy-start.7
  746.0 1.2 copy-start.20
  746.3 3.4 collective-permute-start.1
  751.5 159.1 %reduce-scatter.13.cloned.1.call-start = ((), (), s32[]{:S(2)}) async-start(), calls=%async_computation.21 | async-start | bytes 4718592 | tf_op jit(solution)/shard_map/reduce_scatter | solution.py:421
  760.6 163.9 %reduce-scatter.9.cloned.1.call-start = ((), (), s32[]{:S(2)}) async-start(), calls=%async_computation.18 | async-start | bytes 2621440 | tf_op jit(solution)/shard_map/reduce_scatter | solution.py:394
  831.1 10.7 %copy-start.23 = (bf16[1216,768]{1,0:T(8,128)(2,1)S(1)}, bf16[1216,768]{1,0:T(8,128)(2,1)}, u32[]{:S(2)}) copy-start(bf16[1216,768]{1,0:T(8,128)(2,1)} %get-tuple-element.137) | copy-start | bytes 5603332
  841.8 8.7 copy-start.21
  850.5 10.5 %copy-start.9 = (f32[2048]{0:T(1024)S(1)}, f32[2048]{0:T(1024)}, u32[]{:S(2)}) copy-start(f32[2048]{0:T(1024)} %param.24) | copy-start | bytes 24580
  850.5 10.5 %copy-start.10 = (f32[1,2048]{1,0:T(1,128)S(1)}, f32[1,2048]{1,0:T(1,128)}, u32[]{:S(2)}) copy-start(f32[1,2048]{1,0:T(1,128)} %get-tuple-element.39) | copy-start | bytes 24580
  850.5 10.5 %copy-start.15 = (f32[1,128]{1,0:T(1,128)S(1)}, f32[1,128]{1,0:T(1,128)}, u32[]{:S(2)}) copy-start(f32[1,128]{1,0:T(1,128)} %get-tuple-element.40) | copy-start | bytes 1540
  850.5 10.5 %copy-start.16 = (f32[1,128]{1,0:T(1,128)S(1)}, f32[1,128]{1,0:T(1,128)}, u32[]{:S(2)}) copy-start(f32[1,128]{1,0:T(1,128)} %get-tuple-element.41) | copy-start | bytes 1540
  859.4 51.3 %copy-start.12 = (f32[128]{0:T(128)S(1)}, f32[128]{0:T(128)}, u32[]{:S(2)}) copy-start(f32[128]{0:T(128)} %copy-done.11) | copy-start | bytes 1540
Sparse Core Ops, SparseCore 0:
  11.5 57.4 all-gather.10
  71.5 35.4 all-gather.8
  109.1 48.3 all-gather.16
  159.0 44.1 all-gather.14
  205.5 53.0 all-gather.12
  290.9 47.2 all-gather.18
  555.9 45.1 reduce-scatter.10
  606.3 56.4 all-reduce.4
  665.5 36.0 all-gather.20
  703.8 21.6 reduce-scatter.18
  727.9 42.1 reduce-scatter.16
  772.3 51.4 reduce-scatter.14
  827.1 51.1 reduce-scatter.12
  880.6 43.9 reduce-scatter.8

commit v2 on v1

v2 whole, which is shorter than its diff:
```python
import functools
import math

import jax
import jax.numpy as jnp
from jax import lax
from jax.experimental import pallas as pl
from jax.experimental.pallas import tpu as pltpu
from jax.sharding import PartitionSpec as P

QUERY_HEADS = 32
KEY_VALUE_HEADS = 4
HEAD_SIZE = 128
TOP = 8
EPS = 1e-06
ROTARY_BASE = 1000000.0
VERY_NEGATIVE = -1e30
SOFTMAX_SCALE = HEAD_SIZE ** (-0.5)
LOG2_SCALE = SOFTMAX_SCALE * math.log2(math.e)
VMEM_BYTES = 56 * 1024 * 1024
F32 = jnp.float32
BF16 = jnp.bfloat16


def cost(microseconds):
    return pl.CostEstimate(flops=int(microseconds * 1.1e9) + 1, bytes_accessed=1, transcendentals=0)


def mm(a, b):
    return lax.dot_general(a, b, (((1,), (0,)), ((), ())), preferred_element_type=F32)


def mm_t(a, b):
    return lax.dot_general(a, b, (((1,), (1,)), ((), ())), preferred_element_type=F32)


def t_mm(a, b):
    return lax.dot_general(a, b, (((0,), (0,)), ((), ())), preferred_element_type=F32)


def row_scale(source):
    return lax.rsqrt(jnp.mean(source * source, axis=-1, keepdims=True) + EPS)


def normalize_back(upstream, source, scaling, gain_row):
    unit_rows = source * scaling
    weighted = upstream * gain_row
    inner_mean = jnp.mean(weighted * unit_rows, axis=-1, keepdims=True)
    return (scaling * (weighted - unit_rows * inner_mean), upstream * unit_rows)


def rotary_tables(span):
    half = HEAD_SIZE // 2
    frequency = jnp.power(ROTARY_BASE, -jnp.arange(half, dtype=F32) * 2.0 / HEAD_SIZE)
    angles = jnp.arange(span, dtype=jnp.int32).astype(F32)[:, None] * frequency[None, :]
    cosine, sine = jnp.cos(angles), jnp.sin(angles)
    return (
        jnp.concatenate([cosine, cosine], axis=-1),
        jnp.concatenate([-sine, sine], axis=-1),
    )


def turned(u, gain, cosine, sine):
    n = u * row_scale(u) * gain
    return (n * cosine + pltpu.roll(n, HEAD_SIZE // 2, 1) * sine).astype(BF16)


def pieces_product(x, refs):
    size = refs[0].shape[0]
    total = mm(x[:, :size], refs[0][...])
    for s in range(1, len(refs)):
        total += mm(x[:, s * size:(s + 1) * size], refs[s][...])
    return total


def project_query_kernel(x_ref, cos_ref, sin_ref, gain_ref, *refs):
    raw_ref, low_ref = refs[-2:]
    q = pieces_product(x_ref[...], refs[:-2])
    raw_ref[...] = q
    for h in range(q.shape[1] // HEAD_SIZE):
        cols = slice(h * HEAD_SIZE, (h + 1) * HEAD_SIZE)
        low_ref[:, cols] = turned(q[:, cols], gain_ref[...], cos_ref[...], sin_ref[...])


def project_key_kernel(x_ref, cos_ref, sin_ref, gain_ref, w_ref, raw_ref, k_ref, v_ref):
    kv = mm(x_ref[...], w_ref[...])
    raw_ref[...] = kv[:, :HEAD_SIZE]
    v_ref[...] = kv[:, HEAD_SIZE:].astype(BF16)
    k_ref[...] = turned(kv[:, :HEAD_SIZE], gain_ref[...], cos_ref[...], sin_ref[...])


def project(kernel, x, weights, cosine, sine, gain, out):
    span, model = x.shape
    tile = 512
    row = lambda w: pl.BlockSpec((tile, w), lambda i: (i, 0))
    whole = lambda a, b: pl.BlockSpec((a, b), lambda i: (0, 0))
    return pl.pallas_call(
        kernel,
        grid=(span // tile,),
        in_specs=[row(model), row(HEAD_SIZE), row(HEAD_SIZE), whole(1, HEAD_SIZE)] + [whole(*w.shape) for w in weights],
        out_specs=[row(w) for w, _ in out],
        out_shape=[jax.ShapeDtypeStruct((span, w), t) for w, t in out],
        compiler_params=pltpu.CompilerParams(vmem_limit_bytes=VMEM_BYTES),
        cost_estimate=cost(0),
        name=kernel.__name__,
    )(x, cosine, sine, gain[None], *weights)


def block_limits(span, tile):
    return [(r0, max(r0 + tile, span // 2)) for r0 in range(0, span, tile)]


def masked(values, r0, limit, prefix):
    tile = values.shape[0]
    rows = r0 + lax.broadcasted_iota(jnp.int32, (tile, limit - r0), 0)
    cols = r0 + lax.broadcasted_iota(jnp.int32, (tile, limit - r0), 1)
    right = jnp.where((cols <= rows) | (cols < prefix), values[:, r0:], 0.0)
    return right if r0 == 0 else jnp.concatenate([values[:, :r0], right], axis=1)


def attend_kernel(tile, prefix_ref, q_ref, k_ref, v_ref, o_ref, l_ref, wide_ref):
    span = q_ref.shape[0]

    @pl.when(pl.program_id(0) == 0)
    def _():
        wide_ref[:, :HEAD_SIZE] = v_ref[...]
        wide_ref[:, HEAD_SIZE:] = jnp.ones((span, HEAD_SIZE), BF16)

    prefix = prefix_ref[0]
    for r0, limit in block_limits(span, tile):
        rows = slice(r0, r0 + tile)
        scores = mm_t(q_ref[rows, :], k_ref[:limit, :])
        weights = masked(jnp.exp2(scores * LOG2_SCALE), r0, limit, prefix)
        sums = mm(weights.astype(BF16), wide_ref[:limit, :])
        inverse = 1.0 / sums[:, HEAD_SIZE:]
        o_ref[rows, :] = (sums[:, :HEAD_SIZE] * inverse).astype(BF16)
        l_ref[rows, :] = inverse


def attend(prefix, q, k, v):
    span, width = q.shape
    heads = width // HEAD_SIZE
    head = pl.BlockSpec((span, HEAD_SIZE), lambda h: (0, h))
    shared = pl.BlockSpec((span, HEAD_SIZE), lambda h: (0, 0))
    return pl.pallas_call(
        functools.partial(attend_kernel, 256),
        grid=(heads,),
        in_specs=[pl.BlockSpec(memory_space=pltpu.SMEM), head, shared, shared],
        out_specs=[head, head],
        out_shape=[jax.ShapeDtypeStruct((span, width), BF16), jax.ShapeDtypeStruct((span, width), F32)],
        scratch_shapes=[pltpu.VMEM((span, 2 * HEAD_SIZE), BF16)],
        compiler_params=pltpu.CompilerParams(vmem_limit_bytes=VMEM_BYTES),
        cost_estimate=cost(0),
        name="attend",
    )(prefix, q, k, v)


def attend_back_kernel(tile, prefix_ref, q_ref, k_ref, v_ref, o_ref, l_ref, do_ref, qraw_ref, kraw_ref, cos_ref, sin_ref,
                       qg_ref, kg_ref, dq_ref, dk_ref, dv_ref, qgg_ref, kgg_ref, dk_sum, dv_sum):
    span = q_ref.shape[0]
    step = pl.program_id(0)

    @pl.when(step == 0)
    def _():
        dk_sum[...] = jnp.zeros_like(dk_sum)
        dv_sum[...] = jnp.zeros_like(dv_sum)
        qgg_ref[...] = jnp.zeros_like(qgg_ref)

    def unturned(grad, rows):
        return grad * cos_ref[rows, :] - pltpu.roll(grad, HEAD_SIZE // 2, 1) * sin_ref[rows, :]

    prefix = prefix_ref[0]
    for r0, limit in block_limits(span, tile):
        rows = slice(r0, r0 + tile)
        q, do = q_ref[rows, :], do_ref[rows, :]
        keys, values = k_ref[:limit, :], v_ref[:limit, :]
        weights = masked(jnp.exp2(mm_t(q, keys) * LOG2_SCALE), r0, limit, prefix)
        probs = weights * jnp.concatenate([l_ref[rows, :]] * (limit // HEAD_SIZE), axis=1)
        delta = jnp.sum(do.astype(F32) * o_ref[rows, :].astype(F32), axis=1, keepdims=True)
        score_grad = (probs * (mm_t(do, values) - delta)).astype(BF16)
        dv_sum[:limit, :] += t_mm(probs.astype(BF16), do)
        dk_sum[:limit, :] += t_mm(score_grad, q)
        turn = unturned(mm(score_grad, keys) * SOFTMAX_SCALE, rows)
        raw = qraw_ref[rows, :]
        back, terms = normalize_back(turn, raw, row_scale(raw), qg_ref[...])
        dq_ref[rows, :] = back.astype(BF16)
        qgg_ref[...] += jnp.sum(terms, axis=0, keepdims=True)

    @pl.when(step == pl.num_programs(0) - 1)
    def _():
        raw = kraw_ref[...]
        turn = unturned(dk_sum[...] * SOFTMAX_SCALE, slice(None))
        back, terms = normalize_back(turn, raw, row_scale(raw), kg_ref[...])
        dk_ref[...] = back.astype(BF16)
        dv_ref[...] = dv_sum[...].astype(BF16)
        kgg_ref[...] = jnp.sum(terms, axis=0, keepdims=True)


def attend_back(prefix, q, k, v, o, inverse, do, qraw, kraw, cosine, sine, q_gain, k_gain):
    span, width = q.shape
    heads = width // HEAD_SIZE
    head = pl.BlockSpec((span, HEAD_SIZE), lambda h: (0, h))
    shared = pl.BlockSpec((span, HEAD_SIZE), lambda h: (0, 0))
    gain = pl.BlockSpec((1, HEAD_SIZE), lambda h: (0, 0))
    return pl.pallas_call(
        functools.partial(attend_back_kernel, 256),
        grid=(heads,),
        in_specs=[pl.BlockSpec(memory_space=pltpu.SMEM), head, shared, shared, head, head, head, head, shared, shared,
                  shared, gain, gain],
        out_specs=[head, shared, shared, gain, gain],
        out_shape=[
            jax.ShapeDtypeStruct((span, width), BF16),
            jax.ShapeDtypeStruct((span, HEAD_SIZE), BF16),
            jax.ShapeDtypeStruct((span, HEAD_SIZE), BF16),
            jax.ShapeDtypeStruct((1, HEAD_SIZE), F32),
            jax.ShapeDtypeStruct((1, HEAD_SIZE), F32),
        ],
        scratch_shapes=[pltpu.VMEM((span, HEAD_SIZE), F32), pltpu.VMEM((span, HEAD_SIZE), F32)],
        compiler_params=pltpu.CompilerParams(vmem_limit_bytes=VMEM_BYTES),
        cost_estimate=cost(0),
        name="attend_back",
    )(prefix, q, k, v, o, inverse, do, qraw, kraw, cosine, sine, q_gain[None], k_gain[None])


def unproject_kernel(own_rows, dq_ref, dk_ref, dv_ref, wkv_ref, x_ref, gain_ref, router_ref, mix_ref, qg_ref, kg_ref,
                     *refs):
    weights, out_ref, sum_ref = refs[:-2], refs[-2], refs[-1]
    span, model = x_ref.shape
    size = weights[0].shape[0]
    tile = 512
    each = tile // own_rows
    for r in range(span // tile):
        rows = slice(r * tile, (r + 1) * tile)
        dq, dk, dv = dq_ref[rows, :], dk_ref[rows, :], dv_ref[rows, :]
        for s, weight in enumerate(weights):
            cols = slice(s * size, (s + 1) * size)
            total = mm_t(dq, weight[...])
            total += mm_t(dk, wkv_ref[cols, :HEAD_SIZE]) + mm_t(dv, wkv_ref[cols, HEAD_SIZE:])
            low = total.astype(BF16)
            for m in range(each):
                out_ref[r * each + m, :own_rows, cols] = low[m * own_rows:(m + 1) * own_rows]
            part = jnp.sum(total * x_ref[rows, cols].astype(F32), axis=0, keepdims=True)
            if r == 0:
                sum_ref[:, cols] = part
            else:
                sum_ref[:, cols] += part
    heads = jnp.concatenate([qg_ref[...], kg_ref[...], jnp.zeros((1, model - 2 * HEAD_SIZE), F32)], axis=1)
    place = lax.broadcasted_iota(jnp.int32, (8, model), 0)
    sums = jnp.zeros((8, model), F32)
    for n, values in enumerate((sum_ref[...] / gain_ref[...], mix_ref[...], heads)):
        high = values.astype(BF16).astype(F32)
        sums = jnp.where(place == 2 * n, high, jnp.where(place == 2 * n + 1, values - high, sums))
    sums = sums.astype(BF16)
    for m in range(out_ref.shape[0]):
        out_ref[m, own_rows:own_rows + 8, :] = router_ref[m]
        out_ref[m, own_rows + 8:, :] = sums


def unproject(own_rows, dq, dk, dv, pieces, wkv, x, gain, router_part, mixture_part, query_part, key_part):
    span, model = x.shape
    return pl.pallas_call(
        functools.partial(unproject_kernel, own_rows),
        out_shape=jax.ShapeDtypeStruct((span // own_rows, own_rows + 16, model), BF16),
        scratch_shapes=[pltpu.VMEM((1, model), F32)],
        compiler_params=pltpu.CompilerParams(vmem_limit_bytes=VMEM_BYTES),
        cost_estimate=cost(0),
        name="unproject",
    )(dq, dk, dv, wkv, x, gain[None], router_part, mixture_part, query_part, key_part, *pieces)


def out_project_kernel(a_ref, w_ref, out_ref):
    total = mm(a_ref[0], w_ref[0])
    for m in range(1, a_ref.shape[0]):
        total += mm(a_ref[m], w_ref[m])
    out_ref[...] = total.astype(BF16)


def out_project(attended_all, weight):
    members, span, width = attended_all.shape
    columns = weight.shape[2]
    tile = 512
    return pl.pallas_call(
        out_project_kernel,
        grid=(span // tile,),
        in_specs=[pl.BlockSpec((members, tile, width), lambda i: (0, i, 0)),
                  pl.BlockSpec((members, width, columns), lambda i: (0, 0, 0))],
        out_specs=pl.BlockSpec((tile, columns), lambda i: (i, 0)),
        out_shape=jax.ShapeDtypeStruct((span, columns), BF16),
        compiler_params=pltpu.CompilerParams(vmem_limit_bytes=VMEM_BYTES),
        cost_estimate=cost(0),
        name="out_project",
    )(attended_all, weight)


def out_back_kernel(g_ref, w_ref, out_ref):
    columns = w_ref.shape[2]
    total = mm_t(g_ref[:, :columns], w_ref[0])
    for m in range(1, w_ref.shape[0]):
        total += mm_t(g_ref[:, m * columns:(m + 1) * columns], w_ref[m])
    out_ref[...] = total.astype(BF16)


def out_back(after_all, heads):
    span, model = after_all.shape
    members, width, columns = heads.shape
    tile = 512
    return pl.pallas_call(
        out_back_kernel,
        grid=(span // tile,),
        in_specs=[pl.BlockSpec((tile, model), lambda i: (i, 0)),
                  pl.BlockSpec((members, width, columns), lambda i: (0, 0, 0))],
        out_specs=pl.BlockSpec((tile, width), lambda i: (i, 0)),
        out_shape=jax.ShapeDtypeStruct((span, width), BF16),
        compiler_params=pltpu.CompilerParams(vmem_limit_bytes=VMEM_BYTES),
        cost_estimate=cost(0),
        name="out_back",
    )(after_all, heads)


def out_gradient_kernel(member_ref, a_ref, g_ref, out_ref):
    out_ref[0] = t_mm(a_ref[0], g_ref[...]).astype(BF16)


def out_gradient(member, attended_all, after_all, columns):
    members, span, width = attended_all.shape
    return pl.pallas_call(
        out_gradient_kernel,
        grid_spec=pltpu.PrefetchScalarGridSpec(
            num_scalar_prefetch=1,
            grid=(members,),
            in_specs=[pl.BlockSpec((1, span, width), lambda m, me: (m, 0, 0)),
                      pl.BlockSpec((span, columns), lambda m, me: (0, me[0]))],
            out_specs=pl.BlockSpec((1, width, columns), lambda m, me: (m, 0, 0)),
        ),
        out_shape=jax.ShapeDtypeStruct((members, width, columns), BF16),
        compiler_params=pltpu.CompilerParams(vmem_limit_bytes=VMEM_BYTES),
        cost_estimate=cost(0),
        name="out_gradient",
    )(member, attended_all, after_all)


def expert_kernel(experts, own_ref, xa_ref, xb_ref, mask_ref, router_ref, gate_ref, up_ref, down_ref,
                  act_ref, gg_ref, ug_ref, w_ref, route_ref, sum_ref):
    half = xa_ref.shape[1]
    step = pl.program_id(0)
    own = own_ref[0]

    def product(left, right, weight):
        return mm(left[...], weight[:half, :]) + mm(right[...], weight[half:, :])

    @pl.when(step == 0)
    def _():
        mask = mask_ref[...].astype(F32)
        logits = mm_t(xa_ref[...], router_ref[:, :half]) + mm_t(xb_ref[...], router_ref[:, half:])
        logits = jnp.where(mask > 0, logits, VERY_NEGATIVE)
        raised = jnp.where(mask > 0, jnp.exp(logits - jnp.max(logits, axis=-1, keepdims=True)), 0.0)
        total = jnp.maximum(jnp.sum(raised, axis=-1, keepdims=True), 1e-30)
        lanes = lax.broadcasted_iota(jnp.int32, raised.shape, 1)
        weight = jnp.sum(jnp.where(lanes == own, raised, 0.0), axis=-1, keepdims=True) / total
        w_ref[...] = jnp.broadcast_to(weight, w_ref.shape)

    gate_raw, up_raw = product(xa_ref, xb_ref, gate_ref), product(xa_ref, xb_ref, up_ref)
    down = down_ref[...]
    weight = w_ref[:, :1]
    sig = 1.0 / (1.0 + jnp.exp(-gate_raw))
    silu = gate_raw * sig
    activated = (silu * up_raw).astype(BF16)
    act_ref[...] = activated
    route = jnp.sum(activated.astype(F32) * down, axis=-1, keepdims=True)
    grad = weight * down
    gg_ref[...] = (grad * up_raw * sig * (1.0 + gate_raw * (1.0 - sig))).astype(BF16)
    ug_ref[...] = (grad * silu).astype(BF16)
    route = jnp.broadcast_to(route, sum_ref.shape)

    @pl.when(step == 0)
    def _():
        sum_ref[...] = route

    @pl.when(step > 0)
    def _():
        sum_ref[...] += route

    @pl.when(step == pl.num_programs(0) - 1)
    def _():
        total = sum_ref[:, :1]
        high = total.astype(BF16).astype(F32)
        lanes = lax.broadcasted_iota(jnp.int32, route_ref.shape, 1)
        route_ref[...] = jnp.where(
            lanes == own, high, jnp.where(lanes == experts + own, total - high, 0.0)).astype(BF16)


def expert_forward(experts, own, xa, xb, masked_rows, router, gate, up, upstream_down):
    rows, half = xa.shape
    model, hidden = gate.shape
    padded = router.shape[0]
    route_width = -(-2 * experts // HEAD_SIZE) * HEAD_SIZE
    tile = 256
    whole = lambda a, b: pl.BlockSpec((a, b), lambda i: (0, 0))
    column = lambda a: pl.BlockSpec((a, tile), lambda i: (0, i))
    return pl.pallas_call(
        functools.partial(expert_kernel, experts),
        grid=(hidden // tile,),
        in_specs=[pl.BlockSpec(memory_space=pltpu.SMEM), whole(rows, half), whole(rows, half),
                  pl.BlockSpec((rows, padded), lambda i: (0, model // padded)), whole(padded, model), column(model),
                  column(model), column(rows)],
        out_specs=[column(rows), column(rows), column(rows), whole(rows, HEAD_SIZE), whole(rows, route_width)],
        out_shape=[
            jax.ShapeDtypeStruct((rows, hidden), BF16),
            jax.ShapeDtypeStruct((rows, hidden), BF16),
            jax.ShapeDtypeStruct((rows, hidden), BF16),
            jax.ShapeDtypeStruct((rows, HEAD_SIZE), F32),
            jax.ShapeDtypeStruct((rows, route_width), BF16),
        ],
        scratch_shapes=[pltpu.VMEM((rows, HEAD_SIZE), F32)],
        compiler_params=pltpu.CompilerParams(vmem_limit_bytes=VMEM_BYTES),
        cost_estimate=cost(18),
        name="expert_forward",
    )(own, xa, xb, masked_rows, router, gate, up, upstream_down)


def row_gradient_kernel(gg_ref, ug_ref, gate_ref, up_ref, *rest):
    total = (mm_t(gg_ref[...], gate_ref[...]) + mm_t(ug_ref[...], up_ref[...])).astype(BF16)
    out_ref = rest[-1]
    out_ref[:, :total.shape[1]] = total
    if len(rest) == 2:
        out_ref[:, total.shape[1]:] = rest[0][...]


def row_gradient(gg, ug, gate, up, part, route=None):
    rows, hidden = gg.shape
    half = gate.shape[0] // 2
    tile = rows // 4
    row = lambda w: pl.BlockSpec((tile, w), lambda i: (i, 0))
    weight = pl.BlockSpec((half, hidden), lambda i: (part, 0))
    extra = [] if route is None else [route]
    width = half + sum(e.shape[1] for e in extra)
    return pl.pallas_call(
        row_gradient_kernel,
        grid=(rows // tile,),
        in_specs=[row(hidden), row(hidden), weight, weight] + [row(e.shape[1]) for e in extra],
        out_specs=row(width),
        out_shape=jax.ShapeDtypeStruct((rows, width), BF16),
        compiler_params=pltpu.CompilerParams(vmem_limit_bytes=VMEM_BYTES),
        cost_estimate=cost(8),
        name="row_gradient",
    )(gg, ug, gate, up, *extra)


def down_back_kernel(c_ref, down_ref, out_ref):
    out_ref[...] = mm_t(c_ref[...], down_ref[...])


def down_back(upstream_rows, down):
    rows = upstream_rows.shape[0]
    hidden, model = down.shape
    tile = 256
    return pl.pallas_call(
        down_back_kernel,
        grid=(hidden // tile,),
        in_specs=[pl.BlockSpec((rows, model), lambda i: (0, 0)), pl.BlockSpec((tile, model), lambda i: (i, 0))],
        out_specs=pl.BlockSpec((rows, tile), lambda i: (0, i)),
        out_shape=jax.ShapeDtypeStruct((rows, hidden), F32),
        compiler_params=pltpu.CompilerParams(vmem_limit_bytes=VMEM_BYTES),
        cost_estimate=cost(8),
        name="down_back",
    )(upstream_rows, down)


def produce_kernel(act_ref, w_ref, down_ref, *outs):
    total = (w_ref[:, :1] * mm(act_ref[...], down_ref[...])).astype(BF16)
    half = total.shape[1] // 2
    outs[0][...] = total[:, :half]
    outs[1][...] = total[:, half:]


def produce(activated, weight, down):
    rows, hidden = activated.shape
    model = down.shape[1]
    tile = rows // 4
    row = lambda w: pl.BlockSpec((tile, w), lambda i: (i, 0))
    return pl.pallas_call(
        produce_kernel,
        grid=(rows // tile,),
        in_specs=[row(hidden), row(HEAD_SIZE), pl.BlockSpec((hidden, model), lambda i: (0, 0))],
        out_specs=[row(model // 2)] * 2,
        out_shape=[jax.ShapeDtypeStruct((rows, model // 2), BF16)] * 2,
        compiler_params=pltpu.CompilerParams(vmem_limit_bytes=VMEM_BYTES),
        cost_estimate=cost(0),
        name="produce",
    )(activated, weight, down)


def hidden_gradient_kernel(xa_ref, xb_ref, gg_ref, ug_ref, dg_ref, du_ref):
    in_first = pl.program_id(0) < pl.num_programs(0) // 2
    for x_ref, now in ((xa_ref, in_first), (xb_ref, jnp.logical_not(in_first))):
        @pl.when(now)
        def _():
            dg_ref[0] = t_mm(x_ref[...], gg_ref[...])
            du_ref[0] = t_mm(x_ref[...], ug_ref[...])


def hidden_gradient(xa, xb, gg, ug):
    rows, half = xa.shape
    hidden = gg.shape[1]
    tile = 256
    count = half // tile
    whole = pl.BlockSpec((rows, hidden), lambda i: (0, 0))
    out = pl.BlockSpec((1, tile, hidden), lambda i: (0, i, 0))
    return pl.pallas_call(
        hidden_gradient_kernel,
        grid=(2 * count,),
        in_specs=[pl.BlockSpec((rows, tile), lambda i: (0, jnp.minimum(i, count - 1))),
                  pl.BlockSpec((rows, tile), lambda i: (0, jnp.maximum(i - count, 0))), whole, whole],
        out_specs=[out, out],
        out_shape=[jax.ShapeDtypeStruct((1, 2 * half, hidden), F32)] * 2,
        compiler_params=pltpu.CompilerParams(vmem_limit_bytes=VMEM_BYTES),
        cost_estimate=cost(0),
        name="hidden_gradient",
    )(xa, xb, gg, ug)


def down_gradient_kernel(c_ref, w_ref, act_ref, out_ref):
    out_ref[0] = t_mm(act_ref[...], (w_ref[:, :1] * c_ref[...].astype(F32)).astype(BF16))


def down_gradient(upstream_rows, model, weight, activated):
    rows, hidden = activated.shape
    tile = 256
    return pl.pallas_call(
        down_gradient_kernel,
        grid=(model // tile,),
        in_specs=[pl.BlockSpec((rows, tile), lambda i: (0, i)), pl.BlockSpec((rows, HEAD_SIZE), lambda i: (0, 0)),
                  pl.BlockSpec((rows, hidden), lambda i: (0, 0))],
        out_specs=pl.BlockSpec((1, hidden, tile), lambda i: (0, 0, i)),
        out_shape=jax.ShapeDtypeStruct((1, hidden, model), F32),
        compiler_params=pltpu.CompilerParams(vmem_limit_bytes=VMEM_BYTES),
        cost_estimate=cost(0),
        name="down_gradient",
    )(upstream_rows, weight, activated)


def dispatch_kernel(pick_ref, *refs):
    out_ref, all_ref = refs[-2:]
    size = all_ref.shape[0] // (len(refs) - 2)

    @pl.when(pl.program_id(0) == 0)
    def _():
        for s, ref in enumerate(refs[:-2]):
            all_ref[s * size:(s + 1) * size, :] = ref[...]

    out_ref[...] = mm(pick_ref[...], all_ref[...]).astype(BF16)


def dispatch(pick, pieces):
    rows, column = pick.shape
    size, width = column // len(pieces), pieces[0].shape[1]
    tile = rows // 4
    return pl.pallas_call(
        dispatch_kernel,
        grid=(rows // tile,),
        in_specs=[pl.BlockSpec((tile, column), lambda i: (i, 0))]
        + [pl.BlockSpec((size, width), lambda i: (0, 0))] * len(pieces),
        out_specs=pl.BlockSpec((tile, width), lambda i: (i, 0)),
        out_shape=jax.ShapeDtypeStruct((rows, width), BF16),
        scratch_shapes=[pltpu.VMEM((column, width), BF16)],
        compiler_params=pltpu.CompilerParams(vmem_limit_bytes=VMEM_BYTES),
        cost_estimate=cost(0),
        name="dispatch",
    )(pick, *pieces)


def combine_kernel(pick_ref, rows_ref, *outs):
    total = mm(pick_ref[...], rows_ref[...]).astype(BF16)
    size = total.shape[0] // len(outs)
    for s, out in enumerate(outs):
        out[...] = total[s * size:(s + 1) * size]


def combine(pick, rows, count, microseconds=0):
    column, slots = pick.shape
    width = rows.shape[1]
    tile = math.gcd(width, 512)
    size = column // count
    out = pl.BlockSpec((size, tile), lambda i: (0, i))
    return pl.pallas_call(
        combine_kernel,
        grid=(width // tile,),
        in_specs=[pl.BlockSpec((column, slots), lambda i: (0, 0)), pl.BlockSpec((slots, tile), lambda i: (0, i))],
        out_specs=[out] * count,
        out_shape=[jax.ShapeDtypeStruct((size, width), BF16)] * count,
        compiler_params=pltpu.CompilerParams(vmem_limit_bytes=VMEM_BYTES),
        cost_estimate=cost(microseconds),
        name="combine",
    )(pick, rows)


def after(array, *earlier):
    return lax.optimization_barrier((array, *earlier))[0]


def shards(
    tokens,
    routes,
    prefix_len,
    query_weight,
    key_matrix,
    value_matrix,
    out_weight,
    router_weight,
    attention_gain,
    mixture_gain,
    query_gain,
    key_norm_gain,
    expert_gate,
    expert_up,
    expert_down,
    cotangent,
):
    planes, members = lax.axis_size("dp"), lax.axis_size("expert")
    devices = planes * members
    plane, member = lax.axis_index("dp"), lax.axis_index("expert")
    own_rows, model = tokens.shape
    span = own_rows * members
    column = own_rows * planes
    experts = devices
    width = query_weight.shape[1]
    piece = key_matrix.shape[1]
    group = HEAD_SIZE // piece
    block_slots = max(2, 6 * own_rows * TOP // (5 * experts))
    slots = planes * block_slots
    padded = -(-experts // HEAD_SIZE) * HEAD_SIZE
    half = model // 2
    part_rows = model // planes
    gate, up, down = expert_gate[0], expert_up[0], expert_down[0]

    def gather(array, axis, dimension=0):
        return lax.all_gather(array, axis, axis=dimension, tiled=True)

    def exchange(array, axis):
        return lax.all_to_all(array, axis, split_axis=0, concat_axis=0, tiled=True)

    def plane_pieces(array):
        def shift(value, by):
            return lax.ppermute(value, "dp", [(i, (i + by) % planes) for i in range(planes)])

        pieces = [array] + [None] * (planes - 1)
        for s in range(1, planes // 2 + 1):
            pieces[s] = shift(pieces[s - 1], 1)
            if planes - s > s:
                pieces[planes - s] = shift(pieces[(planes - s + 1) % planes], -1)
        return pieces

    def plane_sum(pieces):
        total = pieces[0].astype(F32)
        for s in range(1, planes):
            total += lax.ppermute(pieces[s], "dp", [(i, (i - s) % planes) for i in range(planes)]).astype(F32)
        return total

    def reorder(array, dimension):
        size = array.shape[dimension] // planes
        return jnp.concatenate(
            [lax.dynamic_slice_in_dim(array, (plane - s) % planes * size, size, dimension) for s in range(planes)],
            axis=dimension)

    def cut(array):
        return [array[s * (array.shape[0] // planes):(s + 1) * (array.shape[0] // planes)] for s in range(planes)]

    residual_in = tokens.astype(F32)
    scale_attention = row_scale(residual_in)
    normed_own = (residual_in * scale_attention * attention_gain).astype(BF16)
    normed = gather(reorder(normed_own, 1), "expert")

    kv_pieces = plane_pieces(jnp.concatenate([key_matrix, value_matrix], axis=1))
    wq_pieces = plane_pieces(query_weight)
    out_piece = out_weight.shape[1]
    out_columns = gather(after(out_weight, *kv_pieces[1:]), "dp").reshape(members, width, out_piece)

    expert_ids = jnp.arange(experts, dtype=jnp.int32)
    mask_own = jnp.sum((routes[:, :, None] == expert_ids[None, None, :]).astype(F32), axis=1)
    mask_wide = jnp.pad(mask_own, ((0, 0), (0, padded - experts))).astype(BF16)
    router_rows = gather(after(router_weight.T, wq_pieces[1], wq_pieces[-1]), "expert").reshape(members, model)
    upstream_own = jnp.concatenate(
        [jnp.concatenate([cotangent, mask_wide], axis=1), jnp.pad(router_rows, ((0, 0), (0, padded)))], axis=0)
    upstream_pieces = plane_pieces(after(upstream_own, *wq_pieces[1:]))
    cosine, sine = rotary_tables(span)

    kv_own = jnp.concatenate(kv_pieces, axis=0)
    place = member % group
    kv_parts = [kv_own]
    for shift in range(1, group):
        pairs = [(e - e % group + (e % group + shift) % group, e) for e in range(members)]
        kv_parts.append(lax.ppermute(kv_own, "expert", pairs))

    def kv_piece(j):
        value = kv_parts[0]
        for shift in range(1, group):
            value = jnp.where((place + shift) % group == j, kv_parts[shift], value)
        return value

    ordered = [kv_piece(j) for j in range(group)]
    kv_weight = jnp.concatenate([p[:, :piece] for p in ordered] + [p[:, piece:] for p in ordered], axis=1)

    kraw, key_low, value_low = project(
        project_key_kernel, after(normed, cosine, sine, upstream_own), [kv_weight], cosine, sine, key_norm_gain,
        [(HEAD_SIZE, F32), (HEAD_SIZE, BF16), (HEAD_SIZE, BF16)])
    qraw, query_low = project(
        project_query_kernel, normed, wq_pieces, cosine, sine, query_gain, [(width, F32), (width, BF16)])
    attended_low, inverse = attend(prefix_len, after(query_low, out_columns), key_low, value_low)
    attended_all = gather(attended_low, "expert").reshape(members, span, width)

    out_rows = out_project(after(attended_all, *upstream_pieces), out_columns)
    projected = exchange(out_rows, "expert").reshape(members, own_rows, out_piece)
    projected = jnp.transpose(projected, (1, 0, 2)).reshape(own_rows, model)

    upstream_pieces = after(upstream_pieces, out_rows)
    mask_plane = jnp.concatenate(
        [lax.dynamic_slice(p, (0, model + plane * members), (own_rows, members)) for p in upstream_pieces], axis=0)
    triangle = (jnp.arange(column)[:, None] >= jnp.arange(column)[None, :]).astype(BF16)
    rank = jnp.where(mask_plane > 0, mm(triangle, mask_plane) - 1.0, -1.0).astype(jnp.int32)
    pick = (rank.T[:, None, :] == jnp.arange(slots, dtype=jnp.int32)[None, :, None])
    pick = pick.reshape(members * slots, column).astype(BF16)
    unpick = rank[:, :, None] == jnp.arange(slots, dtype=jnp.int32)[None, None, :]
    unpick = unpick.reshape(column, members * slots).astype(BF16)
    upstream_sent = dispatch(pick, upstream_pieces)
    upstream_rows = exchange(upstream_sent, "expert")
    pick = after(pick, upstream_sent)
    router = jnp.concatenate([p[own_rows:, :model].reshape(experts, part_rows) for p in upstream_pieces], axis=1)
    router = jnp.pad(reorder(router, 1), ((0, padded - experts), (0, 0)))

    after_attn = residual_in + projected.astype(F32)
    scale_mixture = row_scale(after_attn)
    mixed_low = (after_attn * scale_mixture * mixture_gain).astype(BF16)
    arrived = []
    for columns in (slice(0, half), slice(half, model)):
        sent = dispatch(pick, plane_pieces(mixed_low[:, columns]))
        arrived.append(exchange(after(sent, upstream_rows), "expert"))

    out_heads = exchange(after(out_columns, arrived[1]), "expert")
    upstream_down = down_back(upstream_rows, down)
    own_expert = (plane * members + member).astype(jnp.int32).reshape(1)
    activated, gate_grad, up_grad, weight_wide, route_columns = expert_forward(
        experts, own_expert, arrived[0], arrived[1], upstream_rows, router, gate, up, upstream_down)
    back_first = exchange(row_gradient(gate_grad, up_grad, gate, up, 0), "expert")
    back_second = exchange(row_gradient(gate_grad, up_grad, gate, up, 1, route_columns), "expert")
    produced = produce(activated, weight_wide, down)
    back_first = after(back_first, out_heads, *produced)
    mixed_first = plane_sum(combine(unpick, back_first, planes, 40))
    mixed_second = plane_sum(combine(unpick, back_second, planes, 40))
    mixture_rows = exchange(after(produced[0], back_second), "expert")

    upstream = cotangent.astype(F32)
    mask = mask_own > 0
    logits = jnp.where(mask, mm_t(mixed_low, router[:experts]), VERY_NEGATIVE)
    raised = jnp.where(mask, jnp.exp(logits - jnp.max(logits, axis=-1, keepdims=True)), 0.0)
    weight_own = raised / jnp.sum(raised, axis=-1, keepdims=True)
    route_back = mixed_second[:, half:half + experts] + mixed_second[:, half + experts:half + 2 * experts]
    chosen_grad = weight_own * (route_back - jnp.sum(weight_own * route_back, axis=-1, keepdims=True))
    logit_grad = chosen_grad.astype(BF16)
    mixed_first = after(mixed_first, mixture_rows)
    mixed_grad = mm(logit_grad, router[:experts]) + jnp.concatenate([mixed_first, mixed_second[:, :half]], axis=1)
    mixture_back, mixture_terms = normalize_back(mixed_grad, after_attn, scale_mixture, mixture_gain)
    after_grad = upstream + mixture_back
    after_low = after_grad.astype(BF16)

    router_part = t_mm(logit_grad, mixed_low).astype(BF16).reshape(members, planes, model)
    router_part = jnp.pad(router_part, ((0, 0), (0, 8 - planes), (0, 0)))
    mixture_part = jnp.sum(mixture_terms, axis=0, keepdims=True)

    after_all = gather(after_low, "expert")
    mixture_parts = combine(unpick, after(mixture_rows, after_low), planes)
    mixture_first = plane_sum(mixture_parts)
    gate_gradient, up_gradient = hidden_gradient(
        arrived[0], arrived[1], *after((gate_grad, up_grad), after_low, *mixture_parts))
    after_all = after(after_all, gate_gradient, router_part, mixture_part, mixture_first)
    mixture_rows = exchange(after(produced[1], after_all), "expert")
    out_partial = out_gradient(member.astype(jnp.int32).reshape(1), attended_all, after_all, out_piece)
    out_share = lax.psum_scatter(
        after(out_partial, mixture_first).reshape(members * width, out_piece), "dp", scatter_dimension=0, tiled=True).astype(F32)
    attended_grad = out_back(after(after_all, out_partial), out_heads)
    dq, dk, dv, query_terms, key_terms = attend_back(
        prefix_len, query_low, key_low, value_low, attended_low, inverse, attended_grad, qraw, kraw, cosine, sine,
        query_gain, key_norm_gain)
    normed_partial = unproject(
        own_rows, dq, dk, dv, wq_pieces, kv_weight, normed, reorder(attention_gain, 0), router_part, mixture_part,
        query_terms, key_terms)
    mixture_parts = combine(unpick, after(mixture_rows, normed_partial), planes)
    arrived_sums = exchange(after(normed_partial, out_share, *mixture_parts), "expert")
    normed_sums = jnp.sum(arrived_sums.astype(F32), axis=0)
    input_back, _ = normalize_back(
        reorder(normed_sums[:own_rows], 1), residual_in, scale_attention, attention_gain)
    input_grad = after_grad + input_back
    mixture_second = plane_sum(mixture_parts)
    layer_out = (after_attn + jnp.concatenate([mixture_first, mixture_second], axis=1)).astype(BF16)

    query_partial = t_mm(normed, dq).astype(BF16)
    query_share = plane_sum(cut(after(query_partial, mixture_second)))
    down_grad = down_gradient(upstream_rows, model, weight_wide, after(activated, query_partial))
    kv_partial = jnp.concatenate([t_mm(normed, dk), t_mm(normed, dv)], axis=1)

    def kv_cols(j):
        start = j * piece
        return jnp.concatenate(
            [lax.dynamic_slice(kv_partial, (0, start), (model, piece)),
             lax.dynamic_slice(kv_partial, (0, HEAD_SIZE + start), (model, piece))], axis=1)

    kv_total = kv_cols(place)
    for shift in range(1, group):
        pairs = [(e, e - e % group + (e % group + shift) % group) for e in range(members)]
        kv_total += lax.ppermute(kv_cols((place + shift) % group).astype(BF16), "expert", pairs).astype(F32)
    kv_share = plane_sum(cut(kv_total.astype(BF16)))
    key_share = kv_share[:, :piece]
    value_share = kv_share[:, piece:]

    last = normed_sums[own_rows:]
    attention_sum, mixture_sum, head_sum = (last[8 + 2 * n] + last[9 + 2 * n] for n in range(3))
    gains = jnp.concatenate([reorder(attention_sum, 0), mixture_sum, head_sum[:2 * HEAD_SIZE]])
    total = jnp.concatenate([gains, last[:planes].reshape(-1)]).reshape(-1, HEAD_SIZE)
    step = 1
    while step < planes:
        total = total + lax.ppermute(total, "dp", [(i, i ^ step) for i in range(planes)])
        step *= 2
    total = total.reshape(-1)
    gains, router_total = total[:gains.shape[0]], total[gains.shape[0]:].reshape(planes, model)
    router_share = lax.dynamic_slice(router_total, (0, plane * part_rows), (planes, part_rows)).T
    attention_total, mixture_total = gains[:model], gains[model:2 * model]
    query_total, key_total = gains[2 * model:2 * model + HEAD_SIZE], gains[2 * model + HEAD_SIZE:]
    return (
        layer_out,
        input_grad,
        query_share,
        key_share,
        value_share,
        out_share,
        router_share,
        attention_total,
        mixture_total,
        query_total,
        key_total,
        gate_gradient,
        up_gradient,
        down_grad,
    )


def solution(mesh):
    rows = P(("dp", "expert"), None)
    grid = P("dp", "expert")
    experts = P(("dp", "expert"), None, None)
    in_specs = (rows, rows, P("dp"), grid, grid, grid, grid, grid, P(), P(), P(), P(), experts, experts, experts, rows)
    out_specs = (rows, rows, grid, grid, grid, grid, grid, P(), P(), P(), P(), experts, experts, experts)
    return jax.shard_map(shards, mesh=mesh, in_specs=in_specs, out_specs=out_specs, check_vma=False)
```

time: 946 us -> 710 us (0.75)
  blocking collectives: 240 us -> 9.23 us
  Pallas kernels: 40.3 us -> 182 us
  matrix products: 148 us -> 11 us
  waiting for transfers between devices: 402 us -> 328 us
  starting transfers between devices: 19.1 us -> 90.5 us
    all_gather x7 -> x4, waiting for transfers between devices: 296 us -> 30.1 us  [gather(): return lax.all_gather(array, axis, axis=dimension, tiled=True)]
    ppermute x0 -> x35, waiting for transfers between devices: none -> 208 us  [the longest x15 121 us: shift(): lax.ppermute(value, 'dp', [(i, (i + by) % planes) for i in range(planes)])]
    pallas_call x2 -> x20, Pallas kernels: 17.6 us -> 160 us  [the longest x4 21.1 us: combine(): pl.pallas_call(combine_kernel, grid=(width // tile,), in_specs=[pl.BlockS...]
    all_to_all x2 -> x0, blocking collectives: 125 us -> none  [exchange(): return lax.all_to_all(array, axis, split_axis=0, concat_axis=0, tiled=True)]
    all_gather x2 -> x1, blocking collectives: 74.1 us -> 9.23 us  [gather(): return lax.all_gather(array, axis, axis=dimension, tiled=True)]
    all_to_all x4 -> x10, waiting for transfers between devices: 31.2 us -> 87.6 us  [exchange(): return lax.all_to_all(array, axis, split_axis=0, concat_axis=0, tiled=True)]
    dot_general x17 -> x4, matrix products: 62.7 us -> 6.53 us  [t_mm(): lax.dot_general(a, b, (((0,), (0,)), ((), ())), preferred_element_type=F32)]
    reduce_scatter x5 -> x1, waiting for transfers between devices: 56 us -> 1.96 us  [shards(): lax.psum_scatter(after(out_partial, mixture_first).reshape(members * widt...]
  transfers between devices with their start and end apart: 20 -> 52, of which waited for: 13 -> 34; matrix products, arithmetic and copies ran while one was open for 14% -> 7% of each run, Pallas kernels for 4% -> 22%
where the time goes in v2:
time: 710 us; the launch traced here: 699 us
  waiting for transfers between devices  328 us (46%)
  Pallas kernels  182 us (26%)
  starting transfers between devices  90.5 us (13%)
  other arithmetic  34.2 us (5%)
  local copies, waits for them, and re-layouts  27.7 us (4%)
  between operations  16.1 us (2%)
  matrix products  11 us (2%)
  blocking collectives  9.23 us (1%)
    ppermute x15, waiting for transfers between devices, shift(): lax.ppermute(value, 'dp', [(i, (i + by) % planes) for i in range(planes)])  121 us
    all_to_all x10, waiting for transfers between devices, exchange(): return lax.all_to_all(array, axis, split_axis=0, concat_axis=0, tiled=True)  87.6 us
    ppermute x18, waiting for transfers between devices, plane_sum(): lax.ppermute(pieces[s], 'dp', [(i, (i - s) % planes) for i in range(plane...  83.2 us
    all_to_all x10, starting transfers between devices, exchange(): return lax.all_to_all(array, axis, split_axis=0, concat_axis=0, tiled=True)  40.9 us
    all_gather x4, waiting for transfers between devices, gather(): return lax.all_gather(array, axis, axis=dimension, tiled=True)  30.1 us
    ppermute x18, starting transfers between devices, plane_sum(): lax.ppermute(pieces[s], 'dp', [(i, (i - s) % planes) for i in range(plane...  24.5 us
    ppermute x15, starting transfers between devices, shift(): lax.ppermute(value, 'dp', [(i, (i + by) % planes) for i in range(planes)])  21.3 us
    pallas_call x4, Pallas kernels, combine(): pl.pallas_call(combine_kernel, grid=(width // tile,), in_specs=[pl.BlockS...  21.1 us
  transfers between devices with their start and end apart: 52, of which 34 were waited for; matrix products, arithmetic and copies ran while one was open for 7% of the time, Pallas kernels for 22%

profile of v2, /device:TPU:0, one launch (start us, length us, event | category | flops | bytes accessed | tf_op | source)
XLA Modules:
  0.0 699.1 jit_solution(17574542033624580633)
XLA Ops:
  16.4 4.3 collective-permute-done.3
  22.1 5.4 collective-permute-done.4
  27.7 3.8 collective-permute-start.2
  37.6 6.7 collective-permute-done.refs_1_
  44.3 5.8 collective-permute-done.2.refs_3_
  50.2 9.2 %all-gather = bf16[8,4,512]{2,1,0:T(4,128)(2,1)S(1)} all-gather(bf16[1,4,512]{2,1,0:T(4,128)(2,1)S(1)} %bitcast.108), channel_id=1, replica_groups=mesh['dp'=4,'expert'=8] {'expert'}, dimensions={0}, use_global_device_ids=true | all-gather | bytes 36864 | tf_op jit(solution)/shard_map/all_gather | solution.py:637
  63.8 22.9 %collective-permute-done.1.refs_2_ = bf16[512,512]{1,0:T(8,128)(2,1)S(1)} collective-permute-done((bf16[512,512]{1,0:T(8,128)(2,1)S(1)}, bf16[512,512]{1,0:T(8,128)(2,1)S(1)}, u32[]{:S(2)}, u32[]{:S(2)}) %collective-permute-start.1) | collective-permute-done | bytes 524320 | tf_op jit(solution)/shard_map/ppermute | solution.py:644
  87.5 8.4 %project_query_kernel.1 = (f32[1024,512]{1,0:T(8,128)}, bf16[1024,512]{1,0:T(8,128)(2,1)}) custom-call(bf16[1024,2048]{1,0:T(8,128)(2,1)} %all-gather.6.cloned.1.call-done.x_ref, f32[1024,128]{1,0:T(8,128)} %get-tuple-element.204.cos_ref, f32[1024,128]{1,0:T(8,128)} %get-tuple-element.205.sin_ref, f32[1,128]{1,0:T(1,128)} %bitcast.112, ...), custom_call_target="tpu_custom_call" | custom-call | flops 1 | bytes 1 | tf_op jit(solution)/shard_map/project_query_kernel/pallas_call | solution.py:97
  96.0 13.3 %all-gather.8.cloned.1.call-done = bf16[4096,256]{1,0:T(8,128)(2,1)} async-done(((bf16[1024,256]{1,0:T(8,128)(2,1)}), bf16[4096,256]{1,0:T(8,128)(2,1)}) %all-gather.8.cloned.1.call-update) | async-done | bytes 2097168 | tf_op jit(solution)/shard_map/all_gather | solution.py:637
  109.3 5.1 project_key_kernel.1
  114.4 6.9 attend.1
  121.3 3.8 collective-permute-start.9
  125.2 14.2 %collective-permute-done.7.refs_1_ = bf16[136,2176]{1,0:T(8,128)(2,1)S(1)} collective-permute-done((bf16[136,2176]{1,0:T(8,128)(2,1)S(1)}, bf16[136,2176]{1,0:T(8,128)(2,1)S(1)}, u32[]{:S(2)}, u32[]{:S(2)}) %collective-permute-start.7) | collective-permute-done | bytes 591904 | tf_op jit(solution)/shard_map/ppermute | solution.py:644
  139.5 9.7 %collective-permute-done.9.refs_3_ = bf16[136,2176]{1,0:T(8,128)(2,1)S(1)} collective-permute-done((bf16[136,2176]{1,0:T(8,128)(2,1)S(1)}, bf16[136,2176]{1,0:T(8,128)(2,1)S(1)}, u32[]{:S(2)}, u32[]{:S(2)}) %collective-permute-start.9) | collective-permute-done | bytes 591904 | tf_op jit(solution)/shard_map/ppermute | solution.py:644
  149.2 14.5 %collective-permute-done.8.refs_2_ = bf16[136,2176]{1,0:T(8,128)(2,1)S(1)} collective-permute-done((bf16[136,2176]{1,0:T(8,128)(2,1)S(1)}, bf16[136,2176]{1,0:T(8,128)(2,1)S(1)}, u32[]{:S(2)}, u32[]{:S(2)}) %collective-permute-start.8) | collective-permute-done | bytes 591904 | tf_op jit(solution)/shard_map/ppermute | solution.py:644
  163.6 10.2 %all-gather.10.cloned.1.call-done = bf16[8192,512]{1,0:T(8,128)(2,1)} async-done(((bf16[1024,512]{1,0:T(8,128)(2,1)}), bf16[8192,512]{1,0:T(8,128)(2,1)}) %all-gather.10.cloned.1.call-update) | async-done | bytes 8388624 | tf_op jit(solution)/shard_map/all_gather | solution.py:637
  173.8 6.1 out_project.1
  180.0 4.0 all-to-all-start
  186.2 6.9 dispatch.3
  193.6 4.7 all-to-all-start.1
  204.6 7.1 %collective-permute-done.13.refs_1_ = bf16[128,1024]{1,0:T(8,128)(2,1)S(1)} collective-permute-done((bf16[128,1024]{1,0:T(8,128)(2,1)S(1)}, bf16[128,1024]{1,0:T(8,128)(2,1)S(1)}, u32[]{:S(2)}, u32[]{:S(2)}) %collective-permute-start.13) | collective-permute-done | bytes 262176 | tf_op jit(solution)/shard_map/ppermute | solution.py:644
  211.8 4.4 collective-permute-done.15.refs_3_
  216.2 6.2 collective-permute-done.14.refs_2_
  223.2 5.0 dispatch.5
  228.1 31.0 %all-to-all-done.1 = bf16[8,152,2176]{2,1,0:T(8,128)(2,1)} async-done(((bf16[8,152,2176]{2,1,0:T(8,128)(2,1)}), bf16[8,152,2176]{2,1,0:T(8,128)(2,1)}, u32[]{:S(2)}, u32[]{:S(2)}) %all-to-all-start.1) | async-done | bytes 5292064 | tf_op jit(solution)/shard_map/all_to_all | solution.py:640
  259.1 3.6 all-to-all-start.3
  266.7 7.1 %collective-permute-done.10.refs_1_ = bf16[128,1024]{1,0:T(8,128)(2,1)S(1)} collective-permute-done((bf16[128,1024]{1,0:T(8,128)(2,1)S(1)}, bf16[128,1024]{1,0:T(8,128)(2,1)S(1)}, u32[]{:S(2)}, u32[]{:S(2)}) %collective-permute-start.10) | collective-permute-done | bytes 262176 | tf_op jit(solution)/shard_map/ppermute | solution.py:644
  273.8 4.4 collective-permute-done.12.refs_3_
  278.2 6.2 collective-permute-done.11.refs_2_
  285.2 5.0 dispatch.4
  290.1 3.4 all-to-all-done.3
  295.0 4.4 all-to-all-start.2
  303.6 8.4 %down_back.1.down_ref = f32[1216,768]{1,0:T(8,128)} custom-call(bf16[1216,2176]{1,0:T(8,128)(2,1)} %bitcast.13.c_ref.mask_ref, bf16[768,2048]{1,0:T(8,128)(2,1)} %bitcast.88), custom_call_target="tpu_custom_call" | custom-call | flops 8800000000 | bytes 1 | tf_op jit(solution)/shard_map/down_back/pallas_call | solution.py:457
  312.0 18.2 %all-to-all-done.2 = bf16[8,152,1024]{2,1,0:T(8,128)(2,1)} async-done(((bf16[8,152,1024]{2,1,0:T(8,128)(2,1)}), bf16[8,152,1024]{2,1,0:T(8,128)(2,1)}, u32[]{:S(2)}, u32[]{:S(2)}) %all-to-all-start.2) | async-done | bytes 2490400 | tf_op jit(solution)/shard_map/all_to_all | solution.py:640
  330.3 3.6 all-to-all-start.7
  333.9 18.3 %expert_forward.1 = (bf16[1216,768]{1,0:T(8,128)(2,1)}, bf16[1216,768]{1,0:T(8,128)(2,1)}, bf16[1216,768]{1,0:T(8,128)(2,1)}, f32[1216,128]{1,0:T(8,128)}, bf16[1216,128]{1,0:T(8,128)(2,1)}) custom-call(s32[1]{0:T(128)} %bitcast.9.own_ref, bf16[1216,1024]{1,0:T(8,128)(2,1)} %bitcast.15.xa_ref, bf16[1216,1024]{1,0:T(8,128)(2,1)} %bitcast.77, ...), custom_call_target="tpu_custom_call" | custom-call | flops 19800000512 | bytes 1 | tf_op jit(solution)/shard_map/expert_forward/pallas_call | solution.py:400
  352.2 8.0 %row_gradient.3 = bf16[1216,1024]{1,0:T(8,128)(2,1)} custom-call(bf16[1216,768]{1,0:T(8,128)(2,1)} %get-tuple-element.120.gg_ref, bf16[1216,768]{1,0:T(8,128)(2,1)} %get-tuple-element.121.ug_ref, bf16[2048,768]{1,0:T(8,128)(2,1)} %bitcast.115, bf16[2048,768]{1,0:T(8,128)(2,1)} %bitcast.118), custom_call_target="tpu_custom_call" | custom-call | flops 8800000000 | bytes 1 | tf_op jit(solution)/shard_map/row_gradient/pallas_call | solution.py:437
  361.8 4.6 all-to-all-start.6
  372.6 7.8 %produce.1 = (bf16[1216,1024]{1,0:T(8,128)(2,1)}, bf16[1216,1024]{1,0:T(8,128)(2,1)}) custom-call(bf16[1216,768]{1,0:T(8,128)(2,1)} %get-tuple-element.143.act_ref, f32[1216,128]{1,0:T(8,128)} %get-tuple-element.97.w_ref, bf16[768,2048]{1,0:T(8,128)(2,1)} %bitcast.89), custom_call_target="tpu_custom_call" | custom-call | flops 1 | bytes 1 | tf_op jit(solution)/shard_map/produce/pallas_call | solution.py:481
  380.5 8.2 %row_gradient.2 = bf16[1216,1152]{1,0:T(8,128)(2,1)} custom-call(bf16[1216,768]{1,0:T(8,128)(2,1)} %get-tuple-element.120.gg_ref, bf16[1216,768]{1,0:T(8,128)(2,1)} %get-tuple-element.121.ug_ref, bf16[2048,768]{1,0:T(8,128)(2,1)} %bitcast.116, bf16[2048,768]{1,0:T(8,128)(2,1)} %bitcast.119, bf16[1216,128]{1,0:T(8,128)(2,1)} %get-tuple-element.101.rest_0_), custom_call_target="tpu_custom_call" | custom-call | flops 8800000000 | bytes 1 | tf_op jit(solution)/shard_map/row_gradient/pallas_call | solution.py:437
  388.7 8.6 %all-to-all-done.6 = bf16[8,152,1024]{2,1,0:T(8,128)(2,1)} async-done(((bf16[8,152,1024]{2,1,0:T(8,128)(2,1)}), bf16[8,152,1024]{2,1,0:T(8,128)(2,1)}, u32[]{:S(2)}, u32[]{:S(2)}) %all-to-all-start.6) | async-done | bytes 2490400 | tf_op jit(solution)/shard_map/all_to_all | solution.py:640
  397.3 3.6 all-to-all-start.4
  400.9 4.1 combine.5
  409.5 25.6 %all-to-all-done.4 = bf16[8,152,1152]{2,1,0:T(8,128)(2,1)S(1)} async-done(((bf16[8,152,1152]{2,1,0:T(8,128)(2,1)}), bf16[8,152,1152]{2,1,0:T(8,128)(2,1)S(1)}, u32[]{:S(2)}, u32[]{:S(2)}) %all-to-all-start.4) | async-done | bytes 2801696 | tf_op jit(solution)/shard_map/all_to_all | solution.py:640
  436.6 3.6 all-to-all-start.5
  440.3 8.7 %combine.4 = (bf16[128,1152]{1,0:T(8,128)(2,1)}, bf16[128,1152]{1,0:T(8,128)(2,1)}, bf16[128,1152]{1,0:T(8,128)(2,1)}, bf16[128,1152]{1,0:T(8,128)(2,1)}) custom-call(bf16[512,1216]{1,0:T(8,128)(2,1)} %compare_convert_fusion.pick_ref, bf16[1216,1152]{1,0:T(8,128)(2,1)} %bitcast.90), custom_call_target="tpu_custom_call" | custom-call | flops 44000002048 | bytes 1 | tf_op jit(solution)/shard_map/combine/pallas_call | solution.py:585
  449.0 3.4 collective-permute-start.16
  455.9 4.2 collective-permute-done.16
  460.1 18.3 %collective-permute-done.17 = bf16[128,1152]{1,0:T(8,128)(2,1)S(1)} collective-permute-done((bf16[128,1152]{1,0:T(8,128)(2,1)}, bf16[128,1152]{1,0:T(8,128)(2,1)S(1)}, u32[]{:S(2)}, u32[]{:S(2)}) %collective-permute-start.17) | collective-permute-done | bytes 294944 | tf_op jit(solution)/shard_map/ppermute | solution.py:656
  486.9 4.2 combine.6
  496.8 14.6 %hidden_gradient.1 = (f32[1,2048,768]{2,1,0:T(8,128)}, f32[1,2048,768]{2,1,0:T(8,128)}) custom-call(bf16[1216,1024]{1,0:T(8,128)(2,1)} %bitcast.15.xa_ref, bf16[1216,1024]{1,0:T(8,128)(2,1)} %bitcast.78, bf16[1216,768]{1,0:T(8,128)(2,1)} %get-tuple-element.120.gg_ref, bf16[1216,768]{1,0:T(8,128)(2,1)} %get-tuple-element.121.ug_ref), custom_call_target="tpu_custom_call" | custom-call | flops 1 | bytes 1 | tf_op jit(solution)/shard_map/hidden_gradient/pallas_call | solution.py:509
  511.4 5.2 collective-permute-done.23
  517.6 6.5 all-gather.12.cloned.1.call-done.g_ref
  524.2 8.8 %out_gradient.1 = bf16[8,512,256]{2,1,0:T(8,128)(2,1)} custom-call(s32[1]{0:T(128)} %bitcast.30.member_ref, bf16[8,1024,512]{2,1,0:T(8,128)(2,1)} %bitcast.75, bf16[1024,2048]{1,0:T(8,128)(2,1)} %all-gather.12.cloned.1.call-done.g_ref), custom_call_target="tpu_custom_call" | custom-call | flops 1 | bytes 1 | tf_op jit(solution)/shard_map/out_gradient/pallas_call | solution.py:326
  533.1 3.8 all-to-all-start.8
  537.7 6.0 out_back.1.do_ref
  543.6 15.5 %attend_back.1 = (bf16[1024,512]{1,0:T(8,128)(2,1)}, bf16[1024,128]{1,0:T(8,128)(2,1)}, bf16[1024,128]{1,0:T(8,128)(2,1)}, f32[1,128]{1,0:T(1,128)}, f32[1,128]{1,0:T(1,128)}) custom-call(s32[1]{0:T(128)S(6)} %copy.92.prefix_ref, bf16[1024,512]{1,0:T(8,128)(2,1)} %get-tuple-element.81.q_ref, bf16[1024,128]{1,0:T(8,128)(2,1)} %get-tuple-element.84.k_ref, ...), custom_call_target="tpu_custom_call" | custom-call | flops 1 | bytes 1 | tf_op jit(solution)/shard_map/attend_back/pallas_call | solution.py:205
  559.1 10.4 %unproject.1 = bf16[8,144,2048]{2,1,0:T(8,128)(2,1)} custom-call(bf16[1024,512]{1,0:T(8,128)(2,1)} %get-tuple-element.129.dq_ref, bf16[1024,128]{1,0:T(8,128)(2,1)} %get-tuple-element.130.dk_ref, bf16[1024,128]{1,0:T(8,128)(2,1)} %get-tuple-element.131.dv_ref, bf16[2048,256]{1,0:T(8,128)(2,1)} %pad_maximum_fusion.w_ref.wkv_ref, ...), custom_call_target="tpu_custom_call" | custom-call | flops 1 | bytes 1 | tf_op jit(solution)/shard_map/unproject/pallas_call | solution.py:261
  571.0 4.1 combine.7
  579.2 5.0 all-to-all-start.9
  602.7 21.1 %collective-permute-done.26 = bf16[128,1024]{1,0:T(8,128)(2,1)S(1)} collective-permute-done((bf16[128,1024]{1,0:T(8,128)(2,1)S(1)}, bf16[128,1024]{1,0:T(8,128)(2,1)S(1)}, u32[]{:S(2)}, u32[]{:S(2)}) %collective-permute-start.26) | collective-permute-done | bytes 262176 | tf_op jit(solution)/shard_map/ppermute | solution.py:656
  629.4 11.8 %down_gradient.1 = f32[1,768,2048]{2,1,0:T(8,128)} custom-call(bf16[1216,2176]{1,0:T(8,128)(2,1)} %bitcast.13.c_ref.mask_ref, f32[1216,128]{1,0:T(8,128)} %get-tuple-element.97.w_ref, bf16[1216,768]{1,0:T(8,128)(2,1)} %get-tuple-element.143.act_ref), custom_call_target="tpu_custom_call" | custom-call | flops 1 | bytes 1 | tf_op jit(solution)/shard_map/down_gradient/pallas_call | solution.py:529
  643.0 31.3 %collective-permute-done.29 = bf16[512,512]{1,0:T(8,128)(2,1)} collective-permute-done((bf16[512,512]{1,0:T(8,128)(2,1)}, bf16[512,512]{1,0:T(8,128)(2,1)}, u32[]{:S(2)}, u32[]{:S(2)}) %collective-permute-start.29) | collective-permute-done | bytes 524320 | tf_op jit(solution)/shard_map/ppermute | solution.py:656
  676.8 3.3 convert_reduce_fusion
  (322 shorter events, 119.9 us)
Async XLA Ops:
  7.2 79.5 %all-gather.6.cloned.1.call-start = ((), (), s32[]{:S(2)}) async-start(), calls=%async_computation.11 | async-start | bytes 4718592 | tf_op jit(solution)/shard_map/all_gather | solution.py:637
  10.8 98.5 %all-gather.8.cloned.1.call-start = ((), (), s32[]{:S(2)}) async-start(), calls=%async_computation.12 | async-start | bytes 2621440 | tf_op jit(solution)/shard_map/all_gather | solution.py:637
  11.3 9.4 %collective-permute-start.3 = (bf16[512,128]{1,0:T(8,128)(2,1)S(1)}, bf16[512,128]{1,0:T(8,128)(2,1)S(1)}, u32[]{:S(2)}, u32[]{:S(2)}) collective-permute-start(bf16[512,128]{1,0:T(8,128)(2,1)S(1)} %pad_maximum_fusion.6), channel_id=1, source_target_pairs={{0,8},{8,16},{16,24},{24,0},{1,9},{9,17},{17,25},{25,1},{2,10},{10... | collective-permute-start | bytes 393224 | tf_op jit(solution)/shard_map/ppermute | solution.py:644
  14.4 7.8 %collective-permute-start.5 = (bf16[512,128]{1,0:T(8,128)(2,1)S(1)}, bf16[512,128]{1,0:T(8,128)(2,1)S(1)}, u32[]{:S(2)}, u32[]{:S(2)}) collective-permute-start(bf16[512,128]{1,0:T(8,128)(2,1)S(1)} %pad_maximum_fusion.6), channel_id=1, source_target_pairs={{0,24},{8,0},{16,8},{24,16},{1,25},{9,1},{17,9},{25,17},{2,26},{10... | collective-permute-start | bytes 393224 | tf_op jit(solution)/shard_map/ppermute | solution.py:644
  20.7 6.8 collective-permute-start.4
  27.5 146.3 %all-gather.10.cloned.1.call-start = ((), (), s32[]{:S(2)}) async-start(), calls=%async_computation.13 | async-start | bytes 9437184 | tf_op jit(solution)/shard_map/all_gather | solution.py:637
  27.6 16.7 %collective-permute-start = (bf16[512,512]{1,0:T(8,128)(2,1)S(1)}, bf16[512,512]{1,0:T(8,128)(2,1)S(1)}, u32[]{:S(2)}, u32[]{:S(2)}) collective-permute-start(bf16[512,512]{1,0:T(8,128)(2,1)S(1)} %copy-done.20), channel_id=1, source_target_pairs={{0,8},{8,16},{16,24},{24,0},{1,9},{9,17},{17,25},{25,1},{2,10},{10... | collective-permute-start | bytes 1572872 | tf_op jit(solution)/shard_map/ppermute | solution.py:644
  27.7 22.5 %collective-permute-start.2 = (bf16[512,512]{1,0:T(8,128)(2,1)S(1)}, bf16[512,512]{1,0:T(8,128)(2,1)}, u32[]{:S(2)}, u32[]{:S(2)}) collective-permute-start(bf16[512,512]{1,0:T(8,128)(2,1)S(1)} %copy-done.20), channel_id=1, source_target_pairs={{0,24},{8,0},{16,8},{24,16},{1,25},{9,1},{17,9},{25,17},{2,26},{10... | collective-permute-start | bytes 1572872 | tf_op jit(solution)/shard_map/ppermute | solution.py:644
  35.4 24.7 %collective-permute-start.6 = (bf16[2048,128]{1,0:T(8,128)(2,1)}, bf16[2048,128]{1,0:T(8,128)(2,1)}, u32[]{:S(2)}, u32[]{:S(2)}) collective-permute-start(bf16[2048,128]{1,0:T(8,128)(2,1)} %pad_maximum_fusion.4), channel_id=1, source_target_pairs={{1,0},{0,1},{3,2},{2,3},{5,4},{4,5},{7,6},{6,7},{9,8},{8,9},{11,10... | collective-permute-start | bytes 1572872 | tf_op jit(solution)/shard_map/ppermute | solution.py:692
  59.4 27.3 %collective-permute-start.1 = (bf16[512,512]{1,0:T(8,128)(2,1)S(1)}, bf16[512,512]{1,0:T(8,128)(2,1)S(1)}, u32[]{:S(2)}, u32[]{:S(2)}) collective-permute-start(bf16[512,512]{1,0:T(8,128)(2,1)S(1)} %collective-permute-done.refs_1_), channel_id=1, source_target_pairs={{0,8},{8,16},{16,24},{24,0},{1,9},{9,17},{17,25},{25,1},{2,10},{10... | collective-permute-start | bytes 1572872 | tf_op jit(solution)/shard_map/ppermute | solution.py:644
  60.0 123.9 %copy-start.17 = (bf16[136,2176]{1,0:T(8,128)(2,1)}, bf16[136,2176]{1,0:T(8,128)(2,1)S(1)}, u32[]{:S(2)}) copy-start(bf16[136,2176]{1,0:T(8,128)(2,1)S(1)} %fusion.18.refs_0_) | copy-start | bytes 1775620
  121.3 18.1 %collective-permute-start.7 = (bf16[136,2176]{1,0:T(8,128)(2,1)S(1)}, bf16[136,2176]{1,0:T(8,128)(2,1)S(1)}, u32[]{:S(2)}, u32[]{:S(2)}) collective-permute-start(bf16[136,2176]{1,0:T(8,128)(2,1)S(1)} %fusion.18.refs_0_), channel_id=1, source_target_pairs={{0,8},{8,16},{16,24},{24,0},{1,9},{9,17},{17,25},{25,1},{2,10},{10... | collective-permute-start | bytes 1775624 | tf_op jit(solution)/shard_map/ppermute | solution.py:644
  121.3 27.8 %collective-permute-start.9 = (bf16[136,2176]{1,0:T(8,128)(2,1)S(1)}, bf16[136,2176]{1,0:T(8,128)(2,1)S(1)}, u32[]{:S(2)}, u32[]{:S(2)}) collective-permute-start(bf16[136,2176]{1,0:T(8,128)(2,1)S(1)} %fusion.18.refs_0_), channel_id=1, source_target_pairs={{0,24},{8,0},{16,8},{24,16},{1,25},{9,1},{17,9},{25,17},{2,26},{10... | collective-permute-start | bytes 1775624 | tf_op jit(solution)/shard_map/ppermute | solution.py:644
  139.4 44.7 %copy-start.31 = (bf16[136,2176]{1,0:T(8,128)(2,1)}, bf16[136,2176]{1,0:T(8,128)(2,1)S(1)}, u32[]{:S(2)}) copy-start(bf16[136,2176]{1,0:T(8,128)(2,1)S(1)} %collective-permute-done.7.refs_1_) | copy-start | bytes 1775620
  139.4 24.2 %collective-permute-start.8 = (bf16[136,2176]{1,0:T(8,128)(2,1)S(1)}, bf16[136,2176]{1,0:T(8,128)(2,1)S(1)}, u32[]{:S(2)}, u32[]{:S(2)}) collective-permute-start(bf16[136,2176]{1,0:T(8,128)(2,1)S(1)} %collective-permute-done.7.refs_1_), channel_id=1, source_target_pairs={{0,8},{8,16},{16,24},{24,0},{1,9},{9,17},{17,25},{25,1},{2,10},{10... | collective-permute-start | bytes 1775624 | tf_op jit(solution)/shard_map/ppermute | solution.py:644
  149.2 35.3 %copy-start.32 = (bf16[136,2176]{1,0:T(8,128)(2,1)}, bf16[136,2176]{1,0:T(8,128)(2,1)S(1)}, u32[]{:S(2)}) copy-start(bf16[136,2176]{1,0:T(8,128)(2,1)S(1)} %collective-permute-done.9.refs_3_) | copy-start | bytes 1775620
  180.0 13.6 %all-to-all-start = ((bf16[8,128,256]{2,1,0:T(8,128)(2,1)}), bf16[8,128,256]{2,1,0:T(8,128)(2,1)S(1)}, u32[]{:S(2)}, u32[]{:S(2)}) async-start(bf16[8,128,256]{2,1,0:T(8,128)(2,1)} %bitcast.95), calls=%async_computation | async-start | bytes 1048576 | tf_op jit(solution)/shard_map/all_to_all | solution.py:640
  193.6 65.6 %all-to-all-start.1 = ((bf16[8,152,2176]{2,1,0:T(8,128)(2,1)}), bf16[8,152,2176]{2,1,0:T(8,128)(2,1)}, u32[]{:S(2)}, u32[]{:S(2)}) async-start(bf16[8,152,2176]{2,1,0:T(8,128)(2,1)} %bitcast.76), calls=%async_computation.1 | async-start | bytes 10584064 | tf_op jit(solution)/shard_map/all_to_all | solution.py:640
  200.7 171.0 %copy-start.14 = (bf16[128,2048]{1,0:T(8,128)(2,1)}, bf16[128,2048]{1,0:T(8,128)(2,1)S(1)}, u32[]{:S(2)}) copy-start(bf16[128,2048]{1,0:T(8,128)(2,1)S(1)} %multiply_convert_fusion) | copy-start | bytes 1572868
  200.7 63.6 %copy-start.25 = (bf16[128,1024]{1,0:T(8,128)(2,1)}, bf16[128,1024]{1,0:T(8,128)(2,1)S(1)}, u32[]{:S(2)}) copy-start(bf16[128,1024]{1,0:T(8,128)(2,1)S(1)} %get-tuple-element.171.refs_0_) | copy-start | bytes 786436
  200.7 11.0 %collective-permute-start.13 = (bf16[128,1024]{1,0:T(8,128)(2,1)S(1)}, bf16[128,1024]{1,0:T(8,128)(2,1)S(1)}, u32[]{:S(2)}, u32[]{:S(2)}) collective-permute-start(bf16[128,1024]{1,0:T(8,128)(2,1)S(1)} %get-tuple-element.170.refs_0_), channel_id=1, source_target_pairs={{0,8},{8,16},{16,24},{24,0},{1,9},{9,17},{17,25},{25,1},{2,10},{10... | collective-permute-start | bytes 786440 | tf_op jit(solution)/shard_map/ppermute | solution.py:644
  202.3 13.9 %collective-permute-start.15 = (bf16[128,1024]{1,0:T(8,128)(2,1)S(1)}, bf16[128,1024]{1,0:T(8,128)(2,1)S(1)}, u32[]{:S(2)}, u32[]{:S(2)}) collective-permute-start(bf16[128,1024]{1,0:T(8,128)(2,1)S(1)} %get-tuple-element.170.refs_0_), channel_id=1, source_target_pairs={{0,24},{8,0},{16,8},{24,16},{1,25},{9,1},{17,9},{25,17},{2,26},{10... | collective-permute-start | bytes 786440 | tf_op jit(solution)/shard_map/ppermute | solution.py:644
  211.8 10.7 %collective-permute-start.14 = (bf16[128,1024]{1,0:T(8,128)(2,1)S(1)}, bf16[128,1024]{1,0:T(8,128)(2,1)S(1)}, u32[]{:S(2)}, u32[]{:S(2)}) collective-permute-start(bf16[128,1024]{1,0:T(8,128)(2,1)S(1)} %collective-permute-done.13.refs_1_), channel_id=1, source_target_pairs={{0,8},{8,16},{16,24},{24,0},{1,9},{9,17},{17,25},{25,1},{2,10},{10... | collective-permute-start | bytes 786440 | tf_op jit(solution)/shard_map/ppermute | solution.py:644
  259.1 34.4 %all-to-all-start.3 = ((bf16[8,152,1024]{2,1,0:T(8,128)(2,1)}), bf16[8,152,1024]{2,1,0:T(8,128)(2,1)S(1)}, u32[]{:S(2)}, u32[]{:S(2)}) async-start(bf16[8,152,1024]{2,1,0:T(8,128)(2,1)} %bitcast.80), calls=%async_computation.3 | async-start | bytes 4980736 | tf_op jit(solution)/shard_map/all_to_all | solution.py:640
  262.8 11.0 %collective-permute-start.10 = (bf16[128,1024]{1,0:T(8,128)(2,1)S(1)}, bf16[128,1024]{1,0:T(8,128)(2,1)S(1)}, u32[]{:S(2)}, u32[]{:S(2)}) collective-permute-start(bf16[128,1024]{1,0:T(8,128)(2,1)S(1)} %get-tuple-element.171.refs_0_), channel_id=1, source_target_pairs={{0,8},{8,16},{16,24},{24,0},{1,9},{9,17},{17,25},{25,1},{2,10},{10... | collective-permute-start | bytes 786440 | tf_op jit(solution)/shard_map/ppermute | solution.py:644
  264.3 13.9 %collective-permute-start.12 = (bf16[128,1024]{1,0:T(8,128)(2,1)S(1)}, bf16[128,1024]{1,0:T(8,128)(2,1)S(1)}, u32[]{:S(2)}, u32[]{:S(2)}) collective-permute-start(bf16[128,1024]{1,0:T(8,128)(2,1)S(1)} %get-tuple-element.171.refs_0_), channel_id=1, source_target_pairs={{0,24},{8,0},{16,8},{24,16},{1,25},{9,1},{17,9},{25,17},{2,26},{10... | collective-permute-start | bytes 786440 | tf_op jit(solution)/shard_map/ppermute | solution.py:644
  273.8 10.7 %collective-permute-start.11 = (bf16[128,1024]{1,0:T(8,128)(2,1)S(1)}, bf16[128,1024]{1,0:T(8,128)(2,1)S(1)}, u32[]{:S(2)}, u32[]{:S(2)}) collective-permute-start(bf16[128,1024]{1,0:T(8,128)(2,1)S(1)} %collective-permute-done.10.refs_1_), channel_id=1, source_target_pairs={{0,8},{8,16},{16,24},{24,0},{1,9},{9,17},{17,25},{25,1},{2,10},{10... | collective-permute-start | bytes 786440 | tf_op jit(solution)/shard_map/ppermute | solution.py:644
  295.0 35.3 %all-to-all-start.2 = ((bf16[8,152,1024]{2,1,0:T(8,128)(2,1)}), bf16[8,152,1024]{2,1,0:T(8,128)(2,1)}, u32[]{:S(2)}, u32[]{:S(2)}) async-start(bf16[8,152,1024]{2,1,0:T(8,128)(2,1)} %bitcast.79), calls=%async_computation.2 | async-start | bytes 4980736 | tf_op jit(solution)/shard_map/all_to_all | solution.py:640
  302.7 69.0 %copy-start.39 = (bf16[32,512]{1,0:T(8,128)(2,1)}, bf16[32,512]{1,0:T(8,128)(2,1)S(1)}, u32[]{:S(2)}) copy-start(bf16[32,512]{1,0:T(8,128)(2,1)S(1)} %get-tuple-element.182) | copy-start | bytes 98308
  302.7 69.0 %copy-start.40 = (bf16[32,512]{1,0:T(8,128)(2,1)}, bf16[32,512]{1,0:T(8,128)(2,1)S(1)}, u32[]{:S(2)}) copy-start(bf16[32,512]{1,0:T(8,128)(2,1)S(1)} %get-tuple-element.183) | copy-start | bytes 98308
  302.7 69.0 %copy-start.41 = (bf16[32,512]{1,0:T(8,128)(2,1)}, bf16[32,512]{1,0:T(8,128)(2,1)S(1)}, u32[]{:S(2)}) copy-start(bf16[32,512]{1,0:T(8,128)(2,1)S(1)} %get-tuple-element.184) | copy-start | bytes 98308
  302.7 69.0 %copy-start.42 = (bf16[32,512]{1,0:T(8,128)(2,1)}, bf16[32,512]{1,0:T(8,128)(2,1)S(1)}, u32[]{:S(2)}) copy-start(bf16[32,512]{1,0:T(8,128)(2,1)S(1)} %get-tuple-element.185) | copy-start | bytes 98308
  330.3 30.2 %all-to-all-start.7 = ((bf16[8,512,256]{2,1,0:T(8,128)(2,1)}), bf16[8,512,256]{2,1,0:T(8,128)(2,1)S(1)}, u32[]{:S(2)}, u32[]{:S(2)}) async-start(bf16[8,512,256]{2,1,0:T(8,128)(2,1)} %bitcast.85), calls=%async_computation.7 | async-start | bytes 4194304 | tf_op jit(solution)/shard_map/all_to_all | solution.py:640
  361.8 35.4 %all-to-all-start.6 = ((bf16[8,152,1024]{2,1,0:T(8,128)(2,1)}), bf16[8,152,1024]{2,1,0:T(8,128)(2,1)}, u32[]{:S(2)}, u32[]{:S(2)}) async-start(bf16[8,152,1024]{2,1,0:T(8,128)(2,1)} %bitcast.94), calls=%async_computation.6 | async-start | bytes 4980736 | tf_op jit(solution)/shard_map/all_to_all | solution.py:640
  397.3 37.8 %all-to-all-start.4 = ((bf16[8,152,1152]{2,1,0:T(8,128)(2,1)}), bf16[8,152,1152]{2,1,0:T(8,128)(2,1)S(1)}, u32[]{:S(2)}, u32[]{:S(2)}) async-start(bf16[8,152,1152]{2,1,0:T(8,128)(2,1)} %bitcast.91), calls=%async_computation.4 | async-start | bytes 5603328 | tf_op jit(solution)/shard_map/all_to_all | solution.py:640
  405.1 47.3 %collective-permute-start.19 = (bf16[128,1024]{1,0:T(8,128)(2,1)}, bf16[128,1024]{1,0:T(8,128)(2,1)}, u32[]{:S(2)}, u32[]{:S(2)}) collective-permute-start(bf16[128,1024]{1,0:T(8,128)(2,1)} %get-tuple-element.111), channel_id=1, source_target_pairs={{0,24},{8,0},{16,8},{24,16},{1,25},{9,1},{17,9},{25,17},{2,26},{10... | collective-permute-start | bytes 786440 | tf_op jit(solution)/shard_map/ppermute | solution.py:656
  408.4 45.3 %collective-permute-start.20 = (bf16[128,1024]{1,0:T(8,128)(2,1)}, bf16[128,1024]{1,0:T(8,128)(2,1)}, u32[]{:S(2)}, u32[]{:S(2)}) collective-permute-start(bf16[128,1024]{1,0:T(8,128)(2,1)} %get-tuple-element.112), channel_id=1, source_target_pairs={{0,16},{8,24},{16,0},{24,8},{1,17},{9,25},{17,1},{25,9},{2,18},{10... | collective-permute-start | bytes 786440 | tf_op jit(solution)/shard_map/ppermute | solution.py:656
  408.4 45.3 %collective-permute-start.21 = (bf16[128,1024]{1,0:T(8,128)(2,1)}, bf16[128,1024]{1,0:T(8,128)(2,1)}, u32[]{:S(2)}, u32[]{:S(2)}) collective-permute-start(bf16[128,1024]{1,0:T(8,128)(2,1)} %get-tuple-element.113), channel_id=1, source_target_pairs={{0,8},{8,16},{16,24},{24,0},{1,9},{9,17},{17,25},{25,1},{2,10},{10... | collective-permute-start | bytes 786440 | tf_op jit(solution)/shard_map/ppermute | solution.py:656
  436.6 44.8 %all-to-all-start.5 = ((bf16[8,152,1024]{2,1,0:T(8,128)(2,1)}), bf16[8,152,1024]{2,1,0:T(8,128)(2,1)S(1)}, u32[]{:S(2)}, u32[]{:S(2)}) async-start(bf16[8,152,1024]{2,1,0:T(8,128)(2,1)} %bitcast.93), calls=%async_computation.5 | async-start | bytes 4980736 | tf_op jit(solution)/shard_map/all_to_all | solution.py:640
  440.3 83.9 %all-gather.12.cloned.1.call-start = ((), (), s32[]{:S(2)}) async-start(), calls=%async_computation.14 | async-start | bytes 4718592 | tf_op jit(solution)/shard_map/all_gather | solution.py:637
  449.0 31.4 %copy-start.35 = (f32[128,32]{1,0:T(8,128)S(1)}, f32[128,32]{1,0:T(8,128)}, u32[]{:S(2)}) copy-start(f32[128,32]{1,0:T(8,128)} %get-tuple-element.202) | copy-start | bytes 49156
  449.0 11.1 %collective-permute-start.16 = (bf16[128,1152]{1,0:T(8,128)(2,1)}, bf16[128,1152]{1,0:T(8,128)(2,1)S(1)}, u32[]{:S(2)}, u32[]{:S(2)}) collective-permute-start(bf16[128,1152]{1,0:T(8,128)(2,1)} %get-tuple-element.104), channel_id=1, source_target_pairs={{0,24},{8,0},{16,8},{24,16},{1,25},{9,1},{17,9},{25,17},{2,26},{10... | collective-permute-start | bytes 884744 | tf_op jit(solution)/shard_map/ppermute | solution.py:656
  452.4 26.0 %collective-permute-start.17 = (bf16[128,1152]{1,0:T(8,128)(2,1)}, bf16[128,1152]{1,0:T(8,128)(2,1)S(1)}, u32[]{:S(2)}, u32[]{:S(2)}) collective-permute-start(bf16[128,1152]{1,0:T(8,128)(2,1)} %get-tuple-element.105), channel_id=1, source_target_pairs={{0,16},{8,24},{16,0},{24,8},{1,17},{9,25},{17,1},{25,9},{2,18},{10... | collective-permute-start | bytes 884744 | tf_op jit(solution)/shard_map/ppermute | solution.py:656
  452.4 26.0 %collective-permute-start.18 = (bf16[128,1152]{1,0:T(8,128)(2,1)}, bf16[128,1152]{1,0:T(8,128)(2,1)S(1)}, u32[]{:S(2)}, u32[]{:S(2)}) collective-permute-start(bf16[128,1152]{1,0:T(8,128)(2,1)} %get-tuple-element.106), channel_id=1, source_target_pairs={{0,8},{8,16},{16,24},{24,0},{1,9},{9,17},{17,25},{25,1},{2,10},{10... | collective-permute-start | bytes 884744 | tf_op jit(solution)/shard_map/ppermute | solution.py:656
  486.8 90.3 %reduce-scatter.2.cloned.1.call-start = ((), (), s32[]{:S(2)}) async-start(), calls=%async_computation.15 | async-start | bytes 2621440 | tf_op jit(solution)/shard_map/reduce_scatter | solution.py:777
  491.0 20.4 %collective-permute-start.22 = (bf16[128,1024]{1,0:T(8,128)(2,1)}, bf16[128,1024]{1,0:T(8,128)(2,1)S(1)}, u32[]{:S(2)}, u32[]{:S(2)}) collective-permute-start(bf16[128,1024]{1,0:T(8,128)(2,1)} %get-tuple-element.117), channel_id=1, source_target_pairs={{0,24},{8,0},{16,8},{24,16},{1,25},{9,1},{17,9},{25,17},{2,26},{10... | collective-permute-start | bytes 786440 | tf_op jit(solution)/shard_map/ppermute | solution.py:656
  491.0 25.6 %collective-permute-start.23 = (bf16[128,1024]{1,0:T(8,128)(2,1)}, bf16[128,1024]{1,0:T(8,128)(2,1)S(1)}, u32[]{:S(2)}, u32[]{:S(2)}) collective-permute-start(bf16[128,1024]{1,0:T(8,128)(2,1)} %get-tuple-element.118), channel_id=1, source_target_pairs={{0,16},{8,24},{16,0},{24,8},{1,17},{9,25},{17,1},{25,9},{2,18},{10... | collective-permute-start | bytes 786440 | tf_op jit(solution)/shard_map/ppermute | solution.py:656
  493.8 22.9 %collective-permute-start.24 = (bf16[128,1024]{1,0:T(8,128)(2,1)}, bf16[128,1024]{1,0:T(8,128)(2,1)S(1)}, u32[]{:S(2)}, u32[]{:S(2)}) collective-permute-start(bf16[128,1024]{1,0:T(8,128)(2,1)} %get-tuple-element.119), channel_id=1, source_target_pairs={{0,8},{8,16},{16,24},{24,0},{1,9},{9,17},{17,25},{25,1},{2,10},{10... | collective-permute-start | bytes 786440 | tf_op jit(solution)/shard_map/ppermute | solution.py:656
  533.1 36.5 %all-to-all-start.8 = ((bf16[8,152,1024]{2,1,0:T(8,128)(2,1)}), bf16[8,152,1024]{2,1,0:T(8,128)(2,1)S(1)}, u32[]{:S(2)}, u32[]{:S(2)}) async-start(bf16[8,152,1024]{2,1,0:T(8,128)(2,1)} %bitcast.92), calls=%async_computation.8 | async-start | bytes 4980736 | tf_op jit(solution)/shard_map/all_to_all | solution.py:640
  579.2 97.7 %all-to-all-start.9 = ((bf16[8,144,2048]{2,1,0:T(8,128)(2,1)}), bf16[8,144,2048]{2,1,0:T(8,128)(2,1)}, u32[]{:S(2)}, u32[]{:S(2)}) async-start(bf16[8,144,2048]{2,1,0:T(8,128)(2,1)} %unproject.1), calls=%async_computation.10 | async-start | bytes 9437184 | tf_op jit(solution)/shard_map/all_to_all | solution.py:640
  588.7 7.5 %collective-permute-start.31 = (bf16[2048,128]{0,1:T(8,128)(2,1)S(1)}, bf16[2048,128]{0,1:T(8,128)(2,1)S(1)}, u32[]{:S(2)}, u32[]{:S(2)}) collective-permute-start(bf16[2048,128]{0,1:T(8,128)(2,1)S(1)} %pad_maximum_fusion.5), channel_id=1, source_target_pairs={{0,1},{1,0},{2,3},{3,2},{4,5},{5,4},{6,7},{7,6},{8,9},{9,8},{10,11... | collective-permute-start | bytes 1572872 | tf_op jit(solution)/shard_map/ppermute | solution.py:809
  592.4 32.7 %copy-start.19 = (bf16[2048,512]{1,0:T(8,128)(2,1)}, bf16[2048,512]{1,0:T(8,128)(2,1)S(1)}, u32[]{:S(2)}) copy-start(bf16[2048,512]{1,0:T(8,128)(2,1)S(1)} %convolution_convert_fusion) | copy-start | bytes 6291460
  592.4 31.5 %copy-start.50 = (bf16[128,1024]{1,0:T(8,128)(2,1)S(1)}, bf16[128,1024]{1,0:T(8,128)(2,1)}, u32[]{:S(2)}) copy-start(bf16[128,1024]{1,0:T(8,128)(2,1)} %get-tuple-element.135) | copy-start | bytes 786436
  592.4 10.3 %collective-permute-start.25 = (bf16[128,1024]{1,0:T(8,128)(2,1)S(1)}, bf16[128,1024]{1,0:T(8,128)(2,1)S(1)}, u32[]{:S(2)}, u32[]{:S(2)}) collective-permute-start(bf16[128,1024]{1,0:T(8,128)(2,1)S(1)} %copy-done.69), channel_id=1, source_target_pairs={{0,24},{8,0},{16,8},{24,16},{1,25},{9,1},{17,9},{25,17},{2,26},{10... | collective-permute-start | bytes 786440 | tf_op jit(solution)/shard_map/ppermute | solution.py:656
  594.0 29.9 %collective-permute-start.26 = (bf16[128,1024]{1,0:T(8,128)(2,1)S(1)}, bf16[128,1024]{1,0:T(8,128)(2,1)S(1)}, u32[]{:S(2)}, u32[]{:S(2)}) collective-permute-start(bf16[128,1024]{1,0:T(8,128)(2,1)S(1)} %copy-done.68), channel_id=1, source_target_pairs={{0,16},{8,24},{16,0},{24,8},{1,17},{9,25},{17,1},{25,9},{2,18},{10... | collective-permute-start | bytes 786440 | tf_op jit(solution)/shard_map/ppermute | solution.py:656
  594.3 29.5 %collective-permute-start.27 = (bf16[128,1024]{1,0:T(8,128)(2,1)S(1)}, bf16[128,1024]{1,0:T(8,128)(2,1)S(1)}, u32[]{:S(2)}, u32[]{:S(2)}) collective-permute-start(bf16[128,1024]{1,0:T(8,128)(2,1)S(1)} %copy-done.67), channel_id=1, source_target_pairs={{0,8},{8,16},{16,24},{24,0},{1,9},{9,17},{17,25},{25,1},{2,10},{10... | collective-permute-start | bytes 786440 | tf_op jit(solution)/shard_map/ppermute | solution.py:656
  597.1 30.3 %collective-permute-start.32 = (bf16[512,128]{0,1:T(8,128)(2,1)S(1)}, bf16[512,128]{0,1:T(8,128)(2,1)S(1)}, u32[]{:S(2)}, u32[]{:S(2)}) collective-permute-start(bf16[512,128]{0,1:T(8,128)(2,1)S(1)} %get-tuple-element.167), channel_id=1, source_target_pairs={{0,24},{8,0},{16,8},{24,16},{1,25},{9,1},{17,9},{25,17},{2,26},{10... | collective-permute-start | bytes 393224 | tf_op jit(solution)/shard_map/ppermute | solution.py:656
  599.0 42.2 %collective-permute-start.33 = (bf16[512,128]{0,1:T(8,128)(2,1)}, bf16[512,128]{0,1:T(8,128)(2,1)}, u32[]{:S(2)}, u32[]{:S(2)}) collective-permute-start(bf16[512,128]{0,1:T(8,128)(2,1)} %get-tuple-element.169), channel_id=1, source_target_pairs={{0,16},{8,24},{16,0},{24,8},{1,17},{9,25},{17,1},{25,9},{2,18},{10... | collective-permute-start | bytes 393224 | tf_op jit(solution)/shard_map/ppermute | solution.py:656
  602.7 38.5 %collective-permute-start.34 = (bf16[512,128]{0,1:T(8,128)(2,1)S(1)}, bf16[512,128]{0,1:T(8,128)(2,1)}, u32[]{:S(2)}, u32[]{:S(2)}) collective-permute-start(bf16[512,128]{0,1:T(8,128)(2,1)S(1)} %get-tuple-element.168), channel_id=1, source_target_pairs={{0,8},{8,16},{16,24},{24,0},{1,9},{9,17},{17,25},{25,1},{2,10},{10... | collective-permute-start | bytes 393224 | tf_op jit(solution)/shard_map/ppermute | solution.py:656
  625.1 17.9 %collective-permute-start.28 = (bf16[512,512]{1,0:T(8,128)(2,1)}, bf16[512,512]{1,0:T(8,128)(2,1)S(1)}, u32[]{:S(2)}, u32[]{:S(2)}) collective-permute-start(bf16[512,512]{1,0:T(8,128)(2,1)} %get-tuple-element.152), channel_id=1, source_target_pairs={{0,24},{8,0},{16,8},{24,16},{1,25},{9,1},{17,9},{25,17},{2,26},{10... | collective-permute-start | bytes 1572872 | tf_op jit(solution)/shard_map/ppermute | solution.py:656
  625.1 49.2 %collective-permute-start.29 = (bf16[512,512]{1,0:T(8,128)(2,1)}, bf16[512,512]{1,0:T(8,128)(2,1)}, u32[]{:S(2)}, u32[]{:S(2)}) collective-permute-start(bf16[512,512]{1,0:T(8,128)(2,1)} %get-tuple-element.154), channel_id=1, source_target_pairs={{0,16},{8,24},{16,0},{24,8},{1,17},{9,25},{17,1},{25,9},{2,18},{10... | collective-permute-start | bytes 1572872 | tf_op jit(solution)/shard_map/ppermute | solution.py:656
  627.4 46.9 %collective-permute-start.30 = (bf16[512,512]{1,0:T(8,128)(2,1)S(1)}, bf16[512,512]{1,0:T(8,128)(2,1)}, u32[]{:S(2)}, u32[]{:S(2)}) collective-permute-start(bf16[512,512]{1,0:T(8,128)(2,1)S(1)} %get-tuple-element.153), channel_id=1, source_target_pairs={{0,8},{8,16},{16,24},{24,0},{1,9},{9,17},{17,25},{25,1},{2,10},{10... | collective-permute-start | bytes 1572872 | tf_op jit(solution)/shard_map/ppermute | solution.py:656
  680.5 4.2 collective-permute-start.35
  684.8 5.6 collective-permute-start.36
  (58 other events, 533.6 us)
Sparse Core Ops, SparseCore 0:
  10.9 39.4 all-gather.5
  52.0 57.2 all-gather.7
  121.4 52.3 all-gather.9
  486.9 37.2 all-gather.11
  533.2 43.8 reduce-scatter.1

commit v3 on v2

--- a/solution.py
+++ b/solution.py
@@ -17,7 +17,7 @@
 VERY_NEGATIVE = -1e30
 SOFTMAX_SCALE = HEAD_SIZE ** (-0.5)
 LOG2_SCALE = SOFTMAX_SCALE * math.log2(math.e)
-VMEM_BYTES = 56 * 1024 * 1024
+VMEM_BYTES = 24 * 1024 * 1024
 F32 = jnp.float32
 BF16 = jnp.bfloat16
 
@@ -262,34 +262,41 @@
         functools.partial(unproject_kernel, own_rows),
         out_shape=jax.ShapeDtypeStruct((span // own_rows, own_rows + 16, model), BF16),
         scratch_shapes=[pltpu.VMEM((1, model), F32)],
-        compiler_params=pltpu.CompilerParams(vmem_limit_bytes=VMEM_BYTES),
+        compiler_params=pltpu.CompilerParams(vmem_limit_bytes=44 * 1024 * 1024),
         cost_estimate=cost(0),
         name="unproject",
     )(dq, dk, dv, wkv, x, gain[None], router_part, mixture_part, query_part, key_part, *pieces)
 
 
-def out_project_kernel(a_ref, w_ref, out_ref):
-    total = mm(a_ref[0], w_ref[0])
-    for m in range(1, a_ref.shape[0]):
-        total += mm(a_ref[m], w_ref[m])
+def out_project_kernel(plane_ref, a_ref, *refs):
+    out_ref = refs[-1]
+    pieces = refs[:-1]
+    members, _, width = a_ref.shape
+    planes, each = len(pieces), members // len(pieces)
+    total = None
+    for s, piece in enumerate(pieces):
+        block = lax.rem(plane_ref[0] + planes - s, planes) * each
+        for i in range(each):
+            part = mm(a_ref[block + i], piece[i * width:(i + 1) * width, :])
+            total = part if total is None else total + part
     out_ref[...] = total.astype(BF16)
 
 
-def out_project(attended_all, weight):
+def out_project(plane, attended_all, pieces):
     members, span, width = attended_all.shape
-    columns = weight.shape[2]
-    tile = 512
+    size, columns = pieces[0].shape
+    tile = 256
     return pl.pallas_call(
         out_project_kernel,
         grid=(span // tile,),
-        in_specs=[pl.BlockSpec((members, tile, width), lambda i: (0, i, 0)),
-                  pl.BlockSpec((members, width, columns), lambda i: (0, 0, 0))],
+        in_specs=[pl.BlockSpec(memory_space=pltpu.SMEM), pl.BlockSpec((members, tile, width), lambda i: (0, i, 0))]
+        + [pl.BlockSpec((size, columns), lambda i: (0, 0))] * len(pieces),
         out_specs=pl.BlockSpec((tile, columns), lambda i: (i, 0)),
         out_shape=jax.ShapeDtypeStruct((span, columns), BF16),
         compiler_params=pltpu.CompilerParams(vmem_limit_bytes=VMEM_BYTES),
         cost_estimate=cost(0),
         name="out_project",
-    )(attended_all, weight)
+    )(plane, attended_all, *pieces)
 
 
 def out_back_kernel(g_ref, w_ref, out_ref):
@@ -401,7 +408,7 @@
         functools.partial(expert_kernel, experts),
         grid=(hidden // tile,),
         in_specs=[pl.BlockSpec(memory_space=pltpu.SMEM), whole(rows, half), whole(rows, half),
-                  pl.BlockSpec((rows, padded), lambda i: (0, model // padded)), whole(padded, model), column(model),
+                  pl.BlockSpec((rows, padded), lambda i: (0, half // padded)), whole(padded, model), column(model),
                   column(model), column(rows)],
         out_specs=[column(rows), column(rows), column(rows), whole(rows, HEAD_SIZE), whole(rows, route_width)],
         out_shape=[
@@ -412,7 +419,7 @@
             jax.ShapeDtypeStruct((rows, route_width), BF16),
         ],
         scratch_shapes=[pltpu.VMEM((rows, HEAD_SIZE), F32)],
-        compiler_params=pltpu.CompilerParams(vmem_limit_bytes=VMEM_BYTES),
+        compiler_params=pltpu.CompilerParams(vmem_limit_bytes=40 * 1024 * 1024),
         cost_estimate=cost(18),
         name="expert_forward",
     )(own, xa, xb, masked_rows, router, gate, up, upstream_down)
@@ -446,24 +453,26 @@
     )(gg, ug, gate, up, *extra)
 
 
-def down_back_kernel(c_ref, down_ref, out_ref):
-    out_ref[...] = mm_t(c_ref[...], down_ref[...])
-
-
-def down_back(upstream_rows, down):
-    rows = upstream_rows.shape[0]
+def down_back_kernel(ca_ref, cb_ref, down_ref, out_ref):
+    half = cb_ref.shape[1]
+    out_ref[...] = mm_t(ca_ref[...], down_ref[:, :half]) + mm_t(cb_ref[...], down_ref[:, half:])
+
+
+def down_back(ca, cb, down):
+    rows, half = cb.shape
     hidden, model = down.shape
     tile = 256
+    whole = pl.BlockSpec((rows, half), lambda i: (0, 0))
     return pl.pallas_call(
         down_back_kernel,
         grid=(hidden // tile,),
-        in_specs=[pl.BlockSpec((rows, model), lambda i: (0, 0)), pl.BlockSpec((tile, model), lambda i: (i, 0))],
+        in_specs=[whole, whole, pl.BlockSpec((tile, model), lambda i: (i, 0))],
         out_specs=pl.BlockSpec((rows, tile), lambda i: (0, i)),
         out_shape=jax.ShapeDtypeStruct((rows, hidden), F32),
         compiler_params=pltpu.CompilerParams(vmem_limit_bytes=VMEM_BYTES),
-        cost_estimate=cost(8),
+        cost_estimate=cost(0),
         name="down_back",
-    )(upstream_rows, down)
+    )(ca, cb, down)
 
 
 def produce_kernel(act_ref, w_ref, down_ref, *outs):
@@ -519,24 +528,31 @@
     )(xa, xb, gg, ug)
 
 
-def down_gradient_kernel(c_ref, w_ref, act_ref, out_ref):
-    out_ref[0] = t_mm(act_ref[...], (w_ref[:, :1] * c_ref[...].astype(F32)).astype(BF16))
-
-
-def down_gradient(upstream_rows, model, weight, activated):
-    rows, hidden = activated.shape
+def down_gradient_kernel(ca_ref, cb_ref, w_ref, act_ref, out_ref):
+    in_first = pl.program_id(0) < pl.num_programs(0) // 2
+    for c_ref, now in ((ca_ref, in_first), (cb_ref, jnp.logical_not(in_first))):
+        @pl.when(now)
+        def _():
+            out_ref[0] = t_mm(act_ref[...], (w_ref[:, :1] * c_ref[...].astype(F32)).astype(BF16))
+
+
+def down_gradient(ca, cb, weight, activated):
+    rows, half = cb.shape
+    hidden = activated.shape[1]
     tile = 256
+    count = half // tile
     return pl.pallas_call(
         down_gradient_kernel,
-        grid=(model // tile,),
-        in_specs=[pl.BlockSpec((rows, tile), lambda i: (0, i)), pl.BlockSpec((rows, HEAD_SIZE), lambda i: (0, 0)),
-                  pl.BlockSpec((rows, hidden), lambda i: (0, 0))],
+        grid=(2 * count,),
+        in_specs=[pl.BlockSpec((rows, tile), lambda i: (0, jnp.minimum(i, count - 1))),
+                  pl.BlockSpec((rows, tile), lambda i: (0, jnp.maximum(i - count, 0))),
+                  pl.BlockSpec((rows, HEAD_SIZE), lambda i: (0, 0)), pl.BlockSpec((rows, hidden), lambda i: (0, 0))],
         out_specs=pl.BlockSpec((1, hidden, tile), lambda i: (0, 0, i)),
-        out_shape=jax.ShapeDtypeStruct((1, hidden, model), F32),
+        out_shape=jax.ShapeDtypeStruct((1, hidden, 2 * half), F32),
         compiler_params=pltpu.CompilerParams(vmem_limit_bytes=VMEM_BYTES),
         cost_estimate=cost(0),
         name="down_gradient",
-    )(upstream_rows, weight, activated)
+    )(ca, cb, weight, activated)
 
 
 def dispatch_kernel(pick_ref, *refs):
@@ -579,7 +595,7 @@
 def combine(pick, rows, count, microseconds=0):
     column, slots = pick.shape
     width = rows.shape[1]
-    tile = math.gcd(width, 512)
+    tile = max(t for t in range(HEAD_SIZE, 513, HEAD_SIZE) if width % t == 0)
     size = column // count
     out = pl.BlockSpec((size, tile), lambda i: (0, i))
     return pl.pallas_call(
@@ -651,9 +667,17 @@
         return pieces
 
     def plane_sum(pieces):
+        def shift(value, by):
+            return lax.ppermute(value, "dp", [(i, (i + by) % planes) for i in range(planes)]).astype(F32)
+
         total = pieces[0].astype(F32)
-        for s in range(1, planes):
-            total += lax.ppermute(pieces[s], "dp", [(i, (i - s) % planes) for i in range(planes)]).astype(F32)
+        middle = planes // 2
+        for order, by in ((range(middle, 0, -1), -1), (range(middle + 1, planes), 1)):
+            running = None
+            for s in order:
+                running = pieces[s] if running is None else (shift(running, by) + pieces[s].astype(F32)).astype(BF16)
+            if running is not None:
+                total += shift(running, by)
         return total
 
     def reorder(array, dimension):
@@ -670,51 +694,19 @@
     normed_own = (residual_in * scale_attention * attention_gain).astype(BF16)
     normed = gather(reorder(normed_own, 1), "expert")
 
-    kv_pieces = plane_pieces(jnp.concatenate([key_matrix, value_matrix], axis=1))
-    wq_pieces = plane_pieces(query_weight)
-    out_piece = out_weight.shape[1]
-    out_columns = gather(after(out_weight, *kv_pieces[1:]), "dp").reshape(members, width, out_piece)
-
     expert_ids = jnp.arange(experts, dtype=jnp.int32)
     mask_own = jnp.sum((routes[:, :, None] == expert_ids[None, None, :]).astype(F32), axis=1)
     mask_wide = jnp.pad(mask_own, ((0, 0), (0, padded - experts))).astype(BF16)
-    router_rows = gather(after(router_weight.T, wq_pieces[1], wq_pieces[-1]), "expert").reshape(members, model)
-    upstream_own = jnp.concatenate(
-        [jnp.concatenate([cotangent, mask_wide], axis=1), jnp.pad(router_rows, ((0, 0), (0, padded)))], axis=0)
-    upstream_pieces = plane_pieces(after(upstream_own, *wq_pieces[1:]))
+    upstream_pieces = plane_pieces(jnp.concatenate([cotangent[:, :half], mask_wide], axis=1))
+    first_hop = (upstream_pieces[1], upstream_pieces[-1])
+    kv_pieces = plane_pieces(after(jnp.concatenate([key_matrix, value_matrix], axis=1), *first_hop))
+    wq_pieces = plane_pieces(after(query_weight, *first_hop))
+    out_piece = out_weight.shape[1]
+    out_pieces = plane_pieces(after(out_weight, *wq_pieces[1:]))
     cosine, sine = rotary_tables(span)
 
-    kv_own = jnp.concatenate(kv_pieces, axis=0)
-    place = member % group
-    kv_parts = [kv_own]
-    for shift in range(1, group):
-        pairs = [(e - e % group + (e % group + shift) % group, e) for e in range(members)]
-        kv_parts.append(lax.ppermute(kv_own, "expert", pairs))
-
-    def kv_piece(j):
-        value = kv_parts[0]
-        for shift in range(1, group):
-            value = jnp.where((place + shift) % group == j, kv_parts[shift], value)
-        return value
-
-    ordered = [kv_piece(j) for j in range(group)]
-    kv_weight = jnp.concatenate([p[:, :piece] for p in ordered] + [p[:, piece:] for p in ordered], axis=1)
-
-    kraw, key_low, value_low = project(
-        project_key_kernel, after(normed, cosine, sine, upstream_own), [kv_weight], cosine, sine, key_norm_gain,
-        [(HEAD_SIZE, F32), (HEAD_SIZE, BF16), (HEAD_SIZE, BF16)])
-    qraw, query_low = project(
-        project_query_kernel, normed, wq_pieces, cosine, sine, query_gain, [(width, F32), (width, BF16)])
-    attended_low, inverse = attend(prefix_len, after(query_low, out_columns), key_low, value_low)
-    attended_all = gather(attended_low, "expert").reshape(members, span, width)
-
-    out_rows = out_project(after(attended_all, *upstream_pieces), out_columns)
-    projected = exchange(out_rows, "expert").reshape(members, own_rows, out_piece)
-    projected = jnp.transpose(projected, (1, 0, 2)).reshape(own_rows, model)
-
-    upstream_pieces = after(upstream_pieces, out_rows)
     mask_plane = jnp.concatenate(
-        [lax.dynamic_slice(p, (0, model + plane * members), (own_rows, members)) for p in upstream_pieces], axis=0)
+        [lax.dynamic_slice(p, (0, half + plane * members), (own_rows, members)) for p in upstream_pieces], axis=0)
     triangle = (jnp.arange(column)[:, None] >= jnp.arange(column)[None, :]).astype(BF16)
     rank = jnp.where(mask_plane > 0, mm(triangle, mask_plane) - 1.0, -1.0).astype(jnp.int32)
     pick = (rank.T[:, None, :] == jnp.arange(slots, dtype=jnp.int32)[None, :, None])
@@ -722,9 +714,43 @@
     unpick = rank[:, :, None] == jnp.arange(slots, dtype=jnp.int32)[None, None, :]
     unpick = unpick.reshape(column, members * slots).astype(BF16)
     upstream_sent = dispatch(pick, upstream_pieces)
-    upstream_rows = exchange(upstream_sent, "expert")
+    upstream_a = exchange(upstream_sent, "expert")
+
+    kv_own = jnp.concatenate(kv_pieces, axis=0)
+    place = member % group
+    kv_parts = [kv_own]
+    for shift in range(1, group):
+        pairs = [(e - e % group + (e % group + shift) % group, e) for e in range(members)]
+        kv_parts.append(lax.ppermute(kv_own, "expert", pairs))
+
+    def kv_piece(j):
+        value = kv_parts[0]
+        for shift in range(1, group):
+            value = jnp.where((place + shift) % group == j, kv_parts[shift], value)
+        return value
+
+    ordered = [kv_piece(j) for j in range(group)]
+    kv_weight = jnp.concatenate([p[:, :piece] for p in ordered] + [p[:, piece:] for p in ordered], axis=1)
+
+    kraw, key_low, value_low = project(
+        project_key_kernel, after(normed, cosine, sine, upstream_sent), [kv_weight], cosine, sine, key_norm_gain,
+        [(HEAD_SIZE, F32), (HEAD_SIZE, BF16), (HEAD_SIZE, BF16)])
+    qraw, query_low = project(
+        project_query_kernel, normed, wq_pieces, cosine, sine, query_gain, [(width, F32), (width, BF16)])
+    attended_low, inverse = attend(prefix_len, after(query_low, upstream_a), key_low, value_low)
+    attended_all = gather(attended_low, "expert").reshape(members, span, width)
+
+    router_rows = gather(after(router_weight.T, attended_low), "expert").reshape(2 * members, half)
+    upstream_pieces = plane_pieces(after(jnp.concatenate([cotangent[:, half:], router_rows], axis=0), *out_pieces[1:]))
+
+    out_rows = out_project(plane.astype(jnp.int32).reshape(1), attended_all, out_pieces)
+    projected = exchange(out_rows, "expert").reshape(members, own_rows, out_piece)
+    projected = jnp.transpose(projected, (1, 0, 2)).reshape(own_rows, model)
+
+    upstream_sent = dispatch(after(pick, out_rows), upstream_pieces)
+    upstream_b = exchange(upstream_sent, "expert")
     pick = after(pick, upstream_sent)
-    router = jnp.concatenate([p[own_rows:, :model].reshape(experts, part_rows) for p in upstream_pieces], axis=1)
+    router = jnp.concatenate([p[own_rows:].reshape(experts, part_rows) for p in upstream_pieces], axis=1)
     router = jnp.pad(reorder(router, 1), ((0, padded - experts), (0, 0)))
 
     after_attn = residual_in + projected.astype(F32)
@@ -733,13 +759,14 @@
     arrived = []
     for columns in (slice(0, half), slice(half, model)):
         sent = dispatch(pick, plane_pieces(mixed_low[:, columns]))
-        arrived.append(exchange(after(sent, upstream_rows), "expert"))
-
-    out_heads = exchange(after(out_columns, arrived[1]), "expert")
-    upstream_down = down_back(upstream_rows, down)
+        arrived.append(exchange(after(sent, upstream_b), "expert"))
+
+    out_columns = reorder(jnp.concatenate(after(out_pieces, arrived[0]), axis=0), 0)
+    out_heads = exchange(after(out_columns, arrived[1]).reshape(members, width, out_piece), "expert")
+    upstream_down = down_back(upstream_a, upstream_b, down)
     own_expert = (plane * members + member).astype(jnp.int32).reshape(1)
     activated, gate_grad, up_grad, weight_wide, route_columns = expert_forward(
-        experts, own_expert, arrived[0], arrived[1], upstream_rows, router, gate, up, upstream_down)
+        experts, own_expert, arrived[0], arrived[1], upstream_a, router, gate, up, upstream_down)
     back_first = exchange(row_gradient(gate_grad, up_grad, gate, up, 0), "expert")
     back_second = exchange(row_gradient(gate_grad, up_grad, gate, up, 1, route_columns), "expert")
     produced = produce(activated, weight_wide, down)
@@ -783,18 +810,18 @@
     normed_partial = unproject(
         own_rows, dq, dk, dv, wq_pieces, kv_weight, normed, reorder(attention_gain, 0), router_part, mixture_part,
         query_terms, key_terms)
+    query_partial = t_mm(normed, dq).astype(BF16)
     mixture_parts = combine(unpick, after(mixture_rows, normed_partial), planes)
-    arrived_sums = exchange(after(normed_partial, out_share, *mixture_parts), "expert")
+    mixture_second = plane_sum(mixture_parts)
+    arrived_sums = exchange(after(normed_partial, out_share, query_partial, *mixture_parts), "expert")
     normed_sums = jnp.sum(arrived_sums.astype(F32), axis=0)
     input_back, _ = normalize_back(
         reorder(normed_sums[:own_rows], 1), residual_in, scale_attention, attention_gain)
     input_grad = after_grad + input_back
-    mixture_second = plane_sum(mixture_parts)
     layer_out = (after_attn + jnp.concatenate([mixture_first, mixture_second], axis=1)).astype(BF16)
 
-    query_partial = t_mm(normed, dq).astype(BF16)
     query_share = plane_sum(cut(after(query_partial, mixture_second)))
-    down_grad = down_gradient(upstream_rows, model, weight_wide, after(activated, query_partial))
+    down_grad = down_gradient(upstream_a, upstream_b, weight_wide, after(activated, query_partial))
     kv_partial = jnp.concatenate([t_mm(normed, dk), t_mm(normed, dv)], axis=1)
 
     def kv_cols(j):

time: 710 us -> 674 us (0.949)
  waiting for transfers between devices: 328 us -> 260 us
  local copies, waits for them, and re-layouts: 27.7 us -> 74 us
  Pallas kernels: 182 us -> 136 us
  starting transfers between devices: 90.5 us -> 114 us
    ppermute x18 -> x0, waiting for transfers between devices: 83.2 us -> none  [plane_sum(): lax.ppermute(pieces[s], 'dp', [(i, (i - s) % planes) for i in range(plane...]
    ppermute x15 -> x39, waiting for transfers between devices: 121 us -> 176 us  [shift(): lax.ppermute(value, 'dp', [(i, (i + by) % planes) for i in range(planes)])]
    unnamed x154 -> x259, local copies, waits for them, and re-layouts: 12.1 us -> 54.6 us
    ppermute x15 -> x39, starting transfers between devices: 21.3 us -> 63 us  [shift(): lax.ppermute(value, 'dp', [(i, (i + by) % planes) for i in range(planes)])]
    all_to_all x10 -> x11, waiting for transfers between devices: 87.6 us -> 57.9 us  [exchange(): return lax.all_to_all(array, axis, split_axis=0, concat_axis=0, tiled=True)]
    ppermute x18 -> x0, starting transfers between devices: 24.5 us -> none  [plane_sum(): lax.ppermute(pieces[s], 'dp', [(i, (i - s) % planes) for i in range(plane...]
    all_gather x4 -> x3, waiting for transfers between devices: 30.1 us -> 15.2 us  [gather(): return lax.all_gather(array, axis, axis=dimension, tiled=True)]
    all_to_all x10 -> x11, starting transfers between devices: 40.9 us -> 48.8 us  [exchange(): return lax.all_to_all(array, axis, split_axis=0, concat_axis=0, tiled=True)]
  transfers between devices with their start and end apart: 52 -> 58, of which waited for: 34 -> 37; matrix products, arithmetic and copies ran while one was open for 7% -> 9% of each run, Pallas kernels for 22% -> 19%
where the time goes in v3:
time: 674 us; the launch traced here: 663 us
  waiting for transfers between devices  260 us (39%)
  Pallas kernels  136 us (20%)
  starting transfers between devices  114 us (17%)
  local copies, waits for them, and re-layouts  74 us (11%)
  other arithmetic  41 us (6%)
  between operations  16.8 us (2%)
  matrix products  11.5 us (2%)
  blocking collectives  9.25 us (1%)
    ppermute x39, waiting for transfers between devices, shift(): lax.ppermute(value, 'dp', [(i, (i + by) % planes) for i in range(planes)])  176 us
    ppermute x39, starting transfers between devices, shift(): lax.ppermute(value, 'dp', [(i, (i + by) % planes) for i in range(planes)])  63 us
    all_to_all x11, waiting for transfers between devices, exchange(): return lax.all_to_all(array, axis, split_axis=0, concat_axis=0, tiled=True)  57.9 us
    unnamed x259, local copies, waits for them, and re-layouts  54.6 us
    all_to_all x11, starting transfers between devices, exchange(): return lax.all_to_all(array, axis, split_axis=0, concat_axis=0, tiled=True)  48.8 us
    pallas_call x1, Pallas kernels, expert_forward(): pl.pallas_call(functools.partial(expert_kernel, experts), grid=(hidden //...  16.9 us
    all_gather x3, waiting for transfers between devices, gather(): return lax.all_gather(array, axis, axis=dimension, tiled=True)  15.2 us
    pallas_call x4, Pallas kernels, combine(): pl.pallas_call(combine_kernel, grid=(width // tile,), in_specs=[pl.BlockS...  14.2 us
  transfers between devices with their start and end apart: 58, of which 37 were waited for; matrix products, arithmetic and copies ran while one was open for 9% of the time, Pallas kernels for 19%

profile of v3, /device:TPU:0, one launch (start us, length us, event | category | flops | bytes accessed | tf_op | source)
XLA Modules:
  0.0 663.3 jit_solution(12939297222482281678)
XLA Ops:
  17.5 7.3 %collective-permute-done.refs_1_ = bf16[128,1152]{1,0:T(8,128)(2,1)S(1)} collective-permute-done((bf16[128,1152]{1,0:T(8,128)(2,1)S(1)}, bf16[128,1152]{1,0:T(8,128)(2,1)S(1)}, u32[]{:S(2)}, u32[]{:S(2)}) %collective-permute-start) | collective-permute-done | bytes 294944 | tf_op jit(solution)/shard_map/ppermute | solution.py:660
  25.0 4.8 collective-permute-done.1.refs_3_
  31.7 6.2 collective-permute-done.5.refs_2_
  42.7 4.4 all-to-all-start
  47.9 3.8 collective-permute-start.8
  63.6 6.0 collective-permute-done.2.refs_1_
  72.0 8.6 %collective-permute-done.4.refs_3_ = bf16[512,512]{1,0:T(8,128)(2,1)S(1)} collective-permute-done((bf16[512,512]{1,0:T(8,128)(2,1)}, bf16[512,512]{1,0:T(8,128)(2,1)S(1)}, u32[]{:S(2)}, u32[]{:S(2)}) %collective-permute-start.4) | collective-permute-done | bytes 524320 | tf_op jit(solution)/shard_map/ppermute | solution.py:660
  81.5 9.9 %collective-permute-done.3.refs_2_ = bf16[512,512]{1,0:T(8,128)(2,1)S(1)} collective-permute-done((bf16[512,512]{1,0:T(8,128)(2,1)}, bf16[512,512]{1,0:T(8,128)(2,1)S(1)}, u32[]{:S(2)}, u32[]{:S(2)}) %collective-permute-start.3) | collective-permute-done | bytes 524320 | tf_op jit(solution)/shard_map/ppermute | solution.py:660
  96.4 6.4 project_query_kernel.1
  109.7 5.9 attend.1
  117.0 3.8 collective-permute-start.12
  120.8 12.8 %collective-permute-done.10.refs_1_ = bf16[1024,256]{1,0:T(8,128)(2,1)S(1)} collective-permute-done((bf16[1024,256]{1,0:T(8,128)(2,1)S(1)}, bf16[1024,256]{1,0:T(8,128)(2,1)S(1)}, u32[]{:S(2)}, u32[]{:S(2)}) %collective-permute-start.10) | collective-permute-done | bytes 524320 | tf_op jit(solution)/shard_map/ppermute | solution.py:660
  133.7 9.3 %all-gather = bf16[8,4,512]{2,1,0:T(4,128)(2,1)S(1)} all-gather(bf16[1,4,512]{2,1,0:T(4,128)(2,1)S(1)} %bitcast.111), channel_id=1, replica_groups=mesh['dp'=4,'expert'=8] {'expert'}, dimensions={0}, use_global_device_ids=true | all-gather | bytes 36864 | tf_op jit(solution)/shard_map/all_gather | solution.py:653
  144.8 9.9 %collective-permute-done.11.refs_2_ = bf16[1024,256]{1,0:T(8,128)(2,1)S(1)} collective-permute-done((bf16[1024,256]{1,0:T(8,128)(2,1)S(1)}, bf16[1024,256]{1,0:T(8,128)(2,1)S(1)}, u32[]{:S(2)}, u32[]{:S(2)}) %collective-permute-start.11) | collective-permute-done | bytes 524320 | tf_op jit(solution)/shard_map/ppermute | solution.py:660
  155.1 15.2 %all-gather.7.cloned.1.call-done = bf16[8192,512]{1,0:T(8,128)(2,1)} async-done(((bf16[1024,512]{1,0:T(8,128)(2,1)}), bf16[8192,512]{1,0:T(8,128)(2,1)}) %all-gather.7.cloned.1.call-update) | async-done | bytes 8388624 | tf_op jit(solution)/shard_map/all_gather | solution.py:653
  184.9 7.7 %collective-permute-done.15.refs_3_ = bf16[144,1024]{1,0:T(8,128)(2,1)S(1)} collective-permute-done((bf16[144,1024]{1,0:T(8,128)(2,1)}, bf16[144,1024]{1,0:T(8,128)(2,1)S(1)}, u32[]{:S(2)}, u32[]{:S(2)}) %collective-permute-start.15) | collective-permute-done | bytes 294944 | tf_op jit(solution)/shard_map/ppermute | solution.py:660
  192.6 6.6 collective-permute-done.14.refs_2_
  204.7 4.4 all-to-all-start.2
  215.7 7.1 %collective-permute-done.16.refs_1_ = bf16[128,1024]{1,0:T(8,128)(2,1)S(1)} collective-permute-done((bf16[128,1024]{1,0:T(8,128)(2,1)S(1)}, bf16[128,1024]{1,0:T(8,128)(2,1)S(1)}, u32[]{:S(2)}, u32[]{:S(2)}) %collective-permute-start.16) | collective-permute-done | bytes 262176 | tf_op jit(solution)/shard_map/ppermute | solution.py:660
  222.9 4.5 collective-permute-done.18.refs_3_
  227.3 6.2 collective-permute-done.17.refs_2_
  239.9 4.4 all-to-all-start.3
  248.2 7.1 %collective-permute-done.19.refs_1_ = bf16[128,1024]{1,0:T(8,128)(2,1)S(1)} collective-permute-done((bf16[128,1024]{1,0:T(8,128)(2,1)S(1)}, bf16[128,1024]{1,0:T(8,128)(2,1)S(1)}, u32[]{:S(2)}, u32[]{:S(2)}) %collective-permute-start.19) | collective-permute-done | bytes 262176 | tf_op jit(solution)/shard_map/ppermute | solution.py:660
  255.4 4.4 collective-permute-done.21.refs_3_
  259.8 6.2 collective-permute-done.20.refs_2_
  269.5 5.7 all-to-all-done.3
  275.2 4.7 all-to-all-start.4
  286.3 7.3 %down_back.1.down_ref = f32[1216,768]{1,0:T(8,128)S(1)} custom-call(bf16[1216,1152]{1,0:T(8,128)(2,1)} %bitcast.5.ca_ref.mask_ref, bf16[1216,1024]{1,0:T(8,128)(2,1)} %bitcast.15.cb_ref, bf16[768,2048]{1,0:T(8,128)(2,1)S(1)} %bitcast.77), custom_call_target="tpu_custom_call" | custom-call | flops 1 | bytes 1 | tf_op jit(solution)/shard_map/down_back/pallas_call | solution.py:466
  297.0 13.8 %all-to-all-done.4 = bf16[8,152,1024]{2,1,0:T(8,128)(2,1)} async-done(((bf16[8,152,1024]{2,1,0:T(8,128)(2,1)}), bf16[8,152,1024]{2,1,0:T(8,128)(2,1)}, u32[]{:S(2)}, u32[]{:S(2)}) %all-to-all-start.4) | async-done | bytes 2490400 | tf_op jit(solution)/shard_map/all_to_all | solution.py:656
  310.7 4.4 all-to-all-start.8
  316.1 16.9 %expert_forward.1 = (bf16[1216,768]{1,0:T(8,128)(2,1)S(1)}, bf16[1216,768]{1,0:T(8,128)(2,1)S(1)}, bf16[1216,768]{1,0:T(8,128)(2,1)S(1)}, f32[1216,128]{1,0:T(8,128)S(1)}, bf16[1216,128]{1,0:T(8,128)(2,1)S(1)}) custom-call(s32[1]{0:T(128)} %bitcast.11.own_ref, bf16[1216,1024]{1,0:T(8,128)(2,1)} %bitcast.17.xa_ref, bf16[1216,1024]{1,0:T(8,128)(2,1)} %bitcast.19.xb_ref, ...), custom_call_target="tpu_custom_call" | custom-call | flops 19800000512 | bytes 1 | tf_op jit(solution)/shard_map/expert_forward/pallas_call | solution.py:407
  335.2 4.7 row_gradient.3
  343.9 4.7 all-to-all-start.7
  357.5 4.7 produce.1
  366.9 4.7 row_gradient.2
  373.1 6.3 all-to-all-done.7
  379.4 4.5 all-to-all-start.5
  388.9 29.3 %all-to-all-done.5 = bf16[8,152,1152]{2,1,0:T(8,128)(2,1)} async-done(((bf16[8,152,1152]{2,1,0:T(8,128)(2,1)}), bf16[8,152,1152]{2,1,0:T(8,128)(2,1)}, u32[]{:S(2)}, u32[]{:S(2)}) %all-to-all-start.5) | async-done | bytes 2801696 | tf_op jit(solution)/shard_map/all_to_all | solution.py:656
  418.2 4.1 combine.4
  424.1 4.4 all-to-all-start.6
  431.4 3.6 collective-permute-start.26
  436.1 3.9 collective-permute-start.23
  441.1 5.7 collective-permute-done.26
  447.6 5.4 collective-permute-done.24
  453.1 4.9 collective-permute-done.23
  464.7 3.9 combine.6
  471.3 6.5 collective-permute-done.28
  478.5 3.6 collective-permute-start.29
  485.6 13.4 %hidden_gradient.1 = (f32[1,2048,768]{2,1,0:T(8,128)}, f32[1,2048,768]{2,1,0:T(8,128)}) custom-call(bf16[1216,1024]{1,0:T(8,128)(2,1)} %bitcast.17.xa_ref, bf16[1216,1024]{1,0:T(8,128)(2,1)} %bitcast.19.xb_ref, bf16[1216,768]{1,0:T(8,128)(2,1)S(1)} %copy-done.55, bf16[1216,768]{1,0:T(8,128)(2,1)S(1)} %copy-done.58), custom_call_target="tpu_custom_call" | custom-call | flops 1 | bytes 1 | tf_op jit(solution)/shard_map/hidden_gradient/pallas_call | solution.py:518
  506.5 5.4 out_gradient.1
  511.9 4.6 all-to-all-start.9
  518.9 4.6 out_back.1.do_ref
  523.7 13.9 %attend_back.1 = (bf16[1024,512]{1,0:T(8,128)(2,1)S(1)}, bf16[1024,128]{1,0:T(8,128)(2,1)S(1)}, bf16[1024,128]{1,0:T(8,128)(2,1)S(1)}, f32[1,128]{1,0:T(1,128)S(1)}, f32[1,128]{1,0:T(1,128)S(1)}) custom-call(s32[1]{0:T(128)S(6)} %copy.97.prefix_ref, bf16[1024,512]{1,0:T(8,128)(2,1)S(1)} %copy-done.25, bf16[1024,128]{1,0:T(8,128)(2,1)S(1)} %copy-done.60, ...), custom_call_target="tpu_custom_call" | custom-call | flops 1 | bytes 1 | tf_op jit(solution)/shard_map/attend_back/pallas_call | solution.py:205
  537.7 7.9 %unproject.1 = bf16[8,144,2048]{2,1,0:T(8,128)(2,1)} custom-call(bf16[1024,512]{1,0:T(8,128)(2,1)S(1)} %get-tuple-element.133.dq_ref, bf16[1024,128]{1,0:T(8,128)(2,1)S(1)} %get-tuple-element.134.dk_ref, bf16[1024,128]{1,0:T(8,128)(2,1)S(1)} %get-tuple-element.135.dv_ref, bf16[2048,256]{1,0:T(8,128)(2,1)S(1)} %copy-done.15, ...), custom_call_target="tpu_custom_call" | custom-call | flops 1 | bytes 1 | tf_op jit(solution)/shard_map/unproject/pallas_call | solution.py:261
  545.5 3.7 convolution_convert_fusion
  552.3 5.4 reduce-scatter.2.cloned.1.call-done
  559.8 4.9 all-to-all-start.10
  573.6 5.0 collective-permute-done.31
  578.7 4.3 collective-permute-start.32
  586.3 4.7 collective-permute-done.32
  596.9 14.6 %collective-permute-done.38 = bf16[512,128]{0,1:T(8,128)(2,1)S(1)} collective-permute-done((bf16[512,128]{0,1:T(8,128)(2,1)S(1)}, bf16[512,128]{0,1:T(8,128)(2,1)S(1)}, u32[]{:S(2)}, u32[]{:S(2)}) %collective-permute-start.38) | collective-permute-done | bytes 131104 | tf_op jit(solution)/shard_map/ppermute | solution.py:671
  615.2 3.6 collective-permute-start.35
  618.8 11.1 %down_gradient.1 = f32[1,768,2048]{2,1,0:T(8,128)} custom-call(bf16[1216,1152]{1,0:T(8,128)(2,1)} %bitcast.5.ca_ref.mask_ref, bf16[1216,1024]{1,0:T(8,128)(2,1)} %bitcast.15.cb_ref, f32[1216,128]{1,0:T(8,128)S(1)} %copy-done.33, bf16[1216,768]{1,0:T(8,128)(2,1)S(1)} %copy-done.22), custom_call_target="tpu_custom_call" | custom-call | flops 1 | bytes 1 | tf_op jit(solution)/shard_map/down_gradient/pallas_call | solution.py:544
  631.6 7.3 %collective-permute-done.35 = bf16[512,512]{1,0:T(8,128)(2,1)} collective-permute-done((bf16[512,512]{1,0:T(8,128)(2,1)}, bf16[512,512]{1,0:T(8,128)(2,1)}, u32[]{:S(2)}, u32[]{:S(2)}) %collective-permute-start.35) | collective-permute-done | bytes 524320 | tf_op jit(solution)/shard_map/ppermute | solution.py:671
  (452 shorter events, 201.6 us)
Async XLA Ops:
  7.2 85.0 %all-gather.5.cloned.1.call-start = ((), (), s32[]{:S(2)}) async-start(), calls=%async_computation.12 | async-start | bytes 4718592 | tf_op jit(solution)/shard_map/all_gather | solution.py:653
  11.8 13.0 %collective-permute-start = (bf16[128,1152]{1,0:T(8,128)(2,1)S(1)}, bf16[128,1152]{1,0:T(8,128)(2,1)S(1)}, u32[]{:S(2)}, u32[]{:S(2)}) collective-permute-start(bf16[128,1152]{1,0:T(8,128)(2,1)S(1)} %fusion.19.refs_0_), channel_id=1, source_target_pairs={{0,8},{8,16},{16,24},{24,0},{1,9},{9,17},{17,25},{25,1},{2,10},{10... | collective-permute-start | bytes 884744 | tf_op jit(solution)/shard_map/ppermute | solution.py:660
  14.9 15.0 %collective-permute-start.1 = (bf16[128,1152]{1,0:T(8,128)(2,1)S(1)}, bf16[128,1152]{1,0:T(8,128)(2,1)S(1)}, u32[]{:S(2)}, u32[]{:S(2)}) collective-permute-start(bf16[128,1152]{1,0:T(8,128)(2,1)S(1)} %fusion.19.refs_0_), channel_id=1, source_target_pairs={{0,24},{8,0},{16,8},{24,16},{1,25},{9,1},{17,9},{25,17},{2,26},{10... | collective-permute-start | bytes 884744 | tf_op jit(solution)/shard_map/ppermute | solution.py:660
  24.8 13.2 %collective-permute-start.5 = (bf16[128,1152]{1,0:T(8,128)(2,1)S(1)}, bf16[128,1152]{1,0:T(8,128)(2,1)S(1)}, u32[]{:S(2)}, u32[]{:S(2)}) collective-permute-start(bf16[128,1152]{1,0:T(8,128)(2,1)S(1)} %collective-permute-done.refs_1_), channel_id=1, source_target_pairs={{0,8},{8,16},{16,24},{24,0},{1,9},{9,17},{17,25},{25,1},{2,10},{10... | collective-permute-start | bytes 884744 | tf_op jit(solution)/shard_map/ppermute | solution.py:660
  30.0 17.2 %collective-permute-start.6 = (bf16[512,128]{1,0:T(8,128)(2,1)S(1)}, bf16[512,128]{1,0:T(8,128)(2,1)S(1)}, u32[]{:S(2)}, u32[]{:S(2)}) collective-permute-start(bf16[512,128]{1,0:T(8,128)(2,1)S(1)} %pad_maximum_fusion.7), channel_id=1, source_target_pairs={{0,8},{8,16},{16,24},{24,0},{1,9},{9,17},{17,25},{25,1},{2,10},{10... | collective-permute-start | bytes 393224 | tf_op jit(solution)/shard_map/ppermute | solution.py:660
  42.7 62.5 %all-to-all-start = ((bf16[8,152,1152]{2,1,0:T(8,128)(2,1)}), bf16[8,152,1152]{2,1,0:T(8,128)(2,1)}, u32[]{:S(2)}, u32[]{:S(2)}) async-start(bf16[8,152,1152]{2,1,0:T(8,128)(2,1)} %bitcast.79), calls=%async_computation | async-start | bytes 5603328 | tf_op jit(solution)/shard_map/all_to_all | solution.py:656
  47.1 123.2 %all-gather.7.cloned.1.call-start = ((), (), s32[]{:S(2)}) async-start(), calls=%async_computation.13 | async-start | bytes 9437184 | tf_op jit(solution)/shard_map/all_gather | solution.py:653
  47.2 8.2 %collective-permute-start.7 = (bf16[512,128]{1,0:T(8,128)(2,1)S(1)}, bf16[512,128]{1,0:T(8,128)(2,1)S(1)}, u32[]{:S(2)}, u32[]{:S(2)}) collective-permute-start(bf16[512,128]{1,0:T(8,128)(2,1)S(1)} %collective-permute-done.6), channel_id=1, source_target_pairs={{0,8},{8,16},{16,24},{24,0},{1,9},{9,17},{17,25},{25,1},{2,10},{10... | collective-permute-start | bytes 393224 | tf_op jit(solution)/shard_map/ppermute | solution.py:660
  47.9 8.5 %collective-permute-start.8 = (bf16[512,128]{1,0:T(8,128)(2,1)S(1)}, bf16[512,128]{1,0:T(8,128)(2,1)S(1)}, u32[]{:S(2)}, u32[]{:S(2)}) collective-permute-start(bf16[512,128]{1,0:T(8,128)(2,1)S(1)} %pad_maximum_fusion.7), channel_id=1, source_target_pairs={{0,24},{8,0},{16,8},{24,16},{1,25},{9,1},{17,9},{25,17},{2,26},{10... | collective-permute-start | bytes 393224 | tf_op jit(solution)/shard_map/ppermute | solution.py:660
  51.7 17.9 %collective-permute-start.2 = (bf16[512,512]{1,0:T(8,128)(2,1)}, bf16[512,512]{1,0:T(8,128)(2,1)}, u32[]{:S(2)}, u32[]{:S(2)}) collective-permute-start(bf16[512,512]{1,0:T(8,128)(2,1)} %refs_0_.2), channel_id=1, source_target_pairs={{0,8},{8,16},{16,24},{24,0},{1,9},{9,17},{17,25},{25,1},{2,10},{10... | collective-permute-start | bytes 1572872 | tf_op jit(solution)/shard_map/ppermute | solution.py:660
  57.1 12.5 %collective-permute-start.9 = (bf16[2048,128]{1,0:T(8,128)(2,1)}, bf16[2048,128]{1,0:T(8,128)(2,1)}, u32[]{:S(2)}, u32[]{:S(2)}) collective-permute-start(bf16[2048,128]{1,0:T(8,128)(2,1)} %constant_dynamic-update-slice_fusion), channel_id=1, source_target_pairs={{1,0},{0,1},{3,2},{2,3},{5,4},{4,5},{7,6},{6,7},{9,8},{8,9},{11,10... | collective-permute-start | bytes 1572872 | tf_op jit(solution)/shard_map/ppermute | solution.py:724
  60.1 45.1 %copy-start.16 = (f32[1024,128]{1,0:T(8,128)}, f32[1024,128]{1,0:T(8,128)S(1)}, u32[]{:S(2)}) copy-start(f32[1024,128]{1,0:T(8,128)S(1)} %get-tuple-element.212.cos_ref) | copy-start | bytes 1572868
  60.1 45.1 %copy-start.18 = (f32[1024,128]{1,0:T(8,128)}, f32[1024,128]{1,0:T(8,128)S(1)}, u32[]{:S(2)}) copy-start(f32[1024,128]{1,0:T(8,128)S(1)} %get-tuple-element.213.sin_ref) | copy-start | bytes 1572868
  60.1 20.6 %collective-permute-start.4 = (bf16[512,512]{1,0:T(8,128)(2,1)}, bf16[512,512]{1,0:T(8,128)(2,1)S(1)}, u32[]{:S(2)}, u32[]{:S(2)}) collective-permute-start(bf16[512,512]{1,0:T(8,128)(2,1)} %refs_0_.2), channel_id=1, source_target_pairs={{0,24},{8,0},{16,8},{24,16},{1,25},{9,1},{17,9},{25,17},{2,26},{10... | collective-permute-start | bytes 1572872 | tf_op jit(solution)/shard_map/ppermute | solution.py:660
  69.6 21.8 %collective-permute-start.3 = (bf16[512,512]{1,0:T(8,128)(2,1)}, bf16[512,512]{1,0:T(8,128)(2,1)S(1)}, u32[]{:S(2)}, u32[]{:S(2)}) collective-permute-start(bf16[512,512]{1,0:T(8,128)(2,1)} %collective-permute-done.2.refs_1_), channel_id=1, source_target_pairs={{0,8},{8,16},{16,24},{24,0},{1,9},{9,17},{17,25},{25,1},{2,10},{10... | collective-permute-start | bytes 1572872 | tf_op jit(solution)/shard_map/ppermute | solution.py:660
  72.0 33.2 %copy-start.14 = (bf16[2048,256]{1,0:T(8,128)(2,1)}, bf16[2048,256]{1,0:T(8,128)(2,1)S(1)}, u32[]{:S(2)}) copy-start(bf16[2048,256]{1,0:T(8,128)(2,1)S(1)} %pad_maximum_fusion.1.w_ref.wkv_ref) | copy-start | bytes 3145732
  117.0 16.7 %collective-permute-start.10 = (bf16[1024,256]{1,0:T(8,128)(2,1)S(1)}, bf16[1024,256]{1,0:T(8,128)(2,1)S(1)}, u32[]{:S(2)}, u32[]{:S(2)}) collective-permute-start(bf16[1024,256]{1,0:T(8,128)(2,1)S(1)} %copy-done.38), channel_id=1, source_target_pairs={{0,8},{8,16},{16,24},{24,0},{1,9},{9,17},{17,25},{25,1},{2,10},{10... | collective-permute-start | bytes 1572872 | tf_op jit(solution)/shard_map/ppermute | solution.py:660
  117.0 27.7 %collective-permute-start.12 = (bf16[1024,256]{1,0:T(8,128)(2,1)S(1)}, bf16[1024,256]{1,0:T(8,128)(2,1)S(1)}, u32[]{:S(2)}, u32[]{:S(2)}) collective-permute-start(bf16[1024,256]{1,0:T(8,128)(2,1)S(1)} %copy-done.38), channel_id=1, source_target_pairs={{0,24},{8,0},{16,8},{24,16},{1,25},{9,1},{17,9},{25,17},{2,26},{10... | collective-permute-start | bytes 1572872 | tf_op jit(solution)/shard_map/ppermute | solution.py:660
  133.7 43.5 %copy-start.42 = (bf16[1024,256]{1,0:T(8,128)(2,1)}, bf16[1024,256]{1,0:T(8,128)(2,1)S(1)}, u32[]{:S(2)}) copy-start(bf16[1024,256]{1,0:T(8,128)(2,1)S(1)} %collective-permute-done.10.refs_1_) | copy-start | bytes 1572868
  133.7 21.0 %collective-permute-start.11 = (bf16[1024,256]{1,0:T(8,128)(2,1)S(1)}, bf16[1024,256]{1,0:T(8,128)(2,1)S(1)}, u32[]{:S(2)}, u32[]{:S(2)}) collective-permute-start(bf16[1024,256]{1,0:T(8,128)(2,1)S(1)} %collective-permute-done.10.refs_1_), channel_id=1, source_target_pairs={{0,8},{8,16},{16,24},{24,0},{1,9},{9,17},{17,25},{25,1},{2,10},{10... | collective-permute-start | bytes 1572872 | tf_op jit(solution)/shard_map/ppermute | solution.py:660
  144.8 32.4 %copy-start.40 = (bf16[1024,256]{1,0:T(8,128)(2,1)}, bf16[1024,256]{1,0:T(8,128)(2,1)S(1)}, u32[]{:S(2)}) copy-start(bf16[1024,256]{1,0:T(8,128)(2,1)S(1)} %collective-permute-done.12.refs_3_) | copy-start | bytes 1572868
  154.7 30.2 %collective-permute-start.13 = (bf16[144,1024]{1,0:T(8,128)(2,1)}, bf16[144,1024]{1,0:T(8,128)(2,1)}, u32[]{:S(2)}, u32[]{:S(2)}) collective-permute-start(bf16[144,1024]{1,0:T(8,128)(2,1)} %pad_maximum_fusion.6.refs_0_), channel_id=1, source_target_pairs={{0,8},{8,16},{16,24},{24,0},{1,9},{9,17},{17,25},{25,1},{2,10},{10... | collective-permute-start | bytes 884744 | tf_op jit(solution)/shard_map/ppermute | solution.py:660
  178.0 25.9 %all-to-all-start.1 = ((bf16[8,128,256]{2,1,0:T(8,128)(2,1)}), bf16[8,128,256]{2,1,0:T(8,128)(2,1)S(1)}, u32[]{:S(2)}, u32[]{:S(2)}) async-start(bf16[8,128,256]{2,1,0:T(8,128)(2,1)} %bitcast.87), calls=%async_computation.1 | async-start | bytes 1048576 | tf_op jit(solution)/shard_map/all_to_all | solution.py:656
  181.5 11.1 %collective-permute-start.15 = (bf16[144,1024]{1,0:T(8,128)(2,1)}, bf16[144,1024]{1,0:T(8,128)(2,1)S(1)}, u32[]{:S(2)}, u32[]{:S(2)}) collective-permute-start(bf16[144,1024]{1,0:T(8,128)(2,1)} %pad_maximum_fusion.6.refs_0_), channel_id=1, source_target_pairs={{0,24},{8,0},{16,8},{24,16},{1,25},{9,1},{17,9},{25,17},{2,26},{10... | collective-permute-start | bytes 884744 | tf_op jit(solution)/shard_map/ppermute | solution.py:660
  184.9 14.3 %collective-permute-start.14 = (bf16[144,1024]{1,0:T(8,128)(2,1)}, bf16[144,1024]{1,0:T(8,128)(2,1)S(1)}, u32[]{:S(2)}, u32[]{:S(2)}) collective-permute-start(bf16[144,1024]{1,0:T(8,128)(2,1)} %collective-permute-done.13.refs_1_), channel_id=1, source_target_pairs={{0,8},{8,16},{16,24},{24,0},{1,9},{9,17},{17,25},{25,1},{2,10},{10... | collective-permute-start | bytes 884744 | tf_op jit(solution)/shard_map/ppermute | solution.py:660
  204.7 35.3 %all-to-all-start.2 = ((bf16[8,152,1024]{2,1,0:T(8,128)(2,1)}), bf16[8,152,1024]{2,1,0:T(8,128)(2,1)}, u32[]{:S(2)}, u32[]{:S(2)}) async-start(bf16[8,152,1024]{2,1,0:T(8,128)(2,1)} %bitcast.81), calls=%async_computation.2 | async-start | bytes 4980736 | tf_op jit(solution)/shard_map/all_to_all | solution.py:656
  211.8 11.0 %collective-permute-start.16 = (bf16[128,1024]{1,0:T(8,128)(2,1)S(1)}, bf16[128,1024]{1,0:T(8,128)(2,1)S(1)}, u32[]{:S(2)}, u32[]{:S(2)}) collective-permute-start(bf16[128,1024]{1,0:T(8,128)(2,1)S(1)} %get-tuple-element.177.refs_0_), channel_id=1, source_target_pairs={{0,8},{8,16},{16,24},{24,0},{1,9},{9,17},{17,25},{25,1},{2,10},{10... | collective-permute-start | bytes 786440 | tf_op jit(solution)/shard_map/ppermute | solution.py:660
  213.4 13.9 %collective-permute-start.18 = (bf16[128,1024]{1,0:T(8,128)(2,1)S(1)}, bf16[128,1024]{1,0:T(8,128)(2,1)S(1)}, u32[]{:S(2)}, u32[]{:S(2)}) collective-permute-start(bf16[128,1024]{1,0:T(8,128)(2,1)S(1)} %get-tuple-element.177.refs_0_), channel_id=1, source_target_pairs={{0,24},{8,0},{16,8},{24,16},{1,25},{9,1},{17,9},{25,17},{2,26},{10... | collective-permute-start | bytes 786440 | tf_op jit(solution)/shard_map/ppermute | solution.py:660
  222.9 10.7 %collective-permute-start.17 = (bf16[128,1024]{1,0:T(8,128)(2,1)S(1)}, bf16[128,1024]{1,0:T(8,128)(2,1)S(1)}, u32[]{:S(2)}, u32[]{:S(2)}) collective-permute-start(bf16[128,1024]{1,0:T(8,128)(2,1)S(1)} %collective-permute-done.16.refs_1_), channel_id=1, source_target_pairs={{0,8},{8,16},{16,24},{24,0},{1,9},{9,17},{17,25},{25,1},{2,10},{10... | collective-permute-start | bytes 786440 | tf_op jit(solution)/shard_map/ppermute | solution.py:660
  239.9 35.3 %all-to-all-start.3 = ((bf16[8,152,1024]{2,1,0:T(8,128)(2,1)}), bf16[8,152,1024]{2,1,0:T(8,128)(2,1)}, u32[]{:S(2)}, u32[]{:S(2)}) async-start(bf16[8,152,1024]{2,1,0:T(8,128)(2,1)} %bitcast.82), calls=%async_computation.3 | async-start | bytes 4980736 | tf_op jit(solution)/shard_map/all_to_all | solution.py:656
  244.3 11.0 %collective-permute-start.19 = (bf16[128,1024]{1,0:T(8,128)(2,1)S(1)}, bf16[128,1024]{1,0:T(8,128)(2,1)S(1)}, u32[]{:S(2)}, u32[]{:S(2)}) collective-permute-start(bf16[128,1024]{1,0:T(8,128)(2,1)S(1)} %get-tuple-element.176.refs_0_), channel_id=1, source_target_pairs={{0,8},{8,16},{16,24},{24,0},{1,9},{9,17},{17,25},{25,1},{2,10},{10... | collective-permute-start | bytes 786440 | tf_op jit(solution)/shard_map/ppermute | solution.py:660
  245.9 13.9 %collective-permute-start.21 = (bf16[128,1024]{1,0:T(8,128)(2,1)S(1)}, bf16[128,1024]{1,0:T(8,128)(2,1)S(1)}, u32[]{:S(2)}, u32[]{:S(2)}) collective-permute-start(bf16[128,1024]{1,0:T(8,128)(2,1)S(1)} %get-tuple-element.176.refs_0_), channel_id=1, source_target_pairs={{0,24},{8,0},{16,8},{24,16},{1,25},{9,1},{17,9},{25,17},{2,26},{10... | collective-permute-start | bytes 786440 | tf_op jit(solution)/shard_map/ppermute | solution.py:660
  255.4 10.6 %collective-permute-start.20 = (bf16[128,1024]{1,0:T(8,128)(2,1)S(1)}, bf16[128,1024]{1,0:T(8,128)(2,1)S(1)}, u32[]{:S(2)}, u32[]{:S(2)}) collective-permute-start(bf16[128,1024]{1,0:T(8,128)(2,1)S(1)} %collective-permute-done.19.refs_1_), channel_id=1, source_target_pairs={{0,8},{8,16},{16,24},{24,0},{1,9},{9,17},{17,25},{25,1},{2,10},{10... | collective-permute-start | bytes 786440 | tf_op jit(solution)/shard_map/ppermute | solution.py:660
  275.2 35.5 %all-to-all-start.4 = ((bf16[8,152,1024]{2,1,0:T(8,128)(2,1)}), bf16[8,152,1024]{2,1,0:T(8,128)(2,1)}, u32[]{:S(2)}, u32[]{:S(2)}) async-start(bf16[8,152,1024]{2,1,0:T(8,128)(2,1)} %bitcast.80), calls=%async_computation.4 | async-start | bytes 4980736 | tf_op jit(solution)/shard_map/all_to_all | solution.py:656
  310.7 33.1 %all-to-all-start.8 = ((bf16[8,512,256]{2,1,0:T(8,128)(2,1)}), bf16[8,512,256]{2,1,0:T(8,128)(2,1)}, u32[]{:S(2)}, u32[]{:S(2)}) async-start(bf16[8,512,256]{2,1,0:T(8,128)(2,1)} %bitcast.101), calls=%async_computation.8 | async-start | bytes 4194304 | tf_op jit(solution)/shard_map/all_to_all | solution.py:656
  343.9 35.6 %all-to-all-start.7 = ((bf16[8,152,1024]{2,1,0:T(8,128)(2,1)}), bf16[8,152,1024]{2,1,0:T(8,128)(2,1)}, u32[]{:S(2)}, u32[]{:S(2)}) async-start(bf16[8,152,1024]{2,1,0:T(8,128)(2,1)} %bitcast.86), calls=%async_computation.7 | async-start | bytes 4980736 | tf_op jit(solution)/shard_map/all_to_all | solution.py:656
  379.4 38.8 %all-to-all-start.5 = ((bf16[8,152,1152]{2,1,0:T(8,128)(2,1)}), bf16[8,152,1152]{2,1,0:T(8,128)(2,1)}, u32[]{:S(2)}, u32[]{:S(2)}) async-start(bf16[8,152,1152]{2,1,0:T(8,128)(2,1)} %bitcast.83), calls=%async_computation.5 | async-start | bytes 5603328 | tf_op jit(solution)/shard_map/all_to_all | solution.py:656
  387.1 43.3 %collective-permute-start.25 = (bf16[128,1024]{1,0:T(8,128)(2,1)S(1)}, bf16[128,1024]{1,0:T(8,128)(2,1)}, u32[]{:S(2)}, u32[]{:S(2)}) collective-permute-start(bf16[128,1024]{1,0:T(8,128)(2,1)S(1)} %get-tuple-element.115), channel_id=1, source_target_pairs={{0,24},{8,0},{16,8},{24,16},{1,25},{9,1},{17,9},{25,17},{2,26},{10... | collective-permute-start | bytes 786440 | tf_op jit(solution)/shard_map/ppermute | solution.py:671
  422.3 12.7 %collective-permute-start.22 = (bf16[128,1152]{1,0:T(8,128)(2,1)S(1)}, bf16[128,1152]{1,0:T(8,128)(2,1)}, u32[]{:S(2)}, u32[]{:S(2)}) collective-permute-start(bf16[128,1152]{1,0:T(8,128)(2,1)S(1)} %get-tuple-element.104), channel_id=1, source_target_pairs={{0,24},{8,0},{16,8},{24,16},{1,25},{9,1},{17,9},{25,17},{2,26},{10... | collective-permute-start | bytes 884744 | tf_op jit(solution)/shard_map/ppermute | solution.py:671
  424.1 35.8 %all-to-all-start.6 = ((bf16[8,152,1024]{2,1,0:T(8,128)(2,1)}), bf16[8,152,1024]{2,1,0:T(8,128)(2,1)}, u32[]{:S(2)}, u32[]{:S(2)}) async-start(bf16[8,152,1024]{2,1,0:T(8,128)(2,1)} %bitcast.85), calls=%async_computation.6 | async-start | bytes 4980736 | tf_op jit(solution)/shard_map/all_to_all | solution.py:656
  428.5 72.4 %all-gather.9.cloned.1.call-start = ((), (), s32[]{:S(2)}) async-start(), calls=%async_computation.14 | async-start | bytes 4718592 | tf_op jit(solution)/shard_map/all_gather | solution.py:653
  430.1 11.0 %collective-permute-start.27 = (bf16[128,1024]{1,0:T(8,128)(2,1)S(1)}, bf16[128,1024]{1,0:T(8,128)(2,1)S(1)}, u32[]{:S(2)}, u32[]{:S(2)}) collective-permute-start(bf16[128,1024]{1,0:T(8,128)(2,1)S(1)} %get-tuple-element.117), channel_id=1, source_target_pairs={{0,8},{8,16},{16,24},{24,0},{1,9},{9,17},{17,25},{25,1},{2,10},{10... | collective-permute-start | bytes 786440 | tf_op jit(solution)/shard_map/ppermute | solution.py:671
  431.4 15.3 %collective-permute-start.26 = (bf16[128,1024]{1,0:T(8,128)(2,1)S(1)}, bf16[128,1024]{1,0:T(8,128)(2,1)S(1)}, u32[]{:S(2)}, u32[]{:S(2)}) collective-permute-start(bf16[128,1024]{1,0:T(8,128)(2,1)S(1)} %add_convert_fusion.4), channel_id=1, source_target_pairs={{0,24},{8,0},{16,8},{24,16},{1,25},{9,1},{17,9},{25,17},{2,26},{10... | collective-permute-start | bytes 786440 | tf_op jit(solution)/shard_map/ppermute | solution.py:671
  435.0 18.1 %collective-permute-start.24 = (bf16[128,1152]{1,0:T(8,128)(2,1)S(1)}, bf16[128,1152]{1,0:T(8,128)(2,1)S(1)}, u32[]{:S(2)}, u32[]{:S(2)}) collective-permute-start(bf16[128,1152]{1,0:T(8,128)(2,1)S(1)} %get-tuple-element.106), channel_id=1, source_target_pairs={{0,8},{8,16},{16,24},{24,0},{1,9},{9,17},{17,25},{25,1},{2,10},{10... | collective-permute-start | bytes 884744 | tf_op jit(solution)/shard_map/ppermute | solution.py:671
  436.1 21.9 %collective-permute-start.23 = (bf16[128,1152]{1,0:T(8,128)(2,1)S(1)}, bf16[128,1152]{1,0:T(8,128)(2,1)S(1)}, u32[]{:S(2)}, u32[]{:S(2)}) collective-permute-start(bf16[128,1152]{1,0:T(8,128)(2,1)S(1)} %add_convert_fusion.1), channel_id=1, source_target_pairs={{0,24},{8,0},{16,8},{24,16},{1,25},{9,1},{17,9},{25,17},{2,26},{10... | collective-permute-start | bytes 884744 | tf_op jit(solution)/shard_map/ppermute | solution.py:671
  464.6 93.0 %reduce-scatter.2.cloned.1.call-start = ((), (), s32[]{:S(2)}) async-start(), calls=%async_computation.15 | async-start | bytes 2621440 | tf_op jit(solution)/shard_map/reduce_scatter | solution.py:804
  469.3 8.5 %collective-permute-start.28 = (bf16[128,1024]{1,0:T(8,128)(2,1)S(1)}, bf16[128,1024]{1,0:T(8,128)(2,1)S(1)}, u32[]{:S(2)}, u32[]{:S(2)}) collective-permute-start(bf16[128,1024]{1,0:T(8,128)(2,1)S(1)} %get-tuple-element.121), channel_id=1, source_target_pairs={{0,24},{8,0},{16,8},{24,16},{1,25},{9,1},{17,9},{25,17},{2,26},{10... | collective-permute-start | bytes 786440 | tf_op jit(solution)/shard_map/ppermute | solution.py:671
  470.3 28.7 %collective-permute-start.30 = (bf16[128,1024]{1,0:T(8,128)(2,1)}, bf16[128,1024]{1,0:T(8,128)(2,1)}, u32[]{:S(2)}, u32[]{:S(2)}) collective-permute-start(bf16[128,1024]{1,0:T(8,128)(2,1)} %get-tuple-element.123), channel_id=1, source_target_pairs={{0,8},{8,16},{16,24},{24,0},{1,9},{9,17},{17,25},{25,1},{2,10},{10... | collective-permute-start | bytes 786440 | tf_op jit(solution)/shard_map/ppermute | solution.py:671
  478.5 20.5 %collective-permute-start.29 = (bf16[128,1024]{1,0:T(8,128)(2,1)}, bf16[128,1024]{1,0:T(8,128)(2,1)}, u32[]{:S(2)}, u32[]{:S(2)}) collective-permute-start(bf16[128,1024]{1,0:T(8,128)(2,1)} %add_convert_fusion.3), channel_id=1, source_target_pairs={{0,24},{8,0},{16,8},{24,16},{1,25},{9,1},{17,9},{25,17},{2,26},{10... | collective-permute-start | bytes 786440 | tf_op jit(solution)/shard_map/ppermute | solution.py:671
  511.9 37.3 %all-to-all-start.9 = ((bf16[8,152,1024]{2,1,0:T(8,128)(2,1)}), bf16[8,152,1024]{2,1,0:T(8,128)(2,1)}, u32[]{:S(2)}, u32[]{:S(2)}) async-start(bf16[8,152,1024]{2,1,0:T(8,128)(2,1)} %bitcast.84), calls=%async_computation.9 | async-start | bytes 4980736 | tf_op jit(solution)/shard_map/all_to_all | solution.py:656
  559.8 81.7 %all-to-all-start.10 = ((bf16[8,144,2048]{2,1,0:T(8,128)(2,1)}), bf16[8,144,2048]{2,1,0:T(8,128)(2,1)}, u32[]{:S(2)}, u32[]{:S(2)}) async-start(bf16[8,144,2048]{2,1,0:T(8,128)(2,1)} %unproject.1), calls=%async_computation.11 | async-start | bytes 9437184 | tf_op jit(solution)/shard_map/all_to_all | solution.py:656
  569.9 13.1 %collective-permute-start.37 = (bf16[2048,128]{0,1:T(8,128)(2,1)S(1)}, bf16[2048,128]{0,1:T(8,128)(2,1)}, u32[]{:S(2)}, u32[]{:S(2)}) collective-permute-start(bf16[2048,128]{0,1:T(8,128)(2,1)S(1)} %pad_maximum_fusion.5), channel_id=1, source_target_pairs={{0,1},{1,0},{2,3},{3,2},{4,5},{5,4},{6,7},{7,6},{8,9},{9,8},{10,11... | collective-permute-start | bytes 1572872 | tf_op jit(solution)/shard_map/ppermute | solution.py:836
  570.3 8.3 %collective-permute-start.31 = (bf16[128,1024]{1,0:T(8,128)(2,1)S(1)}, bf16[128,1024]{1,0:T(8,128)(2,1)S(1)}, u32[]{:S(2)}, u32[]{:S(2)}) collective-permute-start(bf16[128,1024]{1,0:T(8,128)(2,1)S(1)} %get-tuple-element.140), channel_id=1, source_target_pairs={{0,24},{8,0},{16,8},{24,16},{1,25},{9,1},{17,9},{25,17},{2,26},{10... | collective-permute-start | bytes 786440 | tf_op jit(solution)/shard_map/ppermute | solution.py:671
  573.1 13.3 %collective-permute-start.33 = (bf16[128,1024]{1,0:T(8,128)(2,1)S(1)}, bf16[128,1024]{1,0:T(8,128)(2,1)S(1)}, u32[]{:S(2)}, u32[]{:S(2)}) collective-permute-start(bf16[128,1024]{1,0:T(8,128)(2,1)S(1)} %get-tuple-element.142), channel_id=1, source_target_pairs={{0,8},{8,16},{16,24},{24,0},{1,9},{9,17},{17,25},{25,1},{2,10},{10... | collective-permute-start | bytes 786440 | tf_op jit(solution)/shard_map/ppermute | solution.py:671
  578.7 12.3 %collective-permute-start.32 = (bf16[128,1024]{1,0:T(8,128)(2,1)S(1)}, bf16[128,1024]{1,0:T(8,128)(2,1)S(1)}, u32[]{:S(2)}, u32[]{:S(2)}) collective-permute-start(bf16[128,1024]{1,0:T(8,128)(2,1)S(1)} %add_convert_fusion.2), channel_id=1, source_target_pairs={{0,24},{8,0},{16,8},{24,16},{1,25},{9,1},{17,9},{25,17},{2,26},{10... | collective-permute-start | bytes 786440 | tf_op jit(solution)/shard_map/ppermute | solution.py:671
  591.1 27.6 %copy-start.22 = (bf16[1216,768]{1,0:T(8,128)(2,1)S(1)}, bf16[1216,768]{1,0:T(8,128)(2,1)}, u32[]{:S(2)}) copy-start(bf16[1216,768]{1,0:T(8,128)(2,1)} %copy-done.20) | copy-start | bytes 5603332
  592.0 22.2 %collective-permute-start.34 = (bf16[512,512]{1,0:T(8,128)(2,1)S(1)}, bf16[512,512]{1,0:T(8,128)(2,1)S(1)}, u32[]{:S(2)}, u32[]{:S(2)}) collective-permute-start(bf16[512,512]{1,0:T(8,128)(2,1)S(1)} %get-tuple-element.156), channel_id=1, source_target_pairs={{0,24},{8,0},{16,8},{24,16},{1,25},{9,1},{17,9},{25,17},{2,26},{10... | collective-permute-start | bytes 1572872 | tf_op jit(solution)/shard_map/ppermute | solution.py:671
  594.8 16.7 %collective-permute-start.38 = (bf16[512,128]{0,1:T(8,128)(2,1)S(1)}, bf16[512,128]{0,1:T(8,128)(2,1)S(1)}, u32[]{:S(2)}, u32[]{:S(2)}) collective-permute-start(bf16[512,128]{0,1:T(8,128)(2,1)S(1)} %get-tuple-element.174), channel_id=1, source_target_pairs={{0,24},{8,0},{16,8},{24,16},{1,25},{9,1},{17,9},{25,17},{2,26},{10... | collective-permute-start | bytes 393224 | tf_op jit(solution)/shard_map/ppermute | solution.py:671
  594.9 35.0 %collective-permute-start.40 = (bf16[512,128]{0,1:T(8,128)(2,1)}, bf16[512,128]{0,1:T(8,128)(2,1)}, u32[]{:S(2)}, u32[]{:S(2)}) collective-permute-start(bf16[512,128]{0,1:T(8,128)(2,1)} %get-tuple-element.175), channel_id=1, source_target_pairs={{0,8},{8,16},{16,24},{24,0},{1,9},{9,17},{17,25},{25,1},{2,10},{10... | collective-permute-start | bytes 393224 | tf_op jit(solution)/shard_map/ppermute | solution.py:671
  612.2 17.7 %collective-permute-start.39 = (bf16[512,128]{0,1:T(8,128)(2,1)}, bf16[512,128]{0,1:T(8,128)(2,1)}, u32[]{:S(2)}, u32[]{:S(2)}) collective-permute-start(bf16[512,128]{0,1:T(8,128)(2,1)} %add_convert_fusion.5), channel_id=1, source_target_pairs={{0,24},{8,0},{16,8},{24,16},{1,25},{9,1},{17,9},{25,17},{2,26},{10... | collective-permute-start | bytes 393224 | tf_op jit(solution)/shard_map/ppermute | solution.py:671
  614.0 17.6 %collective-permute-start.36 = (bf16[512,512]{1,0:T(8,128)(2,1)}, bf16[512,512]{1,0:T(8,128)(2,1)}, u32[]{:S(2)}, u32[]{:S(2)}) collective-permute-start(bf16[512,512]{1,0:T(8,128)(2,1)} %get-tuple-element.157), channel_id=1, source_target_pairs={{0,8},{8,16},{16,24},{24,0},{1,9},{9,17},{17,25},{25,1},{2,10},{10... | collective-permute-start | bytes 1572872 | tf_op jit(solution)/shard_map/ppermute | solution.py:671
  615.2 23.8 %collective-permute-start.35 = (bf16[512,512]{1,0:T(8,128)(2,1)}, bf16[512,512]{1,0:T(8,128)(2,1)}, u32[]{:S(2)}, u32[]{:S(2)}) collective-permute-start(bf16[512,512]{1,0:T(8,128)(2,1)} %add_convert_fusion), channel_id=1, source_target_pairs={{0,24},{8,0},{16,8},{24,16},{1,25},{9,1},{17,9},{25,17},{2,26},{10... | collective-permute-start | bytes 1572872 | tf_op jit(solution)/shard_map/ppermute | solution.py:671
  645.2 4.2 collective-permute-start.41
  649.4 5.1 collective-permute-start.42
  (115 other events, 797.0 us)
Sparse Core Ops, SparseCore 0:
  10.9 39.4 all-gather.4
  117.1 53.2 all-gather.6
  464.8 35.8 all-gather.8
  512.0 45.6 reduce-scatter.1

commit v4 on v3

--- a/solution.py
+++ b/solution.py
@@ -73,37 +73,39 @@
     return total
 
 
-def project_query_kernel(x_ref, cos_ref, sin_ref, gain_ref, *refs):
-    raw_ref, low_ref = refs[-2:]
-    q = pieces_product(x_ref[...], refs[:-2])
-    raw_ref[...] = q
-    for h in range(q.shape[1] // HEAD_SIZE):
+def project_kernel(x_ref, cos_ref, sin_ref, qg_ref, kg_ref, *refs):
+    weights, (qraw_ref, kraw_ref, q_ref, k_ref, v_ref) = refs[:-5], refs[-5:]
+    total = pieces_product(x_ref[...], weights)
+    width = q_ref.shape[1]
+    cosine, sine = cos_ref[...], sin_ref[...]
+    qraw_ref[...] = total[:, :width]
+    for h in range(width // HEAD_SIZE):
         cols = slice(h * HEAD_SIZE, (h + 1) * HEAD_SIZE)
-        low_ref[:, cols] = turned(q[:, cols], gain_ref[...], cos_ref[...], sin_ref[...])
-
-
-def project_key_kernel(x_ref, cos_ref, sin_ref, gain_ref, w_ref, raw_ref, k_ref, v_ref):
-    kv = mm(x_ref[...], w_ref[...])
-    raw_ref[...] = kv[:, :HEAD_SIZE]
-    v_ref[...] = kv[:, HEAD_SIZE:].astype(BF16)
-    k_ref[...] = turned(kv[:, :HEAD_SIZE], gain_ref[...], cos_ref[...], sin_ref[...])
-
-
-def project(kernel, x, weights, cosine, sine, gain, out):
+        q_ref[:, cols] = turned(total[:, cols], qg_ref[...], cosine, sine)
+    key = total[:, width:width + HEAD_SIZE]
+    kraw_ref[...] = key
+    k_ref[...] = turned(key, kg_ref[...], cosine, sine)
+    v_ref[...] = total[:, width + HEAD_SIZE:].astype(BF16)
+
+
+def project(x, weights, cosine, sine, q_gain, k_gain):
     span, model = x.shape
+    width = weights[0].shape[1] - 2 * HEAD_SIZE
     tile = 512
     row = lambda w: pl.BlockSpec((tile, w), lambda i: (i, 0))
     whole = lambda a, b: pl.BlockSpec((a, b), lambda i: (0, 0))
-    return pl.pallas_call(
-        kernel,
+    out = [(width, F32), (HEAD_SIZE, F32), (width, BF16), (HEAD_SIZE, BF16), (HEAD_SIZE, BF16)]
+    return pl.pallas_call(
+        project_kernel,
         grid=(span // tile,),
-        in_specs=[row(model), row(HEAD_SIZE), row(HEAD_SIZE), whole(1, HEAD_SIZE)] + [whole(*w.shape) for w in weights],
+        in_specs=[row(model), row(HEAD_SIZE), row(HEAD_SIZE), whole(1, HEAD_SIZE), whole(1, HEAD_SIZE)]
+        + [whole(*w.shape) for w in weights],
         out_specs=[row(w) for w, _ in out],
         out_shape=[jax.ShapeDtypeStruct((span, w), t) for w, t in out],
         compiler_params=pltpu.CompilerParams(vmem_limit_bytes=VMEM_BYTES),
         cost_estimate=cost(0),
-        name=kernel.__name__,
-    )(x, cosine, sine, gain[None], *weights)
+        name="project",
+    )(x, cosine, sine, q_gain[None], k_gain[None], *weights)
 
 
 def block_limits(span, tile):
@@ -222,7 +224,7 @@
     )(prefix, q, k, v, o, inverse, do, qraw, kraw, cosine, sine, q_gain[None], k_gain[None])
 
 
-def unproject_kernel(own_rows, dq_ref, dk_ref, dv_ref, wkv_ref, x_ref, gain_ref, router_ref, mix_ref, qg_ref, kg_ref,
+def unproject_kernel(own_rows, dq_ref, dk_ref, dv_ref, x_ref, gain_ref, router_ref, mix_ref, qg_ref, kg_ref,
                      *refs):
     weights, out_ref, sum_ref = refs[:-2], refs[-2], refs[-1]
     span, model = x_ref.shape
@@ -231,11 +233,10 @@
     each = tile // own_rows
     for r in range(span // tile):
         rows = slice(r * tile, (r + 1) * tile)
-        dq, dk, dv = dq_ref[rows, :], dk_ref[rows, :], dv_ref[rows, :]
+        grads = jnp.concatenate([dq_ref[rows, :], dk_ref[rows, :], dv_ref[rows, :]], axis=1)
         for s, weight in enumerate(weights):
             cols = slice(s * size, (s + 1) * size)
-            total = mm_t(dq, weight[...])
-            total += mm_t(dk, wkv_ref[cols, :HEAD_SIZE]) + mm_t(dv, wkv_ref[cols, HEAD_SIZE:])
+            total = mm_t(grads, weight[...])
             low = total.astype(BF16)
             for m in range(each):
                 out_ref[r * each + m, :own_rows, cols] = low[m * own_rows:(m + 1) * own_rows]
@@ -256,7 +257,7 @@
         out_ref[m, own_rows + 8:, :] = sums
 
 
-def unproject(own_rows, dq, dk, dv, pieces, wkv, x, gain, router_part, mixture_part, query_part, key_part):
+def unproject(own_rows, dq, dk, dv, pieces, x, gain, router_part, mixture_part, query_part, key_part):
     span, model = x.shape
     return pl.pallas_call(
         functools.partial(unproject_kernel, own_rows),
@@ -265,7 +266,7 @@
         compiler_params=pltpu.CompilerParams(vmem_limit_bytes=44 * 1024 * 1024),
         cost_estimate=cost(0),
         name="unproject",
-    )(dq, dk, dv, wkv, x, gain[None], router_part, mixture_part, query_part, key_part, *pieces)
+    )(dq, dk, dv, x, gain[None], router_part, mixture_part, query_part, key_part, *pieces)
 
 
 def out_project_kernel(plane_ref, a_ref, *refs):
@@ -425,24 +426,24 @@
     )(own, xa, xb, masked_rows, router, gate, up, upstream_down)
 
 
-def row_gradient_kernel(gg_ref, ug_ref, gate_ref, up_ref, *rest):
-    total = (mm_t(gg_ref[...], gate_ref[...]) + mm_t(ug_ref[...], up_ref[...])).astype(BF16)
+def row_gradient_kernel(start, stop, gg_ref, ug_ref, gate_ref, up_ref, *rest):
+    part = slice(start, stop)
+    total = (mm_t(gg_ref[...], gate_ref[part, :]) + mm_t(ug_ref[...], up_ref[part, :])).astype(BF16)
     out_ref = rest[-1]
     out_ref[:, :total.shape[1]] = total
     if len(rest) == 2:
         out_ref[:, total.shape[1]:] = rest[0][...]
 
 
-def row_gradient(gg, ug, gate, up, part, route=None):
+def row_gradient(gg, ug, gate, up, start, stop, route=None):
     rows, hidden = gg.shape
-    half = gate.shape[0] // 2
     tile = rows // 4
     row = lambda w: pl.BlockSpec((tile, w), lambda i: (i, 0))
-    weight = pl.BlockSpec((half, hidden), lambda i: (part, 0))
+    weight = pl.BlockSpec(gate.shape, lambda i: (0, 0))
     extra = [] if route is None else [route]
-    width = half + sum(e.shape[1] for e in extra)
-    return pl.pallas_call(
-        row_gradient_kernel,
+    width = stop - start + sum(e.shape[1] for e in extra)
+    return pl.pallas_call(
+        functools.partial(row_gradient_kernel, start, stop),
         grid=(rows // tile,),
         in_specs=[row(hidden), row(hidden), weight, weight] + [row(e.shape[1]) for e in extra],
         out_specs=row(width),
@@ -477,12 +478,12 @@
 
 def produce_kernel(act_ref, w_ref, down_ref, *outs):
     total = (w_ref[:, :1] * mm(act_ref[...], down_ref[...])).astype(BF16)
-    half = total.shape[1] // 2
-    outs[0][...] = total[:, :half]
-    outs[1][...] = total[:, half:]
-
-
-def produce(activated, weight, down):
+    first = outs[0].shape[1]
+    outs[0][...] = total[:, :first]
+    outs[1][...] = total[:, first:]
+
+
+def produce(activated, weight, down, first):
     rows, hidden = activated.shape
     model = down.shape[1]
     tile = rows // 4
@@ -491,8 +492,8 @@
         produce_kernel,
         grid=(rows // tile,),
         in_specs=[row(hidden), row(HEAD_SIZE), pl.BlockSpec((hidden, model), lambda i: (0, 0))],
-        out_specs=[row(model // 2)] * 2,
-        out_shape=[jax.ShapeDtypeStruct((rows, model // 2), BF16)] * 2,
+        out_specs=[row(first), row(model - first)],
+        out_shape=[jax.ShapeDtypeStruct((rows, w), BF16) for w in (first, model - first)],
         compiler_params=pltpu.CompilerParams(vmem_limit_bytes=VMEM_BYTES),
         cost_estimate=cost(0),
         name="produce",
@@ -646,6 +647,8 @@
     slots = planes * block_slots
     padded = -(-experts // HEAD_SIZE) * HEAD_SIZE
     half = model // 2
+    first = 5 * model // 8
+    rest = model - first
     part_rows = model // planes
     gate, up, down = expert_gate[0], expert_up[0], expert_down[0]
 
@@ -666,7 +669,13 @@
                 pieces[planes - s] = shift(pieces[(planes - s + 1) % planes], -1)
         return pieces
 
-    def plane_sum(pieces):
+    def plane_sum_direct(pieces):
+        total = pieces[0].astype(F32)
+        for s in range(1, planes):
+            total += lax.ppermute(pieces[s], "dp", [(i, (i - s) % planes) for i in range(planes)]).astype(F32)
+        return total
+
+    def plane_sum(pieces, between=(), last=()):
         def shift(value, by):
             return lax.ppermute(value, "dp", [(i, (i + by) % planes) for i in range(planes)]).astype(F32)
 
@@ -675,9 +684,12 @@
         for order, by in ((range(middle, 0, -1), -1), (range(middle + 1, planes), 1)):
             running = None
             for s in order:
-                running = pieces[s] if running is None else (shift(running, by) + pieces[s].astype(F32)).astype(BF16)
+                if running is None:
+                    running = pieces[s]
+                else:
+                    running = (after(shift(running, by), *between) + pieces[s].astype(F32)).astype(BF16)
             if running is not None:
-                total += shift(running, by)
+                total += after(shift(running, by), *last)
         return total
 
     def reorder(array, dimension):
@@ -694,15 +706,32 @@
     normed_own = (residual_in * scale_attention * attention_gain).astype(BF16)
     normed = gather(reorder(normed_own, 1), "expert")
 
+    kv_own = jnp.concatenate([key_matrix, value_matrix], axis=1)
+    place = member % group
+    kv_parts = [kv_own]
+    for shift in range(1, group):
+        pairs = [(e - e % group + (e % group + shift) % group, e) for e in range(members)]
+        kv_parts.append(lax.ppermute(kv_own, "expert", pairs))
+
+    def kv_piece(j):
+        value = kv_parts[0]
+        for shift in range(1, group):
+            value = jnp.where((place + shift) % group == j, kv_parts[shift], value)
+        return value
+
+    ordered = [kv_piece(j) for j in range(group)]
+    qkv_part = jnp.concatenate(
+        [query_weight] + [p[:, :piece] for p in ordered] + [p[:, piece:] for p in ordered], axis=1)
+
     expert_ids = jnp.arange(experts, dtype=jnp.int32)
     mask_own = jnp.sum((routes[:, :, None] == expert_ids[None, None, :]).astype(F32), axis=1)
     mask_wide = jnp.pad(mask_own, ((0, 0), (0, padded - experts))).astype(BF16)
-    upstream_pieces = plane_pieces(jnp.concatenate([cotangent[:, :half], mask_wide], axis=1))
-    first_hop = (upstream_pieces[1], upstream_pieces[-1])
-    kv_pieces = plane_pieces(after(jnp.concatenate([key_matrix, value_matrix], axis=1), *first_hop))
-    wq_pieces = plane_pieces(after(query_weight, *first_hop))
+    qkv_pieces = plane_pieces(qkv_part)
+    upstream_pieces = plane_pieces(
+        after(jnp.concatenate([cotangent[:, :half], mask_wide], axis=1), *qkv_pieces[1:]))
+    router_rows = gather(after(router_weight.T, normed), "expert").reshape(2 * members, half)
     out_piece = out_weight.shape[1]
-    out_pieces = plane_pieces(after(out_weight, *wq_pieces[1:]))
+    out_pieces = plane_pieces(after(out_weight, *upstream_pieces[1:]))
     cosine, sine = rotary_tables(span)
 
     mask_plane = jnp.concatenate(
@@ -716,35 +745,17 @@
     upstream_sent = dispatch(pick, upstream_pieces)
     upstream_a = exchange(upstream_sent, "expert")
 
-    kv_own = jnp.concatenate(kv_pieces, axis=0)
-    place = member % group
-    kv_parts = [kv_own]
-    for shift in range(1, group):
-        pairs = [(e - e % group + (e % group + shift) % group, e) for e in range(members)]
-        kv_parts.append(lax.ppermute(kv_own, "expert", pairs))
-
-    def kv_piece(j):
-        value = kv_parts[0]
-        for shift in range(1, group):
-            value = jnp.where((place + shift) % group == j, kv_parts[shift], value)
-        return value
-
-    ordered = [kv_piece(j) for j in range(group)]
-    kv_weight = jnp.concatenate([p[:, :piece] for p in ordered] + [p[:, piece:] for p in ordered], axis=1)
-
-    kraw, key_low, value_low = project(
-        project_key_kernel, after(normed, cosine, sine, upstream_sent), [kv_weight], cosine, sine, key_norm_gain,
-        [(HEAD_SIZE, F32), (HEAD_SIZE, BF16), (HEAD_SIZE, BF16)])
-    qraw, query_low = project(
-        project_query_kernel, normed, wq_pieces, cosine, sine, query_gain, [(width, F32), (width, BF16)])
-    attended_low, inverse = attend(prefix_len, after(query_low, upstream_a), key_low, value_low)
+    qraw, kraw, query_low, key_low, value_low = project(
+        after(normed, cosine, sine, router_rows), qkv_pieces, cosine, sine, query_gain, key_norm_gain)
+    attended_low, inverse = attend(prefix_len, query_low, key_low, value_low)
     attended_all = gather(attended_low, "expert").reshape(members, span, width)
 
-    router_rows = gather(after(router_weight.T, attended_low), "expert").reshape(2 * members, half)
     upstream_pieces = plane_pieces(after(jnp.concatenate([cotangent[:, half:], router_rows], axis=0), *out_pieces[1:]))
 
-    out_rows = out_project(plane.astype(jnp.int32).reshape(1), attended_all, out_pieces)
-    projected = exchange(out_rows, "expert").reshape(members, own_rows, out_piece)
+    out_rows = out_project(
+        plane.astype(jnp.int32).reshape(1),
+        after(attended_all, upstream_a, upstream_pieces[1], upstream_pieces[-1]), out_pieces)
+    projected = exchange(after(out_rows, *upstream_pieces[2:-1]), "expert").reshape(members, own_rows, out_piece)
     projected = jnp.transpose(projected, (1, 0, 2)).reshape(own_rows, model)
 
     upstream_sent = dispatch(after(pick, out_rows), upstream_pieces)
@@ -767,12 +778,12 @@
     own_expert = (plane * members + member).astype(jnp.int32).reshape(1)
     activated, gate_grad, up_grad, weight_wide, route_columns = expert_forward(
         experts, own_expert, arrived[0], arrived[1], upstream_a, router, gate, up, upstream_down)
-    back_first = exchange(row_gradient(gate_grad, up_grad, gate, up, 0), "expert")
-    back_second = exchange(row_gradient(gate_grad, up_grad, gate, up, 1, route_columns), "expert")
-    produced = produce(activated, weight_wide, down)
+    back_first = exchange(row_gradient(gate_grad, up_grad, gate, up, 0, first), "expert")
+    back_second = exchange(row_gradient(gate_grad, up_grad, gate, up, first, model, route_columns), "expert")
+    produced = produce(activated, weight_wide, down, first)
     back_first = after(back_first, out_heads, *produced)
-    mixed_first = plane_sum(combine(unpick, back_first, planes, 40))
-    mixed_second = plane_sum(combine(unpick, back_second, planes, 40))
+    mixed_first = plane_sum_direct(combine(unpick, back_first, planes, 40))
+    mixed_second = plane_sum_direct(combine(unpick, back_second, planes, 40))
     mixture_rows = exchange(after(produced[0], back_second), "expert")
 
     upstream = cotangent.astype(F32)
@@ -780,11 +791,11 @@
     logits = jnp.where(mask, mm_t(mixed_low, router[:experts]), VERY_NEGATIVE)
     raised = jnp.where(mask, jnp.exp(logits - jnp.max(logits, axis=-1, keepdims=True)), 0.0)
     weight_own = raised / jnp.sum(raised, axis=-1, keepdims=True)
-    route_back = mixed_second[:, half:half + experts] + mixed_second[:, half + experts:half + 2 * experts]
+    route_back = mixed_second[:, rest:rest + experts] + mixed_second[:, rest + experts:rest + 2 * experts]
     chosen_grad = weight_own * (route_back - jnp.sum(weight_own * route_back, axis=-1, keepdims=True))
     logit_grad = chosen_grad.astype(BF16)
     mixed_first = after(mixed_first, mixture_rows)
-    mixed_grad = mm(logit_grad, router[:experts]) + jnp.concatenate([mixed_first, mixed_second[:, :half]], axis=1)
+    mixed_grad = mm(logit_grad, router[:experts]) + jnp.concatenate([mixed_first, mixed_second[:, :rest]], axis=1)
     mixture_back, mixture_terms = normalize_back(mixed_grad, after_attn, scale_mixture, mixture_gain)
     after_grad = upstream + mixture_back
     after_low = after_grad.astype(BF16)
@@ -799,7 +810,7 @@
     gate_gradient, up_gradient = hidden_gradient(
         arrived[0], arrived[1], *after((gate_grad, up_grad), after_low, *mixture_parts))
     after_all = after(after_all, gate_gradient, router_part, mixture_part, mixture_first)
-    mixture_rows = exchange(after(produced[1], after_all), "expert")
+    mixture_rows = exchange(after(produced[1], gate_gradient), "expert")
     out_partial = out_gradient(member.astype(jnp.int32).reshape(1), attended_all, after_all, out_piece)
     out_share = lax.psum_scatter(
         after(out_partial, mixture_first).reshape(members * width, out_piece), "dp", scatter_dimension=0, tiled=True).astype(F32)
@@ -808,7 +819,7 @@
         prefix_len, query_low, key_low, value_low, attended_low, inverse, attended_grad, qraw, kraw, cosine, sine,
         query_gain, key_norm_gain)
     normed_partial = unproject(
-        own_rows, dq, dk, dv, wq_pieces, kv_weight, normed, reorder(attention_gain, 0), router_part, mixture_part,
+        own_rows, dq, dk, dv, qkv_pieces, normed, reorder(attention_gain, 0), router_part, mixture_part,
         query_terms, key_terms)
     query_partial = t_mm(normed, dq).astype(BF16)
     mixture_parts = combine(unpick, after(mixture_rows, normed_partial), planes)
@@ -820,8 +831,6 @@
     input_grad = after_grad + input_back
     layer_out = (after_attn + jnp.concatenate([mixture_first, mixture_second], axis=1)).astype(BF16)
 
-    query_share = plane_sum(cut(after(query_partial, mixture_second)))
-    down_grad = down_gradient(upstream_a, upstream_b, weight_wide, after(activated, query_partial))
     kv_partial = jnp.concatenate([t_mm(normed, dk), t_mm(normed, dv)], axis=1)
 
     def kv_cols(j):
@@ -835,6 +844,8 @@
         pairs = [(e, e - e % group + (e % group + shift) % group) for e in range(members)]
         kv_total += lax.ppermute(kv_cols((place + shift) % group).astype(BF16), "expert", pairs).astype(F32)
     kv_share = plane_sum(cut(kv_total.astype(BF16)))
+    down_grad = down_gradient(upstream_a, upstream_b, weight_wide, after(activated, normed_partial))
+    query_share = plane_sum(cut(after(query_partial, mixture_second, kv_share)), [down_grad], [normed_sums])
     key_share = kv_share[:, :piece]
     value_share = kv_share[:, piece:]
 

time: 674 us -> 658 us (0.976)
  other arithmetic: 41 us -> 29.3 us
  waiting for transfers between devices: 260 us -> 251 us
  starting transfers between devices: 114 us -> 122 us
    ppermute x0 -> x6, waiting for transfers between devices: none -> 37.6 us  [plane_sum_direct(): lax.ppermute(pieces[s], 'dp', [(i, (i - s) % planes) for i in range(plane...]
    ppermute x39 -> x30, waiting for transfers between devices: 176 us -> 158 us  [shift(): lax.ppermute(value, 'dp', [(i, (i + by) % planes) for i in range(planes)])]
    all_to_all x11, waiting for transfers between devices: 57.9 us -> 39.5 us  [exchange(): return lax.all_to_all(array, axis, split_axis=0, concat_axis=0, tiled=True)]
    ppermute x0 -> x6, starting transfers between devices: none -> 11.5 us  [plane_sum_direct(): lax.ppermute(pieces[s], 'dp', [(i, (i - s) % planes) for i in range(plane...]
    ppermute x39 -> x30, starting transfers between devices: 63 us -> 59.9 us  [shift(): lax.ppermute(value, 'dp', [(i, (i + by) % planes) for i in range(planes)])]
    unnamed x259 -> x246, local copies, waits for them, and re-layouts: 54.6 us -> 55.6 us
    pallas_call x4 -> x3, Pallas kernels: 18 us -> 17.1 us  [the longest x2 9.37 us: row_gradient(): pl.pallas_call(functools.partial(row_gradient_kernel, start, stop), grid=...]
  transfers between devices with their start and end apart: 58 -> 55, of which waited for: 37 -> 40; matrix products, arithmetic and copies ran while one was open for 9% -> 7% of each run, Pallas kernels for 19% -> 18%
where the time goes in v4:
time: 658 us; the launch traced here: 647 us
  waiting for transfers between devices  251 us (38%)
  Pallas kernels  137 us (21%)
  starting transfers between devices  122 us (19%)
  local copies, waits for them, and re-layouts  71.5 us (11%)
  other arithmetic  29.3 us (4%)
  between operations  16.8 us (3%)
  matrix products  10.6 us (2%)
  blocking collectives  9.01 us (1%)
    ppermute x30, waiting for transfers between devices, shift(): lax.ppermute(value, 'dp', [(i, (i + by) % planes) for i in range(planes)])  158 us
    ppermute x30, starting transfers between devices, shift(): lax.ppermute(value, 'dp', [(i, (i + by) % planes) for i in range(planes)])  59.9 us
    unnamed x246, local copies, waits for them, and re-layouts  55.6 us
    all_to_all x11, starting transfers between devices, exchange(): return lax.all_to_all(array, axis, split_axis=0, concat_axis=0, tiled=True)  47.9 us
    all_to_all x11, waiting for transfers between devices, exchange(): return lax.all_to_all(array, axis, split_axis=0, concat_axis=0, tiled=True)  39.5 us
    ppermute x6, waiting for transfers between devices, plane_sum_direct(): lax.ppermute(pieces[s], 'dp', [(i, (i - s) % planes) for i in range(plane...  37.6 us
    pallas_call x1, Pallas kernels, expert_forward(): pl.pallas_call(functools.partial(expert_kernel, experts), grid=(hidden //...  16.9 us
    pallas_call x4, Pallas kernels, combine(): pl.pallas_call(combine_kernel, grid=(width // tile,), in_specs=[pl.BlockS...  16.7 us
  transfers between devices with their start and end apart: 55, of which 40 were waited for; matrix products, arithmetic and copies ran while one was open for 7% of the time, Pallas kernels for 18%

profile of v4, /device:TPU:0, one launch (start us, length us, event | category | flops | bytes accessed | tf_op | source)
XLA Modules:
  0.0 646.9 jit_solution(8248290788142639108)
XLA Ops:
  18.5 18.3 %collective-permute-done.1.refs_1_ = bf16[512,768]{1,0:T(8,128)(2,1)S(1)} collective-permute-done((bf16[512,768]{1,0:T(8,128)(2,1)S(1)}, bf16[512,768]{1,0:T(8,128)(2,1)S(1)}, u32[]{:S(2)}, u32[]{:S(2)}) %collective-permute-start.1) | collective-permute-done | bytes 786464 | tf_op jit(solution)/shard_map/ppermute | solution.py:663
  39.8 10.6 %all-gather.5.cloned.1.call-done.x_ref = bf16[1024,2048]{1,0:T(8,128)(2,1)} async-done(((bf16[128,2048]{1,0:T(8,128)(2,1)}), bf16[1024,2048]{1,0:T(8,128)(2,1)}) %all-gather.5.cloned.1.call-update) | async-done | bytes 4194320 | tf_op jit(solution)/shard_map/all_gather | solution.py:656
  50.3 9.0 %all-gather = bf16[8,4,512]{2,1,0:T(4,128)(2,1)S(1)} all-gather(bf16[1,4,512]{2,1,0:T(4,128)(2,1)S(1)} %bitcast.113), channel_id=1, replica_groups=mesh['dp'=4,'expert'=8] {'expert'}, dimensions={0}, use_global_device_ids=true | all-gather | bytes 36864 | tf_op jit(solution)/shard_map/all_gather | solution.py:656
  59.4 10.8 %collective-permute-done.2.refs_2_ = bf16[512,768]{1,0:T(8,128)(2,1)} collective-permute-done((bf16[512,768]{1,0:T(8,128)(2,1)S(1)}, bf16[512,768]{1,0:T(8,128)(2,1)}, u32[]{:S(2)}, u32[]{:S(2)}) %collective-permute-start.2) | collective-permute-done | bytes 786464 | tf_op jit(solution)/shard_map/ppermute | solution.py:663
  72.4 7.7 %project.1 = (f32[1024,512]{1,0:T(8,128)S(1)}, f32[1024,128]{1,0:T(8,128)S(1)}, bf16[1024,512]{1,0:T(8,128)(2,1)S(1)}, bf16[1024,128]{1,0:T(8,128)(2,1)S(1)}, bf16[1024,128]{1,0:T(8,128)(2,1)S(1)}) custom-call(bf16[1024,2048]{1,0:T(8,128)(2,1)S(1)} %copy-done, f32[1024,128]{1,0:T(8,128)S(1)} %get-tuple-element.218.cos_ref, ...), custom_call_target="tpu_custom_call" | custom-call | flops 1 | bytes 1 | tf_op jit(solution)/shard_map/project/pallas_call | solution.py:98
  81.5 5.9 attend.1
  90.7 3.8 collective-permute-start.6
  94.6 7.9 %collective-permute-done.4.refs_1_ = bf16[128,1152]{1,0:T(8,128)(2,1)S(1)} collective-permute-done((bf16[128,1152]{1,0:T(8,128)(2,1)S(1)}, bf16[128,1152]{1,0:T(8,128)(2,1)S(1)}, u32[]{:S(2)}, u32[]{:S(2)}) %collective-permute-start.4) | collective-permute-done | bytes 294944 | tf_op jit(solution)/shard_map/ppermute | solution.py:663
  102.9 4.9 collective-permute-done.6.refs_3_
  107.9 3.6 collective-permute-done.5.refs_2_
  116.2 4.5 all-to-all-start
  120.9 3.8 collective-permute-start.9
  124.7 12.8 %collective-permute-done.7.refs_1_ = bf16[1024,256]{1,0:T(8,128)(2,1)S(1)} collective-permute-done((bf16[1024,256]{1,0:T(8,128)(2,1)S(1)}, bf16[1024,256]{1,0:T(8,128)(2,1)S(1)}, u32[]{:S(2)}, u32[]{:S(2)}) %collective-permute-start.7) | collective-permute-done | bytes 524320 | tf_op jit(solution)/shard_map/ppermute | solution.py:663
  139.3 7.0 %collective-permute-done.9.refs_3_ = bf16[1024,256]{1,0:T(8,128)(2,1)S(1)} collective-permute-done((bf16[1024,256]{1,0:T(8,128)(2,1)S(1)}, bf16[1024,256]{1,0:T(8,128)(2,1)S(1)}, u32[]{:S(2)}, u32[]{:S(2)}) %collective-permute-start.9) | collective-permute-done | bytes 524320 | tf_op jit(solution)/shard_map/ppermute | solution.py:663
  146.3 13.0 %collective-permute-done.8.refs_2_ = bf16[1024,256]{1,0:T(8,128)(2,1)S(1)} collective-permute-done((bf16[1024,256]{1,0:T(8,128)(2,1)S(1)}, bf16[1024,256]{1,0:T(8,128)(2,1)S(1)}, u32[]{:S(2)}, u32[]{:S(2)}) %collective-permute-start.8) | collective-permute-done | bytes 524320 | tf_op jit(solution)/shard_map/ppermute | solution.py:663
  159.3 3.8 collective-permute-start.11
  163.2 8.2 %collective-permute-done.10.refs_1_ = bf16[144,1024]{1,0:T(8,128)(2,1)} collective-permute-done((bf16[144,1024]{1,0:T(8,128)(2,1)}, bf16[144,1024]{1,0:T(8,128)(2,1)}, u32[]{:S(2)}, u32[]{:S(2)}) %collective-permute-start.10) | collective-permute-done | bytes 294944 | tf_op jit(solution)/shard_map/ppermute | solution.py:663
  182.6 4.2 all-to-all-start.1
  191.5 5.0 all-to-all-done.1
  196.4 4.4 all-to-all-start.2
  202.4 3.8 collective-permute-start.15
  206.3 7.1 %collective-permute-done.13.refs_1_ = bf16[128,1024]{1,0:T(8,128)(2,1)S(1)} collective-permute-done((bf16[128,1024]{1,0:T(8,128)(2,1)S(1)}, bf16[128,1024]{1,0:T(8,128)(2,1)S(1)}, u32[]{:S(2)}, u32[]{:S(2)}) %collective-permute-start.13) | collective-permute-done | bytes 262176 | tf_op jit(solution)/shard_map/ppermute | solution.py:663
  213.4 5.0 collective-permute-start.14
  218.4 8.0 %collective-permute-done.14.refs_2_ = bf16[128,1024]{1,0:T(8,128)(2,1)S(1)} collective-permute-done((bf16[128,1024]{1,0:T(8,128)(2,1)S(1)}, bf16[128,1024]{1,0:T(8,128)(2,1)S(1)}, u32[]{:S(2)}, u32[]{:S(2)}) %collective-permute-start.14) | collective-permute-done | bytes 262176 | tf_op jit(solution)/shard_map/ppermute | solution.py:663
  231.7 4.4 all-to-all-start.3
  236.2 3.8 collective-permute-start.18
  240.0 7.1 %collective-permute-done.16.refs_1_ = bf16[128,1024]{1,0:T(8,128)(2,1)S(1)} collective-permute-done((bf16[128,1024]{1,0:T(8,128)(2,1)S(1)}, bf16[128,1024]{1,0:T(8,128)(2,1)S(1)}, u32[]{:S(2)}, u32[]{:S(2)}) %collective-permute-start.16) | collective-permute-done | bytes 262176 | tf_op jit(solution)/shard_map/ppermute | solution.py:663
  247.2 4.9 collective-permute-start.17
  252.1 8.0 %collective-permute-done.17.refs_2_ = bf16[128,1024]{1,0:T(8,128)(2,1)S(1)} collective-permute-done((bf16[128,1024]{1,0:T(8,128)(2,1)S(1)}, bf16[128,1024]{1,0:T(8,128)(2,1)S(1)}, u32[]{:S(2)}, u32[]{:S(2)}) %collective-permute-start.17) | collective-permute-done | bytes 262176 | tf_op jit(solution)/shard_map/ppermute | solution.py:663
  267.0 4.7 all-to-all-start.4
  275.8 7.3 %down_back.1.down_ref = f32[1216,768]{1,0:T(8,128)S(1)} custom-call(bf16[1216,1152]{1,0:T(8,128)(2,1)} %bitcast.9.ca_ref.mask_ref, bf16[1216,1024]{1,0:T(8,128)(2,1)} %bitcast.15.cb_ref, bf16[768,2048]{1,0:T(8,128)(2,1)S(1)} %bitcast.77), custom_call_target="tpu_custom_call" | custom-call | flops 1 | bytes 1 | tf_op jit(solution)/shard_map/down_back/pallas_call | solution.py:467
  286.4 16.1 %all-to-all-done.4 = bf16[8,152,1024]{2,1,0:T(8,128)(2,1)} async-done(((bf16[8,152,1024]{2,1,0:T(8,128)(2,1)}), bf16[8,152,1024]{2,1,0:T(8,128)(2,1)}, u32[]{:S(2)}, u32[]{:S(2)}) %all-to-all-start.4) | async-done | bytes 2490400 | tf_op jit(solution)/shard_map/all_to_all | solution.py:659
  302.5 4.3 all-to-all-start.8
  307.9 16.9 %expert_forward.1 = (bf16[1216,768]{1,0:T(8,128)(2,1)S(1)}, bf16[1216,768]{1,0:T(8,128)(2,1)S(1)}, bf16[1216,768]{1,0:T(8,128)(2,1)S(1)}, f32[1216,128]{1,0:T(8,128)S(1)}, bf16[1216,128]{1,0:T(8,128)(2,1)S(1)}) custom-call(s32[1]{0:T(128)} %bitcast.13.own_ref, bf16[1216,1024]{1,0:T(8,128)(2,1)} %bitcast.17.xa_ref, bf16[1216,1024]{1,0:T(8,128)(2,1)} %bitcast.19.xb_ref, ...), custom_call_target="tpu_custom_call" | custom-call | flops 19800000512 | bytes 1 | tf_op jit(solution)/shard_map/expert_forward/pallas_call | solution.py:408
  326.9 3.7 row_gradient.2
  334.6 4.5 all-to-all-start.5
  351.1 5.6 row_gradient.3
  358.5 8.3 %all-to-all-done.5 = bf16[8,152,896]{2,1,0:T(8,128)(2,1)} async-done(((bf16[8,152,896]{2,1,0:T(8,128)(2,1)}), bf16[8,152,896]{2,1,0:T(8,128)(2,1)}, u32[]{:S(2)}, u32[]{:S(2)}) %all-to-all-start.5) | async-done | bytes 2179104 | tf_op jit(solution)/shard_map/all_to_all | solution.py:659
  366.7 4.5 all-to-all-start.7
  372.5 6.2 combine.4
  385.0 4.6 produce.1
  392.5 10.7 %collective-permute-done.20 = bf16[128,896]{1,0:T(8,128)(2,1)S(1)} collective-permute-done((bf16[128,896]{1,0:T(8,128)(2,1)S(1)}, bf16[128,896]{1,0:T(8,128)(2,1)S(1)}, u32[]{:S(2)}, u32[]{:S(2)}) %collective-permute-start.20) | collective-permute-done | bytes 229408 | tf_op jit(solution)/shard_map/ppermute | solution.py:675
  404.9 3.8 all-to-all-done.7
  408.7 3.6 all-to-all-start.6
  413.7 4.9 combine.5
  424.8 5.2 collective-permute-done.22
  430.0 21.7 %collective-permute-done.23 = bf16[128,1280]{1,0:T(8,128)(2,1)S(1)} collective-permute-done((bf16[128,1280]{1,0:T(8,128)(2,1)S(1)}, bf16[128,1280]{1,0:T(8,128)(2,1)S(1)}, u32[]{:S(2)}, u32[]{:S(2)}) %collective-permute-start.23) | collective-permute-done | bytes 327712 | tf_op jit(solution)/shard_map/ppermute | solution.py:675
  463.9 7.4 %collective-permute-done.25 = bf16[128,1280]{1,0:T(8,128)(2,1)S(1)} collective-permute-done((bf16[128,1280]{1,0:T(8,128)(2,1)S(1)}, bf16[128,1280]{1,0:T(8,128)(2,1)S(1)}, u32[]{:S(2)}, u32[]{:S(2)}) %collective-permute-start.25) | collective-permute-done | bytes 327712 | tf_op jit(solution)/shard_map/ppermute | solution.py:680
  477.4 13.4 %hidden_gradient.1 = (f32[1,2048,768]{2,1,0:T(8,128)}, f32[1,2048,768]{2,1,0:T(8,128)}) custom-call(bf16[1216,1024]{1,0:T(8,128)(2,1)} %bitcast.17.xa_ref, bf16[1216,1024]{1,0:T(8,128)(2,1)} %bitcast.19.xb_ref, bf16[1216,768]{1,0:T(8,128)(2,1)S(1)} %copy-done.53, bf16[1216,768]{1,0:T(8,128)(2,1)S(1)} %copy-done.56), custom_call_target="tpu_custom_call" | custom-call | flops 1 | bytes 1 | tf_op jit(solution)/shard_map/hidden_gradient/pallas_call | solution.py:519
  499.4 5.4 out_gradient.1
  504.8 3.8 all-to-all-start.9
  511.1 4.4 out_back.1.do_ref
  515.6 13.9 %attend_back.1 = (bf16[1024,512]{1,0:T(8,128)(2,1)S(1)}, bf16[1024,128]{1,0:T(8,128)(2,1)S(1)}, bf16[1024,128]{1,0:T(8,128)(2,1)S(1)}, f32[1,128]{1,0:T(1,128)S(1)}, f32[1,128]{1,0:T(1,128)S(1)}) custom-call(s32[1]{0:T(128)S(6)} %copy.94.prefix_ref, bf16[1024,512]{1,0:T(8,128)(2,1)S(1)} %copy-done.26, bf16[1024,128]{1,0:T(8,128)(2,1)S(1)} %copy-done.62, ...), custom_call_target="tpu_custom_call" | custom-call | flops 1 | bytes 1 | tf_op jit(solution)/shard_map/attend_back/pallas_call | solution.py:207
  529.6 6.9 %unproject.1 = bf16[8,144,2048]{2,1,0:T(8,128)(2,1)} custom-call(bf16[1024,512]{1,0:T(8,128)(2,1)S(1)} %get-tuple-element.136.dq_ref, bf16[1024,128]{1,0:T(8,128)(2,1)S(1)} %get-tuple-element.137.dk_ref, bf16[1024,128]{1,0:T(8,128)(2,1)S(1)} %get-tuple-element.138.dv_ref, bf16[1024,2048]{1,0:T(8,128)(2,1)S(1)} %copy-done.1, f32[1,2048]{1,0:T(1,128)S(1)} %bitcast.91, ...), custom_call_target="tpu_custom_call" | custom-call | flops 1 | bytes 1 | tf_op jit(solution)/shard_map/unproject/pallas_call | solution.py:262
  547.5 3.8 convolution_convert_fusion
  553.4 4.9 all-to-all-start.10
  562.8 5.0 collective-permute-done.28
  568.0 4.3 collective-permute-start.29
  579.7 4.3 collective-permute-start.33
  587.1 3.9 collective-permute-start.35
  591.0 11.1 %down_gradient.1 = f32[1,768,2048]{2,1,0:T(8,128)} custom-call(bf16[1216,1152]{1,0:T(8,128)(2,1)} %bitcast.9.ca_ref.mask_ref, bf16[1216,1024]{1,0:T(8,128)(2,1)} %bitcast.15.cb_ref, f32[1216,128]{1,0:T(8,128)S(1)} %copy-done.36, bf16[1216,768]{1,0:T(8,128)(2,1)S(1)} %copy-done.18), custom_call_target="tpu_custom_call" | custom-call | flops 1 | bytes 1 | tf_op jit(solution)/shard_map/down_gradient/pallas_call | solution.py:545
  602.4 3.9 collective-permute-start.36
  607.0 11.8 %collective-permute-done.37 = bf16[512,512]{1,0:T(8,128)(2,1)S(1)} collective-permute-done((bf16[512,512]{1,0:T(8,128)(2,1)S(1)}, bf16[512,512]{1,0:T(8,128)(2,1)S(1)}, u32[]{:S(2)}, u32[]{:S(2)}) %collective-permute-start.37) | collective-permute-done | bytes 524320 | tf_op jit(solution)/shard_map/ppermute | solution.py:680
  618.9 5.9 collective-permute-done.36
  (440 shorter events, 178.0 us)
Async XLA Ops:
  7.2 43.1 %all-gather.5.cloned.1.call-start = ((), (), s32[]{:S(2)}) async-start(), calls=%async_computation.12 | async-start | bytes 4718592 | tf_op jit(solution)/shard_map/all_gather | solution.py:656
  10.8 163.6 %all-gather.7.cloned.1.call-start = ((), (), s32[]{:S(2)}) async-start(), calls=%async_computation.13 | async-start | bytes 9437184 | tf_op jit(solution)/shard_map/all_gather | solution.py:656
  11.2 1.5 collective-permute-start
  13.4 66.7 %copy-start.19 = (bf16[512,768]{1,0:T(8,128)(2,1)}, bf16[512,768]{1,0:T(8,128)(2,1)S(1)}, u32[]{:S(2)}) copy-start(bf16[512,768]{1,0:T(8,128)(2,1)S(1)} %concatenate.65.refs_0_) | copy-start | bytes 2359300
  13.4 36.9 %copy-start.113 = (bf16[512,4]{0,1:T(4,128)(2,1)S(1)}, bf16[512,4]{0,1:T(4,128)(2,1)}, u32[]{:S(2)}) copy-start(bf16[512,4]{0,1:T(4,128)(2,1)} %param.23) | copy-start | bytes 12292
  13.4 56.7 %copy-start.74 = (f32[128]{0:T(128)S(1)}, f32[128]{0:T(128)}, u32[]{:S(2)}) copy-start(f32[128]{0:T(128)} %param.26) | copy-start | bytes 1540
  13.4 56.7 %copy-start.76 = (f32[128]{0:T(128)S(1)}, f32[128]{0:T(128)}, u32[]{:S(2)}) copy-start(f32[128]{0:T(128)} %param.27) | copy-start | bytes 1540
  13.5 23.4 %collective-permute-start.1 = (bf16[512,768]{1,0:T(8,128)(2,1)S(1)}, bf16[512,768]{1,0:T(8,128)(2,1)S(1)}, u32[]{:S(2)}, u32[]{:S(2)}) collective-permute-start(bf16[512,768]{1,0:T(8,128)(2,1)S(1)} %concatenate.65.refs_0_), channel_id=1, source_target_pairs={{0,8},{8,16},{16,24},{24,0},{1,9},{9,17},{17,25},{25,1},{2,10},{10... | collective-permute-start | bytes 2359304 | tf_op jit(solution)/shard_map/ppermute | solution.py:663
  16.4 42.9 %collective-permute-start.3 = (bf16[512,768]{1,0:T(8,128)(2,1)S(1)}, bf16[512,768]{1,0:T(8,128)(2,1)S(1)}, u32[]{:S(2)}, u32[]{:S(2)}) collective-permute-start(bf16[512,768]{1,0:T(8,128)(2,1)S(1)} %concatenate.65.refs_0_), channel_id=1, source_target_pairs={{0,24},{8,0},{16,8},{24,16},{1,25},{9,1},{17,9},{25,17},{2,26},{10... | collective-permute-start | bytes 2359304 | tf_op jit(solution)/shard_map/ppermute | solution.py:663
  36.8 43.3 %copy-start.28 = (bf16[512,768]{1,0:T(8,128)(2,1)}, bf16[512,768]{1,0:T(8,128)(2,1)S(1)}, u32[]{:S(2)}) copy-start(bf16[512,768]{1,0:T(8,128)(2,1)S(1)} %collective-permute-done.1.refs_1_) | copy-start | bytes 2359300
  36.8 33.3 %collective-permute-start.2 = (bf16[512,768]{1,0:T(8,128)(2,1)S(1)}, bf16[512,768]{1,0:T(8,128)(2,1)}, u32[]{:S(2)}, u32[]{:S(2)}) collective-permute-start(bf16[512,768]{1,0:T(8,128)(2,1)S(1)} %collective-permute-done.1.refs_1_), channel_id=1, source_target_pairs={{0,8},{8,16},{16,24},{24,0},{1,9},{9,17},{17,25},{25,1},{2,10},{10... | collective-permute-start | bytes 2359304 | tf_op jit(solution)/shard_map/ppermute | solution.py:663
  39.8 40.3 %copy-start.21 = (f32[1024,128]{1,0:T(8,128)}, f32[1024,128]{1,0:T(8,128)S(1)}, u32[]{:S(2)}) copy-start(f32[1024,128]{1,0:T(8,128)S(1)} %get-tuple-element.218.cos_ref) | copy-start | bytes 1572868
  39.8 40.3 %copy-start.23 = (f32[1024,128]{1,0:T(8,128)}, f32[1024,128]{1,0:T(8,128)S(1)}, u32[]{:S(2)}) copy-start(f32[1024,128]{1,0:T(8,128)S(1)} %get-tuple-element.219.sin_ref) | copy-start | bytes 1572868
  90.7 11.9 %collective-permute-start.4 = (bf16[128,1152]{1,0:T(8,128)(2,1)S(1)}, bf16[128,1152]{1,0:T(8,128)(2,1)S(1)}, u32[]{:S(2)}, u32[]{:S(2)}) collective-permute-start(bf16[128,1152]{1,0:T(8,128)(2,1)S(1)} %fusion.19.refs_0_), channel_id=1, source_target_pairs={{0,8},{8,16},{16,24},{24,0},{1,9},{9,17},{17,25},{25,1},{2,10},{10... | collective-permute-start | bytes 884744 | tf_op jit(solution)/shard_map/ppermute | solution.py:663
  90.7 17.0 %collective-permute-start.6 = (bf16[128,1152]{1,0:T(8,128)(2,1)S(1)}, bf16[128,1152]{1,0:T(8,128)(2,1)S(1)}, u32[]{:S(2)}, u32[]{:S(2)}) collective-permute-start(bf16[128,1152]{1,0:T(8,128)(2,1)S(1)} %fusion.19.refs_0_), channel_id=1, source_target_pairs={{0,24},{8,0},{16,8},{24,16},{1,25},{9,1},{17,9},{25,17},{2,26},{10... | collective-permute-start | bytes 884744 | tf_op jit(solution)/shard_map/ppermute | solution.py:663
  102.6 9.0 %collective-permute-start.5 = (bf16[128,1152]{1,0:T(8,128)(2,1)S(1)}, bf16[128,1152]{1,0:T(8,128)(2,1)S(1)}, u32[]{:S(2)}, u32[]{:S(2)}) collective-permute-start(bf16[128,1152]{1,0:T(8,128)(2,1)S(1)} %collective-permute-done.4.refs_1_), channel_id=1, source_target_pairs={{0,8},{8,16},{16,24},{24,0},{1,9},{9,17},{17,25},{25,1},{2,10},{10... | collective-permute-start | bytes 884744 | tf_op jit(solution)/shard_map/ppermute | solution.py:663
  116.2 56.4 %all-to-all-start = ((bf16[8,152,1152]{2,1,0:T(8,128)(2,1)}), bf16[8,152,1152]{2,1,0:T(8,128)(2,1)}, u32[]{:S(2)}, u32[]{:S(2)}) async-start(bf16[8,152,1152]{2,1,0:T(8,128)(2,1)} %bitcast.80), calls=%async_computation | async-start | bytes 5603328 | tf_op jit(solution)/shard_map/all_to_all | solution.py:659
  120.8 16.6 %collective-permute-start.7 = (bf16[1024,256]{1,0:T(8,128)(2,1)S(1)}, bf16[1024,256]{1,0:T(8,128)(2,1)S(1)}, u32[]{:S(2)}, u32[]{:S(2)}) collective-permute-start(bf16[1024,256]{1,0:T(8,128)(2,1)S(1)} %copy-done.42), channel_id=1, source_target_pairs={{0,8},{8,16},{16,24},{24,0},{1,9},{9,17},{17,25},{25,1},{2,10},{10... | collective-permute-start | bytes 1572872 | tf_op jit(solution)/shard_map/ppermute | solution.py:663
  120.9 25.4 %collective-permute-start.9 = (bf16[1024,256]{1,0:T(8,128)(2,1)S(1)}, bf16[1024,256]{1,0:T(8,128)(2,1)S(1)}, u32[]{:S(2)}, u32[]{:S(2)}) collective-permute-start(bf16[1024,256]{1,0:T(8,128)(2,1)S(1)} %copy-done.42), channel_id=1, source_target_pairs={{0,24},{8,0},{16,8},{24,16},{1,25},{9,1},{17,9},{25,17},{2,26},{10... | collective-permute-start | bytes 1572872 | tf_op jit(solution)/shard_map/ppermute | solution.py:663
  137.5 43.8 %copy-start.46 = (bf16[1024,256]{1,0:T(8,128)(2,1)}, bf16[1024,256]{1,0:T(8,128)(2,1)S(1)}, u32[]{:S(2)}) copy-start(bf16[1024,256]{1,0:T(8,128)(2,1)S(1)} %collective-permute-done.7.refs_1_) | copy-start | bytes 1572868
  137.5 21.9 %collective-permute-start.8 = (bf16[1024,256]{1,0:T(8,128)(2,1)S(1)}, bf16[1024,256]{1,0:T(8,128)(2,1)S(1)}, u32[]{:S(2)}, u32[]{:S(2)}) collective-permute-start(bf16[1024,256]{1,0:T(8,128)(2,1)S(1)} %collective-permute-done.7.refs_1_), channel_id=1, source_target_pairs={{0,8},{8,16},{16,24},{24,0},{1,9},{9,17},{17,25},{25,1},{2,10},{10... | collective-permute-start | bytes 1572872 | tf_op jit(solution)/shard_map/ppermute | solution.py:663
  146.3 35.0 %copy-start.44 = (bf16[1024,256]{1,0:T(8,128)(2,1)}, bf16[1024,256]{1,0:T(8,128)(2,1)S(1)}, u32[]{:S(2)}) copy-start(bf16[1024,256]{1,0:T(8,128)(2,1)S(1)} %collective-permute-done.9.refs_3_) | copy-start | bytes 1572868
  159.3 12.1 %collective-permute-start.10 = (bf16[144,1024]{1,0:T(8,128)(2,1)}, bf16[144,1024]{1,0:T(8,128)(2,1)}, u32[]{:S(2)}, u32[]{:S(2)}) collective-permute-start(bf16[144,1024]{1,0:T(8,128)(2,1)} %pad_maximum_fusion.5.refs_0_), channel_id=1, source_target_pairs={{0,8},{8,16},{16,24},{24,0},{1,9},{9,17},{17,25},{25,1},{2,10},{10... | collective-permute-start | bytes 884744 | tf_op jit(solution)/shard_map/ppermute | solution.py:663
  159.3 15.1 %collective-permute-start.11 = (bf16[144,1024]{1,0:T(8,128)(2,1)}, bf16[144,1024]{1,0:T(8,128)(2,1)}, u32[]{:S(2)}, u32[]{:S(2)}) collective-permute-start(bf16[144,1024]{1,0:T(8,128)(2,1)} %pad_maximum_fusion.5.refs_0_), channel_id=1, source_target_pairs={{0,24},{8,0},{16,8},{24,16},{1,25},{9,1},{17,9},{25,17},{2,26},{10... | collective-permute-start | bytes 884744 | tf_op jit(solution)/shard_map/ppermute | solution.py:663
  171.4 11.2 %collective-permute-start.12 = (bf16[144,1024]{1,0:T(8,128)(2,1)}, bf16[144,1024]{1,0:T(8,128)(2,1)}, u32[]{:S(2)}, u32[]{:S(2)}) collective-permute-start(bf16[144,1024]{1,0:T(8,128)(2,1)} %collective-permute-done.10.refs_1_), channel_id=1, source_target_pairs={{0,8},{8,16},{16,24},{24,0},{1,9},{9,17},{17,25},{25,1},{2,10},{10... | collective-permute-start | bytes 884744 | tf_op jit(solution)/shard_map/ppermute | solution.py:663
  182.6 13.9 %all-to-all-start.1 = ((bf16[8,128,256]{2,1,0:T(8,128)(2,1)}), bf16[8,128,256]{2,1,0:T(8,128)(2,1)S(1)}, u32[]{:S(2)}, u32[]{:S(2)}) async-start(bf16[8,128,256]{2,1,0:T(8,128)(2,1)} %bitcast.88), calls=%async_computation.1 | async-start | bytes 1048576 | tf_op jit(solution)/shard_map/all_to_all | solution.py:659
  196.4 35.3 %all-to-all-start.2 = ((bf16[8,152,1024]{2,1,0:T(8,128)(2,1)}), bf16[8,152,1024]{2,1,0:T(8,128)(2,1)}, u32[]{:S(2)}, u32[]{:S(2)}) async-start(bf16[8,152,1024]{2,1,0:T(8,128)(2,1)} %bitcast.82), calls=%async_computation.2 | async-start | bytes 4980736 | tf_op jit(solution)/shard_map/all_to_all | solution.py:659
  202.4 11.0 %collective-permute-start.13 = (bf16[128,1024]{1,0:T(8,128)(2,1)S(1)}, bf16[128,1024]{1,0:T(8,128)(2,1)S(1)}, u32[]{:S(2)}, u32[]{:S(2)}) collective-permute-start(bf16[128,1024]{1,0:T(8,128)(2,1)S(1)} %get-tuple-element.181.refs_0_), channel_id=1, source_target_pairs={{0,8},{8,16},{16,24},{24,0},{1,9},{9,17},{17,25},{25,1},{2,10},{10... | collective-permute-start | bytes 786440 | tf_op jit(solution)/shard_map/ppermute | solution.py:663
  202.4 16.0 %collective-permute-start.15 = (bf16[128,1024]{1,0:T(8,128)(2,1)S(1)}, bf16[128,1024]{1,0:T(8,128)(2,1)S(1)}, u32[]{:S(2)}, u32[]{:S(2)}) collective-permute-start(bf16[128,1024]{1,0:T(8,128)(2,1)S(1)} %get-tuple-element.181.refs_0_), channel_id=1, source_target_pairs={{0,24},{8,0},{16,8},{24,16},{1,25},{9,1},{17,9},{25,17},{2,26},{10... | collective-permute-start | bytes 786440 | tf_op jit(solution)/shard_map/ppermute | solution.py:663
  213.4 13.0 %collective-permute-start.14 = (bf16[128,1024]{1,0:T(8,128)(2,1)S(1)}, bf16[128,1024]{1,0:T(8,128)(2,1)S(1)}, u32[]{:S(2)}, u32[]{:S(2)}) collective-permute-start(bf16[128,1024]{1,0:T(8,128)(2,1)S(1)} %collective-permute-done.13.refs_1_), channel_id=1, source_target_pairs={{0,8},{8,16},{16,24},{24,0},{1,9},{9,17},{17,25},{25,1},{2,10},{10... | collective-permute-start | bytes 786440 | tf_op jit(solution)/shard_map/ppermute | solution.py:663
  231.7 35.3 %all-to-all-start.3 = ((bf16[8,152,1024]{2,1,0:T(8,128)(2,1)}), bf16[8,152,1024]{2,1,0:T(8,128)(2,1)}, u32[]{:S(2)}, u32[]{:S(2)}) async-start(bf16[8,152,1024]{2,1,0:T(8,128)(2,1)} %bitcast.83), calls=%async_computation.3 | async-start | bytes 4980736 | tf_op jit(solution)/shard_map/all_to_all | solution.py:659
  236.1 11.0 %collective-permute-start.16 = (bf16[128,1024]{1,0:T(8,128)(2,1)S(1)}, bf16[128,1024]{1,0:T(8,128)(2,1)S(1)}, u32[]{:S(2)}, u32[]{:S(2)}) collective-permute-start(bf16[128,1024]{1,0:T(8,128)(2,1)S(1)} %get-tuple-element.180.refs_0_), channel_id=1, source_target_pairs={{0,8},{8,16},{16,24},{24,0},{1,9},{9,17},{17,25},{25,1},{2,10},{10... | collective-permute-start | bytes 786440 | tf_op jit(solution)/shard_map/ppermute | solution.py:663
  236.2 15.9 %collective-permute-start.18 = (bf16[128,1024]{1,0:T(8,128)(2,1)S(1)}, bf16[128,1024]{1,0:T(8,128)(2,1)S(1)}, u32[]{:S(2)}, u32[]{:S(2)}) collective-permute-start(bf16[128,1024]{1,0:T(8,128)(2,1)S(1)} %get-tuple-element.180.refs_0_), channel_id=1, source_target_pairs={{0,24},{8,0},{16,8},{24,16},{1,25},{9,1},{17,9},{25,17},{2,26},{10... | collective-permute-start | bytes 786440 | tf_op jit(solution)/shard_map/ppermute | solution.py:663
  247.2 12.9 %collective-permute-start.17 = (bf16[128,1024]{1,0:T(8,128)(2,1)S(1)}, bf16[128,1024]{1,0:T(8,128)(2,1)S(1)}, u32[]{:S(2)}, u32[]{:S(2)}) collective-permute-start(bf16[128,1024]{1,0:T(8,128)(2,1)S(1)} %collective-permute-done.16.refs_1_), channel_id=1, source_target_pairs={{0,8},{8,16},{16,24},{24,0},{1,9},{9,17},{17,25},{25,1},{2,10},{10... | collective-permute-start | bytes 786440 | tf_op jit(solution)/shard_map/ppermute | solution.py:663
  267.0 35.5 %all-to-all-start.4 = ((bf16[8,152,1024]{2,1,0:T(8,128)(2,1)}), bf16[8,152,1024]{2,1,0:T(8,128)(2,1)}, u32[]{:S(2)}, u32[]{:S(2)}) async-start(bf16[8,152,1024]{2,1,0:T(8,128)(2,1)} %bitcast.81), calls=%async_computation.4 | async-start | bytes 4980736 | tf_op jit(solution)/shard_map/all_to_all | solution.py:659
  302.5 32.1 %all-to-all-start.8 = ((bf16[8,512,256]{2,1,0:T(8,128)(2,1)}), bf16[8,512,256]{2,1,0:T(8,128)(2,1)}, u32[]{:S(2)}, u32[]{:S(2)}) async-start(bf16[8,512,256]{2,1,0:T(8,128)(2,1)} %bitcast.103), calls=%async_computation.8 | async-start | bytes 4194304 | tf_op jit(solution)/shard_map/all_to_all | solution.py:659
  334.6 32.1 %all-to-all-start.5 = ((bf16[8,152,896]{2,1,0:T(8,128)(2,1)}), bf16[8,152,896]{2,1,0:T(8,128)(2,1)}, u32[]{:S(2)}, u32[]{:S(2)}) async-start(bf16[8,152,896]{2,1,0:T(8,128)(2,1)} %bitcast.87), calls=%async_computation.5 | async-start | bytes 4358144 | tf_op jit(solution)/shard_map/all_to_all | solution.py:659
  366.7 42.0 %all-to-all-start.7 = ((bf16[8,152,1280]{2,1,0:T(8,128)(2,1)}), bf16[8,152,1280]{2,1,0:T(8,128)(2,1)}, u32[]{:S(2)}, u32[]{:S(2)}) async-start(bf16[8,152,1280]{2,1,0:T(8,128)(2,1)} %bitcast.86), calls=%async_computation.7 | async-start | bytes 6225920 | tf_op jit(solution)/shard_map/all_to_all | solution.py:659
  378.7 13.9 %collective-permute-start.19 = (bf16[128,896]{1,0:T(8,128)(2,1)S(1)}, bf16[128,896]{1,0:T(8,128)(2,1)S(1)}, u32[]{:S(2)}, u32[]{:S(2)}) collective-permute-start(bf16[128,896]{1,0:T(8,128)(2,1)S(1)} %get-tuple-element.107), channel_id=1, source_target_pairs={{0,24},{8,0},{16,8},{24,16},{1,25},{9,1},{17,9},{25,17},{2,26},{10... | collective-permute-start | bytes 688136 | tf_op jit(solution)/shard_map/ppermute | solution.py:675
  381.9 21.4 %collective-permute-start.20 = (bf16[128,896]{1,0:T(8,128)(2,1)S(1)}, bf16[128,896]{1,0:T(8,128)(2,1)S(1)}, u32[]{:S(2)}, u32[]{:S(2)}) collective-permute-start(bf16[128,896]{1,0:T(8,128)(2,1)S(1)} %get-tuple-element.108), channel_id=1, source_target_pairs={{0,16},{8,24},{16,0},{24,8},{1,17},{9,25},{17,1},{25,9},{2,18},{10... | collective-permute-start | bytes 688136 | tf_op jit(solution)/shard_map/ppermute | solution.py:675
  382.5 20.8 %collective-permute-start.21 = (bf16[128,896]{1,0:T(8,128)(2,1)S(1)}, bf16[128,896]{1,0:T(8,128)(2,1)S(1)}, u32[]{:S(2)}, u32[]{:S(2)}) collective-permute-start(bf16[128,896]{1,0:T(8,128)(2,1)S(1)} %get-tuple-element.109), channel_id=1, source_target_pairs={{0,8},{8,16},{16,24},{24,0},{1,9},{9,17},{17,25},{25,1},{2,10},{10... | collective-permute-start | bytes 688136 | tf_op jit(solution)/shard_map/ppermute | solution.py:675
  408.7 43.9 %all-to-all-start.6 = ((bf16[8,152,1280]{2,1,0:T(8,128)(2,1)}), bf16[8,152,1280]{2,1,0:T(8,128)(2,1)S(1)}, u32[]{:S(2)}, u32[]{:S(2)}) async-start(bf16[8,152,1280]{2,1,0:T(8,128)(2,1)} %bitcast.85), calls=%async_computation.6 | async-start | bytes 6225920 | tf_op jit(solution)/shard_map/all_to_all | solution.py:659
  412.4 81.4 %all-gather.9.cloned.1.call-start = ((), (), s32[]{:S(2)}) async-start(), calls=%async_computation.14 | async-start | bytes 4718592 | tf_op jit(solution)/shard_map/all_gather | solution.py:656
  418.7 11.3 %collective-permute-start.22 = (bf16[128,1280]{1,0:T(8,128)(2,1)S(1)}, bf16[128,1280]{1,0:T(8,128)(2,1)S(1)}, u32[]{:S(2)}, u32[]{:S(2)}) collective-permute-start(bf16[128,1280]{1,0:T(8,128)(2,1)S(1)} %get-tuple-element.118), channel_id=1, source_target_pairs={{0,24},{8,0},{16,8},{24,16},{1,25},{9,1},{17,9},{25,17},{2,26},{10... | collective-permute-start | bytes 983048 | tf_op jit(solution)/shard_map/ppermute | solution.py:675
  421.8 29.8 %collective-permute-start.23 = (bf16[128,1280]{1,0:T(8,128)(2,1)S(1)}, bf16[128,1280]{1,0:T(8,128)(2,1)S(1)}, u32[]{:S(2)}, u32[]{:S(2)}) collective-permute-start(bf16[128,1280]{1,0:T(8,128)(2,1)S(1)} %get-tuple-element.119), channel_id=1, source_target_pairs={{0,16},{8,24},{16,0},{24,8},{1,17},{9,25},{17,1},{25,9},{2,18},{10... | collective-permute-start | bytes 983048 | tf_op jit(solution)/shard_map/ppermute | solution.py:675
  422.5 29.2 %collective-permute-start.24 = (bf16[128,1280]{1,0:T(8,128)(2,1)S(1)}, bf16[128,1280]{1,0:T(8,128)(2,1)S(1)}, u32[]{:S(2)}, u32[]{:S(2)}) collective-permute-start(bf16[128,1280]{1,0:T(8,128)(2,1)S(1)} %get-tuple-element.120), channel_id=1, source_target_pairs={{0,8},{8,16},{16,24},{24,0},{1,9},{9,17},{17,25},{25,1},{2,10},{10... | collective-permute-start | bytes 983048 | tf_op jit(solution)/shard_map/ppermute | solution.py:675
  456.9 94.4 %reduce-scatter.2.cloned.1.call-start = ((), (), s32[]{:S(2)}) async-start(), calls=%async_computation.15 | async-start | bytes 2621440 | tf_op jit(solution)/shard_map/reduce_scatter | solution.py:815
  461.9 9.4 %collective-permute-start.25 = (bf16[128,1280]{1,0:T(8,128)(2,1)S(1)}, bf16[128,1280]{1,0:T(8,128)(2,1)S(1)}, u32[]{:S(2)}, u32[]{:S(2)}) collective-permute-start(bf16[128,1280]{1,0:T(8,128)(2,1)S(1)} %get-tuple-element.124), channel_id=1, source_target_pairs={{0,24},{8,0},{16,8},{24,16},{1,25},{9,1},{17,9},{25,17},{2,26},{10... | collective-permute-start | bytes 983048 | tf_op jit(solution)/shard_map/ppermute | solution.py:680
  462.2 28.6 %collective-permute-start.27 = (bf16[128,1280]{1,0:T(8,128)(2,1)}, bf16[128,1280]{1,0:T(8,128)(2,1)S(1)}, u32[]{:S(2)}, u32[]{:S(2)}) collective-permute-start(bf16[128,1280]{1,0:T(8,128)(2,1)} %get-tuple-element.126), channel_id=1, source_target_pairs={{0,8},{8,16},{16,24},{24,0},{1,9},{9,17},{17,25},{25,1},{2,10},{10... | collective-permute-start | bytes 983048 | tf_op jit(solution)/shard_map/ppermute | solution.py:680
  471.4 19.4 %collective-permute-start.26 = (bf16[128,1280]{1,0:T(8,128)(2,1)S(1)}, bf16[128,1280]{1,0:T(8,128)(2,1)S(1)}, u32[]{:S(2)}, u32[]{:S(2)}) collective-permute-start(bf16[128,1280]{1,0:T(8,128)(2,1)S(1)} %add_convert_fusion.1), channel_id=1, source_target_pairs={{0,24},{8,0},{16,8},{24,16},{1,25},{9,1},{17,9},{25,17},{2,26},{10... | collective-permute-start | bytes 983048 | tf_op jit(solution)/shard_map/ppermute | solution.py:680
  504.8 33.3 %all-to-all-start.9 = ((bf16[8,152,768]{2,1,0:T(8,128)(2,1)}), bf16[8,152,768]{2,1,0:T(8,128)(2,1)S(1)}, u32[]{:S(2)}, u32[]{:S(2)}) async-start(bf16[8,152,768]{2,1,0:T(8,128)(2,1)} %bitcast.89), calls=%async_computation.9 | async-start | bytes 3735552 | tf_op jit(solution)/shard_map/all_to_all | solution.py:659
  553.4 71.5 %all-to-all-start.10 = ((bf16[8,144,2048]{2,1,0:T(8,128)(2,1)}), bf16[8,144,2048]{2,1,0:T(8,128)(2,1)}, u32[]{:S(2)}, u32[]{:S(2)}) async-start(bf16[8,144,2048]{2,1,0:T(8,128)(2,1)} %unproject.1), calls=%async_computation.11 | async-start | bytes 9437184 | tf_op jit(solution)/shard_map/all_to_all | solution.py:659
  558.7 13.7 %collective-permute-start.31 = (bf16[2048,128]{0,1:T(8,128)(2,1)S(1)}, bf16[2048,128]{0,1:T(8,128)(2,1)}, u32[]{:S(2)}, u32[]{:S(2)}) collective-permute-start(bf16[2048,128]{0,1:T(8,128)(2,1)S(1)} %pad_maximum_fusion.4), channel_id=1, source_target_pairs={{0,1},{1,0},{2,3},{3,2},{4,5},{5,4},{6,7},{7,6},{8,9},{9,8},{10,11... | collective-permute-start | bytes 1572872 | tf_op jit(solution)/shard_map/ppermute | solution.py:845
  559.2 8.6 %collective-permute-start.28 = (bf16[128,768]{1,0:T(8,128)(2,1)S(1)}, bf16[128,768]{1,0:T(8,128)(2,1)S(1)}, u32[]{:S(2)}, u32[]{:S(2)}) collective-permute-start(bf16[128,768]{1,0:T(8,128)(2,1)S(1)} %copy-done.85), channel_id=1, source_target_pairs={{0,24},{8,0},{16,8},{24,16},{1,25},{9,1},{17,9},{25,17},{2,26},{10... | collective-permute-start | bytes 589832 | tf_op jit(solution)/shard_map/ppermute | solution.py:680
  562.6 11.0 %collective-permute-start.30 = (bf16[128,768]{1,0:T(8,128)(2,1)S(1)}, bf16[128,768]{1,0:T(8,128)(2,1)S(1)}, u32[]{:S(2)}, u32[]{:S(2)}) collective-permute-start(bf16[128,768]{1,0:T(8,128)(2,1)S(1)} %copy-done.83), channel_id=1, source_target_pairs={{0,8},{8,16},{16,24},{24,0},{1,9},{9,17},{17,25},{25,1},{2,10},{10... | collective-permute-start | bytes 589832 | tf_op jit(solution)/shard_map/ppermute | solution.py:680
  568.0 9.3 %collective-permute-start.29 = (bf16[128,768]{1,0:T(8,128)(2,1)S(1)}, bf16[128,768]{1,0:T(8,128)(2,1)S(1)}, u32[]{:S(2)}, u32[]{:S(2)}) collective-permute-start(bf16[128,768]{1,0:T(8,128)(2,1)S(1)} %add_convert_fusion.2), channel_id=1, source_target_pairs={{0,24},{8,0},{16,8},{24,16},{1,25},{9,1},{17,9},{25,17},{2,26},{10... | collective-permute-start | bytes 589832 | tf_op jit(solution)/shard_map/ppermute | solution.py:680
  573.5 6.1 collective-permute-start.32
  577.3 8.4 %collective-permute-start.34 = (bf16[512,128]{0,1:T(8,128)(2,1)S(1)}, bf16[512,128]{0,1:T(8,128)(2,1)S(1)}, u32[]{:S(2)}, u32[]{:S(2)}) collective-permute-start(bf16[512,128]{0,1:T(8,128)(2,1)S(1)} %get-tuple-element.179), channel_id=1, source_target_pairs={{0,8},{8,16},{16,24},{24,0},{1,9},{9,17},{17,25},{25,1},{2,10},{10... | collective-permute-start | bytes 393224 | tf_op jit(solution)/shard_map/ppermute | solution.py:680
  579.7 7.2 %collective-permute-start.33 = (bf16[512,128]{0,1:T(8,128)(2,1)S(1)}, bf16[512,128]{0,1:T(8,128)(2,1)S(1)}, u32[]{:S(2)}, u32[]{:S(2)}) collective-permute-start(bf16[512,128]{0,1:T(8,128)(2,1)S(1)} %add_convert_fusion.3), channel_id=1, source_target_pairs={{0,24},{8,0},{16,8},{24,16},{1,25},{9,1},{17,9},{25,17},{2,26},{10... | collective-permute-start | bytes 393224 | tf_op jit(solution)/shard_map/ppermute | solution.py:680
  587.1 15.0 %collective-permute-start.35 = (bf16[512,512]{1,0:T(8,128)(2,1)S(1)}, bf16[512,512]{1,0:T(8,128)(2,1)S(1)}, u32[]{:S(2)}, u32[]{:S(2)}) collective-permute-start(bf16[512,512]{1,0:T(8,128)(2,1)S(1)} %get-tuple-element.158), channel_id=1, source_target_pairs={{0,24},{8,0},{16,8},{24,16},{1,25},{9,1},{17,9},{25,17},{2,26},{10... | collective-permute-start | bytes 1572872 | tf_op jit(solution)/shard_map/ppermute | solution.py:680
  602.1 16.7 %collective-permute-start.37 = (bf16[512,512]{1,0:T(8,128)(2,1)S(1)}, bf16[512,512]{1,0:T(8,128)(2,1)S(1)}, u32[]{:S(2)}, u32[]{:S(2)}) collective-permute-start(bf16[512,512]{1,0:T(8,128)(2,1)S(1)} %get-tuple-element.159), channel_id=1, source_target_pairs={{0,8},{8,16},{16,24},{24,0},{1,9},{9,17},{17,25},{25,1},{2,10},{10... | collective-permute-start | bytes 1572872 | tf_op jit(solution)/shard_map/ppermute | solution.py:680
  602.4 22.4 %collective-permute-start.36 = (bf16[512,512]{1,0:T(8,128)(2,1)S(1)}, bf16[512,512]{1,0:T(8,128)(2,1)S(1)}, u32[]{:S(2)}, u32[]{:S(2)}) collective-permute-start(bf16[512,512]{1,0:T(8,128)(2,1)S(1)} %add_convert_fusion), channel_id=1, source_target_pairs={{0,24},{8,0},{16,8},{24,16},{1,25},{9,1},{17,9},{25,17},{2,26},{10... | collective-permute-start | bytes 1572872 | tf_op jit(solution)/shard_map/ppermute | solution.py:680
  628.7 4.2 collective-permute-start.38
  632.9 5.3 collective-permute-start.39
  (106 other events, 649.5 us)
Sparse Core Ops, SparseCore 0:
  10.9 39.4 all-gather.4
  89.9 76.2 all-gather.6
  457.0 36.6 all-gather.8
  504.9 43.8 reduce-scatter.1

commit v5 on v4

--- a/solution.py
+++ b/solution.py
@@ -91,7 +91,7 @@
 def project(x, weights, cosine, sine, q_gain, k_gain):
     span, model = x.shape
     width = weights[0].shape[1] - 2 * HEAD_SIZE
-    tile = 512
+    tile = 256
     row = lambda w: pl.BlockSpec((tile, w), lambda i: (i, 0))
     whole = lambda a, b: pl.BlockSpec((a, b), lambda i: (0, 0))
     out = [(width, F32), (HEAD_SIZE, F32), (width, BF16), (HEAD_SIZE, BF16), (HEAD_SIZE, BF16)]
@@ -319,7 +319,7 @@
                   pl.BlockSpec((members, width, columns), lambda i: (0, 0, 0))],
         out_specs=pl.BlockSpec((tile, width), lambda i: (i, 0)),
         out_shape=jax.ShapeDtypeStruct((span, width), BF16),
-        compiler_params=pltpu.CompilerParams(vmem_limit_bytes=VMEM_BYTES),
+        compiler_params=pltpu.CompilerParams(vmem_limit_bytes=56 * 1024 * 1024),
         cost_estimate=cost(0),
         name="out_back",
     )(after_all, heads)
@@ -341,60 +341,44 @@
             out_specs=pl.BlockSpec((1, width, columns), lambda m, me: (m, 0, 0)),
         ),
         out_shape=jax.ShapeDtypeStruct((members, width, columns), BF16),
-        compiler_params=pltpu.CompilerParams(vmem_limit_bytes=VMEM_BYTES),
+        compiler_params=pltpu.CompilerParams(vmem_limit_bytes=56 * 1024 * 1024),
         cost_estimate=cost(0),
         name="out_gradient",
     )(member, attended_all, after_all)
 
 
 def expert_kernel(experts, own_ref, xa_ref, xb_ref, mask_ref, router_ref, gate_ref, up_ref, down_ref,
-                  act_ref, gg_ref, ug_ref, w_ref, route_ref, sum_ref):
+                  act_ref, gg_ref, ug_ref, w_ref, route_ref):
     half = xa_ref.shape[1]
-    step = pl.program_id(0)
     own = own_ref[0]
-
-    def product(left, right, weight):
-        return mm(left[...], weight[:half, :]) + mm(right[...], weight[half:, :])
-
-    @pl.when(step == 0)
-    def _():
-        mask = mask_ref[...].astype(F32)
-        logits = mm_t(xa_ref[...], router_ref[:, :half]) + mm_t(xb_ref[...], router_ref[:, half:])
-        logits = jnp.where(mask > 0, logits, VERY_NEGATIVE)
-        raised = jnp.where(mask > 0, jnp.exp(logits - jnp.max(logits, axis=-1, keepdims=True)), 0.0)
-        total = jnp.maximum(jnp.sum(raised, axis=-1, keepdims=True), 1e-30)
-        lanes = lax.broadcasted_iota(jnp.int32, raised.shape, 1)
-        weight = jnp.sum(jnp.where(lanes == own, raised, 0.0), axis=-1, keepdims=True) / total
-        w_ref[...] = jnp.broadcast_to(weight, w_ref.shape)
-
-    gate_raw, up_raw = product(xa_ref, xb_ref, gate_ref), product(xa_ref, xb_ref, up_ref)
-    down = down_ref[...]
-    weight = w_ref[:, :1]
+    xa, xb = xa_ref[...], xb_ref[...]
+
+    def product(weight):
+        return mm(xa, weight[:half, :]) + mm(xb, weight[half:, :])
+
+    gate_raw, up_raw = product(gate_ref), product(up_ref)
+    mask = mask_ref[...].astype(F32)
+    logits = mm_t(xa, router_ref[:, :half]) + mm_t(xb, router_ref[:, half:])
+    logits = jnp.where(mask > 0, logits, VERY_NEGATIVE)
+    raised = jnp.where(mask > 0, jnp.exp(logits - jnp.max(logits, axis=-1, keepdims=True)), 0.0)
+    total = jnp.maximum(jnp.sum(raised, axis=-1, keepdims=True), 1e-30)
+    lanes = lax.broadcasted_iota(jnp.int32, raised.shape, 1)
+    weight = jnp.sum(jnp.where(lanes == own, raised, 0.0), axis=-1, keepdims=True) / total
+    w_ref[...] = jnp.broadcast_to(weight, w_ref.shape)
+
     sig = 1.0 / (1.0 + jnp.exp(-gate_raw))
     silu = gate_raw * sig
     activated = (silu * up_raw).astype(BF16)
     act_ref[...] = activated
+    down = down_ref[...]
     route = jnp.sum(activated.astype(F32) * down, axis=-1, keepdims=True)
     grad = weight * down
     gg_ref[...] = (grad * up_raw * sig * (1.0 + gate_raw * (1.0 - sig))).astype(BF16)
     ug_ref[...] = (grad * silu).astype(BF16)
-    route = jnp.broadcast_to(route, sum_ref.shape)
-
-    @pl.when(step == 0)
-    def _():
-        sum_ref[...] = route
-
-    @pl.when(step > 0)
-    def _():
-        sum_ref[...] += route
-
-    @pl.when(step == pl.num_programs(0) - 1)
-    def _():
-        total = sum_ref[:, :1]
-        high = total.astype(BF16).astype(F32)
-        lanes = lax.broadcasted_iota(jnp.int32, route_ref.shape, 1)
-        route_ref[...] = jnp.where(
-            lanes == own, high, jnp.where(lanes == experts + own, total - high, 0.0)).astype(BF16)
+    high = route.astype(BF16).astype(F32)
+    lanes = lax.broadcasted_iota(jnp.int32, route_ref.shape, 1)
+    route_ref[...] = jnp.where(
+        lanes == own, high, jnp.where(lanes == experts + own, route - high, 0.0)).astype(BF16)
 
 
 def expert_forward(experts, own, xa, xb, masked_rows, router, gate, up, upstream_down):
@@ -402,25 +386,19 @@
     model, hidden = gate.shape
     padded = router.shape[0]
     route_width = -(-2 * experts // HEAD_SIZE) * HEAD_SIZE
-    tile = 256
+    tile = rows // 4
+    row = lambda w: pl.BlockSpec((tile, w), lambda i: (i, 0))
     whole = lambda a, b: pl.BlockSpec((a, b), lambda i: (0, 0))
-    column = lambda a: pl.BlockSpec((a, tile), lambda i: (0, i))
+    out = [(hidden, BF16), (hidden, BF16), (hidden, BF16), (HEAD_SIZE, F32), (route_width, BF16)]
     return pl.pallas_call(
         functools.partial(expert_kernel, experts),
-        grid=(hidden // tile,),
-        in_specs=[pl.BlockSpec(memory_space=pltpu.SMEM), whole(rows, half), whole(rows, half),
-                  pl.BlockSpec((rows, padded), lambda i: (0, half // padded)), whole(padded, model), column(model),
-                  column(model), column(rows)],
-        out_specs=[column(rows), column(rows), column(rows), whole(rows, HEAD_SIZE), whole(rows, route_width)],
-        out_shape=[
-            jax.ShapeDtypeStruct((rows, hidden), BF16),
-            jax.ShapeDtypeStruct((rows, hidden), BF16),
-            jax.ShapeDtypeStruct((rows, hidden), BF16),
-            jax.ShapeDtypeStruct((rows, HEAD_SIZE), F32),
-            jax.ShapeDtypeStruct((rows, route_width), BF16),
-        ],
-        scratch_shapes=[pltpu.VMEM((rows, HEAD_SIZE), F32)],
-        compiler_params=pltpu.CompilerParams(vmem_limit_bytes=40 * 1024 * 1024),
+        grid=(rows // tile,),
+        in_specs=[pl.BlockSpec(memory_space=pltpu.SMEM), row(half), row(half),
+                  pl.BlockSpec((tile, padded), lambda i: (i, half // padded)), whole(padded, model),
+                  whole(model, hidden), whole(model, hidden), row(hidden)],
+        out_specs=[row(w) for w, _ in out],
+        out_shape=[jax.ShapeDtypeStruct((rows, w), t) for w, t in out],
+        compiler_params=pltpu.CompilerParams(vmem_limit_bytes=32 * 1024 * 1024),
         cost_estimate=cost(18),
         name="expert_forward",
     )(own, xa, xb, masked_rows, router, gate, up, upstream_down)

time: 658 us -> 656 us (level)
  waiting for transfers between devices: 251 us -> 239 us
  starting transfers between devices: 122 us -> 133 us
    ppermute x6, waiting for transfers between devices: 37.6 us -> 26.3 us  [plane_sum_direct(): lax.ppermute(pieces[s], 'dp', [(i, (i - s) % planes) for i in range(plane...]
    ppermute x6, starting transfers between devices: 11.5 us -> 22.8 us  [plane_sum_direct(): lax.ppermute(pieces[s], 'dp', [(i, (i - s) % planes) for i in range(plane...]
  transfers between devices with their start and end apart: 55 -> 55, of which waited for: 40 -> 38; matrix products, arithmetic and copies ran while one was open for 7% -> 7% of each run, Pallas kernels for 18% -> 18%
where the time goes in v5:
time: 656 us; the launch traced here: 644 us
  waiting for transfers between devices  239 us (36%)
  Pallas kernels  137 us (21%)
  starting transfers between devices  133 us (20%)
  local copies, waits for them, and re-layouts  70.2 us (11%)
  other arithmetic  29.3 us (4%)
  between operations  16.6 us (3%)
  matrix products  10.6 us (2%)
  blocking collectives  9.01 us (1%)
    ppermute x30, waiting for transfers between devices, shift(): lax.ppermute(value, 'dp', [(i, (i + by) % planes) for i in range(planes)])  158 us
    ppermute x30, starting transfers between devices, shift(): lax.ppermute(value, 'dp', [(i, (i + by) % planes) for i in range(planes)])  60.3 us
    unnamed x246, local copies, waits for them, and re-layouts  54.3 us
    all_to_all x11, starting transfers between devices, exchange(): return lax.all_to_all(array, axis, split_axis=0, concat_axis=0, tiled=True)  46.9 us
    all_to_all x11, waiting for transfers between devices, exchange(): return lax.all_to_all(array, axis, split_axis=0, concat_axis=0, tiled=True)  39.3 us
    ppermute x6, waiting for transfers between devices, plane_sum_direct(): lax.ppermute(pieces[s], 'dp', [(i, (i - s) % planes) for i in range(plane...  26.3 us
    ppermute x6, starting transfers between devices, plane_sum_direct(): lax.ppermute(pieces[s], 'dp', [(i, (i - s) % planes) for i in range(plane...  22.8 us
    pallas_call x4, Pallas kernels, combine(): pl.pallas_call(combine_kernel, grid=(width // tile,), in_specs=[pl.BlockS...  16.7 us
  transfers between devices with their start and end apart: 55, of which 38 were waited for; matrix products, arithmetic and copies ran while one was open for 7% of the time, Pallas kernels for 18%

profile of v5, /device:TPU:0, one launch (start us, length us, event | category | flops | bytes accessed | tf_op | source)
XLA Modules:
  0.0 644.3 jit_solution(12997516698686570324)
XLA Ops:
  18.5 18.3 %collective-permute-done.1.refs_1_ = bf16[512,768]{1,0:T(8,128)(2,1)S(1)} collective-permute-done((bf16[512,768]{1,0:T(8,128)(2,1)S(1)}, bf16[512,768]{1,0:T(8,128)(2,1)S(1)}, u32[]{:S(2)}, u32[]{:S(2)}) %collective-permute-start.1) | collective-permute-done | bytes 786464 | tf_op jit(solution)/shard_map/ppermute | solution.py:641
  39.8 10.6 %all-gather.5.cloned.1.call-done.x_ref = bf16[1024,2048]{1,0:T(8,128)(2,1)} async-done(((bf16[128,2048]{1,0:T(8,128)(2,1)}), bf16[1024,2048]{1,0:T(8,128)(2,1)}) %all-gather.5.cloned.1.call-update) | async-done | bytes 4194320 | tf_op jit(solution)/shard_map/all_gather | solution.py:634
  50.3 9.0 %all-gather = bf16[8,4,512]{2,1,0:T(4,128)(2,1)S(1)} all-gather(bf16[1,4,512]{2,1,0:T(4,128)(2,1)S(1)} %bitcast.114), channel_id=1, replica_groups=mesh['dp'=4,'expert'=8] {'expert'}, dimensions={0}, use_global_device_ids=true | all-gather | bytes 36864 | tf_op jit(solution)/shard_map/all_gather | solution.py:634
  59.4 10.8 %collective-permute-done.2.refs_2_ = bf16[512,768]{1,0:T(8,128)(2,1)} collective-permute-done((bf16[512,768]{1,0:T(8,128)(2,1)S(1)}, bf16[512,768]{1,0:T(8,128)(2,1)}, u32[]{:S(2)}, u32[]{:S(2)}) %collective-permute-start.2) | collective-permute-done | bytes 786464 | tf_op jit(solution)/shard_map/ppermute | solution.py:641
  72.4 6.6 %project.1 = (f32[1024,512]{1,0:T(8,128)S(1)}, f32[1024,128]{1,0:T(8,128)S(1)}, bf16[1024,512]{1,0:T(8,128)(2,1)S(1)}, bf16[1024,128]{1,0:T(8,128)(2,1)S(1)}, bf16[1024,128]{1,0:T(8,128)(2,1)S(1)}) custom-call(bf16[1024,2048]{1,0:T(8,128)(2,1)S(1)} %copy-done, f32[1024,128]{1,0:T(8,128)S(1)} %get-tuple-element.218.cos_ref, ...), custom_call_target="tpu_custom_call" | custom-call | flops 1 | bytes 1 | tf_op jit(solution)/shard_map/project/pallas_call | solution.py:98
  80.4 5.9 attend.1
  89.6 3.8 collective-permute-start.6
  93.5 7.9 %collective-permute-done.4.refs_1_ = bf16[128,1152]{1,0:T(8,128)(2,1)S(1)} collective-permute-done((bf16[128,1152]{1,0:T(8,128)(2,1)S(1)}, bf16[128,1152]{1,0:T(8,128)(2,1)S(1)}, u32[]{:S(2)}, u32[]{:S(2)}) %collective-permute-start.4) | collective-permute-done | bytes 294944 | tf_op jit(solution)/shard_map/ppermute | solution.py:641
  101.7 4.9 collective-permute-done.6.refs_3_
  106.8 3.6 collective-permute-done.5.refs_2_
  115.1 4.5 all-to-all-start
  119.7 3.8 collective-permute-start.9
  123.5 12.8 %collective-permute-done.7.refs_1_ = bf16[1024,256]{1,0:T(8,128)(2,1)S(1)} collective-permute-done((bf16[1024,256]{1,0:T(8,128)(2,1)S(1)}, bf16[1024,256]{1,0:T(8,128)(2,1)S(1)}, u32[]{:S(2)}, u32[]{:S(2)}) %collective-permute-start.7) | collective-permute-done | bytes 524320 | tf_op jit(solution)/shard_map/ppermute | solution.py:641
  138.2 7.0 %collective-permute-done.9.refs_3_ = bf16[1024,256]{1,0:T(8,128)(2,1)S(1)} collective-permute-done((bf16[1024,256]{1,0:T(8,128)(2,1)S(1)}, bf16[1024,256]{1,0:T(8,128)(2,1)S(1)}, u32[]{:S(2)}, u32[]{:S(2)}) %collective-permute-start.9) | collective-permute-done | bytes 524320 | tf_op jit(solution)/shard_map/ppermute | solution.py:641
  145.2 13.0 %collective-permute-done.8.refs_2_ = bf16[1024,256]{1,0:T(8,128)(2,1)S(1)} collective-permute-done((bf16[1024,256]{1,0:T(8,128)(2,1)S(1)}, bf16[1024,256]{1,0:T(8,128)(2,1)S(1)}, u32[]{:S(2)}, u32[]{:S(2)}) %collective-permute-start.8) | collective-permute-done | bytes 524320 | tf_op jit(solution)/shard_map/ppermute | solution.py:641
  158.2 3.8 collective-permute-start.11
  162.0 8.2 %collective-permute-done.10.refs_1_ = bf16[144,1024]{1,0:T(8,128)(2,1)} collective-permute-done((bf16[144,1024]{1,0:T(8,128)(2,1)}, bf16[144,1024]{1,0:T(8,128)(2,1)}, u32[]{:S(2)}, u32[]{:S(2)}) %collective-permute-start.10) | collective-permute-done | bytes 294944 | tf_op jit(solution)/shard_map/ppermute | solution.py:641
  181.4 3.7 all-to-all-start.1
  189.8 5.0 all-to-all-done.1
  194.8 4.4 all-to-all-start.2
  200.8 3.8 collective-permute-start.15
  204.6 7.1 %collective-permute-done.13.refs_1_ = bf16[128,1024]{1,0:T(8,128)(2,1)S(1)} collective-permute-done((bf16[128,1024]{1,0:T(8,128)(2,1)S(1)}, bf16[128,1024]{1,0:T(8,128)(2,1)S(1)}, u32[]{:S(2)}, u32[]{:S(2)}) %collective-permute-start.13) | collective-permute-done | bytes 262176 | tf_op jit(solution)/shard_map/ppermute | solution.py:641
  211.8 5.2 collective-permute-start.14
  217.0 8.1 %collective-permute-done.14.refs_2_ = bf16[128,1024]{1,0:T(8,128)(2,1)S(1)} collective-permute-done((bf16[128,1024]{1,0:T(8,128)(2,1)S(1)}, bf16[128,1024]{1,0:T(8,128)(2,1)S(1)}, u32[]{:S(2)}, u32[]{:S(2)}) %collective-permute-start.14) | collective-permute-done | bytes 262176 | tf_op jit(solution)/shard_map/ppermute | solution.py:641
  230.1 4.4 all-to-all-start.3
  234.6 3.8 collective-permute-start.18
  238.4 7.1 %collective-permute-done.16.refs_1_ = bf16[128,1024]{1,0:T(8,128)(2,1)S(1)} collective-permute-done((bf16[128,1024]{1,0:T(8,128)(2,1)S(1)}, bf16[128,1024]{1,0:T(8,128)(2,1)S(1)}, u32[]{:S(2)}, u32[]{:S(2)}) %collective-permute-start.16) | collective-permute-done | bytes 262176 | tf_op jit(solution)/shard_map/ppermute | solution.py:641
  245.5 4.9 collective-permute-start.17
  250.5 8.0 %collective-permute-done.17.refs_2_ = bf16[128,1024]{1,0:T(8,128)(2,1)S(1)} collective-permute-done((bf16[128,1024]{1,0:T(8,128)(2,1)S(1)}, bf16[128,1024]{1,0:T(8,128)(2,1)S(1)}, u32[]{:S(2)}, u32[]{:S(2)}) %collective-permute-start.17) | collective-permute-done | bytes 262176 | tf_op jit(solution)/shard_map/ppermute | solution.py:641
  265.4 4.7 all-to-all-start.4
  274.2 7.3 %down_back.1.down_ref = f32[1216,768]{1,0:T(8,128)S(1)} custom-call(bf16[1216,1152]{1,0:T(8,128)(2,1)} %bitcast.9.ca_ref.mask_ref, bf16[1216,1024]{1,0:T(8,128)(2,1)} %bitcast.15.cb_ref, bf16[768,2048]{1,0:T(8,128)(2,1)S(1)} %bitcast.77), custom_call_target="tpu_custom_call" | custom-call | flops 1 | bytes 1 | tf_op jit(solution)/shard_map/down_back/pallas_call | solution.py:445
  284.8 16.1 %all-to-all-done.4 = bf16[8,152,1024]{2,1,0:T(8,128)(2,1)} async-done(((bf16[8,152,1024]{2,1,0:T(8,128)(2,1)}), bf16[8,152,1024]{2,1,0:T(8,128)(2,1)}, u32[]{:S(2)}, u32[]{:S(2)}) %all-to-all-start.4) | async-done | bytes 2490400 | tf_op jit(solution)/shard_map/all_to_all | solution.py:637
  300.9 4.3 all-to-all-start.8
  310.1 13.0 %expert_forward.1 = (bf16[1216,768]{1,0:T(8,128)(2,1)S(1)}, bf16[1216,768]{1,0:T(8,128)(2,1)S(1)}, bf16[1216,768]{1,0:T(8,128)(2,1)S(1)}, f32[1216,128]{1,0:T(8,128)S(1)}, bf16[1216,128]{1,0:T(8,128)(2,1)S(1)}) custom-call(s32[1]{0:T(128)} %bitcast.13.own_ref, bf16[1216,1024]{1,0:T(8,128)(2,1)} %bitcast.17.xa_ref, bf16[1216,1024]{1,0:T(8,128)(2,1)} %bitcast.19.xb_ref, ...), custom_call_target="tpu_custom_call" | custom-call | flops 19800000512 | bytes 1 | tf_op jit(solution)/shard_map/expert_forward/pallas_call | solution.py:393
  325.2 3.7 row_gradient.2
  332.9 4.4 all-to-all-start.5
  349.2 5.6 row_gradient.3
  356.5 8.2 %all-to-all-done.5 = bf16[8,152,896]{2,1,0:T(8,128)(2,1)} async-done(((bf16[8,152,896]{2,1,0:T(8,128)(2,1)}), bf16[8,152,896]{2,1,0:T(8,128)(2,1)}, u32[]{:S(2)}, u32[]{:S(2)}) %all-to-all-start.5) | async-done | bytes 2179104 | tf_op jit(solution)/shard_map/all_to_all | solution.py:637
  364.8 4.5 all-to-all-start.7
  370.5 6.2 combine.4
  383.0 4.6 produce.1
  390.6 10.7 %collective-permute-done.20 = bf16[128,896]{1,0:T(8,128)(2,1)S(1)} collective-permute-done((bf16[128,896]{1,0:T(8,128)(2,1)S(1)}, bf16[128,896]{1,0:T(8,128)(2,1)S(1)}, u32[]{:S(2)}, u32[]{:S(2)}) %collective-permute-start.20) | collective-permute-done | bytes 229408 | tf_op jit(solution)/shard_map/ppermute | solution.py:653
  403.0 3.8 all-to-all-done.7
  406.8 3.6 all-to-all-start.6
  411.8 4.9 combine.5
  420.5 13.3 %collective-permute-start.24 = (bf16[128,1280]{1,0:T(8,128)(2,1)S(1)}, bf16[128,1280]{1,0:T(8,128)(2,1)S(1)}, u32[]{:S(2)}, u32[]{:S(2)}) collective-permute-start(bf16[128,1280]{1,0:T(8,128)(2,1)S(1)} %get-tuple-element.120), channel_id=1, source_target_pairs={{0,8},{8,16},{16,24},{24,0},{1,9},{9,17},{17,25},{25,1},{2,10},{10... | collective-permute-start | bytes 983048 | tf_op jit(solution)/shard_map/ppermute | solution.py:653
  434.2 15.5 %collective-permute-done.23 = bf16[128,1280]{1,0:T(8,128)(2,1)S(1)} collective-permute-done((bf16[128,1280]{1,0:T(8,128)(2,1)S(1)}, bf16[128,1280]{1,0:T(8,128)(2,1)S(1)}, u32[]{:S(2)}, u32[]{:S(2)}) %collective-permute-start.23) | collective-permute-done | bytes 327712 | tf_op jit(solution)/shard_map/ppermute | solution.py:653
  462.0 7.4 %collective-permute-done.25 = bf16[128,1280]{1,0:T(8,128)(2,1)S(1)} collective-permute-done((bf16[128,1280]{1,0:T(8,128)(2,1)S(1)}, bf16[128,1280]{1,0:T(8,128)(2,1)S(1)}, u32[]{:S(2)}, u32[]{:S(2)}) %collective-permute-start.25) | collective-permute-done | bytes 327712 | tf_op jit(solution)/shard_map/ppermute | solution.py:658
  469.4 3.7 collective-permute-start.26
  475.7 13.5 %hidden_gradient.1 = (f32[1,2048,768]{2,1,0:T(8,128)}, f32[1,2048,768]{2,1,0:T(8,128)}) custom-call(bf16[1216,1024]{1,0:T(8,128)(2,1)} %bitcast.17.xa_ref, bf16[1216,1024]{1,0:T(8,128)(2,1)} %bitcast.19.xb_ref, bf16[1216,768]{1,0:T(8,128)(2,1)S(1)} %copy-done.51, bf16[1216,768]{1,0:T(8,128)(2,1)S(1)} %copy-done.54), custom_call_target="tpu_custom_call" | custom-call | flops 1 | bytes 1 | tf_op jit(solution)/shard_map/hidden_gradient/pallas_call | solution.py:497
  491.8 8.8 %out_gradient.1 = bf16[8,512,256]{2,1,0:T(8,128)(2,1)} custom-call(s32[1]{0:T(128)} %bitcast.33.member_ref, bf16[8,1024,512]{2,1,0:T(8,128)(2,1)} %bitcast.75, bf16[1024,2048]{1,0:T(8,128)(2,1)} %all-gather.9.cloned.1.call-done.g_ref), custom_call_target="tpu_custom_call" | custom-call | flops 1 | bytes 1 | tf_op jit(solution)/shard_map/out_gradient/pallas_call | solution.py:334
  504.5 5.8 out_back.1.do_ref
  513.2 13.9 %attend_back.1 = (bf16[1024,512]{1,0:T(8,128)(2,1)S(1)}, bf16[1024,128]{1,0:T(8,128)(2,1)S(1)}, bf16[1024,128]{1,0:T(8,128)(2,1)S(1)}, f32[1,128]{1,0:T(1,128)S(1)}, f32[1,128]{1,0:T(1,128)S(1)}) custom-call(s32[1]{0:T(128)S(6)} %copy.94.prefix_ref, bf16[1024,512]{1,0:T(8,128)(2,1)S(1)} %copy-done.24, bf16[1024,128]{1,0:T(8,128)(2,1)S(1)} %copy-done.60, ...), custom_call_target="tpu_custom_call" | custom-call | flops 1 | bytes 1 | tf_op jit(solution)/shard_map/attend_back/pallas_call | solution.py:207
  527.2 6.9 %unproject.1 = bf16[8,144,2048]{2,1,0:T(8,128)(2,1)} custom-call(bf16[1024,512]{1,0:T(8,128)(2,1)S(1)} %get-tuple-element.136.dq_ref, bf16[1024,128]{1,0:T(8,128)(2,1)S(1)} %get-tuple-element.137.dk_ref, bf16[1024,128]{1,0:T(8,128)(2,1)S(1)} %get-tuple-element.138.dv_ref, bf16[1024,2048]{1,0:T(8,128)(2,1)S(1)} %copy-done.1, f32[1,2048]{1,0:T(1,128)S(1)} %bitcast.91, ...), custom_call_target="tpu_custom_call" | custom-call | flops 1 | bytes 1 | tf_op jit(solution)/shard_map/unproject/pallas_call | solution.py:262
  545.3 3.8 convolution_convert_fusion
  551.2 4.8 all-to-all-start.10
  560.5 5.0 collective-permute-done.28
  565.6 4.3 collective-permute-start.29
  577.3 4.3 collective-permute-start.33
  584.7 3.9 collective-permute-start.35
  588.7 11.1 %down_gradient.1 = f32[1,768,2048]{2,1,0:T(8,128)} custom-call(bf16[1216,1152]{1,0:T(8,128)(2,1)} %bitcast.9.ca_ref.mask_ref, bf16[1216,1024]{1,0:T(8,128)(2,1)} %bitcast.15.cb_ref, f32[1216,128]{1,0:T(8,128)S(1)} %copy-done.34, bf16[1216,768]{1,0:T(8,128)(2,1)S(1)} %copy-done.15), custom_call_target="tpu_custom_call" | custom-call | flops 1 | bytes 1 | tf_op jit(solution)/shard_map/down_gradient/pallas_call | solution.py:523
  600.1 3.9 collective-permute-start.36
  604.7 11.8 %collective-permute-done.37 = bf16[512,512]{1,0:T(8,128)(2,1)S(1)} collective-permute-done((bf16[512,512]{1,0:T(8,128)(2,1)S(1)}, bf16[512,512]{1,0:T(8,128)(2,1)S(1)}, u32[]{:S(2)}, u32[]{:S(2)}) %collective-permute-start.37) | collective-permute-done | bytes 524320 | tf_op jit(solution)/shard_map/ppermute | solution.py:658
  616.6 5.8 collective-permute-done.36
  (440 shorter events, 174.3 us)
Async XLA Ops:
  7.2 43.1 %all-gather.5.cloned.1.call-start = ((), (), s32[]{:S(2)}) async-start(), calls=%async_computation.12 | async-start | bytes 4718592 | tf_op jit(solution)/shard_map/all_gather | solution.py:634
  10.8 162.5 %all-gather.7.cloned.1.call-start = ((), (), s32[]{:S(2)}) async-start(), calls=%async_computation.13 | async-start | bytes 9437184 | tf_op jit(solution)/shard_map/all_gather | solution.py:634
  11.2 1.5 collective-permute-start
  13.4 65.5 %copy-start.16 = (bf16[512,768]{1,0:T(8,128)(2,1)}, bf16[512,768]{1,0:T(8,128)(2,1)S(1)}, u32[]{:S(2)}) copy-start(bf16[512,768]{1,0:T(8,128)(2,1)S(1)} %concatenate.65.refs_0_) | copy-start | bytes 2359300
  13.4 36.9 %copy-start.113 = (bf16[512,4]{0,1:T(4,128)(2,1)S(1)}, bf16[512,4]{0,1:T(4,128)(2,1)}, u32[]{:S(2)}) copy-start(bf16[512,4]{0,1:T(4,128)(2,1)} %param.23) | copy-start | bytes 12292
  13.4 56.7 %copy-start.72 = (f32[128]{0:T(128)S(1)}, f32[128]{0:T(128)}, u32[]{:S(2)}) copy-start(f32[128]{0:T(128)} %param.26) | copy-start | bytes 1540
  13.4 56.7 %copy-start.74 = (f32[128]{0:T(128)S(1)}, f32[128]{0:T(128)}, u32[]{:S(2)}) copy-start(f32[128]{0:T(128)} %param.27) | copy-start | bytes 1540
  13.5 23.4 %collective-permute-start.1 = (bf16[512,768]{1,0:T(8,128)(2,1)S(1)}, bf16[512,768]{1,0:T(8,128)(2,1)S(1)}, u32[]{:S(2)}, u32[]{:S(2)}) collective-permute-start(bf16[512,768]{1,0:T(8,128)(2,1)S(1)} %concatenate.65.refs_0_), channel_id=1, source_target_pairs={{0,8},{8,16},{16,24},{24,0},{1,9},{9,17},{17,25},{25,1},{2,10},{10... | collective-permute-start | bytes 2359304 | tf_op jit(solution)/shard_map/ppermute | solution.py:641
  16.4 42.9 %collective-permute-start.3 = (bf16[512,768]{1,0:T(8,128)(2,1)S(1)}, bf16[512,768]{1,0:T(8,128)(2,1)S(1)}, u32[]{:S(2)}, u32[]{:S(2)}) collective-permute-start(bf16[512,768]{1,0:T(8,128)(2,1)S(1)} %concatenate.65.refs_0_), channel_id=1, source_target_pairs={{0,24},{8,0},{16,8},{24,16},{1,25},{9,1},{17,9},{25,17},{2,26},{10... | collective-permute-start | bytes 2359304 | tf_op jit(solution)/shard_map/ppermute | solution.py:641
  36.8 42.1 %copy-start.26 = (bf16[512,768]{1,0:T(8,128)(2,1)}, bf16[512,768]{1,0:T(8,128)(2,1)S(1)}, u32[]{:S(2)}) copy-start(bf16[512,768]{1,0:T(8,128)(2,1)S(1)} %collective-permute-done.1.refs_1_) | copy-start | bytes 2359300
  36.8 33.3 %collective-permute-start.2 = (bf16[512,768]{1,0:T(8,128)(2,1)S(1)}, bf16[512,768]{1,0:T(8,128)(2,1)}, u32[]{:S(2)}, u32[]{:S(2)}) collective-permute-start(bf16[512,768]{1,0:T(8,128)(2,1)S(1)} %collective-permute-done.1.refs_1_), channel_id=1, source_target_pairs={{0,8},{8,16},{16,24},{24,0},{1,9},{9,17},{17,25},{25,1},{2,10},{10... | collective-permute-start | bytes 2359304 | tf_op jit(solution)/shard_map/ppermute | solution.py:641
  39.8 39.2 %copy-start.18 = (f32[1024,128]{1,0:T(8,128)}, f32[1024,128]{1,0:T(8,128)S(1)}, u32[]{:S(2)}) copy-start(f32[1024,128]{1,0:T(8,128)S(1)} %get-tuple-element.218.cos_ref) | copy-start | bytes 1572868
  39.8 39.2 %copy-start.20 = (f32[1024,128]{1,0:T(8,128)}, f32[1024,128]{1,0:T(8,128)S(1)}, u32[]{:S(2)}) copy-start(f32[1024,128]{1,0:T(8,128)S(1)} %get-tuple-element.219.sin_ref) | copy-start | bytes 1572868
  89.5 11.9 %collective-permute-start.4 = (bf16[128,1152]{1,0:T(8,128)(2,1)S(1)}, bf16[128,1152]{1,0:T(8,128)(2,1)S(1)}, u32[]{:S(2)}, u32[]{:S(2)}) collective-permute-start(bf16[128,1152]{1,0:T(8,128)(2,1)S(1)} %fusion.19.refs_0_), channel_id=1, source_target_pairs={{0,8},{8,16},{16,24},{24,0},{1,9},{9,17},{17,25},{25,1},{2,10},{10... | collective-permute-start | bytes 884744 | tf_op jit(solution)/shard_map/ppermute | solution.py:641
  89.6 17.0 %collective-permute-start.6 = (bf16[128,1152]{1,0:T(8,128)(2,1)S(1)}, bf16[128,1152]{1,0:T(8,128)(2,1)S(1)}, u32[]{:S(2)}, u32[]{:S(2)}) collective-permute-start(bf16[128,1152]{1,0:T(8,128)(2,1)S(1)} %fusion.19.refs_0_), channel_id=1, source_target_pairs={{0,24},{8,0},{16,8},{24,16},{1,25},{9,1},{17,9},{25,17},{2,26},{10... | collective-permute-start | bytes 884744 | tf_op jit(solution)/shard_map/ppermute | solution.py:641
  101.4 9.0 %collective-permute-start.5 = (bf16[128,1152]{1,0:T(8,128)(2,1)S(1)}, bf16[128,1152]{1,0:T(8,128)(2,1)S(1)}, u32[]{:S(2)}, u32[]{:S(2)}) collective-permute-start(bf16[128,1152]{1,0:T(8,128)(2,1)S(1)} %collective-permute-done.4.refs_1_), channel_id=1, source_target_pairs={{0,8},{8,16},{16,24},{24,0},{1,9},{9,17},{17,25},{25,1},{2,10},{10... | collective-permute-start | bytes 884744 | tf_op jit(solution)/shard_map/ppermute | solution.py:641
  115.1 56.4 %all-to-all-start = ((bf16[8,152,1152]{2,1,0:T(8,128)(2,1)}), bf16[8,152,1152]{2,1,0:T(8,128)(2,1)}, u32[]{:S(2)}, u32[]{:S(2)}) async-start(bf16[8,152,1152]{2,1,0:T(8,128)(2,1)} %bitcast.80), calls=%async_computation | async-start | bytes 5603328 | tf_op jit(solution)/shard_map/all_to_all | solution.py:637
  119.7 16.6 %collective-permute-start.7 = (bf16[1024,256]{1,0:T(8,128)(2,1)S(1)}, bf16[1024,256]{1,0:T(8,128)(2,1)S(1)}, u32[]{:S(2)}, u32[]{:S(2)}) collective-permute-start(bf16[1024,256]{1,0:T(8,128)(2,1)S(1)} %copy-done.40), channel_id=1, source_target_pairs={{0,8},{8,16},{16,24},{24,0},{1,9},{9,17},{17,25},{25,1},{2,10},{10... | collective-permute-start | bytes 1572872 | tf_op jit(solution)/shard_map/ppermute | solution.py:641
  119.7 25.4 %collective-permute-start.9 = (bf16[1024,256]{1,0:T(8,128)(2,1)S(1)}, bf16[1024,256]{1,0:T(8,128)(2,1)S(1)}, u32[]{:S(2)}, u32[]{:S(2)}) collective-permute-start(bf16[1024,256]{1,0:T(8,128)(2,1)S(1)} %copy-done.40), channel_id=1, source_target_pairs={{0,24},{8,0},{16,8},{24,16},{1,25},{9,1},{17,9},{25,17},{2,26},{10... | collective-permute-start | bytes 1572872 | tf_op jit(solution)/shard_map/ppermute | solution.py:641
  136.3 43.8 %copy-start.44 = (bf16[1024,256]{1,0:T(8,128)(2,1)}, bf16[1024,256]{1,0:T(8,128)(2,1)S(1)}, u32[]{:S(2)}) copy-start(bf16[1024,256]{1,0:T(8,128)(2,1)S(1)} %collective-permute-done.7.refs_1_) | copy-start | bytes 1572868
  136.3 21.9 %collective-permute-start.8 = (bf16[1024,256]{1,0:T(8,128)(2,1)S(1)}, bf16[1024,256]{1,0:T(8,128)(2,1)S(1)}, u32[]{:S(2)}, u32[]{:S(2)}) collective-permute-start(bf16[1024,256]{1,0:T(8,128)(2,1)S(1)} %collective-permute-done.7.refs_1_), channel_id=1, source_target_pairs={{0,8},{8,16},{16,24},{24,0},{1,9},{9,17},{17,25},{25,1},{2,10},{10... | collective-permute-start | bytes 1572872 | tf_op jit(solution)/shard_map/ppermute | solution.py:641
  145.2 35.0 %copy-start.42 = (bf16[1024,256]{1,0:T(8,128)(2,1)}, bf16[1024,256]{1,0:T(8,128)(2,1)S(1)}, u32[]{:S(2)}) copy-start(bf16[1024,256]{1,0:T(8,128)(2,1)S(1)} %collective-permute-done.9.refs_3_) | copy-start | bytes 1572868
  158.2 12.1 %collective-permute-start.10 = (bf16[144,1024]{1,0:T(8,128)(2,1)}, bf16[144,1024]{1,0:T(8,128)(2,1)}, u32[]{:S(2)}, u32[]{:S(2)}) collective-permute-start(bf16[144,1024]{1,0:T(8,128)(2,1)} %pad_maximum_fusion.5.refs_0_), channel_id=1, source_target_pairs={{0,8},{8,16},{16,24},{24,0},{1,9},{9,17},{17,25},{25,1},{2,10},{10... | collective-permute-start | bytes 884744 | tf_op jit(solution)/shard_map/ppermute | solution.py:641
  158.2 15.1 %collective-permute-start.11 = (bf16[144,1024]{1,0:T(8,128)(2,1)}, bf16[144,1024]{1,0:T(8,128)(2,1)}, u32[]{:S(2)}, u32[]{:S(2)}) collective-permute-start(bf16[144,1024]{1,0:T(8,128)(2,1)} %pad_maximum_fusion.5.refs_0_), channel_id=1, source_target_pairs={{0,24},{8,0},{16,8},{24,16},{1,25},{9,1},{17,9},{25,17},{2,26},{10... | collective-permute-start | bytes 884744 | tf_op jit(solution)/shard_map/ppermute | solution.py:641
  170.2 11.2 %collective-permute-start.12 = (bf16[144,1024]{1,0:T(8,128)(2,1)}, bf16[144,1024]{1,0:T(8,128)(2,1)}, u32[]{:S(2)}, u32[]{:S(2)}) collective-permute-start(bf16[144,1024]{1,0:T(8,128)(2,1)} %collective-permute-done.10.refs_1_), channel_id=1, source_target_pairs={{0,8},{8,16},{16,24},{24,0},{1,9},{9,17},{17,25},{25,1},{2,10},{10... | collective-permute-start | bytes 884744 | tf_op jit(solution)/shard_map/ppermute | solution.py:641
  181.4 13.4 %all-to-all-start.1 = ((bf16[8,128,256]{2,1,0:T(8,128)(2,1)}), bf16[8,128,256]{2,1,0:T(8,128)(2,1)S(1)}, u32[]{:S(2)}, u32[]{:S(2)}) async-start(bf16[8,128,256]{2,1,0:T(8,128)(2,1)} %bitcast.88), calls=%async_computation.1 | async-start | bytes 1048576 | tf_op jit(solution)/shard_map/all_to_all | solution.py:637
  194.8 35.3 %all-to-all-start.2 = ((bf16[8,152,1024]{2,1,0:T(8,128)(2,1)}), bf16[8,152,1024]{2,1,0:T(8,128)(2,1)}, u32[]{:S(2)}, u32[]{:S(2)}) async-start(bf16[8,152,1024]{2,1,0:T(8,128)(2,1)} %bitcast.82), calls=%async_computation.2 | async-start | bytes 4980736 | tf_op jit(solution)/shard_map/all_to_all | solution.py:637
  200.8 11.0 %collective-permute-start.13 = (bf16[128,1024]{1,0:T(8,128)(2,1)S(1)}, bf16[128,1024]{1,0:T(8,128)(2,1)S(1)}, u32[]{:S(2)}, u32[]{:S(2)}) collective-permute-start(bf16[128,1024]{1,0:T(8,128)(2,1)S(1)} %get-tuple-element.181.refs_0_), channel_id=1, source_target_pairs={{0,8},{8,16},{16,24},{24,0},{1,9},{9,17},{17,25},{25,1},{2,10},{10... | collective-permute-start | bytes 786440 | tf_op jit(solution)/shard_map/ppermute | solution.py:641
  200.8 16.2 %collective-permute-start.15 = (bf16[128,1024]{1,0:T(8,128)(2,1)S(1)}, bf16[128,1024]{1,0:T(8,128)(2,1)S(1)}, u32[]{:S(2)}, u32[]{:S(2)}) collective-permute-start(bf16[128,1024]{1,0:T(8,128)(2,1)S(1)} %get-tuple-element.181.refs_0_), channel_id=1, source_target_pairs={{0,24},{8,0},{16,8},{24,16},{1,25},{9,1},{17,9},{25,17},{2,26},{10... | collective-permute-start | bytes 786440 | tf_op jit(solution)/shard_map/ppermute | solution.py:641
  211.8 13.3 %collective-permute-start.14 = (bf16[128,1024]{1,0:T(8,128)(2,1)S(1)}, bf16[128,1024]{1,0:T(8,128)(2,1)S(1)}, u32[]{:S(2)}, u32[]{:S(2)}) collective-permute-start(bf16[128,1024]{1,0:T(8,128)(2,1)S(1)} %collective-permute-done.13.refs_1_), channel_id=1, source_target_pairs={{0,8},{8,16},{16,24},{24,0},{1,9},{9,17},{17,25},{25,1},{2,10},{10... | collective-permute-start | bytes 786440 | tf_op jit(solution)/shard_map/ppermute | solution.py:641
  230.1 35.3 %all-to-all-start.3 = ((bf16[8,152,1024]{2,1,0:T(8,128)(2,1)}), bf16[8,152,1024]{2,1,0:T(8,128)(2,1)}, u32[]{:S(2)}, u32[]{:S(2)}) async-start(bf16[8,152,1024]{2,1,0:T(8,128)(2,1)} %bitcast.83), calls=%async_computation.3 | async-start | bytes 4980736 | tf_op jit(solution)/shard_map/all_to_all | solution.py:637
  234.5 11.0 %collective-permute-start.16 = (bf16[128,1024]{1,0:T(8,128)(2,1)S(1)}, bf16[128,1024]{1,0:T(8,128)(2,1)S(1)}, u32[]{:S(2)}, u32[]{:S(2)}) collective-permute-start(bf16[128,1024]{1,0:T(8,128)(2,1)S(1)} %get-tuple-element.180.refs_0_), channel_id=1, source_target_pairs={{0,8},{8,16},{16,24},{24,0},{1,9},{9,17},{17,25},{25,1},{2,10},{10... | collective-permute-start | bytes 786440 | tf_op jit(solution)/shard_map/ppermute | solution.py:641
  234.6 15.9 %collective-permute-start.18 = (bf16[128,1024]{1,0:T(8,128)(2,1)S(1)}, bf16[128,1024]{1,0:T(8,128)(2,1)S(1)}, u32[]{:S(2)}, u32[]{:S(2)}) collective-permute-start(bf16[128,1024]{1,0:T(8,128)(2,1)S(1)} %get-tuple-element.180.refs_0_), channel_id=1, source_target_pairs={{0,24},{8,0},{16,8},{24,16},{1,25},{9,1},{17,9},{25,17},{2,26},{10... | collective-permute-start | bytes 786440 | tf_op jit(solution)/shard_map/ppermute | solution.py:641
  245.5 12.9 %collective-permute-start.17 = (bf16[128,1024]{1,0:T(8,128)(2,1)S(1)}, bf16[128,1024]{1,0:T(8,128)(2,1)S(1)}, u32[]{:S(2)}, u32[]{:S(2)}) collective-permute-start(bf16[128,1024]{1,0:T(8,128)(2,1)S(1)} %collective-permute-done.16.refs_1_), channel_id=1, source_target_pairs={{0,8},{8,16},{16,24},{24,0},{1,9},{9,17},{17,25},{25,1},{2,10},{10... | collective-permute-start | bytes 786440 | tf_op jit(solution)/shard_map/ppermute | solution.py:641
  265.4 35.5 %all-to-all-start.4 = ((bf16[8,152,1024]{2,1,0:T(8,128)(2,1)}), bf16[8,152,1024]{2,1,0:T(8,128)(2,1)}, u32[]{:S(2)}, u32[]{:S(2)}) async-start(bf16[8,152,1024]{2,1,0:T(8,128)(2,1)} %bitcast.81), calls=%async_computation.4 | async-start | bytes 4980736 | tf_op jit(solution)/shard_map/all_to_all | solution.py:637
  300.9 31.9 %all-to-all-start.8 = ((bf16[8,512,256]{2,1,0:T(8,128)(2,1)}), bf16[8,512,256]{2,1,0:T(8,128)(2,1)}, u32[]{:S(2)}, u32[]{:S(2)}) async-start(bf16[8,512,256]{2,1,0:T(8,128)(2,1)} %bitcast.103), calls=%async_computation.8 | async-start | bytes 4194304 | tf_op jit(solution)/shard_map/all_to_all | solution.py:637
  332.9 31.9 %all-to-all-start.5 = ((bf16[8,152,896]{2,1,0:T(8,128)(2,1)}), bf16[8,152,896]{2,1,0:T(8,128)(2,1)}, u32[]{:S(2)}, u32[]{:S(2)}) async-start(bf16[8,152,896]{2,1,0:T(8,128)(2,1)} %bitcast.87), calls=%async_computation.5 | async-start | bytes 4358144 | tf_op jit(solution)/shard_map/all_to_all | solution.py:637
  364.8 42.0 %all-to-all-start.7 = ((bf16[8,152,1280]{2,1,0:T(8,128)(2,1)}), bf16[8,152,1280]{2,1,0:T(8,128)(2,1)}, u32[]{:S(2)}, u32[]{:S(2)}) async-start(bf16[8,152,1280]{2,1,0:T(8,128)(2,1)} %bitcast.86), calls=%async_computation.7 | async-start | bytes 6225920 | tf_op jit(solution)/shard_map/all_to_all | solution.py:637
  376.7 13.9 %collective-permute-start.19 = (bf16[128,896]{1,0:T(8,128)(2,1)S(1)}, bf16[128,896]{1,0:T(8,128)(2,1)S(1)}, u32[]{:S(2)}, u32[]{:S(2)}) collective-permute-start(bf16[128,896]{1,0:T(8,128)(2,1)S(1)} %get-tuple-element.107), channel_id=1, source_target_pairs={{0,24},{8,0},{16,8},{24,16},{1,25},{9,1},{17,9},{25,17},{2,26},{10... | collective-permute-start | bytes 688136 | tf_op jit(solution)/shard_map/ppermute | solution.py:653
  379.9 21.4 %collective-permute-start.20 = (bf16[128,896]{1,0:T(8,128)(2,1)S(1)}, bf16[128,896]{1,0:T(8,128)(2,1)S(1)}, u32[]{:S(2)}, u32[]{:S(2)}) collective-permute-start(bf16[128,896]{1,0:T(8,128)(2,1)S(1)} %get-tuple-element.108), channel_id=1, source_target_pairs={{0,16},{8,24},{16,0},{24,8},{1,17},{9,25},{17,1},{25,9},{2,18},{10... | collective-permute-start | bytes 688136 | tf_op jit(solution)/shard_map/ppermute | solution.py:653
  380.5 20.8 %collective-permute-start.21 = (bf16[128,896]{1,0:T(8,128)(2,1)S(1)}, bf16[128,896]{1,0:T(8,128)(2,1)S(1)}, u32[]{:S(2)}, u32[]{:S(2)}) collective-permute-start(bf16[128,896]{1,0:T(8,128)(2,1)S(1)} %get-tuple-element.109), channel_id=1, source_target_pairs={{0,8},{8,16},{16,24},{24,0},{1,9},{9,17},{17,25},{25,1},{2,10},{10... | collective-permute-start | bytes 688136 | tf_op jit(solution)/shard_map/ppermute | solution.py:653
  406.8 43.9 %all-to-all-start.6 = ((bf16[8,152,1280]{2,1,0:T(8,128)(2,1)}), bf16[8,152,1280]{2,1,0:T(8,128)(2,1)S(1)}, u32[]{:S(2)}, u32[]{:S(2)}) async-start(bf16[8,152,1280]{2,1,0:T(8,128)(2,1)} %bitcast.85), calls=%async_computation.6 | async-start | bytes 6225920 | tf_op jit(solution)/shard_map/all_to_all | solution.py:637
  410.4 81.4 %all-gather.9.cloned.1.call-start = ((), (), s32[]{:S(2)}) async-start(), calls=%async_computation.14 | async-start | bytes 4718592 | tf_op jit(solution)/shard_map/all_gather | solution.py:634
  416.7 17.5 %collective-permute-start.22 = (bf16[128,1280]{1,0:T(8,128)(2,1)S(1)}, bf16[128,1280]{1,0:T(8,128)(2,1)S(1)}, u32[]{:S(2)}, u32[]{:S(2)}) collective-permute-start(bf16[128,1280]{1,0:T(8,128)(2,1)S(1)} %get-tuple-element.118), channel_id=1, source_target_pairs={{0,24},{8,0},{16,8},{24,16},{1,25},{9,1},{17,9},{25,17},{2,26},{10... | collective-permute-start | bytes 983048 | tf_op jit(solution)/shard_map/ppermute | solution.py:653
  419.9 29.8 %collective-permute-start.23 = (bf16[128,1280]{1,0:T(8,128)(2,1)S(1)}, bf16[128,1280]{1,0:T(8,128)(2,1)S(1)}, u32[]{:S(2)}, u32[]{:S(2)}) collective-permute-start(bf16[128,1280]{1,0:T(8,128)(2,1)S(1)} %get-tuple-element.119), channel_id=1, source_target_pairs={{0,16},{8,24},{16,0},{24,8},{1,17},{9,25},{17,1},{25,9},{2,18},{10... | collective-permute-start | bytes 983048 | tf_op jit(solution)/shard_map/ppermute | solution.py:653
  420.5 29.2 %collective-permute-start.24 = (bf16[128,1280]{1,0:T(8,128)(2,1)S(1)}, bf16[128,1280]{1,0:T(8,128)(2,1)S(1)}, u32[]{:S(2)}, u32[]{:S(2)}) collective-permute-start(bf16[128,1280]{1,0:T(8,128)(2,1)S(1)} %get-tuple-element.120), channel_id=1, source_target_pairs={{0,8},{8,16},{16,24},{24,0},{1,9},{9,17},{17,25},{25,1},{2,10},{10... | collective-permute-start | bytes 983048 | tf_op jit(solution)/shard_map/ppermute | solution.py:653
  455.0 94.1 %reduce-scatter.2.cloned.1.call-start = ((), (), s32[]{:S(2)}) async-start(), calls=%async_computation.15 | async-start | bytes 2621440 | tf_op jit(solution)/shard_map/reduce_scatter | solution.py:793
  459.9 9.4 %collective-permute-start.25 = (bf16[128,1280]{1,0:T(8,128)(2,1)S(1)}, bf16[128,1280]{1,0:T(8,128)(2,1)S(1)}, u32[]{:S(2)}, u32[]{:S(2)}) collective-permute-start(bf16[128,1280]{1,0:T(8,128)(2,1)S(1)} %get-tuple-element.124), channel_id=1, source_target_pairs={{0,24},{8,0},{16,8},{24,16},{1,25},{9,1},{17,9},{25,17},{2,26},{10... | collective-permute-start | bytes 983048 | tf_op jit(solution)/shard_map/ppermute | solution.py:658
  460.4 28.7 %collective-permute-start.27 = (bf16[128,1280]{1,0:T(8,128)(2,1)}, bf16[128,1280]{1,0:T(8,128)(2,1)S(1)}, u32[]{:S(2)}, u32[]{:S(2)}) collective-permute-start(bf16[128,1280]{1,0:T(8,128)(2,1)} %get-tuple-element.126), channel_id=1, source_target_pairs={{0,8},{8,16},{16,24},{24,0},{1,9},{9,17},{17,25},{25,1},{2,10},{10... | collective-permute-start | bytes 983048 | tf_op jit(solution)/shard_map/ppermute | solution.py:658
  469.4 19.8 %collective-permute-start.26 = (bf16[128,1280]{1,0:T(8,128)(2,1)S(1)}, bf16[128,1280]{1,0:T(8,128)(2,1)S(1)}, u32[]{:S(2)}, u32[]{:S(2)}) collective-permute-start(bf16[128,1280]{1,0:T(8,128)(2,1)S(1)} %add_convert_fusion.1), channel_id=1, source_target_pairs={{0,24},{8,0},{16,8},{24,16},{1,25},{9,1},{17,9},{25,17},{2,26},{10... | collective-permute-start | bytes 983048 | tf_op jit(solution)/shard_map/ppermute | solution.py:658
  500.7 35.1 %all-to-all-start.9 = ((bf16[8,152,768]{2,1,0:T(8,128)(2,1)}), bf16[8,152,768]{2,1,0:T(8,128)(2,1)S(1)}, u32[]{:S(2)}, u32[]{:S(2)}) async-start(bf16[8,152,768]{2,1,0:T(8,128)(2,1)} %bitcast.89), calls=%async_computation.9 | async-start | bytes 3735552 | tf_op jit(solution)/shard_map/all_to_all | solution.py:637
  551.2 71.3 %all-to-all-start.10 = ((bf16[8,144,2048]{2,1,0:T(8,128)(2,1)}), bf16[8,144,2048]{2,1,0:T(8,128)(2,1)}, u32[]{:S(2)}, u32[]{:S(2)}) async-start(bf16[8,144,2048]{2,1,0:T(8,128)(2,1)} %unproject.1), calls=%async_computation.11 | async-start | bytes 9437184 | tf_op jit(solution)/shard_map/all_to_all | solution.py:637
  556.4 13.6 %collective-permute-start.31 = (bf16[2048,128]{0,1:T(8,128)(2,1)S(1)}, bf16[2048,128]{0,1:T(8,128)(2,1)}, u32[]{:S(2)}, u32[]{:S(2)}) collective-permute-start(bf16[2048,128]{0,1:T(8,128)(2,1)S(1)} %pad_maximum_fusion.4), channel_id=1, source_target_pairs={{0,1},{1,0},{2,3},{3,2},{4,5},{5,4},{6,7},{7,6},{8,9},{9,8},{10,11... | collective-permute-start | bytes 1572872 | tf_op jit(solution)/shard_map/ppermute | solution.py:823
  557.0 8.6 %collective-permute-start.28 = (bf16[128,768]{1,0:T(8,128)(2,1)S(1)}, bf16[128,768]{1,0:T(8,128)(2,1)S(1)}, u32[]{:S(2)}, u32[]{:S(2)}) collective-permute-start(bf16[128,768]{1,0:T(8,128)(2,1)S(1)} %copy-done.85), channel_id=1, source_target_pairs={{0,24},{8,0},{16,8},{24,16},{1,25},{9,1},{17,9},{25,17},{2,26},{10... | collective-permute-start | bytes 589832 | tf_op jit(solution)/shard_map/ppermute | solution.py:658
  560.2 11.0 %collective-permute-start.30 = (bf16[128,768]{1,0:T(8,128)(2,1)S(1)}, bf16[128,768]{1,0:T(8,128)(2,1)S(1)}, u32[]{:S(2)}, u32[]{:S(2)}) collective-permute-start(bf16[128,768]{1,0:T(8,128)(2,1)S(1)} %copy-done.83), channel_id=1, source_target_pairs={{0,8},{8,16},{16,24},{24,0},{1,9},{9,17},{17,25},{25,1},{2,10},{10... | collective-permute-start | bytes 589832 | tf_op jit(solution)/shard_map/ppermute | solution.py:658
  565.6 9.3 %collective-permute-start.29 = (bf16[128,768]{1,0:T(8,128)(2,1)S(1)}, bf16[128,768]{1,0:T(8,128)(2,1)S(1)}, u32[]{:S(2)}, u32[]{:S(2)}) collective-permute-start(bf16[128,768]{1,0:T(8,128)(2,1)S(1)} %add_convert_fusion.2), channel_id=1, source_target_pairs={{0,24},{8,0},{16,8},{24,16},{1,25},{9,1},{17,9},{25,17},{2,26},{10... | collective-permute-start | bytes 589832 | tf_op jit(solution)/shard_map/ppermute | solution.py:658
  571.1 6.1 collective-permute-start.32
  574.9 8.4 %collective-permute-start.34 = (bf16[512,128]{0,1:T(8,128)(2,1)S(1)}, bf16[512,128]{0,1:T(8,128)(2,1)S(1)}, u32[]{:S(2)}, u32[]{:S(2)}) collective-permute-start(bf16[512,128]{0,1:T(8,128)(2,1)S(1)} %get-tuple-element.179), channel_id=1, source_target_pairs={{0,8},{8,16},{16,24},{24,0},{1,9},{9,17},{17,25},{25,1},{2,10},{10... | collective-permute-start | bytes 393224 | tf_op jit(solution)/shard_map/ppermute | solution.py:658
  577.3 7.2 %collective-permute-start.33 = (bf16[512,128]{0,1:T(8,128)(2,1)S(1)}, bf16[512,128]{0,1:T(8,128)(2,1)S(1)}, u32[]{:S(2)}, u32[]{:S(2)}) collective-permute-start(bf16[512,128]{0,1:T(8,128)(2,1)S(1)} %add_convert_fusion.3), channel_id=1, source_target_pairs={{0,24},{8,0},{16,8},{24,16},{1,25},{9,1},{17,9},{25,17},{2,26},{10... | collective-permute-start | bytes 393224 | tf_op jit(solution)/shard_map/ppermute | solution.py:658
  584.7 15.1 %collective-permute-start.35 = (bf16[512,512]{1,0:T(8,128)(2,1)S(1)}, bf16[512,512]{1,0:T(8,128)(2,1)S(1)}, u32[]{:S(2)}, u32[]{:S(2)}) collective-permute-start(bf16[512,512]{1,0:T(8,128)(2,1)S(1)} %get-tuple-element.158), channel_id=1, source_target_pairs={{0,24},{8,0},{16,8},{24,16},{1,25},{9,1},{17,9},{25,17},{2,26},{10... | collective-permute-start | bytes 1572872 | tf_op jit(solution)/shard_map/ppermute | solution.py:658
  599.8 16.7 %collective-permute-start.37 = (bf16[512,512]{1,0:T(8,128)(2,1)S(1)}, bf16[512,512]{1,0:T(8,128)(2,1)S(1)}, u32[]{:S(2)}, u32[]{:S(2)}) collective-permute-start(bf16[512,512]{1,0:T(8,128)(2,1)S(1)} %get-tuple-element.159), channel_id=1, source_target_pairs={{0,8},{8,16},{16,24},{24,0},{1,9},{9,17},{17,25},{25,1},{2,10},{10... | collective-permute-start | bytes 1572872 | tf_op jit(solution)/shard_map/ppermute | solution.py:658
  600.1 22.3 %collective-permute-start.36 = (bf16[512,512]{1,0:T(8,128)(2,1)S(1)}, bf16[512,512]{1,0:T(8,128)(2,1)S(1)}, u32[]{:S(2)}, u32[]{:S(2)}) collective-permute-start(bf16[512,512]{1,0:T(8,128)(2,1)S(1)} %add_convert_fusion), channel_id=1, source_target_pairs={{0,24},{8,0},{16,8},{24,16},{1,25},{9,1},{17,9},{25,17},{2,26},{10... | collective-permute-start | bytes 1572872 | tf_op jit(solution)/shard_map/ppermute | solution.py:658
  626.2 4.2 collective-permute-start.38
  630.4 5.4 collective-permute-start.39
  (106 other events, 659.8 us)
Sparse Core Ops, SparseCore 0:
  10.9 39.4 all-gather.4
  88.7 76.2 all-gather.6
  455.1 36.6 all-gather.8
  500.8 43.8 reduce-scatter.1

commit v6 on v5

--- a/solution.py
+++ b/solution.py
@@ -668,7 +668,8 @@
                     running = (after(shift(running, by), *between) + pieces[s].astype(F32)).astype(BF16)
             if running is not None:
                 total += after(shift(running, by), *last)
-        return total
+                sent = running if by < 0 else sent
+        return total, sent
 
     def reorder(array, dimension):
         size = array.shape[dimension] // planes
@@ -784,7 +785,7 @@
 
     after_all = gather(after_low, "expert")
     mixture_parts = combine(unpick, after(mixture_rows, after_low), planes)
-    mixture_first = plane_sum(mixture_parts)
+    mixture_first, _ = plane_sum(mixture_parts)
     gate_gradient, up_gradient = hidden_gradient(
         arrived[0], arrived[1], *after((gate_grad, up_grad), after_low, *mixture_parts))
     after_all = after(after_all, gate_gradient, router_part, mixture_part, mixture_first)
@@ -801,7 +802,7 @@
         query_terms, key_terms)
     query_partial = t_mm(normed, dq).astype(BF16)
     mixture_parts = combine(unpick, after(mixture_rows, normed_partial), planes)
-    mixture_second = plane_sum(mixture_parts)
+    mixture_second, _ = plane_sum(mixture_parts)
     arrived_sums = exchange(after(normed_partial, out_share, query_partial, *mixture_parts), "expert")
     normed_sums = jnp.sum(arrived_sums.astype(F32), axis=0)
     input_back, _ = normalize_back(
@@ -821,9 +822,9 @@
     for shift in range(1, group):
         pairs = [(e, e - e % group + (e % group + shift) % group) for e in range(members)]
         kv_total += lax.ppermute(kv_cols((place + shift) % group).astype(BF16), "expert", pairs).astype(F32)
-    kv_share = plane_sum(cut(kv_total.astype(BF16)))
     down_grad = down_gradient(upstream_a, upstream_b, weight_wide, after(activated, normed_partial))
-    query_share = plane_sum(cut(after(query_partial, mixture_second, kv_share)), [down_grad], [normed_sums])
+    query_share, halfway = plane_sum(cut(after(query_partial, mixture_second)), [down_grad], [normed_sums])
+    kv_share = plane_sum_direct(cut(after(kv_total.astype(BF16), halfway)))
     key_share = kv_share[:, :piece]
     value_share = kv_share[:, piece:]
 

time: 656 us -> 653 us (level)
    ppermute x30 -> x27, waiting for transfers between devices: 158 us -> 145 us  [shift(): lax.ppermute(value, 'dp', [(i, (i + by) % planes) for i in range(planes)])]
    ppermute x6 -> x9, waiting for transfers between devices: 26.3 us -> 35.3 us  [plane_sum_direct(): lax.ppermute(pieces[s], 'dp', [(i, (i - s) % planes) for i in range(plane...]
    ppermute x30 -> x27, starting transfers between devices: 60.3 us -> 54.4 us  [shift(): lax.ppermute(value, 'dp', [(i, (i + by) % planes) for i in range(planes)])]
    ppermute x6 -> x9, starting transfers between devices: 22.8 us -> 26.5 us  [plane_sum_direct(): lax.ppermute(pieces[s], 'dp', [(i, (i - s) % planes) for i in range(plane...]
  transfers between devices with their start and end apart: 55 -> 55, of which waited for: 38 -> 37; matrix products, arithmetic and copies ran while one was open for 7% -> 7% of each run, Pallas kernels for 18% -> 18%
where the time goes in v6:
time: 653 us; the launch traced here: 642 us
  waiting for transfers between devices  234 us (36%)
  Pallas kernels  137 us (21%)
  starting transfers between devices  134 us (21%)
  local copies, waits for them, and re-layouts  68.9 us (11%)
  other arithmetic  30 us (5%)
  between operations  16.6 us (3%)
  matrix products  12.6 us (2%)
  blocking collectives  9.01 us (1%)
    ppermute x27, waiting for transfers between devices, shift(): lax.ppermute(value, 'dp', [(i, (i + by) % planes) for i in range(planes)])  145 us
    ppermute x27, starting transfers between devices, shift(): lax.ppermute(value, 'dp', [(i, (i + by) % planes) for i in range(planes)])  54.4 us
    unnamed x246, local copies, waits for them, and re-layouts  52.3 us
    all_to_all x11, starting transfers between devices, exchange(): return lax.all_to_all(array, axis, split_axis=0, concat_axis=0, tiled=True)  46.8 us
    all_to_all x11, waiting for transfers between devices, exchange(): return lax.all_to_all(array, axis, split_axis=0, concat_axis=0, tiled=True)  39.3 us
    ppermute x9, waiting for transfers between devices, plane_sum_direct(): lax.ppermute(pieces[s], 'dp', [(i, (i - s) % planes) for i in range(plane...  35.3 us
    ppermute x9, starting transfers between devices, plane_sum_direct(): lax.ppermute(pieces[s], 'dp', [(i, (i - s) % planes) for i in range(plane...  26.5 us
    pallas_call x4, Pallas kernels, combine(): pl.pallas_call(combine_kernel, grid=(width // tile,), in_specs=[pl.BlockS...  16.7 us
  transfers between devices with their start and end apart: 55, of which 37 were waited for; matrix products, arithmetic and copies ran while one was open for 7% of the time, Pallas kernels for 18%

profile of v6, /device:TPU:0, one launch (start us, length us, event | category | flops | bytes accessed | tf_op | source)
XLA Modules:
  0.0 642.2 jit_solution(14184460824487622233)
XLA Ops:
  18.5 18.3 %collective-permute-done.1.refs_1_ = bf16[512,768]{1,0:T(8,128)(2,1)S(1)} collective-permute-done((bf16[512,768]{1,0:T(8,128)(2,1)S(1)}, bf16[512,768]{1,0:T(8,128)(2,1)S(1)}, u32[]{:S(2)}, u32[]{:S(2)}) %collective-permute-start.1) | collective-permute-done | bytes 786464 | tf_op jit(solution)/shard_map/ppermute | solution.py:641
  39.8 10.6 %all-gather.5.cloned.1.call-done.x_ref = bf16[1024,2048]{1,0:T(8,128)(2,1)} async-done(((bf16[128,2048]{1,0:T(8,128)(2,1)}), bf16[1024,2048]{1,0:T(8,128)(2,1)}) %all-gather.5.cloned.1.call-update) | async-done | bytes 4194320 | tf_op jit(solution)/shard_map/all_gather | solution.py:634
  50.3 9.0 %all-gather = bf16[8,4,512]{2,1,0:T(4,128)(2,1)S(1)} all-gather(bf16[1,4,512]{2,1,0:T(4,128)(2,1)S(1)} %bitcast.114), channel_id=1, replica_groups=mesh['dp'=4,'expert'=8] {'expert'}, dimensions={0}, use_global_device_ids=true | all-gather | bytes 36864 | tf_op jit(solution)/shard_map/all_gather | solution.py:634
  59.4 10.8 %collective-permute-done.2.refs_2_ = bf16[512,768]{1,0:T(8,128)(2,1)} collective-permute-done((bf16[512,768]{1,0:T(8,128)(2,1)S(1)}, bf16[512,768]{1,0:T(8,128)(2,1)}, u32[]{:S(2)}, u32[]{:S(2)}) %collective-permute-start.2) | collective-permute-done | bytes 786464 | tf_op jit(solution)/shard_map/ppermute | solution.py:641
  72.4 6.6 %project.1 = (f32[1024,512]{1,0:T(8,128)S(1)}, f32[1024,128]{1,0:T(8,128)S(1)}, bf16[1024,512]{1,0:T(8,128)(2,1)S(1)}, bf16[1024,128]{1,0:T(8,128)(2,1)S(1)}, bf16[1024,128]{1,0:T(8,128)(2,1)S(1)}) custom-call(bf16[1024,2048]{1,0:T(8,128)(2,1)S(1)} %copy-done, f32[1024,128]{1,0:T(8,128)S(1)} %get-tuple-element.221.cos_ref, ...), custom_call_target="tpu_custom_call" | custom-call | flops 1 | bytes 1 | tf_op jit(solution)/shard_map/project/pallas_call | solution.py:98
  80.4 5.9 attend.1
  89.6 3.8 collective-permute-start.6
  93.5 7.9 %collective-permute-done.4.refs_1_ = bf16[128,1152]{1,0:T(8,128)(2,1)S(1)} collective-permute-done((bf16[128,1152]{1,0:T(8,128)(2,1)S(1)}, bf16[128,1152]{1,0:T(8,128)(2,1)S(1)}, u32[]{:S(2)}, u32[]{:S(2)}) %collective-permute-start.4) | collective-permute-done | bytes 294944 | tf_op jit(solution)/shard_map/ppermute | solution.py:641
  101.7 4.9 collective-permute-done.6.refs_3_
  106.8 3.6 collective-permute-done.5.refs_2_
  115.1 4.5 all-to-all-start
  119.7 3.8 collective-permute-start.9
  123.5 12.8 %collective-permute-done.7.refs_1_ = bf16[1024,256]{1,0:T(8,128)(2,1)S(1)} collective-permute-done((bf16[1024,256]{1,0:T(8,128)(2,1)S(1)}, bf16[1024,256]{1,0:T(8,128)(2,1)S(1)}, u32[]{:S(2)}, u32[]{:S(2)}) %collective-permute-start.7) | collective-permute-done | bytes 524320 | tf_op jit(solution)/shard_map/ppermute | solution.py:641
  138.1 7.0 %collective-permute-done.9.refs_3_ = bf16[1024,256]{1,0:T(8,128)(2,1)S(1)} collective-permute-done((bf16[1024,256]{1,0:T(8,128)(2,1)S(1)}, bf16[1024,256]{1,0:T(8,128)(2,1)S(1)}, u32[]{:S(2)}, u32[]{:S(2)}) %collective-permute-start.9) | collective-permute-done | bytes 524320 | tf_op jit(solution)/shard_map/ppermute | solution.py:641
  145.1 13.0 %collective-permute-done.8.refs_2_ = bf16[1024,256]{1,0:T(8,128)(2,1)S(1)} collective-permute-done((bf16[1024,256]{1,0:T(8,128)(2,1)S(1)}, bf16[1024,256]{1,0:T(8,128)(2,1)S(1)}, u32[]{:S(2)}, u32[]{:S(2)}) %collective-permute-start.8) | collective-permute-done | bytes 524320 | tf_op jit(solution)/shard_map/ppermute | solution.py:641
  158.2 3.8 collective-permute-start.11
  162.0 8.2 %collective-permute-done.10.refs_1_ = bf16[144,1024]{1,0:T(8,128)(2,1)} collective-permute-done((bf16[144,1024]{1,0:T(8,128)(2,1)}, bf16[144,1024]{1,0:T(8,128)(2,1)}, u32[]{:S(2)}, u32[]{:S(2)}) %collective-permute-start.10) | collective-permute-done | bytes 294944 | tf_op jit(solution)/shard_map/ppermute | solution.py:641
  181.4 3.7 all-to-all-start.1
  189.8 5.0 all-to-all-done.1
  194.8 4.4 all-to-all-start.2
  200.8 3.8 collective-permute-start.15
  204.6 7.1 %collective-permute-done.13.refs_1_ = bf16[128,1024]{1,0:T(8,128)(2,1)S(1)} collective-permute-done((bf16[128,1024]{1,0:T(8,128)(2,1)S(1)}, bf16[128,1024]{1,0:T(8,128)(2,1)S(1)}, u32[]{:S(2)}, u32[]{:S(2)}) %collective-permute-start.13) | collective-permute-done | bytes 262176 | tf_op jit(solution)/shard_map/ppermute | solution.py:641
  211.8 5.2 collective-permute-start.14
  217.0 8.1 %collective-permute-done.14.refs_2_ = bf16[128,1024]{1,0:T(8,128)(2,1)S(1)} collective-permute-done((bf16[128,1024]{1,0:T(8,128)(2,1)S(1)}, bf16[128,1024]{1,0:T(8,128)(2,1)S(1)}, u32[]{:S(2)}, u32[]{:S(2)}) %collective-permute-start.14) | collective-permute-done | bytes 262176 | tf_op jit(solution)/shard_map/ppermute | solution.py:641
  230.1 4.4 all-to-all-start.3
  234.6 3.8 collective-permute-start.18
  238.4 7.1 %collective-permute-done.16.refs_1_ = bf16[128,1024]{1,0:T(8,128)(2,1)S(1)} collective-permute-done((bf16[128,1024]{1,0:T(8,128)(2,1)S(1)}, bf16[128,1024]{1,0:T(8,128)(2,1)S(1)}, u32[]{:S(2)}, u32[]{:S(2)}) %collective-permute-start.16) | collective-permute-done | bytes 262176 | tf_op jit(solution)/shard_map/ppermute | solution.py:641
  245.5 4.9 collective-permute-start.17
  250.5 8.0 %collective-permute-done.17.refs_2_ = bf16[128,1024]{1,0:T(8,128)(2,1)S(1)} collective-permute-done((bf16[128,1024]{1,0:T(8,128)(2,1)S(1)}, bf16[128,1024]{1,0:T(8,128)(2,1)S(1)}, u32[]{:S(2)}, u32[]{:S(2)}) %collective-permute-start.17) | collective-permute-done | bytes 262176 | tf_op jit(solution)/shard_map/ppermute | solution.py:641
  265.4 4.6 all-to-all-start.4
  274.1 7.3 %down_back.1.down_ref = f32[1216,768]{1,0:T(8,128)S(1)} custom-call(bf16[1216,1152]{1,0:T(8,128)(2,1)} %bitcast.9.ca_ref.mask_ref, bf16[1216,1024]{1,0:T(8,128)(2,1)} %bitcast.15.cb_ref, bf16[768,2048]{1,0:T(8,128)(2,1)S(1)} %bitcast.77), custom_call_target="tpu_custom_call" | custom-call | flops 1 | bytes 1 | tf_op jit(solution)/shard_map/down_back/pallas_call | solution.py:445
  284.8 16.1 %all-to-all-done.4 = bf16[8,152,1024]{2,1,0:T(8,128)(2,1)} async-done(((bf16[8,152,1024]{2,1,0:T(8,128)(2,1)}), bf16[8,152,1024]{2,1,0:T(8,128)(2,1)}, u32[]{:S(2)}, u32[]{:S(2)}) %all-to-all-start.4) | async-done | bytes 2490400 | tf_op jit(solution)/shard_map/all_to_all | solution.py:637
  300.9 4.4 all-to-all-start.8
  310.1 13.0 %expert_forward.1 = (bf16[1216,768]{1,0:T(8,128)(2,1)S(1)}, bf16[1216,768]{1,0:T(8,128)(2,1)S(1)}, bf16[1216,768]{1,0:T(8,128)(2,1)S(1)}, f32[1216,128]{1,0:T(8,128)S(1)}, bf16[1216,128]{1,0:T(8,128)(2,1)S(1)}) custom-call(s32[1]{0:T(128)} %bitcast.13.own_ref, bf16[1216,1024]{1,0:T(8,128)(2,1)} %bitcast.17.xa_ref, bf16[1216,1024]{1,0:T(8,128)(2,1)} %bitcast.19.xb_ref, ...), custom_call_target="tpu_custom_call" | custom-call | flops 19800000512 | bytes 1 | tf_op jit(solution)/shard_map/expert_forward/pallas_call | solution.py:393
  325.1 3.7 row_gradient.2
  332.7 4.4 all-to-all-start.5
  349.1 5.6 row_gradient.3
  356.4 8.2 %all-to-all-done.5 = bf16[8,152,896]{2,1,0:T(8,128)(2,1)} async-done(((bf16[8,152,896]{2,1,0:T(8,128)(2,1)}), bf16[8,152,896]{2,1,0:T(8,128)(2,1)}, u32[]{:S(2)}, u32[]{:S(2)}) %all-to-all-start.5) | async-done | bytes 2179104 | tf_op jit(solution)/shard_map/all_to_all | solution.py:637
  364.6 4.4 all-to-all-start.7
  370.4 6.2 combine.4
  382.9 4.6 produce.1
  390.4 10.7 %collective-permute-done.20 = bf16[128,896]{1,0:T(8,128)(2,1)S(1)} collective-permute-done((bf16[128,896]{1,0:T(8,128)(2,1)S(1)}, bf16[128,896]{1,0:T(8,128)(2,1)S(1)}, u32[]{:S(2)}, u32[]{:S(2)}) %collective-permute-start.20) | collective-permute-done | bytes 229408 | tf_op jit(solution)/shard_map/ppermute | solution.py:653
  402.8 3.8 all-to-all-done.7
  406.6 3.6 all-to-all-start.6
  411.6 4.9 combine.5
  420.3 12.6 %collective-permute-start.24 = (bf16[128,1280]{1,0:T(8,128)(2,1)S(1)}, bf16[128,1280]{1,0:T(8,128)(2,1)S(1)}, u32[]{:S(2)}, u32[]{:S(2)}) collective-permute-start(bf16[128,1280]{1,0:T(8,128)(2,1)S(1)} %get-tuple-element.121), channel_id=1, source_target_pairs={{0,8},{8,16},{16,24},{24,0},{1,9},{9,17},{17,25},{25,1},{2,10},{10... | collective-permute-start | bytes 983048 | tf_op jit(solution)/shard_map/ppermute | solution.py:653
  433.3 16.3 %collective-permute-done.23 = bf16[128,1280]{1,0:T(8,128)(2,1)S(1)} collective-permute-done((bf16[128,1280]{1,0:T(8,128)(2,1)S(1)}, bf16[128,1280]{1,0:T(8,128)(2,1)S(1)}, u32[]{:S(2)}, u32[]{:S(2)}) %collective-permute-start.23) | collective-permute-done | bytes 327712 | tf_op jit(solution)/shard_map/ppermute | solution.py:653
  456.2 3.6 combine.6
  461.8 7.4 %collective-permute-done.25 = bf16[128,1280]{1,0:T(8,128)(2,1)S(1)} collective-permute-done((bf16[128,1280]{1,0:T(8,128)(2,1)S(1)}, bf16[128,1280]{1,0:T(8,128)(2,1)S(1)}, u32[]{:S(2)}, u32[]{:S(2)}) %collective-permute-start.25) | collective-permute-done | bytes 327712 | tf_op jit(solution)/shard_map/ppermute | solution.py:658
  475.2 13.4 %hidden_gradient.1 = (f32[1,2048,768]{2,1,0:T(8,128)}, f32[1,2048,768]{2,1,0:T(8,128)}) custom-call(bf16[1216,1024]{1,0:T(8,128)(2,1)} %bitcast.17.xa_ref, bf16[1216,1024]{1,0:T(8,128)(2,1)} %bitcast.19.xb_ref, bf16[1216,768]{1,0:T(8,128)(2,1)S(1)} %copy-done.51, bf16[1216,768]{1,0:T(8,128)(2,1)S(1)} %copy-done.54), custom_call_target="tpu_custom_call" | custom-call | flops 1 | bytes 1 | tf_op jit(solution)/shard_map/hidden_gradient/pallas_call | solution.py:497
  491.6 8.8 %out_gradient.1 = bf16[8,512,256]{2,1,0:T(8,128)(2,1)} custom-call(s32[1]{0:T(128)} %bitcast.33.member_ref, bf16[8,1024,512]{2,1,0:T(8,128)(2,1)} %bitcast.75, bf16[1024,2048]{1,0:T(8,128)(2,1)} %all-gather.9.cloned.1.call-done.g_ref), custom_call_target="tpu_custom_call" | custom-call | flops 1 | bytes 1 | tf_op jit(solution)/shard_map/out_gradient/pallas_call | solution.py:334
  500.5 3.6 all-to-all-start.9
  504.3 5.8 out_back.1.do_ref
  513.1 13.9 %attend_back.1 = (bf16[1024,512]{1,0:T(8,128)(2,1)S(1)}, bf16[1024,128]{1,0:T(8,128)(2,1)S(1)}, bf16[1024,128]{1,0:T(8,128)(2,1)S(1)}, f32[1,128]{1,0:T(1,128)S(1)}, f32[1,128]{1,0:T(1,128)S(1)}) custom-call(s32[1]{0:T(128)S(6)} %copy.94.prefix_ref, bf16[1024,512]{1,0:T(8,128)(2,1)S(1)} %copy-done.24, bf16[1024,128]{1,0:T(8,128)(2,1)S(1)} %copy-done.60, ...), custom_call_target="tpu_custom_call" | custom-call | flops 1 | bytes 1 | tf_op jit(solution)/shard_map/attend_back/pallas_call | solution.py:207
  527.0 6.9 %unproject.1 = bf16[8,144,2048]{2,1,0:T(8,128)(2,1)} custom-call(bf16[1024,512]{1,0:T(8,128)(2,1)S(1)} %get-tuple-element.137.dq_ref, bf16[1024,128]{1,0:T(8,128)(2,1)S(1)} %get-tuple-element.138.dk_ref, bf16[1024,128]{1,0:T(8,128)(2,1)S(1)} %get-tuple-element.139.dv_ref, bf16[1024,2048]{1,0:T(8,128)(2,1)S(1)} %copy-done.1, f32[1,2048]{1,0:T(1,128)S(1)} %bitcast.91, ...), custom_call_target="tpu_custom_call" | custom-call | flops 1 | bytes 1 | tf_op jit(solution)/shard_map/unproject/pallas_call | solution.py:262
  540.3 6.0 convolution_convert_fusion
  548.4 4.8 all-to-all-start.10
  561.9 4.3 collective-permute-start.29
  566.8 3.8 collective-permute-done.29
  574.5 11.1 %down_gradient.1 = f32[1,768,2048]{2,1,0:T(8,128)} custom-call(bf16[1216,1152]{1,0:T(8,128)(2,1)} %bitcast.9.ca_ref.mask_ref, bf16[1216,1024]{1,0:T(8,128)(2,1)} %bitcast.15.cb_ref, f32[1216,128]{1,0:T(8,128)S(1)} %copy-done.34, bf16[1216,768]{1,0:T(8,128)(2,1)S(1)} %copy-done.15), custom_call_target="tpu_custom_call" | custom-call | flops 1 | bytes 1 | tf_op jit(solution)/shard_map/down_gradient/pallas_call | solution.py:523
  587.5 3.8 collective-permute-start.35
  595.2 7.1 %collective-permute-done.33 = bf16[512,512]{1,0:T(8,128)(2,1)S(1)} collective-permute-done((bf16[512,512]{1,0:T(8,128)(2,1)S(1)}, bf16[512,512]{1,0:T(8,128)(2,1)S(1)}, u32[]{:S(2)}, u32[]{:S(2)}) %collective-permute-start.33) | collective-permute-done | bytes 524320 | tf_op jit(solution)/shard_map/ppermute | solution.py:658
  602.5 8.1 %collective-permute-done.36 = bf16[512,128]{0,1:T(8,128)(2,1)} collective-permute-done((bf16[512,128]{0,1:T(8,128)(2,1)}, bf16[512,128]{0,1:T(8,128)(2,1)}, u32[]{:S(2)}, u32[]{:S(2)}) %collective-permute-start.36) | collective-permute-done | bytes 131104 | tf_op jit(solution)/shard_map/ppermute | solution.py:653
  612.5 6.4 collective-permute-done.32
  (436 shorter events, 172.2 us)
Async XLA Ops:
  7.2 43.1 %all-gather.5.cloned.1.call-start = ((), (), s32[]{:S(2)}) async-start(), calls=%async_computation.12 | async-start | bytes 4718592 | tf_op jit(solution)/shard_map/all_gather | solution.py:634
  10.8 162.4 %all-gather.7.cloned.1.call-start = ((), (), s32[]{:S(2)}) async-start(), calls=%async_computation.13 | async-start | bytes 9437184 | tf_op jit(solution)/shard_map/all_gather | solution.py:634
  11.2 1.5 collective-permute-start
  13.4 65.5 %copy-start.16 = (bf16[512,768]{1,0:T(8,128)(2,1)}, bf16[512,768]{1,0:T(8,128)(2,1)S(1)}, u32[]{:S(2)}) copy-start(bf16[512,768]{1,0:T(8,128)(2,1)S(1)} %concatenate.65.refs_0_) | copy-start | bytes 2359300
  13.4 36.9 %copy-start.113 = (bf16[512,4]{0,1:T(4,128)(2,1)S(1)}, bf16[512,4]{0,1:T(4,128)(2,1)}, u32[]{:S(2)}) copy-start(bf16[512,4]{0,1:T(4,128)(2,1)} %param.23) | copy-start | bytes 12292
  13.4 56.7 %copy-start.72 = (f32[128]{0:T(128)S(1)}, f32[128]{0:T(128)}, u32[]{:S(2)}) copy-start(f32[128]{0:T(128)} %param.26) | copy-start | bytes 1540
  13.4 56.7 %copy-start.74 = (f32[128]{0:T(128)S(1)}, f32[128]{0:T(128)}, u32[]{:S(2)}) copy-start(f32[128]{0:T(128)} %param.27) | copy-start | bytes 1540
  13.5 23.4 %collective-permute-start.1 = (bf16[512,768]{1,0:T(8,128)(2,1)S(1)}, bf16[512,768]{1,0:T(8,128)(2,1)S(1)}, u32[]{:S(2)}, u32[]{:S(2)}) collective-permute-start(bf16[512,768]{1,0:T(8,128)(2,1)S(1)} %concatenate.65.refs_0_), channel_id=1, source_target_pairs={{0,8},{8,16},{16,24},{24,0},{1,9},{9,17},{17,25},{25,1},{2,10},{10... | collective-permute-start | bytes 2359304 | tf_op jit(solution)/shard_map/ppermute | solution.py:641
  16.4 42.9 %collective-permute-start.3 = (bf16[512,768]{1,0:T(8,128)(2,1)S(1)}, bf16[512,768]{1,0:T(8,128)(2,1)S(1)}, u32[]{:S(2)}, u32[]{:S(2)}) collective-permute-start(bf16[512,768]{1,0:T(8,128)(2,1)S(1)} %concatenate.65.refs_0_), channel_id=1, source_target_pairs={{0,24},{8,0},{16,8},{24,16},{1,25},{9,1},{17,9},{25,17},{2,26},{10... | collective-permute-start | bytes 2359304 | tf_op jit(solution)/shard_map/ppermute | solution.py:641
  36.8 42.1 %copy-start.26 = (bf16[512,768]{1,0:T(8,128)(2,1)}, bf16[512,768]{1,0:T(8,128)(2,1)S(1)}, u32[]{:S(2)}) copy-start(bf16[512,768]{1,0:T(8,128)(2,1)S(1)} %collective-permute-done.1.refs_1_) | copy-start | bytes 2359300
  36.8 33.3 %collective-permute-start.2 = (bf16[512,768]{1,0:T(8,128)(2,1)S(1)}, bf16[512,768]{1,0:T(8,128)(2,1)}, u32[]{:S(2)}, u32[]{:S(2)}) collective-permute-start(bf16[512,768]{1,0:T(8,128)(2,1)S(1)} %collective-permute-done.1.refs_1_), channel_id=1, source_target_pairs={{0,8},{8,16},{16,24},{24,0},{1,9},{9,17},{17,25},{25,1},{2,10},{10... | collective-permute-start | bytes 2359304 | tf_op jit(solution)/shard_map/ppermute | solution.py:641
  39.8 39.2 %copy-start.18 = (f32[1024,128]{1,0:T(8,128)}, f32[1024,128]{1,0:T(8,128)S(1)}, u32[]{:S(2)}) copy-start(f32[1024,128]{1,0:T(8,128)S(1)} %get-tuple-element.221.cos_ref) | copy-start | bytes 1572868
  39.8 39.2 %copy-start.20 = (f32[1024,128]{1,0:T(8,128)}, f32[1024,128]{1,0:T(8,128)S(1)}, u32[]{:S(2)}) copy-start(f32[1024,128]{1,0:T(8,128)S(1)} %get-tuple-element.222.sin_ref) | copy-start | bytes 1572868
  89.5 11.9 %collective-permute-start.4 = (bf16[128,1152]{1,0:T(8,128)(2,1)S(1)}, bf16[128,1152]{1,0:T(8,128)(2,1)S(1)}, u32[]{:S(2)}, u32[]{:S(2)}) collective-permute-start(bf16[128,1152]{1,0:T(8,128)(2,1)S(1)} %fusion.19.refs_0_), channel_id=1, source_target_pairs={{0,8},{8,16},{16,24},{24,0},{1,9},{9,17},{17,25},{25,1},{2,10},{10... | collective-permute-start | bytes 884744 | tf_op jit(solution)/shard_map/ppermute | solution.py:641
  89.6 17.0 %collective-permute-start.6 = (bf16[128,1152]{1,0:T(8,128)(2,1)S(1)}, bf16[128,1152]{1,0:T(8,128)(2,1)S(1)}, u32[]{:S(2)}, u32[]{:S(2)}) collective-permute-start(bf16[128,1152]{1,0:T(8,128)(2,1)S(1)} %fusion.19.refs_0_), channel_id=1, source_target_pairs={{0,24},{8,0},{16,8},{24,16},{1,25},{9,1},{17,9},{25,17},{2,26},{10... | collective-permute-start | bytes 884744 | tf_op jit(solution)/shard_map/ppermute | solution.py:641
  101.4 9.0 %collective-permute-start.5 = (bf16[128,1152]{1,0:T(8,128)(2,1)S(1)}, bf16[128,1152]{1,0:T(8,128)(2,1)S(1)}, u32[]{:S(2)}, u32[]{:S(2)}) collective-permute-start(bf16[128,1152]{1,0:T(8,128)(2,1)S(1)} %collective-permute-done.4.refs_1_), channel_id=1, source_target_pairs={{0,8},{8,16},{16,24},{24,0},{1,9},{9,17},{17,25},{25,1},{2,10},{10... | collective-permute-start | bytes 884744 | tf_op jit(solution)/shard_map/ppermute | solution.py:641
  115.1 56.4 %all-to-all-start = ((bf16[8,152,1152]{2,1,0:T(8,128)(2,1)}), bf16[8,152,1152]{2,1,0:T(8,128)(2,1)}, u32[]{:S(2)}, u32[]{:S(2)}) async-start(bf16[8,152,1152]{2,1,0:T(8,128)(2,1)} %bitcast.80), calls=%async_computation | async-start | bytes 5603328 | tf_op jit(solution)/shard_map/all_to_all | solution.py:637
  119.6 16.6 %collective-permute-start.7 = (bf16[1024,256]{1,0:T(8,128)(2,1)S(1)}, bf16[1024,256]{1,0:T(8,128)(2,1)S(1)}, u32[]{:S(2)}, u32[]{:S(2)}) collective-permute-start(bf16[1024,256]{1,0:T(8,128)(2,1)S(1)} %copy-done.40), channel_id=1, source_target_pairs={{0,8},{8,16},{16,24},{24,0},{1,9},{9,17},{17,25},{25,1},{2,10},{10... | collective-permute-start | bytes 1572872 | tf_op jit(solution)/shard_map/ppermute | solution.py:641
  119.7 25.4 %collective-permute-start.9 = (bf16[1024,256]{1,0:T(8,128)(2,1)S(1)}, bf16[1024,256]{1,0:T(8,128)(2,1)S(1)}, u32[]{:S(2)}, u32[]{:S(2)}) collective-permute-start(bf16[1024,256]{1,0:T(8,128)(2,1)S(1)} %copy-done.40), channel_id=1, source_target_pairs={{0,24},{8,0},{16,8},{24,16},{1,25},{9,1},{17,9},{25,17},{2,26},{10... | collective-permute-start | bytes 1572872 | tf_op jit(solution)/shard_map/ppermute | solution.py:641
  136.3 43.8 %copy-start.44 = (bf16[1024,256]{1,0:T(8,128)(2,1)}, bf16[1024,256]{1,0:T(8,128)(2,1)S(1)}, u32[]{:S(2)}) copy-start(bf16[1024,256]{1,0:T(8,128)(2,1)S(1)} %collective-permute-done.7.refs_1_) | copy-start | bytes 1572868
  136.3 21.9 %collective-permute-start.8 = (bf16[1024,256]{1,0:T(8,128)(2,1)S(1)}, bf16[1024,256]{1,0:T(8,128)(2,1)S(1)}, u32[]{:S(2)}, u32[]{:S(2)}) collective-permute-start(bf16[1024,256]{1,0:T(8,128)(2,1)S(1)} %collective-permute-done.7.refs_1_), channel_id=1, source_target_pairs={{0,8},{8,16},{16,24},{24,0},{1,9},{9,17},{17,25},{25,1},{2,10},{10... | collective-permute-start | bytes 1572872 | tf_op jit(solution)/shard_map/ppermute | solution.py:641
  145.1 35.0 %copy-start.42 = (bf16[1024,256]{1,0:T(8,128)(2,1)}, bf16[1024,256]{1,0:T(8,128)(2,1)S(1)}, u32[]{:S(2)}) copy-start(bf16[1024,256]{1,0:T(8,128)(2,1)S(1)} %collective-permute-done.9.refs_3_) | copy-start | bytes 1572868
  158.2 12.1 %collective-permute-start.10 = (bf16[144,1024]{1,0:T(8,128)(2,1)}, bf16[144,1024]{1,0:T(8,128)(2,1)}, u32[]{:S(2)}, u32[]{:S(2)}) collective-permute-start(bf16[144,1024]{1,0:T(8,128)(2,1)} %pad_maximum_fusion.5.refs_0_), channel_id=1, source_target_pairs={{0,8},{8,16},{16,24},{24,0},{1,9},{9,17},{17,25},{25,1},{2,10},{10... | collective-permute-start | bytes 884744 | tf_op jit(solution)/shard_map/ppermute | solution.py:641
  158.2 15.1 %collective-permute-start.11 = (bf16[144,1024]{1,0:T(8,128)(2,1)}, bf16[144,1024]{1,0:T(8,128)(2,1)}, u32[]{:S(2)}, u32[]{:S(2)}) collective-permute-start(bf16[144,1024]{1,0:T(8,128)(2,1)} %pad_maximum_fusion.5.refs_0_), channel_id=1, source_target_pairs={{0,24},{8,0},{16,8},{24,16},{1,25},{9,1},{17,9},{25,17},{2,26},{10... | collective-permute-start | bytes 884744 | tf_op jit(solution)/shard_map/ppermute | solution.py:641
  170.2 11.2 %collective-permute-start.12 = (bf16[144,1024]{1,0:T(8,128)(2,1)}, bf16[144,1024]{1,0:T(8,128)(2,1)}, u32[]{:S(2)}, u32[]{:S(2)}) collective-permute-start(bf16[144,1024]{1,0:T(8,128)(2,1)} %collective-permute-done.10.refs_1_), channel_id=1, source_target_pairs={{0,8},{8,16},{16,24},{24,0},{1,9},{9,17},{17,25},{25,1},{2,10},{10... | collective-permute-start | bytes 884744 | tf_op jit(solution)/shard_map/ppermute | solution.py:641
  181.4 13.4 %all-to-all-start.1 = ((bf16[8,128,256]{2,1,0:T(8,128)(2,1)}), bf16[8,128,256]{2,1,0:T(8,128)(2,1)S(1)}, u32[]{:S(2)}, u32[]{:S(2)}) async-start(bf16[8,128,256]{2,1,0:T(8,128)(2,1)} %bitcast.88), calls=%async_computation.1 | async-start | bytes 1048576 | tf_op jit(solution)/shard_map/all_to_all | solution.py:637
  194.8 35.3 %all-to-all-start.2 = ((bf16[8,152,1024]{2,1,0:T(8,128)(2,1)}), bf16[8,152,1024]{2,1,0:T(8,128)(2,1)}, u32[]{:S(2)}, u32[]{:S(2)}) async-start(bf16[8,152,1024]{2,1,0:T(8,128)(2,1)} %bitcast.82), calls=%async_computation.2 | async-start | bytes 4980736 | tf_op jit(solution)/shard_map/all_to_all | solution.py:637
  200.7 11.0 %collective-permute-start.13 = (bf16[128,1024]{1,0:T(8,128)(2,1)S(1)}, bf16[128,1024]{1,0:T(8,128)(2,1)S(1)}, u32[]{:S(2)}, u32[]{:S(2)}) collective-permute-start(bf16[128,1024]{1,0:T(8,128)(2,1)S(1)} %get-tuple-element.184.refs_0_), channel_id=1, source_target_pairs={{0,8},{8,16},{16,24},{24,0},{1,9},{9,17},{17,25},{25,1},{2,10},{10... | collective-permute-start | bytes 786440 | tf_op jit(solution)/shard_map/ppermute | solution.py:641
  200.8 16.2 %collective-permute-start.15 = (bf16[128,1024]{1,0:T(8,128)(2,1)S(1)}, bf16[128,1024]{1,0:T(8,128)(2,1)S(1)}, u32[]{:S(2)}, u32[]{:S(2)}) collective-permute-start(bf16[128,1024]{1,0:T(8,128)(2,1)S(1)} %get-tuple-element.184.refs_0_), channel_id=1, source_target_pairs={{0,24},{8,0},{16,8},{24,16},{1,25},{9,1},{17,9},{25,17},{2,26},{10... | collective-permute-start | bytes 786440 | tf_op jit(solution)/shard_map/ppermute | solution.py:641
  211.8 13.3 %collective-permute-start.14 = (bf16[128,1024]{1,0:T(8,128)(2,1)S(1)}, bf16[128,1024]{1,0:T(8,128)(2,1)S(1)}, u32[]{:S(2)}, u32[]{:S(2)}) collective-permute-start(bf16[128,1024]{1,0:T(8,128)(2,1)S(1)} %collective-permute-done.13.refs_1_), channel_id=1, source_target_pairs={{0,8},{8,16},{16,24},{24,0},{1,9},{9,17},{17,25},{25,1},{2,10},{10... | collective-permute-start | bytes 786440 | tf_op jit(solution)/shard_map/ppermute | solution.py:641
  230.1 35.3 %all-to-all-start.3 = ((bf16[8,152,1024]{2,1,0:T(8,128)(2,1)}), bf16[8,152,1024]{2,1,0:T(8,128)(2,1)}, u32[]{:S(2)}, u32[]{:S(2)}) async-start(bf16[8,152,1024]{2,1,0:T(8,128)(2,1)} %bitcast.83), calls=%async_computation.3 | async-start | bytes 4980736 | tf_op jit(solution)/shard_map/all_to_all | solution.py:637
  234.5 11.0 %collective-permute-start.16 = (bf16[128,1024]{1,0:T(8,128)(2,1)S(1)}, bf16[128,1024]{1,0:T(8,128)(2,1)S(1)}, u32[]{:S(2)}, u32[]{:S(2)}) collective-permute-start(bf16[128,1024]{1,0:T(8,128)(2,1)S(1)} %get-tuple-element.183.refs_0_), channel_id=1, source_target_pairs={{0,8},{8,16},{16,24},{24,0},{1,9},{9,17},{17,25},{25,1},{2,10},{10... | collective-permute-start | bytes 786440 | tf_op jit(solution)/shard_map/ppermute | solution.py:641
  234.6 15.9 %collective-permute-start.18 = (bf16[128,1024]{1,0:T(8,128)(2,1)S(1)}, bf16[128,1024]{1,0:T(8,128)(2,1)S(1)}, u32[]{:S(2)}, u32[]{:S(2)}) collective-permute-start(bf16[128,1024]{1,0:T(8,128)(2,1)S(1)} %get-tuple-element.183.refs_0_), channel_id=1, source_target_pairs={{0,24},{8,0},{16,8},{24,16},{1,25},{9,1},{17,9},{25,17},{2,26},{10... | collective-permute-start | bytes 786440 | tf_op jit(solution)/shard_map/ppermute | solution.py:641
  245.5 12.9 %collective-permute-start.17 = (bf16[128,1024]{1,0:T(8,128)(2,1)S(1)}, bf16[128,1024]{1,0:T(8,128)(2,1)S(1)}, u32[]{:S(2)}, u32[]{:S(2)}) collective-permute-start(bf16[128,1024]{1,0:T(8,128)(2,1)S(1)} %collective-permute-done.16.refs_1_), channel_id=1, source_target_pairs={{0,8},{8,16},{16,24},{24,0},{1,9},{9,17},{17,25},{25,1},{2,10},{10... | collective-permute-start | bytes 786440 | tf_op jit(solution)/shard_map/ppermute | solution.py:641
  265.4 35.5 %all-to-all-start.4 = ((bf16[8,152,1024]{2,1,0:T(8,128)(2,1)}), bf16[8,152,1024]{2,1,0:T(8,128)(2,1)}, u32[]{:S(2)}, u32[]{:S(2)}) async-start(bf16[8,152,1024]{2,1,0:T(8,128)(2,1)} %bitcast.81), calls=%async_computation.4 | async-start | bytes 4980736 | tf_op jit(solution)/shard_map/all_to_all | solution.py:637
  300.9 31.8 %all-to-all-start.8 = ((bf16[8,512,256]{2,1,0:T(8,128)(2,1)}), bf16[8,512,256]{2,1,0:T(8,128)(2,1)}, u32[]{:S(2)}, u32[]{:S(2)}) async-start(bf16[8,512,256]{2,1,0:T(8,128)(2,1)} %bitcast.103), calls=%async_computation.8 | async-start | bytes 4194304 | tf_op jit(solution)/shard_map/all_to_all | solution.py:637
  332.7 31.9 %all-to-all-start.5 = ((bf16[8,152,896]{2,1,0:T(8,128)(2,1)}), bf16[8,152,896]{2,1,0:T(8,128)(2,1)}, u32[]{:S(2)}, u32[]{:S(2)}) async-start(bf16[8,152,896]{2,1,0:T(8,128)(2,1)} %bitcast.87), calls=%async_computation.5 | async-start | bytes 4358144 | tf_op jit(solution)/shard_map/all_to_all | solution.py:637
  364.6 42.0 %all-to-all-start.7 = ((bf16[8,152,1280]{2,1,0:T(8,128)(2,1)}), bf16[8,152,1280]{2,1,0:T(8,128)(2,1)}, u32[]{:S(2)}, u32[]{:S(2)}) async-start(bf16[8,152,1280]{2,1,0:T(8,128)(2,1)} %bitcast.86), calls=%async_computation.7 | async-start | bytes 6225920 | tf_op jit(solution)/shard_map/all_to_all | solution.py:637
  376.5 13.9 %collective-permute-start.19 = (bf16[128,896]{1,0:T(8,128)(2,1)S(1)}, bf16[128,896]{1,0:T(8,128)(2,1)S(1)}, u32[]{:S(2)}, u32[]{:S(2)}) collective-permute-start(bf16[128,896]{1,0:T(8,128)(2,1)S(1)} %get-tuple-element.108), channel_id=1, source_target_pairs={{0,24},{8,0},{16,8},{24,16},{1,25},{9,1},{17,9},{25,17},{2,26},{10... | collective-permute-start | bytes 688136 | tf_op jit(solution)/shard_map/ppermute | solution.py:653
  379.7 21.4 %collective-permute-start.20 = (bf16[128,896]{1,0:T(8,128)(2,1)S(1)}, bf16[128,896]{1,0:T(8,128)(2,1)S(1)}, u32[]{:S(2)}, u32[]{:S(2)}) collective-permute-start(bf16[128,896]{1,0:T(8,128)(2,1)S(1)} %get-tuple-element.109), channel_id=1, source_target_pairs={{0,16},{8,24},{16,0},{24,8},{1,17},{9,25},{17,1},{25,9},{2,18},{10... | collective-permute-start | bytes 688136 | tf_op jit(solution)/shard_map/ppermute | solution.py:653
  380.3 20.8 %collective-permute-start.21 = (bf16[128,896]{1,0:T(8,128)(2,1)S(1)}, bf16[128,896]{1,0:T(8,128)(2,1)S(1)}, u32[]{:S(2)}, u32[]{:S(2)}) collective-permute-start(bf16[128,896]{1,0:T(8,128)(2,1)S(1)} %get-tuple-element.110), channel_id=1, source_target_pairs={{0,8},{8,16},{16,24},{24,0},{1,9},{9,17},{17,25},{25,1},{2,10},{10... | collective-permute-start | bytes 688136 | tf_op jit(solution)/shard_map/ppermute | solution.py:653
  406.6 44.0 %all-to-all-start.6 = ((bf16[8,152,1280]{2,1,0:T(8,128)(2,1)}), bf16[8,152,1280]{2,1,0:T(8,128)(2,1)S(1)}, u32[]{:S(2)}, u32[]{:S(2)}) async-start(bf16[8,152,1280]{2,1,0:T(8,128)(2,1)} %bitcast.85), calls=%async_computation.6 | async-start | bytes 6225920 | tf_op jit(solution)/shard_map/all_to_all | solution.py:637
  410.2 81.4 %all-gather.9.cloned.1.call-start = ((), (), s32[]{:S(2)}) async-start(), calls=%async_computation.14 | async-start | bytes 4718592 | tf_op jit(solution)/shard_map/all_gather | solution.py:634
  416.5 16.7 %collective-permute-start.22 = (bf16[128,1280]{1,0:T(8,128)(2,1)S(1)}, bf16[128,1280]{1,0:T(8,128)(2,1)S(1)}, u32[]{:S(2)}, u32[]{:S(2)}) collective-permute-start(bf16[128,1280]{1,0:T(8,128)(2,1)S(1)} %get-tuple-element.119), channel_id=1, source_target_pairs={{0,24},{8,0},{16,8},{24,16},{1,25},{9,1},{17,9},{25,17},{2,26},{10... | collective-permute-start | bytes 983048 | tf_op jit(solution)/shard_map/ppermute | solution.py:653
  419.7 29.8 %collective-permute-start.23 = (bf16[128,1280]{1,0:T(8,128)(2,1)S(1)}, bf16[128,1280]{1,0:T(8,128)(2,1)S(1)}, u32[]{:S(2)}, u32[]{:S(2)}) collective-permute-start(bf16[128,1280]{1,0:T(8,128)(2,1)S(1)} %get-tuple-element.120), channel_id=1, source_target_pairs={{0,16},{8,24},{16,0},{24,8},{1,17},{9,25},{17,1},{25,9},{2,18},{10... | collective-permute-start | bytes 983048 | tf_op jit(solution)/shard_map/ppermute | solution.py:653
  420.3 29.2 %collective-permute-start.24 = (bf16[128,1280]{1,0:T(8,128)(2,1)S(1)}, bf16[128,1280]{1,0:T(8,128)(2,1)S(1)}, u32[]{:S(2)}, u32[]{:S(2)}) collective-permute-start(bf16[128,1280]{1,0:T(8,128)(2,1)S(1)} %get-tuple-element.121), channel_id=1, source_target_pairs={{0,8},{8,16},{16,24},{24,0},{1,9},{9,17},{17,25},{25,1},{2,10},{10... | collective-permute-start | bytes 983048 | tf_op jit(solution)/shard_map/ppermute | solution.py:653
  454.8 91.5 %reduce-scatter.2.cloned.1.call-start = ((), (), s32[]{:S(2)}) async-start(), calls=%async_computation.15 | async-start | bytes 2621440 | tf_op jit(solution)/shard_map/reduce_scatter | solution.py:794
  459.8 9.4 %collective-permute-start.25 = (bf16[128,1280]{1,0:T(8,128)(2,1)S(1)}, bf16[128,1280]{1,0:T(8,128)(2,1)S(1)}, u32[]{:S(2)}, u32[]{:S(2)}) collective-permute-start(bf16[128,1280]{1,0:T(8,128)(2,1)S(1)} %get-tuple-element.125), channel_id=1, source_target_pairs={{0,24},{8,0},{16,8},{24,16},{1,25},{9,1},{17,9},{25,17},{2,26},{10... | collective-permute-start | bytes 983048 | tf_op jit(solution)/shard_map/ppermute | solution.py:658
  460.0 28.5 %collective-permute-start.27 = (bf16[128,1280]{1,0:T(8,128)(2,1)}, bf16[128,1280]{1,0:T(8,128)(2,1)S(1)}, u32[]{:S(2)}, u32[]{:S(2)}) collective-permute-start(bf16[128,1280]{1,0:T(8,128)(2,1)} %get-tuple-element.127), channel_id=1, source_target_pairs={{0,8},{8,16},{16,24},{24,0},{1,9},{9,17},{17,25},{25,1},{2,10},{10... | collective-permute-start | bytes 983048 | tf_op jit(solution)/shard_map/ppermute | solution.py:658
  469.3 19.4 %collective-permute-start.26 = (bf16[128,1280]{1,0:T(8,128)(2,1)S(1)}, bf16[128,1280]{1,0:T(8,128)(2,1)S(1)}, u32[]{:S(2)}, u32[]{:S(2)}) collective-permute-start(bf16[128,1280]{1,0:T(8,128)(2,1)S(1)} %add_convert_fusion.1), channel_id=1, source_target_pairs={{0,24},{8,0},{16,8},{24,16},{1,25},{9,1},{17,9},{25,17},{2,26},{10... | collective-permute-start | bytes 983048 | tf_op jit(solution)/shard_map/ppermute | solution.py:658
  500.5 35.1 %all-to-all-start.9 = ((bf16[8,152,768]{2,1,0:T(8,128)(2,1)}), bf16[8,152,768]{2,1,0:T(8,128)(2,1)S(1)}, u32[]{:S(2)}, u32[]{:S(2)}) async-start(bf16[8,152,768]{2,1,0:T(8,128)(2,1)} %bitcast.89), calls=%async_computation.9 | async-start | bytes 3735552 | tf_op jit(solution)/shard_map/all_to_all | solution.py:637
  548.4 70.6 %all-to-all-start.10 = ((bf16[8,144,2048]{2,1,0:T(8,128)(2,1)}), bf16[8,144,2048]{2,1,0:T(8,128)(2,1)}, u32[]{:S(2)}, u32[]{:S(2)}) async-start(bf16[8,144,2048]{2,1,0:T(8,128)(2,1)} %unproject.1), calls=%async_computation.11 | async-start | bytes 9437184 | tf_op jit(solution)/shard_map/all_to_all | solution.py:637
  553.2 8.6 %collective-permute-start.28 = (bf16[128,768]{1,0:T(8,128)(2,1)S(1)}, bf16[128,768]{1,0:T(8,128)(2,1)S(1)}, u32[]{:S(2)}, u32[]{:S(2)}) collective-permute-start(bf16[128,768]{1,0:T(8,128)(2,1)S(1)} %copy-done.85), channel_id=1, source_target_pairs={{0,24},{8,0},{16,8},{24,16},{1,25},{9,1},{17,9},{25,17},{2,26},{10... | collective-permute-start | bytes 589832 | tf_op jit(solution)/shard_map/ppermute | solution.py:658
  556.5 10.3 %collective-permute-start.30 = (bf16[128,768]{1,0:T(8,128)(2,1)S(1)}, bf16[128,768]{1,0:T(8,128)(2,1)S(1)}, u32[]{:S(2)}, u32[]{:S(2)}) collective-permute-start(bf16[128,768]{1,0:T(8,128)(2,1)S(1)} %copy-done.83), channel_id=1, source_target_pairs={{0,8},{8,16},{16,24},{24,0},{1,9},{9,17},{17,25},{25,1},{2,10},{10... | collective-permute-start | bytes 589832 | tf_op jit(solution)/shard_map/ppermute | solution.py:658
  561.9 8.8 %collective-permute-start.29 = (bf16[128,768]{1,0:T(8,128)(2,1)S(1)}, bf16[128,768]{1,0:T(8,128)(2,1)S(1)}, u32[]{:S(2)}, u32[]{:S(2)}) collective-permute-start(bf16[128,768]{1,0:T(8,128)(2,1)S(1)} %add_convert_fusion.2), channel_id=1, source_target_pairs={{0,24},{8,0},{16,8},{24,16},{1,25},{9,1},{17,9},{25,17},{2,26},{10... | collective-permute-start | bytes 589832 | tf_op jit(solution)/shard_map/ppermute | solution.py:658
  566.3 19.3 %collective-permute-start.34 = (bf16[2048,128]{0,1:T(8,128)(2,1)S(1)}, bf16[2048,128]{0,1:T(8,128)(2,1)S(1)}, u32[]{:S(2)}, u32[]{:S(2)}) collective-permute-start(bf16[2048,128]{0,1:T(8,128)(2,1)S(1)} %pad_maximum_fusion.4), channel_id=1, source_target_pairs={{0,1},{1,0},{2,3},{3,2},{4,5},{5,4},{6,7},{7,6},{8,9},{9,8},{10,11... | collective-permute-start | bytes 1572872 | tf_op jit(solution)/shard_map/ppermute | solution.py:824
  570.9 14.8 %collective-permute-start.31 = (bf16[512,512]{1,0:T(8,128)(2,1)S(1)}, bf16[512,512]{1,0:T(8,128)(2,1)S(1)}, u32[]{:S(2)}, u32[]{:S(2)}) collective-permute-start(bf16[512,512]{1,0:T(8,128)(2,1)S(1)} %get-tuple-element.164), channel_id=1, source_target_pairs={{0,24},{8,0},{16,8},{24,16},{1,25},{9,1},{17,9},{25,17},{2,26},{10... | collective-permute-start | bytes 1572872 | tf_op jit(solution)/shard_map/ppermute | solution.py:658
  585.6 16.7 %collective-permute-start.33 = (bf16[512,512]{1,0:T(8,128)(2,1)S(1)}, bf16[512,512]{1,0:T(8,128)(2,1)S(1)}, u32[]{:S(2)}, u32[]{:S(2)}) collective-permute-start(bf16[512,512]{1,0:T(8,128)(2,1)S(1)} %get-tuple-element.165), channel_id=1, source_target_pairs={{0,8},{8,16},{16,24},{24,0},{1,9},{9,17},{17,25},{25,1},{2,10},{10... | collective-permute-start | bytes 1572872 | tf_op jit(solution)/shard_map/ppermute | solution.py:658
  587.5 14.9 %collective-permute-start.35 = (bf16[512,128]{0,1:T(8,128)(2,1)}, bf16[512,128]{0,1:T(8,128)(2,1)S(1)}, u32[]{:S(2)}, u32[]{:S(2)}) collective-permute-start(bf16[512,128]{0,1:T(8,128)(2,1)} %get-tuple-element.180), channel_id=1, source_target_pairs={{0,24},{8,0},{16,8},{24,16},{1,25},{9,1},{17,9},{25,17},{2,26},{10... | collective-permute-start | bytes 393224 | tf_op jit(solution)/shard_map/ppermute | solution.py:653
  591.3 19.2 %collective-permute-start.36 = (bf16[512,128]{0,1:T(8,128)(2,1)}, bf16[512,128]{0,1:T(8,128)(2,1)}, u32[]{:S(2)}, u32[]{:S(2)}) collective-permute-start(bf16[512,128]{0,1:T(8,128)(2,1)} %get-tuple-element.182), channel_id=1, source_target_pairs={{0,16},{8,24},{16,0},{24,8},{1,17},{9,25},{17,1},{25,9},{2,18},{10... | collective-permute-start | bytes 393224 | tf_op jit(solution)/shard_map/ppermute | solution.py:653
  591.3 19.4 %collective-permute-start.37 = (bf16[512,128]{0,1:T(8,128)(2,1)S(1)}, bf16[512,128]{0,1:T(8,128)(2,1)}, u32[]{:S(2)}, u32[]{:S(2)}) collective-permute-start(bf16[512,128]{0,1:T(8,128)(2,1)S(1)} %get-tuple-element.181), channel_id=1, source_target_pairs={{0,8},{8,16},{16,24},{24,0},{1,9},{9,17},{17,25},{25,1},{2,10},{10... | collective-permute-start | bytes 393224 | tf_op jit(solution)/shard_map/ppermute | solution.py:653
  591.9 27.0 %collective-permute-start.32 = (bf16[512,512]{1,0:T(8,128)(2,1)}, bf16[512,512]{1,0:T(8,128)(2,1)S(1)}, u32[]{:S(2)}, u32[]{:S(2)}) collective-permute-start(bf16[512,512]{1,0:T(8,128)(2,1)} %add_convert_fusion), channel_id=1, source_target_pairs={{0,24},{8,0},{16,8},{24,16},{1,25},{9,1},{17,9},{25,17},{2,26},{10... | collective-permute-start | bytes 1572872 | tf_op jit(solution)/shard_map/ppermute | solution.py:658
  622.7 5.6 collective-permute-start.38
  628.3 5.3 collective-permute-start.39
  (106 other events, 659.1 us)
Sparse Core Ops, SparseCore 0:
  10.9 39.4 all-gather.4
  88.7 76.2 all-gather.6
  454.9 36.6 all-gather.8
  500.6 43.8 reduce-scatter.1
